TPU v7x, 32 devices: a whole 2x2x4 slice. The times are simulated.
32 devices in a mesh: vox: 4 (over x, core), dp: 8 (over z, y).
Axes of the slice: x: 2, y: 2, z: 4, core: 2. Of those that a mesh axis runs over, the one named last changes fastest.
Arguments:
- fmri: bfloat16 [2048, 8192], P('dp', 'vox'), may hold values from -6 to 6
- subject: int32 [2048, 1], P('dp'), may hold values from 0 to 7; in each aligned block of 256 rows (0 to 255, 256 to 511, ...) at most 64 rows name the same one
- ridge_maps: bfloat16 [8, 8192, 4096], P('dp', 'vox'), may hold values from -0.09375 to 0.09375
- voxel_count: int32 [8], replicated, may hold values from 4096 to 8192, as said below
- w_first: bfloat16 [8192, 256], replicated, may hold values from -0.125 to 0.125
- w_second: bfloat16 [4096, 128], replicated, may hold values from -0.1875 to 0.1875
- w_third: bfloat16 [2048, 64], replicated, may hold values from -0.25 to 0.25
- target: bfloat16 [2048, 16, 32, 64], P(('dp', 'vox')), may hold values from -6 to 6
Outputs:
- decoded: bfloat16 [2048, 16, 32, 64], P(('dp', 'vox'))
- grad_first: bfloat16 [8192, 256], replicated
- grad_second: bfloat16 [4096, 128], replicated
- grad_third: bfloat16 [2048, 64], replicated
Inputs may be any that keep to these rules, and one draw needn't show every extreme that they name: Among the 256 samples of one index of dp (aligned blocks) no subject appears more than 64 times, and in some block some subject appears exactly 64 times; every subject appears somewhere. Readings of a subject at voxel positions voxel_count or beyond are unused; some subject has 8192 and some 8192 // 2.
All inputs are finite; a program needn't handle non-finite values.
Results may differ from a plain program's by a relative error of at most 0.008.
Values may be sent and summed in bfloat16 or wider, within the bound.
No kernel may reach another device: no remote copies, remote signals or barrier semaphores. Data moves between devices by JAX's collectives and lax.ppermute only.
A program may use at most 384 MiB of HBM per device.

v0:
```python
import functools
import jax
import jax.numpy as jnp
from jax import lax
from jax.experimental import pallas as pl
from jax.sharding import PartitionSpec as P
from jax.experimental.pallas import tpu as pltpu

H0 = 2
W0 = 4
SAMP_DEV = 256
ROW_TAPS = ((1, 3), (2, 0))
ROW_SHIFT = (-1, 1)
COL_TAPS = (1, 2, 3, 0)
VMEM_BYTES = 60 * 1024 * 1024


def paired_weight(weights, in_chan):
    out_chan = weights.shape[1]
    kernel = weights.reshape(4, 4, in_chan, out_chan)
    halves = []
    for parity in (0, 1):
        rows = []
        for row_tap in ROW_TAPS[parity]:
            rows.append(jnp.concatenate([kernel[row_tap, col_tap] for col_tap in COL_TAPS], axis=1))
        halves.append(jnp.concatenate(rows, axis=0))
    return jnp.stack(halves)


def product(left, right):
    return jnp.dot(left, right, preferred_element_type=jnp.float32)


def product_nt(left, right):
    return lax.dot_general(left, right, (((1,), (1,)), ((), ())), preferred_element_type=jnp.float32)


def product_tn(left, right):
    return lax.dot_general(left, right, (((0,), (0,)), ((), ())), preferred_element_type=jnp.float32)


def gelu_pair(value):
    root = 0.7978845608028654
    square = value * value
    tanh = jnp.tanh(root * (value + 0.044715 * (square * value)))
    half = 0.5 * (1.0 + tanh)
    slope = half + (0.5 * value) * (1.0 - tanh * tanh) * (root + (3 * 0.044715 * root) * square)
    return value * half, slope


def up_rows(product_ref, act_ref, slope_ref, act_row, slope_row, count, breadth, out_chan):
    width = 2 * out_chan
    for col in range(breadth):
        here = pl.ds(col * count, count)
        for col_par in (0, 1):
            lanes = pl.ds(col_par * out_chan, out_chan)
            side = pl.ds(width + col_par * out_chan, out_chan)
            value = product_ref[here, lanes]
            other = col - 1 if col_par == 0 else col + 1
            if 0 <= other < breadth:
                value = value + product_ref[pl.ds(other * count, count), side]
            act, slope = gelu_pair(value)
            rows = pl.ds((2 * col + col_par) * count, count)
            act_ref[act_row, rows, :] = act.astype(jnp.bfloat16)
            slope_ref[slope_row, rows, :] = slope


def forward_kernel(count, latent_ref, w_one_ref, w_two_ref, act_one_ref, slope_one_ref, act_two_ref, slope_two_ref, tmp_one, tmp_two):
    in_chan = w_one_ref.shape[1] // 2
    mid_chan = w_two_ref.shape[1] // 2
    out_chan = w_two_ref.shape[2] // 4

    def latent_row(row):
        return jnp.concatenate(
            [latent_ref[:, pl.ds((row * W0 + col) * in_chan, in_chan)] for col in range(W0)], axis=0
        )

    for row in range(H0):
        for parity in (0, 1):
            tmp_one[...] = product(latent_row(row), w_one_ref[parity, :in_chan, :])
            other = row + ROW_SHIFT[parity]
            if 0 <= other < H0:
                tmp_one[...] += product(latent_row(other), w_one_ref[parity, in_chan:, :])
            at = 2 * row + parity
            up_rows(tmp_one, act_one_ref, slope_one_ref, at, at, count, W0, mid_chan)
    height = 2 * H0
    breadth = 2 * W0
    act_two_ref[0] = jnp.zeros_like(act_two_ref[0])
    act_two_ref[2 * height + 1] = jnp.zeros_like(act_two_ref[0])
    for row in range(height):
        for parity in (0, 1):
            tmp_two[...] = product(act_one_ref[row], w_two_ref[parity, :mid_chan, :])
            other = row + ROW_SHIFT[parity]
            if 0 <= other < height:
                tmp_two[...] += product(act_one_ref[other], w_two_ref[parity, mid_chan:, :])
            at = 2 * row + parity
            up_rows(tmp_two, act_two_ref, slope_two_ref, at + 1, at, count, breadth, out_chan)


def last_kernel(count, act_ref, slope_ref, w_ref, target_ref, decoded_ref, grad_ref, kgrad_ref, tmp, grads, adj):
    step = pl.program_id(0)
    steps = pl.num_programs(0)
    breadth = act_ref.shape[1] // count
    in_chan = act_ref.shape[2]
    lanes = 2 * (w_ref.shape[2] // 4)

    @pl.when(step == 0)
    def _():
        adj[...] = jnp.zeros_like(adj)
        kgrad_ref[...] = jnp.zeros_like(kgrad_ref)
        grads[...] = jnp.zeros_like(grads)

    low = lax.broadcasted_iota(jnp.int32, (count, lanes), 1) < lanes // 2
    for parity in (0, 1):
        other = step + 1 + ROW_SHIFT[parity]
        left = jnp.concatenate([act_ref[step + 1], act_ref[other]], axis=1)
        tmp[...] = product(left, w_ref[parity])
        zero = jnp.zeros((count, lanes), jnp.float32)
        for col in range(breadth):
            here = pl.ds(col * count, count)
            before = tmp[pl.ds((col - 1) * count, count), lanes:] if col > 0 else zero
            after = tmp[pl.ds((col + 1) * count, count), lanes:] if col < breadth - 1 else zero
            value = tmp[here, :lanes] + jnp.where(low, before, after)
            decoded_ref[parity, here, :] = value.astype(jnp.bfloat16)
            grad = (value - target_ref[parity, here, :].astype(jnp.float32)) * (1.0 / SAMP_DEV)
            grads[pl.ds((col + 1) * count, count), :] = grad
        pieces = []
        for col in range(breadth):
            before = grads[pl.ds(col * count, count), :]
            here = grads[pl.ds((col + 1) * count, count), :]
            after = grads[pl.ds((col + 2) * count, count), :]
            side = jnp.where(low, after, before)
            pieces.append(jnp.concatenate([here.astype(jnp.bfloat16), side.astype(jnp.bfloat16)], axis=1))
        taps = jnp.concatenate(pieces, axis=0)
        kgrad_ref[parity] += product_tn(left, taps)
        back = product_nt(taps, w_ref[parity])
        adj[step + 1] += back[:, :in_chan]
        adj[other] += back[:, in_chan:]

    @pl.when(step == steps - 1)
    def _():
        def finish(row, carry):
            upstream = adj[row + 1].astype(jnp.bfloat16).astype(jnp.float32)
            grad_ref[row] = (upstream * slope_ref[row]).astype(jnp.bfloat16)
            return carry

        lax.fori_loop(0, steps, finish, 0)


def side_taps(grad_ref, row, count, breadth):
    def at(col):
        if 0 <= col < 2 * breadth:
            return grad_ref[row, pl.ds(col * count, count), :]
        return jnp.zeros((count, grad_ref.shape[2]), jnp.bfloat16)

    pieces = []
    for col in range(breadth):
        pieces.append(jnp.concatenate([at(2 * col), at(2 * col + 1), at(2 * col + 2), at(2 * col - 1)], axis=1))
    return jnp.concatenate(pieces, axis=0)


def backward_kernel(count, latent_ref, act_ref, slope_ref, w_ref, grad_two_ref, kgrad_one_ref, kgrad_two_ref, grad_one, adj, total_one, total_two):
    height = act_ref.shape[0]
    breadth = act_ref.shape[1] // count
    mid_chan = act_ref.shape[2]
    out_chan = grad_two_ref.shape[2]
    for row in range(height):
        for parity in (0, 1):
            taps = side_taps(grad_two_ref, 2 * row + parity, count, breadth)
            back = product_nt(taps, w_ref[parity])
            other = row + ROW_SHIFT[parity]
            if parity == 0 and row == 0:
                adj[0] = back[:, :mid_chan]
            else:
                adj[row] += back[:, :mid_chan]
            if 0 <= other < height:
                if parity == 0:
                    adj[other] += back[:, mid_chan:]
                else:
                    adj[other] = back[:, mid_chan:]
            mine = product_tn(act_ref[row], taps)
            if row == 0:
                total_two[parity, :mid_chan, :] = mine
            else:
                total_two[parity, :mid_chan, :] += mine
            if 0 <= other < height:
                far = product_tn(act_ref[other], taps)
                if row == (1 if parity == 0 else 0):
                    total_two[parity, mid_chan:, :] = far
                else:
                    total_two[parity, mid_chan:, :] += far
    for parity in (0, 1):
        for which in (0, 1):
            row_tap = ROW_TAPS[parity][which]
            for slot, col_tap in enumerate(COL_TAPS):
                rows = pl.ds((row_tap * 4 + col_tap) * mid_chan, mid_chan)
                kgrad_two_ref[rows, :] = total_two[
                    parity, which * mid_chan:(which + 1) * mid_chan, slot * out_chan:(slot + 1) * out_chan
                ].astype(kgrad_two_ref.dtype)
    for row in range(height):
        upstream = adj[row].astype(jnp.bfloat16).astype(jnp.float32)
        grad_one[row] = (upstream * slope_ref[row]).astype(jnp.bfloat16)
    in_chan = latent_ref.shape[1] // (H0 * W0)

    def latent_row(row):
        return jnp.concatenate(
            [latent_ref[:, pl.ds((row * W0 + col) * in_chan, in_chan)] for col in range(W0)], axis=0
        )

    for parity in (0, 1):
        for which in (0, 1):
            lefts = []
            rights = []
            for row in range(H0):
                source = row + (ROW_SHIFT[parity] if which else 0)
                if 0 <= source < H0:
                    lefts.append(latent_row(source))
                    rights.append(side_taps(grad_one, 2 * row + parity, count, W0))
            left = jnp.concatenate(lefts, axis=0) if len(lefts) > 1 else lefts[0]
            right = jnp.concatenate(rights, axis=0) if len(rights) > 1 else rights[0]
            total_one[...] = product_tn(left, right)
            row_tap = ROW_TAPS[parity][which]
            for slot, col_tap in enumerate(COL_TAPS):
                rows = pl.ds((row_tap * 4 + col_tap) * in_chan, in_chan)
                kgrad_one_ref[rows, :] = total_one[:, slot * mid_chan:(slot + 1) * mid_chan].astype(kgrad_one_ref.dtype)


def params(steps=0):
    if steps:
        return pltpu.CompilerParams(vmem_limit_bytes=VMEM_BYTES, dimension_semantics=("arbitrary",))
    return pltpu.CompilerParams(vmem_limit_bytes=VMEM_BYTES)


def forward(latent, w_one, w_two):
    count = latent.shape[0]
    mid_chan = w_two.shape[1] // 2
    out_chan = w_two.shape[2] // 4
    height, breadth = 2 * H0, 2 * W0
    return pl.pallas_call(
        functools.partial(forward_kernel, count),
        name="decoder_forward",
        out_shape=(
            jax.ShapeDtypeStruct((height, breadth * count, mid_chan), jnp.bfloat16),
            jax.ShapeDtypeStruct((height, breadth * count, mid_chan), jnp.float32),
            jax.ShapeDtypeStruct((2 * height + 2, 2 * breadth * count, out_chan), jnp.bfloat16),
            jax.ShapeDtypeStruct((2 * height, 2 * breadth * count, out_chan), jnp.float32),
        ),
        scratch_shapes=[
            pltpu.VMEM((W0 * count, 4 * mid_chan), jnp.float32),
            pltpu.VMEM((breadth * count, 4 * out_chan), jnp.float32),
        ],
        compiler_params=params(),
    )(latent, w_one, w_two)


def last_layer(act_two, slope_two, w_three, target):
    steps, rows, in_chan = slope_two.shape
    count = rows // (4 * W0)
    lanes = target.shape[2]
    whole = lambda shape: pl.BlockSpec(shape, lambda step: (0,) * len(shape))
    return pl.pallas_call(
        functools.partial(last_kernel, count),
        name="decoder_last",
        grid=(steps,),
        in_specs=[
            whole(act_two.shape),
            whole(slope_two.shape),
            whole(w_three.shape),
            pl.BlockSpec((2, rows, lanes), lambda step: (step, 0, 0)),
        ],
        out_specs=(
            pl.BlockSpec((2, rows, lanes), lambda step: (step, 0, 0)),
            whole(slope_two.shape),
            whole(w_three.shape),
        ),
        out_shape=(
            jax.ShapeDtypeStruct(target.shape, jnp.bfloat16),
            jax.ShapeDtypeStruct(slope_two.shape, jnp.bfloat16),
            jax.ShapeDtypeStruct(w_three.shape, jnp.float32),
        ),
        scratch_shapes=[
            pltpu.VMEM((rows, 2 * lanes), jnp.float32),
            pltpu.VMEM((rows + 2 * count, lanes), jnp.float32),
            pltpu.VMEM((steps + 2, rows, in_chan), jnp.float32),
        ],
        compiler_params=params(1),
    )(act_two, slope_two, w_three, target)


def backward(latent, act_one, slope_one, w_two, grad_two, kind):
    count = latent.shape[0]
    in_chan = latent.shape[1] // (H0 * W0)
    mid_chan = act_one.shape[2]
    out_chan = grad_two.shape[2]
    return pl.pallas_call(
        functools.partial(backward_kernel, count),
        name="decoder_backward",
        out_shape=(
            jax.ShapeDtypeStruct((16 * in_chan, mid_chan), kind),
            jax.ShapeDtypeStruct((16 * mid_chan, out_chan), kind),
        ),
        scratch_shapes=[
            pltpu.VMEM(act_one.shape, jnp.bfloat16),
            pltpu.VMEM(act_one.shape, jnp.float32),
            pltpu.VMEM((in_chan, 4 * mid_chan), jnp.float32),
            pltpu.VMEM(w_two.shape, jnp.float32),
        ],
        compiler_params=params(),
    )(latent, act_one, slope_one, w_two, grad_two)


def unpaired_third(paired, in_chan):
    out_chan = paired.shape[2] // 4
    view = paired.reshape(2, 2, in_chan, 4, out_chan)
    pieces = [None] * 16
    for parity in (0, 1):
        for which in (0, 1):
            for slot, col_tap in enumerate(COL_TAPS):
                pieces[ROW_TAPS[parity][which] * 4 + col_tap] = view[parity, which, :, slot, :]
    return jnp.concatenate(pieces, axis=0)


def spatial_first(grid):
    count, height, breadth, chan = grid.shape
    return (
        grid.reshape(count, height, breadth // 2, 2 * chan)
        .transpose(1, 2, 0, 3)
        .reshape(height, breadth // 2 * count, 2 * chan)
    )


def sample_first(rows, count, chan):
    height = rows.shape[0]
    return (
        rows.reshape(height, -1, count, 2 * chan)
        .transpose(2, 0, 1, 3)
        .reshape(count, height, -1, chan)
    )


def rounded(values):
    return lax.optimization_barrier(values.astype(jnp.bfloat16))


def bit_pairs(axis):
    size = lax.axis_size(axis)
    bits = []
    bit = 1
    while bit < size:
        bits.append((axis, bit))
        bit *= 2
    return bits


def exchanged(values, hop):
    axis, bit = hop
    return lax.ppermute(values, axis, [(at, at ^ bit) for at in range(lax.axis_size(axis))])


def upper(hop):
    axis, bit = hop
    return (lax.axis_index(axis) // bit) % 2


def summed_share(values, hops):
    for hop in hops:
        half = values.shape[0] // 2
        side = upper(hop)
        sent = lax.dynamic_slice_in_dim(values, (1 - side) * half, half, 0).astype(jnp.bfloat16)
        kept = lax.dynamic_slice_in_dim(values, side * half, half, 0).astype(jnp.float32)
        values = kept + exchanged(sent, hop).astype(jnp.float32)
    return values


def all_shares(values, hops):
    for hop in reversed(hops):
        other = exchanged(values, hop)
        first = upper(hop) == 0
        values = jnp.concatenate(
            [jnp.where(first, values, other), jnp.where(first, other, values)], axis=0
        )
    return values


def all_summed(values, hops):
    return all_shares(summed_share(values, hops).astype(jnp.bfloat16), hops)


def shards(fmri, subject, ridge_maps, voxel_count, w_first, w_second, w_third, target):
    dp_count = lax.axis_size("dp")
    samp_dev = fmri.shape[0]
    vox_local = fmri.shape[1]
    capacity = max(2, 2 * samp_dev // dp_count)
    mid_chan = w_first.shape[1]
    last_chan = w_second.shape[1]
    owners = subject[:, 0]
    onehot = (owners[:, None] == jnp.arange(dp_count, dtype=jnp.int32)[None, :]).astype(jnp.int32)
    earlier = jnp.cumsum(onehot, axis=0) - onehot
    slot_index = jnp.sum(earlier * onehot, axis=1)
    position = owners * capacity + slot_index
    buckets = jnp.zeros((dp_count * capacity, vox_local), fmri.dtype).at[position].set(fmri)
    buckets, target, w_first, w_second, w_third = lax.optimization_barrier(
        (buckets, target, w_first, w_second, w_third)
    )
    arrived = lax.all_to_all(
        buckets.reshape(dp_count, capacity, vox_local),
        "dp",
        split_axis=0,
        concat_axis=0,
        tiled=True,
    )
    pair_one = paired_weight(w_first, w_first.shape[0] // 16)
    pair_two = paired_weight(w_second, mid_chan)
    pair_three = paired_weight(w_third, last_chan)
    target_rows = spatial_first(target)
    arrived, pair_one, pair_two, pair_three, target_rows = lax.optimization_barrier(
        (arrived, pair_one, pair_two, pair_three, target_rows)
    )
    subject_here = lax.axis_index("dp")
    voxel_ids = lax.axis_index("vox") * vox_local + jnp.arange(vox_local, dtype=jnp.int32)
    voxel_keep = (voxel_ids < voxel_count[subject_here]).astype(fmri.dtype)
    readings = arrived.reshape(dp_count * capacity, vox_local) * voxel_keep[None, :]
    partial_value = jnp.dot(readings, ridge_maps[0], preferred_element_type=jnp.float32)
    latent_part = rounded(lax.psum_scatter(partial_value, "vox", scatter_dimension=1, tiled=True))
    feat_local = latent_part.shape[1]
    returned = lax.all_to_all(
        latent_part.reshape(dp_count, capacity, feat_local),
        "dp",
        split_axis=0,
        concat_axis=0,
        tiled=True,
    )
    own_rows = returned.reshape(dp_count * capacity, feat_local)[position]
    latent = lax.all_to_all(own_rows, "vox", split_axis=0, concat_axis=1, tiled=True)
    count = latent.shape[0]
    act_one, slope_one, act_two, slope_two = forward(latent, pair_one, pair_two)
    decoded_rows, grad_two, paired_three = last_layer(act_two, slope_two, pair_three, target_rows)
    grad_first, grad_second = backward(latent, act_one, slope_one, pair_two, grad_two, jnp.bfloat16)
    vox_bits = bit_pairs("vox")
    dp_bits = bit_pairs("dp")
    core, across = vox_bits[:1], vox_bits[1:]
    near, along = dp_bits[:1], dp_bits[:0:-1]
    half = grad_first.shape[0] // 2
    lanes = grad_second.shape[1]
    flat_three = paired_three.astype(jnp.bfloat16)
    pieces = [flat_three[:, :, at:at + lanes].reshape(-1, lanes) for at in range(0, flat_three.shape[2], lanes)]
    small = jnp.concatenate([grad_second] + pieces, axis=0)
    small = all_summed(small, core + along + across + near)
    upper_half = all_summed(grad_first[:half], core + across + near + along)
    lower_half = all_summed(grad_first[half:], core + near + across + along)
    total_first = jnp.concatenate([upper_half, lower_half], axis=0)
    total_second = small[: grad_second.shape[0]]
    tail = small[grad_second.shape[0]:].reshape(len(pieces), 2, -1, lanes)
    total_third = unpaired_third(jnp.concatenate([tail[at] for at in range(len(pieces))], axis=2), last_chan)
    decoded = sample_first(decoded_rows, count, w_third.shape[1])
    return (decoded, total_first, total_second, total_third)


def solution(mesh):
    placed = (
        P("dp", "vox"),
        P("dp", None),
        P("dp", "vox", None),
        P(),
        P(),
        P(),
        P(),
        P(("dp", "vox"), None, None, None),
    )
    return jax.shard_map(
        shards,
        mesh=mesh,
        in_specs=placed,
        out_specs=(P(("dp", "vox"), None, None, None), P(), P(), P()),
        check_vma=False,
    )
```

profile of v0, /device:TPU:0, one launch (start us, length us, event | category | flops | bytes accessed | tf_op | source)
XLA Modules:
  0.0 390.6 jit_solution(212533271655131012)
XLA Ops:
  10.1 4.4 %scatter_custom_fusion = bf16[512,2048]{1,0:T(8,128)(2,1)} fusion(s32[256]{0:T(256)S(1)} %bitcast.201, bf16[256,2048]{1,0:T(8,128)(2,1)} %param.8, bf16[]{:T(256)} %constant.196.clone.1), kind=kCustom, calls=%fused_computation.21 | custom fusion | bytes 2097664 | tf_op jit(solution)/shard_map/scatter | solution.py:401
  14.5 7.4 %all-to-all-start = ((bf16[8,64,2048]{2,1,0:T(8,128)(2,1)}), bf16[8,64,2048]{2,1,0:T(8,128)(2,1)S(1)}, u32[]{:S(2)}, u32[]{:S(2)}) async-start(bf16[8,64,2048]{2,1,0:T(8,128)(2,1)} %bitcast.186), calls=%async_computation | async-start | bytes 4194304 | tf_op jit(solution)/shard_map/all_to_all | solution.py:405
  22.8 11.3 %reshape.90 = bf16[64,16,16,128]{3,2,1,0:T(8,128)(2,1)} reshape(bf16[64,16,32,64]{3,2,1,0:T(8,128)(2,1)} %param.15) | data formatting | bytes 8388608 | tf_op jit(solution)/shard_map/reshape | solution.py:326
  34.1 6.9 %copy.239 = bf16[64,16,16,128]{3,0,2,1:T(8,128)(2,1)} copy(bf16[64,16,16,128]{3,2,1,0:T(8,128)(2,1)} %reshape.90) | data formatting | bytes 8388608 | tf_op jit(solution)/shard_map/reshape | solution.py:326
  46.3 12.8 %maximum_bitcast_fusion = (bf16[1,1024,1024]{2,1,0:T(8,128)(2,1)S(1)}, bf16[1,1024,1024]{2,1,0:T(8,128)(2,1)S(1)}) fusion(bf16[512,256]{1,0:T(8,128)(2,1)S(1)} %get-tuple-element.53, bf16[512,256]{1,0:T(8,128)(2,1)S(1)} %get-tuple-element.54, bf16[512,256]{1,0:T(8,128)(2,1)S(1)} %get-tuple-element.55, bf16[512,256]{1,0:T(8,128)(2,1)S(1)} %get-tuple-element.56, ...), kind=kLoop, calls=%fused_computation.6 | loop fusion | flops 33554432 | bytes 8388608 | tf_op jit(solution)/shard_map/stack | solution.py:27
  61.4 8.8 %all-to-all-done = bf16[8,64,2048]{2,1,0:T(8,128)(2,1)S(1)} async-done(((bf16[8,64,2048]{2,1,0:T(8,128)(2,1)}), bf16[8,64,2048]{2,1,0:T(8,128)(2,1)S(1)}, u32[]{:S(2)}, u32[]{:S(2)}) %all-to-all-start) | async-done | bytes 2097184 | tf_op jit(solution)/shard_map/all_to_all | solution.py:405
  70.3 14.4 %fusion = f32[512,4096]{1,0:T(8,128)} fusion(bf16[512,2048]{1,0:T(8,128)(2,1)S(1)} %bitcast.191, bf16[1,2048,4096]{2,1,0:T(8,128)(2,1)} %param.10), kind=kOutput, calls=%fused_computation.2 | convolution fusion | flops 8589934592 | bytes 27262976 | tf_op jit(solution)/shard_map/dot_general | solution.py:423
  84.8 70.9 %reduce-scatter.2.cloned.1.call-done = f32[512,1024]{1,0:T(8,128)} async-done(((f32[512,4096]{1,0:T(8,128)}), f32[512,1024]{1,0:T(8,128)}) %reduce-scatter.2.cloned.1.call-update) | async-done | bytes 2097168 | tf_op jit(solution)/shard_map/reduce_scatter | solution.py:424
  155.7 2.7 convert_element_type.122
  158.4 5.7 %all-to-all-start.1 = ((bf16[8,64,1024]{2,1,0:T(8,128)(2,1)}), bf16[8,64,1024]{2,1,0:T(8,128)(2,1)S(1)}, u32[]{:S(2)}, u32[]{:S(2)}) async-start(bf16[8,64,1024]{2,1,0:T(8,128)(2,1)} %bitcast.69), calls=%async_computation.2 | async-start | bytes 2097152 | tf_op jit(solution)/shard_map/all_to_all | solution.py:426
  164.1 25.8 %all-to-all-done.1 = bf16[8,64,1024]{2,1,0:T(8,128)(2,1)S(1)} async-done(((bf16[8,64,1024]{2,1,0:T(8,128)(2,1)}), bf16[8,64,1024]{2,1,0:T(8,128)(2,1)S(1)}, u32[]{:S(2)}, u32[]{:S(2)}) %all-to-all-start.1) | async-done | bytes 1048608 | tf_op jit(solution)/shard_map/all_to_all | solution.py:426
  191.8 3.5 all-to-all-start.2
  195.3 8.8 %all-to-all-done.2 = bf16[4,64,1024]{2,1,0:T(8,128)(2,1)S(1)} async-done(((bf16[4,64,1024]{2,1,0:T(8,128)(2,1)}), bf16[4,64,1024]{2,1,0:T(8,128)(2,1)S(1)}, u32[]{:S(2)}, u32[]{:S(2)}) %all-to-all-start.2) | async-done | bytes 524320 | tf_op jit(solution)/shard_map/all_to_all | solution.py:434
  205.0 11.2 %decoder_forward.1 = (bf16[4,512,256]{2,1,0:T(8,128)(2,1)}, f32[4,512,256]{2,1,0:T(8,128)}, bf16[10,1024,128]{2,1,0:T(8,128)(2,1)}, f32[8,1024,128]{2,1,0:T(8,128)}) custom-call(bf16[64,4096]{1,0:T(8,128)(2,1)} %bitcast.187, bf16[2,1024,1024]{2,1,0:T(8,128)(2,1)} %pad_maximum_fusion.w_one_ref, bf16[2,512,512]{2,1,0:T(8,128)(2,1)} %pad_maximum_fusion.4.w_two_ref.w_ref), custom_call_target="tpu_custom_call" | custom-call | tf_op jit(solution)/shard_map/decoder_forward/pallas_call | solution.py:239
  216.2 15.7 %decoder_last.1 = (bf16[16,1024,128]{2,1,0:T(8,128)(2,1)}, bf16[8,1024,128]{2,1,0:T(8,128)(2,1)}, f32[2,256,256]{2,1,0:T(8,128)}) custom-call(bf16[10,1024,128]{2,1,0:T(8,128)(2,1)} %get-tuple-element.31.act_ref, f32[8,1024,128]{2,1,0:T(8,128)} %get-tuple-element.32.slope_ref, bf16[2,256,256]{2,1,0:T(8,128)(2,1)} %pad_maximum_fusion.11.w_ref, ...), custom_call_target="tpu_custom_call" | custom-call | tf_op jit(solution)/shard_map/decoder_last/pallas_call | solution.py:261
  233.1 10.7 %decoder_backward.1 = (bf16[8192,256]{1,0:T(8,128)(2,1)}, bf16[4096,128]{1,0:T(8,128)(2,1)}) custom-call(bf16[64,4096]{1,0:T(8,128)(2,1)} %bitcast.188, bf16[4,512,256]{2,1,0:T(8,128)(2,1)} %get-tuple-element.36.act_ref, f32[4,512,256]{2,1,0:T(8,128)} %get-tuple-element.37.slope_ref, bf16[2,512,512]{2,1,0:T(8,128)(2,1)} %pad_maximum_fusion.4.w_two_ref.w_ref, ...), custom_call_target="tpu_custom_call" | custom-call | tf_op jit(solution)/shard_map/decoder_backward/pallas_call | solution.py:295
  250.1 14.2 %collective-permute-done.21 = bf16[1280,128]{1,0:T(8,128)(2,1)S(1)} collective-permute-done((bf16[1280,128]{1,0:T(8,128)(2,1)S(1)}, bf16[1280,128]{1,0:T(8,128)(2,1)S(1)}, u32[]{:S(2)}, u32[]{:S(2)}) %collective-permute-start.21) | collective-permute-done | bytes 327712 | tf_op jit(solution)/shard_map/ppermute | solution.py:357
  265.6 5.0 %collective-permute-done.22 = bf16[640,128]{1,0:T(8,128)(2,1)S(1)} collective-permute-done((bf16[640,128]{1,0:T(8,128)(2,1)S(1)}, bf16[640,128]{1,0:T(8,128)(2,1)S(1)}, u32[]{:S(2)}, u32[]{:S(2)}) %collective-permute-start.22) | collective-permute-done | bytes 163872 | tf_op jit(solution)/shard_map/ppermute | solution.py:357
  271.1 4.2 %collective-permute-done.23 = bf16[320,128]{1,0:T(8,128)(2,1)} collective-permute-done((bf16[320,128]{1,0:T(8,128)(2,1)S(1)}, bf16[320,128]{1,0:T(8,128)(2,1)}, u32[]{:S(2)}, u32[]{:S(2)}) %collective-permute-start.23) | collective-permute-done | bytes 81952 | tf_op jit(solution)/shard_map/ppermute | solution.py:357
  279.1 6.9 %copy.241 = bf16[64,16,16,128]{3,2,1,0:T(8,128)(2,1)} copy(bf16[64,16,16,128]{3,0,2,1:T(8,128)(2,1)} %bitcast.190) | data formatting | bytes 8388608 | tf_op jit(solution)/shard_map/transpose | solution.py:336
  285.9 11.3 %reshape.95 = bf16[64,16,32,64]{3,2,1,0:T(8,128)(2,1)} reshape(bf16[64,16,16,128]{3,2,1,0:T(8,128)(2,1)} %copy.241) | data formatting | bytes 8388608 | tf_op jit(solution)/shard_map/reshape | solution.py:337
  303.6 3.2 collective-permute-done.26
  317.5 4.1 %collective-permute-done.11 = bf16[1024,256]{1,0:T(8,128)(2,1)S(1)} collective-permute-done((bf16[1024,256]{1,0:T(8,128)(2,1)S(1)}, bf16[1024,256]{1,0:T(8,128)(2,1)S(1)}, u32[]{:S(2)}, u32[]{:S(2)}) %collective-permute-start.11) | collective-permute-done | bytes 524320 | tf_op jit(solution)/shard_map/ppermute | solution.py:357
  321.8 3.4 collective-permute-done.2
  325.4 2.7 collective-permute-start.3
  328.3 3.6 collective-permute-start.13
  332.1 4.4 %collective-permute-done.3 = bf16[256,256]{1,0:T(8,128)(2,1)S(1)} collective-permute-done((bf16[256,256]{1,0:T(8,128)(2,1)S(1)}, bf16[256,256]{1,0:T(8,128)(2,1)S(1)}, u32[]{:S(2)}, u32[]{:S(2)}) %collective-permute-start.3) | collective-permute-done | bytes 131104 | tf_op jit(solution)/shard_map/ppermute | solution.py:357
  338.8 2.8 collective-permute-done.4
  343.8 2.7 collective-permute-done.5
  349.6 5.5 %collective-permute-done.6 = bf16[256,256]{1,0:T(8,128)(2,1)S(1)} collective-permute-done((bf16[256,256]{1,0:T(8,128)(2,1)S(1)}, bf16[256,256]{1,0:T(8,128)(2,1)S(1)}, u32[]{:S(2)}, u32[]{:S(2)}) %collective-permute-start.6) | collective-permute-done | bytes 131104 | tf_op jit(solution)/shard_map/ppermute | solution.py:357
  358.6 3.1 collective-permute-done.7
  369.1 6.2 %collective-permute-done.8 = bf16[1024,256]{1,0:T(8,128)(2,1)} collective-permute-done((bf16[1024,256]{1,0:T(8,128)(2,1)}, bf16[1024,256]{1,0:T(8,128)(2,1)}, u32[]{:S(2)}, u32[]{:S(2)}) %collective-permute-start.8) | collective-permute-done | bytes 524320 | tf_op jit(solution)/shard_map/ppermute | solution.py:357
  (171 shorter events, 71.2 us)
Async XLA Ops:
  14.5 55.7 %all-to-all-start = ((bf16[8,64,2048]{2,1,0:T(8,128)(2,1)}), bf16[8,64,2048]{2,1,0:T(8,128)(2,1)S(1)}, u32[]{:S(2)}, u32[]{:S(2)}) async-start(bf16[8,64,2048]{2,1,0:T(8,128)(2,1)} %bitcast.186), calls=%async_computation | async-start | bytes 4194304 | tf_op jit(solution)/shard_map/all_to_all | solution.py:405
  21.9 133.7 %reduce-scatter.2.cloned.1.call-start = ((), (), s32[]{:S(2)}) async-start(), calls=%async_computation.4 | async-start | bytes 10485760 | tf_op jit(solution)/shard_map/reduce_scatter | solution.py:424
  158.4 31.5 %all-to-all-start.1 = ((bf16[8,64,1024]{2,1,0:T(8,128)(2,1)}), bf16[8,64,1024]{2,1,0:T(8,128)(2,1)S(1)}, u32[]{:S(2)}, u32[]{:S(2)}) async-start(bf16[8,64,1024]{2,1,0:T(8,128)(2,1)} %bitcast.69), calls=%async_computation.2 | async-start | bytes 2097152 | tf_op jit(solution)/shard_map/all_to_all | solution.py:426
  191.8 12.3 %all-to-all-start.2 = ((bf16[4,64,1024]{2,1,0:T(8,128)(2,1)}), bf16[4,64,1024]{2,1,0:T(8,128)(2,1)S(1)}, u32[]{:S(2)}, u32[]{:S(2)}) async-start(bf16[4,64,1024]{2,1,0:T(8,128)(2,1)} %bitcast.71), calls=%async_computation.3 | async-start | bytes 1048576 | tf_op jit(solution)/shard_map/all_to_all | solution.py:434
  247.5 16.8 %collective-permute-start.21 = (bf16[1280,128]{1,0:T(8,128)(2,1)S(1)}, bf16[1280,128]{1,0:T(8,128)(2,1)S(1)}, u32[]{:S(2)}, u32[]{:S(2)}) collective-permute-start(bf16[1280,128]{1,0:T(8,128)(2,1)S(1)} %dynamic-slice_convert_fusion.2), channel_id=1, source_target_pairs={{0,4},{1,5},{2,6},{3,7},{4,0},{5,1},{6,2},{7,3},{8,12},{9,13},{10,... | collective-permute-start | bytes 983048 | tf_op jit(solution)/shard_map/ppermute | solution.py:357
  264.4 6.2 %collective-permute-start.22 = (bf16[640,128]{1,0:T(8,128)(2,1)S(1)}, bf16[640,128]{1,0:T(8,128)(2,1)S(1)}, u32[]{:S(2)}, u32[]{:S(2)}) collective-permute-start(bf16[640,128]{1,0:T(8,128)(2,1)S(1)} %dynamic-slice_convert_fusion.5), channel_id=1, source_target_pairs={{0,2},{1,3},{2,0},{3,1},{4,6},{5,7},{6,4},{7,5},{8,10},{9,11},{10,... | collective-permute-start | bytes 491528 | tf_op jit(solution)/shard_map/ppermute | solution.py:357
  265.6 32.7 %collective-permute-start = (bf16[2048,256]{1,0:T(8,128)(2,1)}, bf16[2048,256]{1,0:T(8,128)(2,1)S(1)}, u32[]{:S(2)}, u32[]{:S(2)}) collective-permute-start(bf16[2048,256]{1,0:T(8,128)(2,1)} %constant_dynamic-slice_fusion.2), channel_id=1, source_target_pairs={{0,8},{8,0},{16,24},{24,16},{1,9},{9,1},{17,25},{25,17},{2,10},{10... | collective-permute-start | bytes 3145736 | tf_op jit(solution)/shard_map/ppermute | solution.py:357
  270.7 4.6 %collective-permute-start.23 = (bf16[320,128]{1,0:T(8,128)(2,1)S(1)}, bf16[320,128]{1,0:T(8,128)(2,1)}, u32[]{:S(2)}, u32[]{:S(2)}) collective-permute-start(bf16[320,128]{1,0:T(8,128)(2,1)S(1)} %dynamic-slice_convert_fusion.8), channel_id=1, source_target_pairs={{0,16},{8,24},{16,0},{24,8},{1,17},{9,25},{17,1},{25,9},{2,18},{10... | collective-permute-start | bytes 245768 | tf_op jit(solution)/shard_map/ppermute | solution.py:357
  276.9 20.3 %collective-permute-start.24 = (bf16[160,128]{1,0:T(8,128)(2,1)S(1)}, bf16[160,128]{1,0:T(8,128)(2,1)S(1)}, u32[]{:S(2)}, u32[]{:S(2)}) collective-permute-start(bf16[160,128]{1,0:T(8,128)(2,1)S(1)} %dynamic-slice_convert_fusion.11), channel_id=1, source_target_pairs={{0,1},{1,0},{2,3},{3,2},{4,5},{5,4},{6,7},{7,6},{8,9},{9,8},{10,11... | collective-permute-start | bytes 122888 | tf_op jit(solution)/shard_map/ppermute | solution.py:357
  279.1 28.2 %collective-permute-start.10 = (bf16[2048,256]{1,0:T(8,128)(2,1)}, bf16[2048,256]{1,0:T(8,128)(2,1)}, u32[]{:S(2)}, u32[]{:S(2)}) collective-permute-start(bf16[2048,256]{1,0:T(8,128)(2,1)} %constant_dynamic-slice_fusion.1), channel_id=1, source_target_pairs={{0,8},{8,0},{16,24},{24,16},{1,9},{9,1},{17,25},{25,17},{2,10},{10... | collective-permute-start | bytes 3145736 | tf_op jit(solution)/shard_map/ppermute | solution.py:357
  297.3 4.1 %collective-permute-start.25 = (bf16[160,128]{1,0:T(8,128)(2,1)S(1)}, bf16[160,128]{1,0:T(8,128)(2,1)S(1)}, u32[]{:S(2)}, u32[]{:S(2)}) collective-permute-start(bf16[160,128]{1,0:T(8,128)(2,1)S(1)} %add_convert_fusion.2), channel_id=1, source_target_pairs={{0,1},{1,0},{2,3},{3,2},{4,5},{5,4},{6,7},{7,6},{8,9},{9,8},{10,11... | collective-permute-start | bytes 122888 | tf_op jit(solution)/shard_map/ppermute | solution.py:357
  301.4 5.4 %collective-permute-start.26 = (bf16[320,128]{1,0:T(8,128)(2,1)S(1)}, bf16[320,128]{1,0:T(8,128)(2,1)S(1)}, u32[]{:S(2)}, u32[]{:S(2)}) collective-permute-start(bf16[320,128]{1,0:T(8,128)(2,1)S(1)} %pad_maximum_fusion.18), channel_id=1, source_target_pairs={{0,16},{8,24},{16,0},{24,8},{1,17},{9,25},{17,1},{25,9},{2,18},{10... | collective-permute-start | bytes 245768 | tf_op jit(solution)/shard_map/ppermute | solution.py:357
  301.9 14.5 %collective-permute-start.1 = (bf16[1024,256]{1,0:T(8,128)(2,1)S(1)}, bf16[1024,256]{1,0:T(8,128)(2,1)S(1)}, u32[]{:S(2)}, u32[]{:S(2)}) collective-permute-start(bf16[1024,256]{1,0:T(8,128)(2,1)S(1)} %dynamic-slice_convert_fusion.1), channel_id=1, source_target_pairs={{0,16},{8,24},{16,0},{24,8},{1,17},{9,25},{17,1},{25,9},{2,18},{10... | collective-permute-start | bytes 1572872 | tf_op jit(solution)/shard_map/ppermute | solution.py:357
  306.9 5.4 %collective-permute-start.27 = (bf16[640,128]{1,0:T(8,128)(2,1)S(1)}, bf16[640,128]{1,0:T(8,128)(2,1)S(1)}, u32[]{:S(2)}, u32[]{:S(2)}) collective-permute-start(bf16[640,128]{1,0:T(8,128)(2,1)S(1)} %pad_maximum_fusion.15), channel_id=1, source_target_pairs={{0,2},{1,3},{2,0},{3,1},{4,6},{5,7},{6,4},{7,5},{8,10},{9,11},{10,... | collective-permute-start | bytes 491528 | tf_op jit(solution)/shard_map/ppermute | solution.py:357
  308.7 12.9 %collective-permute-start.11 = (bf16[1024,256]{1,0:T(8,128)(2,1)S(1)}, bf16[1024,256]{1,0:T(8,128)(2,1)S(1)}, u32[]{:S(2)}, u32[]{:S(2)}) collective-permute-start(bf16[1024,256]{1,0:T(8,128)(2,1)S(1)} %dynamic-slice_convert_fusion), channel_id=1, source_target_pairs={{0,1},{1,0},{2,3},{3,2},{4,5},{5,4},{6,7},{7,6},{8,9},{9,8},{10,11... | collective-permute-start | bytes 1572872 | tf_op jit(solution)/shard_map/ppermute | solution.py:357
  312.4 19.5 %collective-permute-start.28 = (bf16[1280,128]{1,0:T(8,128)(2,1)S(1)}, bf16[1280,128]{1,0:T(8,128)(2,1)S(1)}, u32[]{:S(2)}, u32[]{:S(2)}) collective-permute-start(bf16[1280,128]{1,0:T(8,128)(2,1)S(1)} %pad_maximum_fusion.10), channel_id=1, source_target_pairs={{0,4},{1,5},{2,6},{3,7},{4,0},{5,1},{6,2},{7,3},{8,12},{9,13},{10,... | collective-permute-start | bytes 983048 | tf_op jit(solution)/shard_map/ppermute | solution.py:357
  316.5 8.7 %collective-permute-start.2 = (bf16[512,256]{1,0:T(8,128)(2,1)S(1)}, bf16[512,256]{1,0:T(8,128)(2,1)S(1)}, u32[]{:S(2)}, u32[]{:S(2)}) collective-permute-start(bf16[512,256]{1,0:T(8,128)(2,1)S(1)} %dynamic-slice_convert_fusion.4), channel_id=1, source_target_pairs={{0,1},{1,0},{2,3},{3,2},{4,5},{5,4},{6,7},{7,6},{8,9},{9,8},{10,11... | collective-permute-start | bytes 786440 | tf_op jit(solution)/shard_map/ppermute | solution.py:357
  321.7 6.4 %collective-permute-start.12 = (bf16[512,256]{1,0:T(8,128)(2,1)S(1)}, bf16[512,256]{1,0:T(8,128)(2,1)S(1)}, u32[]{:S(2)}, u32[]{:S(2)}) collective-permute-start(bf16[512,256]{1,0:T(8,128)(2,1)S(1)} %dynamic-slice_convert_fusion.3), channel_id=1, source_target_pairs={{0,16},{8,24},{16,0},{24,8},{1,17},{9,25},{17,1},{25,9},{2,18},{10... | collective-permute-start | bytes 786440 | tf_op jit(solution)/shard_map/ppermute | solution.py:357
  325.4 11.2 %collective-permute-start.3 = (bf16[256,256]{1,0:T(8,128)(2,1)S(1)}, bf16[256,256]{1,0:T(8,128)(2,1)S(1)}, u32[]{:S(2)}, u32[]{:S(2)}) collective-permute-start(bf16[256,256]{1,0:T(8,128)(2,1)S(1)} %dynamic-slice_convert_fusion.7), channel_id=1, source_target_pairs={{0,4},{1,5},{2,6},{3,7},{4,0},{5,1},{6,2},{7,3},{8,12},{9,13},{10,... | collective-permute-start | bytes 393224 | tf_op jit(solution)/shard_map/ppermute | solution.py:357
  328.3 9.8 %collective-permute-start.13 = (bf16[256,256]{1,0:T(8,128)(2,1)S(1)}, bf16[256,256]{1,0:T(8,128)(2,1)S(1)}, u32[]{:S(2)}, u32[]{:S(2)}) collective-permute-start(bf16[256,256]{1,0:T(8,128)(2,1)S(1)} %dynamic-slice_convert_fusion.6), channel_id=1, source_target_pairs={{0,4},{1,5},{2,6},{3,7},{4,0},{5,1},{6,2},{7,3},{8,12},{9,13},{10,... | collective-permute-start | bytes 393224 | tf_op jit(solution)/shard_map/ppermute | solution.py:357
  332.0 35.8 %collective-permute-start.29 = (bf16[2560,128]{1,0:T(8,128)(2,1)S(1)}, bf16[2560,128]{1,0:T(8,128)(2,1)S(1)}, u32[]{:S(2)}, u32[]{:S(2)}) collective-permute-start(bf16[2560,128]{1,0:T(8,128)(2,1)S(1)} %pad_maximum_fusion.7), channel_id=1, source_target_pairs={{0,8},{8,0},{16,24},{24,16},{1,9},{9,1},{17,25},{25,17},{2,10},{10... | collective-permute-start | bytes 1966088 | tf_op jit(solution)/shard_map/ppermute | solution.py:357
  336.6 5.0 %collective-permute-start.4 = (bf16[128,256]{1,0:T(8,128)(2,1)S(1)}, bf16[128,256]{1,0:T(8,128)(2,1)S(1)}, u32[]{:S(2)}, u32[]{:S(2)}) collective-permute-start(bf16[128,256]{1,0:T(8,128)(2,1)S(1)} %dynamic-slice_convert_fusion.10), channel_id=1, source_target_pairs={{0,2},{1,3},{2,0},{3,1},{4,6},{5,7},{6,4},{7,5},{8,10},{9,11},{10,... | collective-permute-start | bytes 196616 | tf_op jit(solution)/shard_map/ppermute | solution.py:357
  338.1 4.3 %collective-permute-start.14 = (bf16[128,256]{1,0:T(8,128)(2,1)S(1)}, bf16[128,256]{1,0:T(8,128)(2,1)S(1)}, u32[]{:S(2)}, u32[]{:S(2)}) collective-permute-start(bf16[128,256]{1,0:T(8,128)(2,1)S(1)} %dynamic-slice_convert_fusion.9), channel_id=1, source_target_pairs={{0,2},{1,3},{2,0},{3,1},{4,6},{5,7},{6,4},{7,5},{8,10},{9,11},{10,... | collective-permute-start | bytes 196616 | tf_op jit(solution)/shard_map/ppermute | solution.py:357
  341.6 4.9 %collective-permute-start.5 = (bf16[128,256]{1,0:T(8,128)(2,1)S(1)}, bf16[128,256]{1,0:T(8,128)(2,1)S(1)}, u32[]{:S(2)}, u32[]{:S(2)}) collective-permute-start(bf16[128,256]{1,0:T(8,128)(2,1)S(1)} %add_convert_fusion.1), channel_id=1, source_target_pairs={{0,2},{1,3},{2,0},{3,1},{4,6},{5,7},{6,4},{7,5},{8,10},{9,11},{10,... | collective-permute-start | bytes 196616 | tf_op jit(solution)/shard_map/ppermute | solution.py:357
  342.5 4.9 %collective-permute-start.15 = (bf16[128,256]{1,0:T(8,128)(2,1)S(1)}, bf16[128,256]{1,0:T(8,128)(2,1)S(1)}, u32[]{:S(2)}, u32[]{:S(2)}) collective-permute-start(bf16[128,256]{1,0:T(8,128)(2,1)S(1)} %add_convert_fusion), channel_id=1, source_target_pairs={{0,2},{1,3},{2,0},{3,1},{4,6},{5,7},{6,4},{7,5},{8,10},{9,11},{10,... | collective-permute-start | bytes 196616 | tf_op jit(solution)/shard_map/ppermute | solution.py:357
  346.5 8.6 %collective-permute-start.6 = (bf16[256,256]{1,0:T(8,128)(2,1)S(1)}, bf16[256,256]{1,0:T(8,128)(2,1)S(1)}, u32[]{:S(2)}, u32[]{:S(2)}) collective-permute-start(bf16[256,256]{1,0:T(8,128)(2,1)S(1)} %pad_maximum_fusion.16), channel_id=1, source_target_pairs={{0,4},{1,5},{2,6},{3,7},{4,0},{5,1},{6,2},{7,3},{8,12},{9,13},{10,... | collective-permute-start | bytes 393224 | tf_op jit(solution)/shard_map/ppermute | solution.py:357
  347.4 9.1 %collective-permute-start.16 = (bf16[256,256]{1,0:T(8,128)(2,1)S(1)}, bf16[256,256]{1,0:T(8,128)(2,1)S(1)}, u32[]{:S(2)}, u32[]{:S(2)}) collective-permute-start(bf16[256,256]{1,0:T(8,128)(2,1)S(1)} %pad_maximum_fusion.17), channel_id=1, source_target_pairs={{0,4},{1,5},{2,6},{3,7},{4,0},{5,1},{6,2},{7,3},{8,12},{9,13},{10,... | collective-permute-start | bytes 393224 | tf_op jit(solution)/shard_map/ppermute | solution.py:357
  355.2 6.4 %collective-permute-start.7 = (bf16[512,256]{1,0:T(8,128)(2,1)S(1)}, bf16[512,256]{1,0:T(8,128)(2,1)S(1)}, u32[]{:S(2)}, u32[]{:S(2)}) collective-permute-start(bf16[512,256]{1,0:T(8,128)(2,1)S(1)} %pad_maximum_fusion.12), channel_id=1, source_target_pairs={{0,1},{1,0},{2,3},{3,2},{4,5},{5,4},{6,7},{7,6},{8,9},{9,8},{10,11... | collective-permute-start | bytes 786440 | tf_op jit(solution)/shard_map/ppermute | solution.py:357
  356.6 9.3 %collective-permute-start.17 = (bf16[512,256]{1,0:T(8,128)(2,1)S(1)}, bf16[512,256]{1,0:T(8,128)(2,1)S(1)}, u32[]{:S(2)}, u32[]{:S(2)}) collective-permute-start(bf16[512,256]{1,0:T(8,128)(2,1)S(1)} %pad_maximum_fusion.13), channel_id=1, source_target_pairs={{0,16},{8,24},{16,0},{24,8},{1,17},{9,25},{17,1},{25,9},{2,18},{10... | collective-permute-start | bytes 786440 | tf_op jit(solution)/shard_map/ppermute | solution.py:357
  362.6 12.7 %collective-permute-start.8 = (bf16[1024,256]{1,0:T(8,128)(2,1)}, bf16[1024,256]{1,0:T(8,128)(2,1)}, u32[]{:S(2)}, u32[]{:S(2)}) collective-permute-start(bf16[1024,256]{1,0:T(8,128)(2,1)} %pad_maximum_fusion.8), channel_id=1, source_target_pairs={{0,16},{8,24},{16,0},{24,8},{1,17},{9,25},{17,1},{25,9},{2,18},{10... | collective-permute-start | bytes 1572872 | tf_op jit(solution)/shard_map/ppermute | solution.py:357
  366.8 10.2 %collective-permute-start.18 = (bf16[1024,256]{1,0:T(8,128)(2,1)}, bf16[1024,256]{1,0:T(8,128)(2,1)S(1)}, u32[]{:S(2)}, u32[]{:S(2)}) collective-permute-start(bf16[1024,256]{1,0:T(8,128)(2,1)} %pad_maximum_fusion.9), channel_id=1, source_target_pairs={{0,1},{1,0},{2,3},{3,2},{4,5},{5,4},{6,7},{7,6},{8,9},{9,8},{10,11... | collective-permute-start | bytes 1572872 | tf_op jit(solution)/shard_map/ppermute | solution.py:357
  377.3 3.5 collective-permute-start.19
  (10 other events, 58.9 us)
Sparse Core Ops, SparseCore 0:
  84.9 70.7 reduce-scatter.1
where the time goes:
time: 395 us; the launch traced here: 391 us
  waiting for transfers between devices  188 us (48%)
  local copies, waits for them, and re-layouts  53 us (13%)
  starting transfers between devices  43.2 us (11%)
  other arithmetic  38.8 us (10%)
  Pallas kernels  37.6 us (10%)
  between operations  15.1 us (4%)
  matrix products  14.4 us (4%)
    ppermute x30, waiting for transfers between devices, exchanged(): lax.ppermute(values, axis, [(at, at ^ bit) for at in range(lax.axis_size(...  74.1 us
    reduce_scatter x1, waiting for transfers between devices, shards(): lax.psum_scatter(partial_value, 'vox', scatter_dimension=1, tiled=True)  70.9 us
    ppermute x30, starting transfers between devices, exchanged(): lax.ppermute(values, axis, [(at, at ^ bit) for at in range(lax.axis_size(...  26 us
    all_to_all x1, waiting for transfers between devices, shards(): lax.all_to_all(latent_part.reshape(dp_count, capacity, feat_local), 'dp',...  25.8 us
    reshape x2, local copies, waits for them, and re-layouts, spatial_first(): grid.reshape(count, height, breadth // 2, 2 * chan).transpose(1, 2, 0, 3)  18.2 us
    another operation x6, other arithmetic, paired_weight(): return jnp.stack(halves)  17.3 us
    pallas_call x1, Pallas kernels, last_layer(): pl.pallas_call(functools.partial(last_kernel, count), name='decoder_last'...  15.7 us
    dot_general x1, matrix products, shards(): jnp.dot(readings, ridge_maps[0], preferred_element_type=jnp.float32)  14.4 us
  transfers between devices with their start and end apart: 34, of which 29 were waited for; matrix products, arithmetic and copies ran while one was open for 18% of the time, Pallas kernels for 0%

commit v1 on v0

--- a/solution.py
+++ b/solution.py
@@ -65,22 +65,39 @@
             slope_ref[slope_row, rows, :] = slope
 
 
+def holder_of(block, holders):
+    bits = holders.bit_length() - 1
+    depth = (H0 * W0).bit_length() - 1
+    owner = sum(((block >> (depth - 1 - at)) & 1) << at for at in range(bits))
+    return owner, block & (2 ** (depth - bits) - 1)
+
+
+def latent_row(latent_ref, row):
+    holders = latent_ref.shape[0]
+    width = latent_ref.shape[2] * holders // (H0 * W0)
+    pieces = []
+    for col in range(W0):
+        owner, place = holder_of(row * W0 + col, holders)
+        pieces.append(latent_ref[owner, :, pl.ds(place * width, width)])
+    return jnp.concatenate(pieces, axis=0)
+
+
 def forward_kernel(count, latent_ref, w_one_ref, w_two_ref, act_one_ref, slope_one_ref, act_two_ref, slope_two_ref, tmp_one, tmp_two):
-    in_chan = w_one_ref.shape[1] // 2
+    in_chan = w_one_ref.shape[0] // 16
     mid_chan = w_two_ref.shape[1] // 2
     out_chan = w_two_ref.shape[2] // 4
 
-    def latent_row(row):
-        return jnp.concatenate(
-            [latent_ref[:, pl.ds((row * W0 + col) * in_chan, in_chan)] for col in range(W0)], axis=0
-        )
-
     for row in range(H0):
         for parity in (0, 1):
-            tmp_one[...] = product(latent_row(row), w_one_ref[parity, :in_chan, :])
             other = row + ROW_SHIFT[parity]
-            if 0 <= other < H0:
-                tmp_one[...] += product(latent_row(other), w_one_ref[parity, in_chan:, :])
+            for slot, col_tap in enumerate(COL_TAPS):
+                lanes = pl.ds(slot * mid_chan, mid_chan)
+                taps = pl.ds((ROW_TAPS[parity][0] * 4 + col_tap) * in_chan, in_chan)
+                value = product(latent_row(latent_ref, row), w_one_ref[taps, :])
+                if 0 <= other < H0:
+                    taps = pl.ds((ROW_TAPS[parity][1] * 4 + col_tap) * in_chan, in_chan)
+                    value = value + product(latent_row(latent_ref, other), w_one_ref[taps, :])
+                tmp_one[:, lanes] = value
             at = 2 * row + parity
             up_rows(tmp_one, act_one_ref, slope_one_ref, at, at, count, W0, mid_chan)
     height = 2 * H0
@@ -200,13 +217,7 @@
     for row in range(height):
         upstream = adj[row].astype(jnp.bfloat16).astype(jnp.float32)
         grad_one[row] = (upstream * slope_ref[row]).astype(jnp.bfloat16)
-    in_chan = latent_ref.shape[1] // (H0 * W0)
-
-    def latent_row(row):
-        return jnp.concatenate(
-            [latent_ref[:, pl.ds((row * W0 + col) * in_chan, in_chan)] for col in range(W0)], axis=0
-        )
-
+    in_chan = latent_ref.shape[0] * latent_ref.shape[2] // (H0 * W0)
     for parity in (0, 1):
         for which in (0, 1):
             lefts = []
@@ -214,7 +225,7 @@
             for row in range(H0):
                 source = row + (ROW_SHIFT[parity] if which else 0)
                 if 0 <= source < H0:
-                    lefts.append(latent_row(source))
+                    lefts.append(latent_row(latent_ref, source))
                     rights.append(side_taps(grad_one, 2 * row + parity, count, W0))
             left = jnp.concatenate(lefts, axis=0) if len(lefts) > 1 else lefts[0]
             right = jnp.concatenate(rights, axis=0) if len(rights) > 1 else rights[0]
@@ -232,7 +243,7 @@
 
 
 def forward(latent, w_one, w_two):
-    count = latent.shape[0]
+    count = latent.shape[1]
     mid_chan = w_two.shape[1] // 2
     out_chan = w_two.shape[2] // 4
     height, breadth = 2 * H0, 2 * W0
@@ -288,8 +299,8 @@
 
 
 def backward(latent, act_one, slope_one, w_two, grad_two, kind):
-    count = latent.shape[0]
-    in_chan = latent.shape[1] // (H0 * W0)
+    count = latent.shape[1]
+    in_chan = latent.shape[0] * latent.shape[2] // (H0 * W0)
     mid_chan = act_one.shape[2]
     out_chan = grad_two.shape[2]
     return pl.pallas_call(
@@ -338,6 +349,98 @@
     )
 
 
+def bucket_kernel(subject_ref, count_ref, shift_ref, fmri_ref, first_ref, second_ref, place_ref):
+    samples, voxels = fmri_ref.shape
+    slots = first_ref.shape[0]
+    subjects = count_ref.shape[0]
+    room = slots // subjects
+    owner = subject_ref[...]
+    lane = lax.broadcasted_iota(jnp.int32, (samples, 128), 1)
+    onehot = jnp.where(owner == lane, 1.0, 0.0)
+    row = lax.broadcasted_iota(jnp.int32, (samples, samples), 0)
+    col = lax.broadcasted_iota(jnp.int32, (samples, samples), 1)
+    before = jnp.where(col < row, 1.0, 0.0).astype(jnp.bfloat16)
+    earlier = product(before, onehot.astype(jnp.bfloat16))
+    rank = jnp.sum(earlier * onehot, axis=1, keepdims=True).astype(jnp.int32)
+    position = owner * room + rank + jnp.where(rank >= room, slots - room, 0)
+    slot = lax.broadcasted_iota(jnp.int32, (samples, 2 * slots), 1)
+    place_ref[...] = jnp.where(slot == position, 1.0, 0.0).astype(jnp.bfloat16)
+    voxel = lax.broadcasted_iota(jnp.int32, (room, voxels), 1) + shift_ref[0]
+    for half, out_ref in enumerate((first_ref, second_ref)):
+        for target in range(subjects):
+            here = pl.ds(half * slots + target * room, room)
+            if room * target % 128 == 0:
+                width = min(128, slots)
+                rows = product_tn(place_ref[:, pl.ds(half * slots + target * room, width)], fmri_ref[...])
+                for inner in range(width // room):
+                    keep = voxel < count_ref[target + inner]
+                    kept = jnp.where(keep, rows[inner * room:(inner + 1) * room], 0.0)
+                    out_ref[pl.ds((target + inner) * room, room), :] = kept.astype(jnp.bfloat16)
+
+
+def bucketed(subject, voxel_count, shift, fmri, slots):
+    samples, voxels = fmri.shape
+    vmem = pl.BlockSpec(memory_space=pltpu.VMEM)
+    smem = pl.BlockSpec(memory_space=pltpu.SMEM)
+    return pl.pallas_call(
+        bucket_kernel,
+        name="bucket_rows",
+        in_specs=[vmem, smem, smem, vmem],
+        out_specs=(vmem, vmem, vmem),
+        out_shape=(
+            jax.ShapeDtypeStruct((slots, voxels), jnp.bfloat16),
+            jax.ShapeDtypeStruct((slots, voxels), jnp.bfloat16),
+            jax.ShapeDtypeStruct((samples, 2 * slots), jnp.bfloat16),
+        ),
+        compiler_params=params(),
+    )(subject, voxel_count, shift, fmri)
+
+
+def project_kernel(rows_ref, map_ref, out_ref):
+    out_ref[0] = product(rows_ref[...], map_ref[0]).astype(jnp.bfloat16)
+
+
+def projected(rows, maps):
+    count, voxels = rows.shape
+    blocks = H0 * W0
+    width = maps.shape[2] // blocks
+    return pl.pallas_call(
+        project_kernel,
+        name="project_rows",
+        grid=(blocks,),
+        in_specs=[
+            pl.BlockSpec((count, voxels), lambda step: (0, 0)),
+            pl.BlockSpec((1, voxels, width), lambda step: (0, 0, step)),
+        ],
+        out_specs=pl.BlockSpec((1, count, width), lambda step: (step, 0, 0)),
+        out_shape=jax.ShapeDtypeStruct((blocks, count, width), jnp.bfloat16),
+        compiler_params=params(1),
+        cost_estimate=pl.CostEstimate(
+            flops=2 * count * voxels * maps.shape[2],
+            bytes_accessed=2 * voxels * maps.shape[2],
+            transcendentals=0,
+        ),
+    )(rows, maps)
+
+
+def collect_kernel(place_ref, first_ref, second_ref, out_ref):
+    subjects, blocks, room, width = first_ref.shape
+    for block in range(blocks):
+        rows = [ref[subject, block] for ref in (first_ref, second_ref) for subject in range(subjects)]
+        value = product(place_ref[...], jnp.concatenate(rows, axis=0))
+        out_ref[:, pl.ds(block * width, width)] = value.astype(jnp.bfloat16)
+
+
+def collected(place, first, second):
+    samples = place.shape[0]
+    return pl.pallas_call(
+        collect_kernel,
+        name="collect_rows",
+        out_shape=jax.ShapeDtypeStruct((samples, first.shape[1] * first.shape[3]), jnp.bfloat16),
+        compiler_params=params(),
+    )(place, first, second)
+
+
 def rounded(values):
     return lax.optimization_barrier(values.astype(jnp.bfloat16))
 
@@ -390,54 +493,45 @@
     dp_count = lax.axis_size("dp")
     samp_dev = fmri.shape[0]
     vox_local = fmri.shape[1]
-    capacity = max(2, 2 * samp_dev // dp_count)
     mid_chan = w_first.shape[1]
     last_chan = w_second.shape[1]
-    owners = subject[:, 0]
-    onehot = (owners[:, None] == jnp.arange(dp_count, dtype=jnp.int32)[None, :]).astype(jnp.int32)
-    earlier = jnp.cumsum(onehot, axis=0) - onehot
-    slot_index = jnp.sum(earlier * onehot, axis=1)
-    position = owners * capacity + slot_index
-    buckets = jnp.zeros((dp_count * capacity, vox_local), fmri.dtype).at[position].set(fmri)
-    buckets, target, w_first, w_second, w_third = lax.optimization_barrier(
-        (buckets, target, w_first, w_second, w_third)
+    slots = samp_dev
+    room = slots // dp_count
+    vox_bits = bit_pairs("vox")
+    dp_bits = bit_pairs("dp")
+    shift = (lax.axis_index("vox") * vox_local).astype(jnp.int32).reshape(1)
+    first, second, place = bucketed(subject, voxel_count, shift, fmri, slots)
+    first, second, target, w_second, w_third = lax.optimization_barrier(
+        (first, second, target, w_second, w_third)
     )
-    arrived = lax.all_to_all(
-        buckets.reshape(dp_count, capacity, vox_local),
-        "dp",
-        split_axis=0,
-        concat_axis=0,
-        tiled=True,
-    )
-    pair_one = paired_weight(w_first, w_first.shape[0] // 16)
+
+    def routed(rows):
+        sent = rows.reshape(dp_count, room, rows.shape[1])
+        return lax.all_to_all(sent, "dp", split_axis=0, concat_axis=0, tiled=True).reshape(rows.shape)
+
+    def returned(rows):
+        partial_value = projected(rows, ridge_maps)
+        latent_part = rounded(summed_share(partial_value, vox_bits))
+        blocks, _, width = latent_part.shape
+        sent = latent_part.reshape(blocks, dp_count, room, width).swapaxes(0, 1)
+        return lax.all_to_all(sent, "dp", split_axis=0, concat_axis=0, tiled=True)
+
+    first = routed(first)
+    second = routed(second)
     pair_two = paired_weight(w_second, mid_chan)
     pair_three = paired_weight(w_third, last_chan)
     target_rows = spatial_first(target)
-    arrived, pair_one, pair_two, pair_three, target_rows = lax.optimization_barrier(
-        (arrived, pair_one, pair_two, pair_three, target_rows)
+    second, pair_two, pair_three, target_rows = lax.optimization_barrier(
+        (second, pair_two, pair_three, target_rows)
     )
-    subject_here = lax.axis_index("dp")
-    voxel_ids = lax.axis_index("vox") * vox_local + jnp.arange(vox_local, dtype=jnp.int32)
-    voxel_keep = (voxel_ids < voxel_count[subject_here]).astype(fmri.dtype)
-    readings = arrived.reshape(dp_count * capacity, vox_local) * voxel_keep[None, :]
-    partial_value = jnp.dot(readings, ridge_maps[0], preferred_element_type=jnp.float32)
-    latent_part = rounded(lax.psum_scatter(partial_value, "vox", scatter_dimension=1, tiled=True))
-    feat_local = latent_part.shape[1]
-    returned = lax.all_to_all(
-        latent_part.reshape(dp_count, capacity, feat_local),
-        "dp",
-        split_axis=0,
-        concat_axis=0,
-        tiled=True,
-    )
-    own_rows = returned.reshape(dp_count * capacity, feat_local)[position]
-    latent = lax.all_to_all(own_rows, "vox", split_axis=0, concat_axis=1, tiled=True)
-    count = latent.shape[0]
-    act_one, slope_one, act_two, slope_two = forward(latent, pair_one, pair_two)
+    own_rows = collected(place, returned(first), returned(second))
+    holders = lax.axis_size("vox")
+    own_rows = own_rows.reshape(holders, samp_dev // holders, own_rows.shape[1])
+    latent = lax.all_to_all(own_rows, "vox", split_axis=0, concat_axis=0, tiled=True)
+    count = latent.shape[1]
+    act_one, slope_one, act_two, slope_two = forward(latent, w_first, pair_two)
     decoded_rows, grad_two, paired_three = last_layer(act_two, slope_two, pair_three, target_rows)
     grad_first, grad_second = backward(latent, act_one, slope_one, pair_two, grad_two, jnp.bfloat16)
-    vox_bits = bit_pairs("vox")
-    dp_bits = bit_pairs("dp")
     core, across = vox_bits[:1], vox_bits[1:]
     near, along = dp_bits[:1], dp_bits[:0:-1]
     half = grad_first.shape[0] // 2

time: 395 us -> 335 us (0.85)
  waiting for transfers between devices: 188 us -> 124 us
  Pallas kernels: 37.6 us -> 66.9 us
  blocking collectives: 0 us -> 18.5 us
  other arithmetic: 38.8 us -> 21.6 us
  matrix products: 14.4 us -> 0 us
  between operations: 15.1 us -> 1.5 us
  starting transfers between devices: 43.2 us -> 48.1 us
    reduce_scatter x1 -> x0, waiting for transfers between devices: 70.9 us -> none  [shards(): lax.psum_scatter(partial_value, 'vox', scatter_dimension=1, tiled=True)]
    pallas_call x0 -> x4, Pallas kernels: none -> 29.5 us  [the longest x2 23.4 us: projected(): pl.pallas_call(project_kernel, name='project_rows', grid=(blocks,), in_sp...]
    ppermute x30 -> x34, waiting for transfers between devices: 74.1 us -> 98.7 us  [exchanged(): lax.ppermute(values, axis, [(at, at ^ bit) for at in range(lax.axis_size(...]
    all_to_all x0 -> x1, blocking collectives: none -> 18.5 us  [returned(): return lax.all_to_all(sent, 'dp', split_axis=0, concat_axis=0, tiled=True)]
    all_to_all x3 -> x4, waiting for transfers between devices: 43.3 us -> 25 us  [the longest x2 16.4 us: routed(): lax.all_to_all(sent, 'dp', split_axis=0, concat_axis=0, tiled=True)]
    dot_general x1 -> x0, matrix products: 14.4 us -> none  [shards(): jnp.dot(readings, ridge_maps[0], preferred_element_type=jnp.float32)]
    another operation x6 -> x4, other arithmetic: 17.3 us -> 2.97 us  [paired_weight(): return jnp.stack(halves)]
    scatter x1 -> x0, local copies, waits for them, and re-layouts: 4.4 us -> none  [shards(): jnp.zeros((dp_count * capacity, vox_local), fmri.dtype).at[position]]
  transfers between devices with their start and end apart: 34 -> 38, of which waited for: 29 -> 29; matrix products, arithmetic and copies ran while one was open for 18% -> 19% of each run, Pallas kernels for 0% -> 7%
where the time goes in v1:
time: 335 us; the launch traced here: 333 us
  waiting for transfers between devices  124 us (37%)
  Pallas kernels  66.9 us (20%)
  local copies, waits for them, and re-layouts  53.2 us (16%)
  starting transfers between devices  48.1 us (14%)
  other arithmetic  21.6 us (6%)
  blocking collectives  18.5 us (6%)
    ppermute x34, waiting for transfers between devices, exchanged(): lax.ppermute(values, axis, [(at, at ^ bit) for at in range(lax.axis_size(...  98.7 us
    ppermute x34, starting transfers between devices, exchanged(): lax.ppermute(values, axis, [(at, at ^ bit) for at in range(lax.axis_size(...  29.9 us
    pallas_call x2, Pallas kernels, projected(): pl.pallas_call(project_kernel, name='project_rows', grid=(blocks,), in_sp...  23.4 us
    all_to_all x1, blocking collectives, returned(): return lax.all_to_all(sent, 'dp', split_axis=0, concat_axis=0, tiled=True)  18.5 us
    reshape x2, local copies, waits for them, and re-layouts, spatial_first(): grid.reshape(count, height, breadth // 2, 2 * chan).transpose(1, 2, 0, 3)  18.2 us
    all_to_all x2, waiting for transfers between devices, routed(): lax.all_to_all(sent, 'dp', split_axis=0, concat_axis=0, tiled=True)  16.4 us
    pallas_call x1, Pallas kernels, last_layer(): pl.pallas_call(functools.partial(last_kernel, count), name='decoder_last'...  15.5 us
    pallas_call x1, Pallas kernels, forward(): pl.pallas_call(functools.partial(forward_kernel, count), name='decoder_fo...  11.1 us
  transfers between devices with their start and end apart: 38, of which 29 were waited for; matrix products, arithmetic and copies ran while one was open for 19% of the time, Pallas kernels for 7%

profile of v1, /device:TPU:0, one launch (start us, length us, event | category | flops | bytes accessed | tf_op | source)
XLA Modules:
  0.0 333.4 jit_solution(4454675363492521601)
XLA Ops:
  2.2 3.7 %bucket_rows.1 = (bf16[256,2048]{1,0:T(8,128)(2,1)}, bf16[256,2048]{1,0:T(8,128)(2,1)}, bf16[256,512]{1,0:T(8,128)(2,1)}) custom-call(s32[256,1]{1,0:T(8,128)} %copy.264.subject_ref, s32[8]{0:T(128)} %count_ref.1, s32[1]{0:T(128)} %bitcast.shift_ref, bf16[256,2048]{1,0:T(8,128)(2,1)} %fmri_ref.1), custom_call_target="tpu_custom_call" | custom-call | tf_op jit(solution)/shard_map/bucket_rows/pallas_call | solution.py:385
  5.8 7.3 %all-to-all-start.2 = ((bf16[8,32,2048]{2,1,0:T(8,128)(2,1)}), bf16[8,32,2048]{2,1,0:T(8,128)(2,1)S(1)}, u32[]{:S(2)}, u32[]{:S(2)}) async-start(bf16[8,32,2048]{2,1,0:T(8,128)(2,1)} %bitcast.147), calls=%async_computation.2 | async-start | bytes 2097152 | tf_op jit(solution)/shard_map/all_to_all | solution.py:510
  13.4 11.3 %reshape.72 = bf16[64,16,16,128]{3,2,1,0:T(8,128)(2,1)} reshape(bf16[64,16,32,64]{3,2,1,0:T(8,128)(2,1)} %param.15) | data formatting | bytes 8388608 | tf_op jit(solution)/shard_map/reshape | solution.py:337
  24.7 6.9 %copy.267 = bf16[64,16,16,128]{3,0,2,1:T(8,128)(2,1)} copy(bf16[64,16,16,128]{3,2,1,0:T(8,128)(2,1)} %reshape.72) | data formatting | bytes 8388608 | tf_op jit(solution)/shard_map/reshape | solution.py:337
  32.3 6.6 %all-to-all-done.2 = bf16[8,32,2048]{2,1,0:T(8,128)(2,1)S(1)} async-done(((bf16[8,32,2048]{2,1,0:T(8,128)(2,1)}), bf16[8,32,2048]{2,1,0:T(8,128)(2,1)S(1)}, u32[]{:S(2)}, u32[]{:S(2)}) %all-to-all-start.2) | async-done | bytes 1048608 | tf_op jit(solution)/shard_map/all_to_all | solution.py:510
  38.9 3.6 %all-to-all-start = ((bf16[8,32,2048]{2,1,0:T(8,128)(2,1)}), bf16[8,32,2048]{2,1,0:T(8,128)(2,1)S(1)}, u32[]{:S(2)}, u32[]{:S(2)}) async-start(bf16[8,32,2048]{2,1,0:T(8,128)(2,1)} %bitcast.146), calls=%async_computation | async-start | bytes 2097152 | tf_op jit(solution)/shard_map/all_to_all | solution.py:510
  45.5 11.7 %project_rows.3 = bf16[8,256,512]{2,1,0:T(8,128)(2,1)} custom-call(bf16[256,2048]{1,0:T(8,128)(2,1)} %bitcast.138, bf16[1,2048,4096]{2,1,0:T(8,128)(2,1)} %map_ref.3), custom_call_target="tpu_custom_call" | custom-call | flops 4294967296 | bytes 16777216 | tf_op jit(solution)/shard_map/project_rows/pallas_call | solution.py:407
  58.7 9.8 %all-to-all-done = bf16[8,32,2048]{2,1,0:T(8,128)(2,1)S(1)} async-done(((bf16[8,32,2048]{2,1,0:T(8,128)(2,1)}), bf16[8,32,2048]{2,1,0:T(8,128)(2,1)S(1)}, u32[]{:S(2)}, u32[]{:S(2)}) %all-to-all-start) | async-done | bytes 1048608 | tf_op jit(solution)/shard_map/all_to_all | solution.py:510
  69.4 11.7 %project_rows.2 = bf16[8,256,512]{2,1,0:T(8,128)(2,1)} custom-call(bf16[256,2048]{1,0:T(8,128)(2,1)} %bitcast.137, bf16[1,2048,4096]{2,1,0:T(8,128)(2,1)} %map_ref.3), custom_call_target="tpu_custom_call" | custom-call | flops 4294967296 | bytes 16777216 | tf_op jit(solution)/shard_map/project_rows/pallas_call | solution.py:407
  86.8 12.8 %collective-permute-done.3 = bf16[2,256,512]{2,1,0:T(8,128)(2,1)S(1)} collective-permute-done((bf16[2,256,512]{2,1,0:T(8,128)(2,1)S(1)}, bf16[2,256,512]{2,1,0:T(8,128)(2,1)S(1)}, u32[]{:S(2)}, u32[]{:S(2)}) %collective-permute-start.3) | collective-permute-done | bytes 524320 | tf_op jit(solution)/shard_map/ppermute | solution.py:460
  101.8 3.6 %all-to-all-start.3 = ((bf16[8,2,32,512]{3,2,1,0:T(8,128)(2,1)}), bf16[8,2,32,512]{3,2,1,0:T(8,128)(2,1)S(1)}, u32[]{:S(2)}, u32[]{:S(2)}) async-start(bf16[8,2,32,512]{3,2,1,0:T(8,128)(2,1)} %bitcast.134), calls=%async_computation.3 | async-start | bytes 1048576 | tf_op jit(solution)/shard_map/all_to_all | solution.py:517
  108.7 11.9 %collective-permute-done.1 = bf16[2,256,512]{2,1,0:T(8,128)(2,1)S(1)} collective-permute-done((bf16[2,256,512]{2,1,0:T(8,128)(2,1)S(1)}, bf16[2,256,512]{2,1,0:T(8,128)(2,1)S(1)}, u32[]{:S(2)}, u32[]{:S(2)}) %collective-permute-start.1) | collective-permute-done | bytes 524320 | tf_op jit(solution)/shard_map/ppermute | solution.py:460
  120.9 18.5 %all_to_all.25.first_ref = bf16[8,2,32,512]{3,2,1,0:T(8,128)(2,1)} all-to-all(bf16[8,2,32,512]{3,2,1,0:T(8,128)(2,1)S(1)} %bitcast.144), channel_id=1, replica_groups=mesh['vox'=4,'dp'=8] {'dp'}, dimensions={0} | all-to-all | bytes 1048576 | tf_op jit(solution)/shard_map/all_to_all | solution.py:517
  141.9 3.7 %all-to-all-start.4 = ((bf16[4,64,1024]{2,1,0:T(8,128)(2,1)}), bf16[4,64,1024]{2,1,0:T(8,128)(2,1)S(1)}, u32[]{:S(2)}, u32[]{:S(2)}) async-start(bf16[4,64,1024]{2,1,0:T(8,128)(2,1)} %bitcast.140), calls=%async_computation.4 | async-start | bytes 1048576 | tf_op jit(solution)/shard_map/all_to_all | solution.py:530
  145.6 8.6 %all-to-all-done.4.latent_ref = bf16[4,64,1024]{2,1,0:T(8,128)(2,1)S(1)} async-done(((bf16[4,64,1024]{2,1,0:T(8,128)(2,1)}), bf16[4,64,1024]{2,1,0:T(8,128)(2,1)S(1)}, u32[]{:S(2)}, u32[]{:S(2)}) %all-to-all-start.4) | async-done | bytes 524320 | tf_op jit(solution)/shard_map/all_to_all | solution.py:530
  155.0 11.1 %decoder_forward.1 = (bf16[4,512,256]{2,1,0:T(8,128)(2,1)}, f32[4,512,256]{2,1,0:T(8,128)}, bf16[10,1024,128]{2,1,0:T(8,128)(2,1)}, f32[8,1024,128]{2,1,0:T(8,128)}) custom-call(bf16[4,64,1024]{2,1,0:T(8,128)(2,1)} %copy-done.4, bf16[8192,256]{1,0:T(8,128)(2,1)} %w_one_ref.1, bf16[2,512,512]{2,1,0:T(8,128)(2,1)} %pad_maximum_fusion.3.w_two_ref.w_ref), custom_call_target="tpu_custom_call" | custom-call | tf_op jit(solution)/shard_map/decoder_forward/pallas_call | solution.py:250
  166.1 15.5 %decoder_last.1 = (bf16[16,1024,128]{2,1,0:T(8,128)(2,1)}, bf16[8,1024,128]{2,1,0:T(8,128)(2,1)}, f32[2,256,256]{2,1,0:T(8,128)}) custom-call(bf16[10,1024,128]{2,1,0:T(8,128)(2,1)} %get-tuple-element.35.act_ref, f32[8,1024,128]{2,1,0:T(8,128)} %get-tuple-element.36.slope_ref, bf16[2,256,256]{2,1,0:T(8,128)(2,1)} %pad_maximum_fusion.10.w_ref, ...), custom_call_target="tpu_custom_call" | custom-call | tf_op jit(solution)/shard_map/decoder_last/pallas_call | solution.py:272
  182.8 10.7 %decoder_backward.1 = (bf16[8192,256]{1,0:T(8,128)(2,1)}, bf16[4096,128]{1,0:T(8,128)(2,1)}) custom-call(bf16[4,64,1024]{2,1,0:T(8,128)(2,1)} %copy-done.4, bf16[4,512,256]{2,1,0:T(8,128)(2,1)} %get-tuple-element.40.act_ref, f32[4,512,256]{2,1,0:T(8,128)} %get-tuple-element.41.slope_ref, bf16[2,512,512]{2,1,0:T(8,128)(2,1)} %pad_maximum_fusion.3.w_two_ref.w_ref, ...), custom_call_target="tpu_custom_call" | custom-call | tf_op jit(solution)/shard_map/decoder_backward/pallas_call | solution.py:306
  200.9 14.1 %collective-permute-done.25 = bf16[1280,128]{1,0:T(8,128)(2,1)S(1)} collective-permute-done((bf16[1280,128]{1,0:T(8,128)(2,1)S(1)}, bf16[1280,128]{1,0:T(8,128)(2,1)S(1)}, u32[]{:S(2)}, u32[]{:S(2)}) %collective-permute-start.25) | collective-permute-done | bytes 327712 | tf_op jit(solution)/shard_map/ppermute | solution.py:460
  216.2 4.5 %collective-permute-done.26 = bf16[640,128]{1,0:T(8,128)(2,1)S(1)} collective-permute-done((bf16[640,128]{1,0:T(8,128)(2,1)S(1)}, bf16[640,128]{1,0:T(8,128)(2,1)S(1)}, u32[]{:S(2)}, u32[]{:S(2)}) %collective-permute-start.26) | collective-permute-done | bytes 163872 | tf_op jit(solution)/shard_map/ppermute | solution.py:460
  221.2 4.2 %collective-permute-done.27 = bf16[320,128]{1,0:T(8,128)(2,1)} collective-permute-done((bf16[320,128]{1,0:T(8,128)(2,1)S(1)}, bf16[320,128]{1,0:T(8,128)(2,1)}, u32[]{:S(2)}, u32[]{:S(2)}) %collective-permute-start.27) | collective-permute-done | bytes 81952 | tf_op jit(solution)/shard_map/ppermute | solution.py:460
  229.3 6.9 %copy.269 = bf16[64,16,16,128]{3,2,1,0:T(8,128)(2,1)} copy(bf16[64,16,16,128]{3,0,2,1:T(8,128)(2,1)} %bitcast.139) | data formatting | bytes 8388608 | tf_op jit(solution)/shard_map/transpose | solution.py:347
  236.2 11.1 %reshape.77 = bf16[64,16,32,64]{3,2,1,0:T(8,128)(2,1)} reshape(bf16[64,16,16,128]{3,2,1,0:T(8,128)(2,1)} %copy.269) | data formatting | bytes 8388608 | tf_op jit(solution)/shard_map/reshape | solution.py:348
  253.6 3.2 collective-permute-done.30
  267.3 4.3 %collective-permute-done.15 = bf16[1024,256]{1,0:T(8,128)(2,1)S(1)} collective-permute-done((bf16[1024,256]{1,0:T(8,128)(2,1)S(1)}, bf16[1024,256]{1,0:T(8,128)(2,1)S(1)}, u32[]{:S(2)}, u32[]{:S(2)}) %collective-permute-start.15) | collective-permute-done | bytes 524320 | tf_op jit(solution)/shard_map/ppermute | solution.py:460
  271.8 3.4 %collective-permute-done.6 = bf16[512,256]{1,0:T(8,128)(2,1)S(1)} collective-permute-done((bf16[512,256]{1,0:T(8,128)(2,1)S(1)}, bf16[512,256]{1,0:T(8,128)(2,1)S(1)}, u32[]{:S(2)}, u32[]{:S(2)}) %collective-permute-start.6) | collective-permute-done | bytes 262176 | tf_op jit(solution)/shard_map/ppermute | solution.py:460
  278.3 3.1 collective-permute-start.17
  281.6 3.0 collective-permute-done.7
  284.8 3.4 %collective-permute-done.17 = bf16[256,256]{1,0:T(8,128)(2,1)S(1)} collective-permute-done((bf16[256,256]{1,0:T(8,128)(2,1)S(1)}, bf16[256,256]{1,0:T(8,128)(2,1)S(1)}, u32[]{:S(2)}, u32[]{:S(2)}) %collective-permute-start.17) | collective-permute-done | bytes 131104 | tf_op jit(solution)/shard_map/ppermute | solution.py:460
  298.7 6.4 %collective-permute-done.10 = bf16[256,256]{1,0:T(8,128)(2,1)S(1)} collective-permute-done((bf16[256,256]{1,0:T(8,128)(2,1)S(1)}, bf16[256,256]{1,0:T(8,128)(2,1)S(1)}, u32[]{:S(2)}, u32[]{:S(2)}) %collective-permute-start.10) | collective-permute-done | bytes 131104 | tf_op jit(solution)/shard_map/ppermute | solution.py:460
  308.6 3.1 collective-permute-done.11
  319.5 5.7 %collective-permute-done.12 = bf16[1024,256]{1,0:T(8,128)(2,1)} collective-permute-done((bf16[1024,256]{1,0:T(8,128)(2,1)}, bf16[1024,256]{1,0:T(8,128)(2,1)}, u32[]{:S(2)}, u32[]{:S(2)}) %collective-permute-start.12) | collective-permute-done | bytes 524320 | tf_op jit(solution)/shard_map/ppermute | solution.py:460
  (185 shorter events, 86.5 us)
Async XLA Ops:
  5.8 33.1 %all-to-all-start.2 = ((bf16[8,32,2048]{2,1,0:T(8,128)(2,1)}), bf16[8,32,2048]{2,1,0:T(8,128)(2,1)S(1)}, u32[]{:S(2)}, u32[]{:S(2)}) async-start(bf16[8,32,2048]{2,1,0:T(8,128)(2,1)} %bitcast.147), calls=%async_computation.2 | async-start | bytes 2097152 | tf_op jit(solution)/shard_map/all_to_all | solution.py:510
  38.9 29.5 %all-to-all-start = ((bf16[8,32,2048]{2,1,0:T(8,128)(2,1)}), bf16[8,32,2048]{2,1,0:T(8,128)(2,1)S(1)}, u32[]{:S(2)}, u32[]{:S(2)}) async-start(bf16[8,32,2048]{2,1,0:T(8,128)(2,1)} %bitcast.146), calls=%async_computation | async-start | bytes 2097152 | tf_op jit(solution)/shard_map/all_to_all | solution.py:510
  58.5 25.0 %collective-permute-start.2 = (bf16[4,256,512]{2,1,0:T(8,128)(2,1)S(1)}, bf16[4,256,512]{2,1,0:T(8,128)(2,1)S(1)}, u32[]{:S(2)}, u32[]{:S(2)}) collective-permute-start(bf16[4,256,512]{2,1,0:T(8,128)(2,1)S(1)} %constant_dynamic-slice_fusion.3), channel_id=1, source_target_pairs={{0,8},{8,0},{16,24},{24,16},{1,9},{9,1},{17,25},{25,17},{2,10},{10... | collective-permute-start | bytes 3145736 | tf_op jit(solution)/shard_map/ppermute | solution.py:460
  83.5 22.0 %collective-permute-start = (bf16[4,256,512]{2,1,0:T(8,128)(2,1)}, bf16[4,256,512]{2,1,0:T(8,128)(2,1)}, u32[]{:S(2)}, u32[]{:S(2)}) collective-permute-start(bf16[4,256,512]{2,1,0:T(8,128)(2,1)} %constant_dynamic-slice_fusion.4), channel_id=1, source_target_pairs={{0,8},{8,0},{16,24},{24,16},{1,9},{9,1},{17,25},{25,17},{2,10},{10... | collective-permute-start | bytes 3145736 | tf_op jit(solution)/shard_map/ppermute | solution.py:460
  85.2 14.4 %collective-permute-start.3 = (bf16[2,256,512]{2,1,0:T(8,128)(2,1)S(1)}, bf16[2,256,512]{2,1,0:T(8,128)(2,1)S(1)}, u32[]{:S(2)}, u32[]{:S(2)}) collective-permute-start(bf16[2,256,512]{2,1,0:T(8,128)(2,1)S(1)} %dynamic-slice_convert_fusion.2), channel_id=1, source_target_pairs={{0,16},{8,24},{16,0},{24,8},{1,17},{9,25},{17,1},{25,9},{2,18},{10... | collective-permute-start | bytes 1572872 | tf_op jit(solution)/shard_map/ppermute | solution.py:460
  101.8 19.0 %all-to-all-start.3 = ((bf16[8,2,32,512]{3,2,1,0:T(8,128)(2,1)}), bf16[8,2,32,512]{3,2,1,0:T(8,128)(2,1)S(1)}, u32[]{:S(2)}, u32[]{:S(2)}) async-start(bf16[8,2,32,512]{3,2,1,0:T(8,128)(2,1)} %bitcast.134), calls=%async_computation.3 | async-start | bytes 1048576 | tf_op jit(solution)/shard_map/all_to_all | solution.py:517
  107.1 13.5 %collective-permute-start.1 = (bf16[2,256,512]{2,1,0:T(8,128)(2,1)S(1)}, bf16[2,256,512]{2,1,0:T(8,128)(2,1)S(1)}, u32[]{:S(2)}, u32[]{:S(2)}) collective-permute-start(bf16[2,256,512]{2,1,0:T(8,128)(2,1)S(1)} %dynamic-slice_convert_fusion.3), channel_id=1, source_target_pairs={{0,16},{8,24},{16,0},{24,8},{1,17},{9,25},{17,1},{25,9},{2,18},{10... | collective-permute-start | bytes 1572872 | tf_op jit(solution)/shard_map/ppermute | solution.py:460
  141.9 12.3 %all-to-all-start.4 = ((bf16[4,64,1024]{2,1,0:T(8,128)(2,1)}), bf16[4,64,1024]{2,1,0:T(8,128)(2,1)S(1)}, u32[]{:S(2)}, u32[]{:S(2)}) async-start(bf16[4,64,1024]{2,1,0:T(8,128)(2,1)} %bitcast.140), calls=%async_computation.4 | async-start | bytes 1048576 | tf_op jit(solution)/shard_map/all_to_all | solution.py:530
  197.2 17.7 %collective-permute-start.25 = (bf16[1280,128]{1,0:T(8,128)(2,1)S(1)}, bf16[1280,128]{1,0:T(8,128)(2,1)S(1)}, u32[]{:S(2)}, u32[]{:S(2)}) collective-permute-start(bf16[1280,128]{1,0:T(8,128)(2,1)S(1)} %dynamic-slice_convert_fusion.4), channel_id=1, source_target_pairs={{0,4},{1,5},{2,6},{3,7},{4,0},{5,1},{6,2},{7,3},{8,12},{9,13},{10,... | collective-permute-start | bytes 983048 | tf_op jit(solution)/shard_map/ppermute | solution.py:460
  215.0 5.7 %collective-permute-start.26 = (bf16[640,128]{1,0:T(8,128)(2,1)S(1)}, bf16[640,128]{1,0:T(8,128)(2,1)S(1)}, u32[]{:S(2)}, u32[]{:S(2)}) collective-permute-start(bf16[640,128]{1,0:T(8,128)(2,1)S(1)} %dynamic-slice_convert_fusion.7), channel_id=1, source_target_pairs={{0,2},{1,3},{2,0},{3,1},{4,6},{5,7},{6,4},{7,5},{8,10},{9,11},{10,... | collective-permute-start | bytes 491528 | tf_op jit(solution)/shard_map/ppermute | solution.py:460
  216.2 31.8 %collective-permute-start.4 = (bf16[2048,256]{1,0:T(8,128)(2,1)}, bf16[2048,256]{1,0:T(8,128)(2,1)S(1)}, u32[]{:S(2)}, u32[]{:S(2)}) collective-permute-start(bf16[2048,256]{1,0:T(8,128)(2,1)} %constant_dynamic-slice_fusion.2), channel_id=1, source_target_pairs={{0,8},{8,0},{16,24},{24,16},{1,9},{9,1},{17,25},{25,17},{2,10},{10... | collective-permute-start | bytes 3145736 | tf_op jit(solution)/shard_map/ppermute | solution.py:460
  220.8 4.6 %collective-permute-start.27 = (bf16[320,128]{1,0:T(8,128)(2,1)S(1)}, bf16[320,128]{1,0:T(8,128)(2,1)}, u32[]{:S(2)}, u32[]{:S(2)}) collective-permute-start(bf16[320,128]{1,0:T(8,128)(2,1)S(1)} %dynamic-slice_convert_fusion.10), channel_id=1, source_target_pairs={{0,16},{8,24},{16,0},{24,8},{1,17},{9,25},{17,1},{25,9},{2,18},{10... | collective-permute-start | bytes 245768 | tf_op jit(solution)/shard_map/ppermute | solution.py:460
  226.9 20.3 %collective-permute-start.28 = (bf16[160,128]{1,0:T(8,128)(2,1)S(1)}, bf16[160,128]{1,0:T(8,128)(2,1)S(1)}, u32[]{:S(2)}, u32[]{:S(2)}) collective-permute-start(bf16[160,128]{1,0:T(8,128)(2,1)S(1)} %dynamic-slice_convert_fusion.13), channel_id=1, source_target_pairs={{0,1},{1,0},{2,3},{3,2},{4,5},{5,4},{6,7},{7,6},{8,9},{9,8},{10,11... | collective-permute-start | bytes 122888 | tf_op jit(solution)/shard_map/ppermute | solution.py:460
  229.3 28.0 %collective-permute-start.14 = (bf16[2048,256]{1,0:T(8,128)(2,1)}, bf16[2048,256]{1,0:T(8,128)(2,1)}, u32[]{:S(2)}, u32[]{:S(2)}) collective-permute-start(bf16[2048,256]{1,0:T(8,128)(2,1)} %constant_dynamic-slice_fusion.1), channel_id=1, source_target_pairs={{0,8},{8,0},{16,24},{24,16},{1,9},{9,1},{17,25},{25,17},{2,10},{10... | collective-permute-start | bytes 3145736 | tf_op jit(solution)/shard_map/ppermute | solution.py:460
  251.4 5.4 %collective-permute-start.30 = (bf16[320,128]{1,0:T(8,128)(2,1)S(1)}, bf16[320,128]{1,0:T(8,128)(2,1)S(1)}, u32[]{:S(2)}, u32[]{:S(2)}) collective-permute-start(bf16[320,128]{1,0:T(8,128)(2,1)S(1)} %pad_maximum_fusion.17), channel_id=1, source_target_pairs={{0,16},{8,24},{16,0},{24,8},{1,17},{9,25},{17,1},{25,9},{2,18},{10... | collective-permute-start | bytes 245768 | tf_op jit(solution)/shard_map/ppermute | solution.py:460
  251.9 14.5 %collective-permute-start.5 = (bf16[1024,256]{1,0:T(8,128)(2,1)S(1)}, bf16[1024,256]{1,0:T(8,128)(2,1)S(1)}, u32[]{:S(2)}, u32[]{:S(2)}) collective-permute-start(bf16[1024,256]{1,0:T(8,128)(2,1)S(1)} %dynamic-slice_convert_fusion.1), channel_id=1, source_target_pairs={{0,16},{8,24},{16,0},{24,8},{1,17},{9,25},{17,1},{25,9},{2,18},{10... | collective-permute-start | bytes 1572872 | tf_op jit(solution)/shard_map/ppermute | solution.py:460
  256.9 5.4 %collective-permute-start.31 = (bf16[640,128]{1,0:T(8,128)(2,1)S(1)}, bf16[640,128]{1,0:T(8,128)(2,1)S(1)}, u32[]{:S(2)}, u32[]{:S(2)}) collective-permute-start(bf16[640,128]{1,0:T(8,128)(2,1)S(1)} %pad_maximum_fusion.14), channel_id=1, source_target_pairs={{0,2},{1,3},{2,0},{3,1},{4,6},{5,7},{6,4},{7,5},{8,10},{9,11},{10,... | collective-permute-start | bytes 491528 | tf_op jit(solution)/shard_map/ppermute | solution.py:460
  258.8 12.9 %collective-permute-start.15 = (bf16[1024,256]{1,0:T(8,128)(2,1)S(1)}, bf16[1024,256]{1,0:T(8,128)(2,1)S(1)}, u32[]{:S(2)}, u32[]{:S(2)}) collective-permute-start(bf16[1024,256]{1,0:T(8,128)(2,1)S(1)} %dynamic-slice_convert_fusion), channel_id=1, source_target_pairs={{0,1},{1,0},{2,3},{3,2},{4,5},{5,4},{6,7},{7,6},{8,9},{9,8},{10,11... | collective-permute-start | bytes 1572872 | tf_op jit(solution)/shard_map/ppermute | solution.py:460
  262.4 19.0 %collective-permute-start.32 = (bf16[1280,128]{1,0:T(8,128)(2,1)S(1)}, bf16[1280,128]{1,0:T(8,128)(2,1)S(1)}, u32[]{:S(2)}, u32[]{:S(2)}) collective-permute-start(bf16[1280,128]{1,0:T(8,128)(2,1)S(1)} %pad_maximum_fusion.9), channel_id=1, source_target_pairs={{0,4},{1,5},{2,6},{3,7},{4,0},{5,1},{6,2},{7,3},{8,12},{9,13},{10,... | collective-permute-start | bytes 983048 | tf_op jit(solution)/shard_map/ppermute | solution.py:460
  266.5 8.7 %collective-permute-start.6 = (bf16[512,256]{1,0:T(8,128)(2,1)S(1)}, bf16[512,256]{1,0:T(8,128)(2,1)S(1)}, u32[]{:S(2)}, u32[]{:S(2)}) collective-permute-start(bf16[512,256]{1,0:T(8,128)(2,1)S(1)} %dynamic-slice_convert_fusion.6), channel_id=1, source_target_pairs={{0,1},{1,0},{2,3},{3,2},{4,5},{5,4},{6,7},{7,6},{8,9},{9,8},{10,11... | collective-permute-start | bytes 786440 | tf_op jit(solution)/shard_map/ppermute | solution.py:460
  271.8 6.4 %collective-permute-start.16 = (bf16[512,256]{1,0:T(8,128)(2,1)S(1)}, bf16[512,256]{1,0:T(8,128)(2,1)S(1)}, u32[]{:S(2)}, u32[]{:S(2)}) collective-permute-start(bf16[512,256]{1,0:T(8,128)(2,1)S(1)} %dynamic-slice_convert_fusion.5), channel_id=1, source_target_pairs={{0,16},{8,24},{16,0},{24,8},{1,17},{9,25},{17,1},{25,9},{2,18},{10... | collective-permute-start | bytes 786440 | tf_op jit(solution)/shard_map/ppermute | solution.py:460
  275.4 9.3 %collective-permute-start.7 = (bf16[256,256]{1,0:T(8,128)(2,1)S(1)}, bf16[256,256]{1,0:T(8,128)(2,1)S(1)}, u32[]{:S(2)}, u32[]{:S(2)}) collective-permute-start(bf16[256,256]{1,0:T(8,128)(2,1)S(1)} %dynamic-slice_convert_fusion.9), channel_id=1, source_target_pairs={{0,4},{1,5},{2,6},{3,7},{4,0},{5,1},{6,2},{7,3},{8,12},{9,13},{10,... | collective-permute-start | bytes 393224 | tf_op jit(solution)/shard_map/ppermute | solution.py:460
  278.3 9.9 %collective-permute-start.17 = (bf16[256,256]{1,0:T(8,128)(2,1)S(1)}, bf16[256,256]{1,0:T(8,128)(2,1)S(1)}, u32[]{:S(2)}, u32[]{:S(2)}) collective-permute-start(bf16[256,256]{1,0:T(8,128)(2,1)S(1)} %dynamic-slice_convert_fusion.8), channel_id=1, source_target_pairs={{0,4},{1,5},{2,6},{3,7},{4,0},{5,1},{6,2},{7,3},{8,12},{9,13},{10,... | collective-permute-start | bytes 393224 | tf_op jit(solution)/shard_map/ppermute | solution.py:460
  281.5 36.7 %collective-permute-start.33 = (bf16[2560,128]{1,0:T(8,128)(2,1)S(1)}, bf16[2560,128]{1,0:T(8,128)(2,1)S(1)}, u32[]{:S(2)}, u32[]{:S(2)}) collective-permute-start(bf16[2560,128]{1,0:T(8,128)(2,1)S(1)} %pad_maximum_fusion.6), channel_id=1, source_target_pairs={{0,8},{8,0},{16,24},{24,16},{1,9},{9,1},{17,25},{25,17},{2,10},{10... | collective-permute-start | bytes 1966088 | tf_op jit(solution)/shard_map/ppermute | solution.py:460
  289.0 4.5 %collective-permute-start.9 = (bf16[128,256]{1,0:T(8,128)(2,1)S(1)}, bf16[128,256]{1,0:T(8,128)(2,1)S(1)}, u32[]{:S(2)}, u32[]{:S(2)}) collective-permute-start(bf16[128,256]{1,0:T(8,128)(2,1)S(1)} %add_convert_fusion.3), channel_id=1, source_target_pairs={{0,2},{1,3},{2,0},{3,1},{4,6},{5,7},{6,4},{7,5},{8,10},{9,11},{10,... | collective-permute-start | bytes 196616 | tf_op jit(solution)/shard_map/ppermute | solution.py:460
  292.6 4.5 %collective-permute-start.19 = (bf16[128,256]{1,0:T(8,128)(2,1)S(1)}, bf16[128,256]{1,0:T(8,128)(2,1)S(1)}, u32[]{:S(2)}, u32[]{:S(2)}) collective-permute-start(bf16[128,256]{1,0:T(8,128)(2,1)S(1)} %add_convert_fusion.2), channel_id=1, source_target_pairs={{0,2},{1,3},{2,0},{3,1},{4,6},{5,7},{6,4},{7,5},{8,10},{9,11},{10,... | collective-permute-start | bytes 196616 | tf_op jit(solution)/shard_map/ppermute | solution.py:460
  293.6 11.6 %collective-permute-start.10 = (bf16[256,256]{1,0:T(8,128)(2,1)S(1)}, bf16[256,256]{1,0:T(8,128)(2,1)S(1)}, u32[]{:S(2)}, u32[]{:S(2)}) collective-permute-start(bf16[256,256]{1,0:T(8,128)(2,1)S(1)} %pad_maximum_fusion.15), channel_id=1, source_target_pairs={{0,4},{1,5},{2,6},{3,7},{4,0},{5,1},{6,2},{7,3},{8,12},{9,13},{10,... | collective-permute-start | bytes 393224 | tf_op jit(solution)/shard_map/ppermute | solution.py:460
  297.2 9.5 %collective-permute-start.20 = (bf16[256,256]{1,0:T(8,128)(2,1)S(1)}, bf16[256,256]{1,0:T(8,128)(2,1)S(1)}, u32[]{:S(2)}, u32[]{:S(2)}) collective-permute-start(bf16[256,256]{1,0:T(8,128)(2,1)S(1)} %pad_maximum_fusion.16), channel_id=1, source_target_pairs={{0,4},{1,5},{2,6},{3,7},{4,0},{5,1},{6,2},{7,3},{8,12},{9,13},{10,... | collective-permute-start | bytes 393224 | tf_op jit(solution)/shard_map/ppermute | solution.py:460
  305.3 6.4 %collective-permute-start.11 = (bf16[512,256]{1,0:T(8,128)(2,1)S(1)}, bf16[512,256]{1,0:T(8,128)(2,1)S(1)}, u32[]{:S(2)}, u32[]{:S(2)}) collective-permute-start(bf16[512,256]{1,0:T(8,128)(2,1)S(1)} %pad_maximum_fusion.11), channel_id=1, source_target_pairs={{0,1},{1,0},{2,3},{3,2},{4,5},{5,4},{6,7},{7,6},{8,9},{9,8},{10,11... | collective-permute-start | bytes 786440 | tf_op jit(solution)/shard_map/ppermute | solution.py:460
  306.7 9.3 %collective-permute-start.21 = (bf16[512,256]{1,0:T(8,128)(2,1)S(1)}, bf16[512,256]{1,0:T(8,128)(2,1)S(1)}, u32[]{:S(2)}, u32[]{:S(2)}) collective-permute-start(bf16[512,256]{1,0:T(8,128)(2,1)S(1)} %pad_maximum_fusion.12), channel_id=1, source_target_pairs={{0,16},{8,24},{16,0},{24,8},{1,17},{9,25},{17,1},{25,9},{2,18},{10... | collective-permute-start | bytes 786440 | tf_op jit(solution)/shard_map/ppermute | solution.py:460
  312.6 12.6 %collective-permute-start.12 = (bf16[1024,256]{1,0:T(8,128)(2,1)}, bf16[1024,256]{1,0:T(8,128)(2,1)}, u32[]{:S(2)}, u32[]{:S(2)}) collective-permute-start(bf16[1024,256]{1,0:T(8,128)(2,1)} %pad_maximum_fusion.7), channel_id=1, source_target_pairs={{0,16},{8,24},{16,0},{24,8},{1,17},{9,25},{17,1},{25,9},{2,18},{10... | collective-permute-start | bytes 1572872 | tf_op jit(solution)/shard_map/ppermute | solution.py:460
  316.9 9.8 %collective-permute-start.22 = (bf16[1024,256]{1,0:T(8,128)(2,1)}, bf16[1024,256]{1,0:T(8,128)(2,1)S(1)}, u32[]{:S(2)}, u32[]{:S(2)}) collective-permute-start(bf16[1024,256]{1,0:T(8,128)(2,1)} %pad_maximum_fusion.8), channel_id=1, source_target_pairs={{0,1},{1,0},{2,3},{3,2},{4,5},{5,4},{6,7},{7,6},{8,9},{9,8},{10,11... | collective-permute-start | bytes 1572872 | tf_op jit(solution)/shard_map/ppermute | solution.py:460
  (19 other events, 128.5 us)

commit v2 on v1

--- a/solution.py
+++ b/solution.py
@@ -176,7 +176,18 @@
     return jnp.concatenate(pieces, axis=0)
 
 
-def backward_kernel(count, latent_ref, act_ref, slope_ref, w_ref, grad_two_ref, kgrad_one_ref, kgrad_two_ref, grad_one, adj, total_one, total_two):
+def backward_kernel(count, side_ref, latent_ref, act_ref, slope_ref, w_ref, grad_two_ref, third_ref, kept_ref, sent_ref, grad_one, adj, total_one, total_two):
+    side = side_ref[0]
+
+    def put(half, rows, values):
+        @pl.when(side == half)
+        def _():
+            kept_ref[rows, :] = values().astype(jnp.bfloat16)
+
+        @pl.when(side != half)
+        def _():
+            sent_ref[rows, :] = values().astype(jnp.bfloat16)
+
     height = act_ref.shape[0]
     breadth = act_ref.shape[1] // count
     mid_chan = act_ref.shape[2]
@@ -206,18 +217,23 @@
                     total_two[parity, mid_chan:, :] = far
                 else:
                     total_two[parity, mid_chan:, :] += far
-    for parity in (0, 1):
-        for which in (0, 1):
-            row_tap = ROW_TAPS[parity][which]
-            for slot, col_tap in enumerate(COL_TAPS):
-                rows = pl.ds((row_tap * 4 + col_tap) * mid_chan, mid_chan)
-                kgrad_two_ref[rows, :] = total_two[
-                    parity, which * mid_chan:(which + 1) * mid_chan, slot * out_chan:(slot + 1) * out_chan
-                ].astype(kgrad_two_ref.dtype)
     for row in range(height):
         upstream = adj[row].astype(jnp.bfloat16).astype(jnp.float32)
         grad_one[row] = (upstream * slope_ref[row]).astype(jnp.bfloat16)
     in_chan = latent_ref.shape[0] * latent_ref.shape[2] // (H0 * W0)
+    tail = 8 * in_chan
+    lanes = 2 * out_chan
+    for parity in (0, 1):
+        for which in (0, 1):
+            for pair in (0, 1):
+                rows = pl.ds(tail + (2 * which + pair) * mid_chan, mid_chan)
+                above, left_edge = which * mid_chan, pair * lanes
+                put(
+                    parity,
+                    rows,
+                    lambda: total_two[parity, above:above + mid_chan, left_edge:left_edge + lanes],
+                )
+        put(parity, pl.ds(tail + 4 * mid_chan, third_ref.shape[1]), lambda: third_ref[parity])
     for parity in (0, 1):
         for which in (0, 1):
             lefts = []
@@ -232,8 +248,8 @@
             total_one[...] = product_tn(left, right)
             row_tap = ROW_TAPS[parity][which]
             for slot, col_tap in enumerate(COL_TAPS):
-                rows = pl.ds((row_tap * 4 + col_tap) * in_chan, in_chan)
-                kgrad_one_ref[rows, :] = total_one[:, slot * mid_chan:(slot + 1) * mid_chan].astype(kgrad_one_ref.dtype)
+                rows = pl.ds(((row_tap % 2) * 4 + col_tap) * in_chan, in_chan)
+                put(row_tap // 2, rows, lambda: total_one[:, slot * mid_chan:(slot + 1) * mid_chan])
 
 
 def params(steps=0):
@@ -298,18 +314,16 @@
     )(act_two, slope_two, w_three, target)
 
 
-def backward(latent, act_one, slope_one, w_two, grad_two, kind):
+def backward(side, latent, act_one, slope_one, w_two, grad_two, third):
     count = latent.shape[1]
     in_chan = latent.shape[0] * latent.shape[2] // (H0 * W0)
     mid_chan = act_one.shape[2]
-    out_chan = grad_two.shape[2]
     return pl.pallas_call(
         functools.partial(backward_kernel, count),
         name="decoder_backward",
-        out_shape=(
-            jax.ShapeDtypeStruct((16 * in_chan, mid_chan), kind),
-            jax.ShapeDtypeStruct((16 * mid_chan, out_chan), kind),
-        ),
+        in_specs=[pl.BlockSpec(memory_space=pltpu.SMEM)] + [pl.BlockSpec(memory_space=pltpu.VMEM)] * 6,
+        out_specs=(pl.BlockSpec(memory_space=pltpu.VMEM),) * 2,
+        out_shape=(jax.ShapeDtypeStruct((8 * in_chan + 4 * mid_chan + third.shape[1], mid_chan), jnp.bfloat16),) * 2,
         scratch_shapes=[
             pltpu.VMEM(act_one.shape, jnp.bfloat16),
             pltpu.VMEM(act_one.shape, jnp.float32),
@@ -317,36 +331,68 @@
             pltpu.VMEM(w_two.shape, jnp.float32),
         ],
         compiler_params=params(),
-    )(latent, act_one, slope_one, w_two, grad_two)
-
-
-def unpaired_third(paired, in_chan):
-    out_chan = paired.shape[2] // 4
-    view = paired.reshape(2, 2, in_chan, 4, out_chan)
-    pieces = [None] * 16
-    for parity in (0, 1):
-        for which in (0, 1):
-            for slot, col_tap in enumerate(COL_TAPS):
-                pieces[ROW_TAPS[parity][which] * 4 + col_tap] = view[parity, which, :, slot, :]
-    return jnp.concatenate(pieces, axis=0)
-
-
-def spatial_first(grid):
+    )(side, latent, act_one, slope_one, w_two, grad_two, third)
+
+
+def spatial_first_kernel(grid_ref, after_ref, rows_ref, tmp):
+    count, height, breadth, chan = grid_ref.shape
+    for row in range(height):
+        tmp[...] = grid_ref[:, row].astype(jnp.float32)
+        even = tmp[:, pl.ds(0, breadth // 2, 2), :]
+        odd = tmp[:, pl.ds(1, breadth // 2, 2), :]
+        turned = jnp.swapaxes(jnp.concatenate([even, odd], axis=2), 0, 1)
+        rows_ref[row] = turned.reshape(breadth // 2 * count, 2 * chan).astype(jnp.bfloat16)
+
+
+def spatial_first(grid, after):
     count, height, breadth, chan = grid.shape
-    return (
-        grid.reshape(count, height, breadth // 2, 2 * chan)
-        .transpose(1, 2, 0, 3)
-        .reshape(height, breadth // 2 * count, 2 * chan)
-    )
-
-
-def sample_first(rows, count, chan):
-    height = rows.shape[0]
-    return (
-        rows.reshape(height, -1, count, 2 * chan)
-        .transpose(2, 0, 1, 3)
-        .reshape(count, height, -1, chan)
-    )
+    per = 4
+    flat = breadth // 2 * count
+    return pl.pallas_call(
+        spatial_first_kernel,
+        name="spatial_first",
+        grid=(height // per,),
+        in_specs=[
+            pl.BlockSpec((count, per, breadth, chan), lambda step: (0, step, 0, 0)),
+            pl.BlockSpec(memory_space=pl.ANY),
+        ],
+        out_specs=pl.BlockSpec((per, flat, 2 * chan), lambda step: (step, 0, 0)),
+        out_shape=jax.ShapeDtypeStruct((height, flat, 2 * chan), jnp.bfloat16),
+        scratch_shapes=[pltpu.VMEM((count, breadth, chan), jnp.float32)],
+        compiler_params=params(1),
+        cost_estimate=pl.CostEstimate(flops=0, bytes_accessed=28000000, transcendentals=0),
+    )(grid, after)
+
+
+def sample_first_kernel(rows_ref, after_ref, out_ref, tmp):
+    height = rows_ref.shape[0]
+    count, _, breadth, chan = out_ref.shape
+    for row in range(height):
+        value = rows_ref[row].astype(jnp.float32).reshape(breadth // 2, count, 2 * chan)
+        turned = jnp.swapaxes(value, 0, 1)
+        tmp[:, pl.ds(0, breadth // 2, 2), :] = turned[:, :, :chan]
+        tmp[:, pl.ds(1, breadth // 2, 2), :] = turned[:, :, chan:]
+        out_ref[:, row] = tmp[...].astype(jnp.bfloat16)
+
+
+def sample_first(rows, count, chan, after):
+    height, flat, lanes = rows.shape
+    breadth = 2 * flat // count
+    per = 4
+    return pl.pallas_call(
+        sample_first_kernel,
+        name="sample_first",
+        grid=(height // per,),
+        in_specs=[
+            pl.BlockSpec((per, flat, lanes), lambda step: (step, 0, 0)),
+            pl.BlockSpec(memory_space=pl.ANY),
+        ],
+        out_specs=pl.BlockSpec((count, per, breadth, chan), lambda step: (0, step, 0, 0)),
+        out_shape=jax.ShapeDtypeStruct((count, height, breadth, chan), jnp.bfloat16),
+        scratch_shapes=[pltpu.VMEM((count, breadth, chan), jnp.float32)],
+        compiler_params=params(1),
+        cost_estimate=pl.CostEstimate(flops=0, bytes_accessed=28000000, transcendentals=0),
+    )(rows, after)
 
 
 def bucket_kernel(subject_ref, count_ref, shift_ref, fmri_ref, first_ref, second_ref, place_ref):
@@ -396,31 +442,35 @@
     )(subject, voxel_count, shift, fmri)
 
 
-def project_kernel(rows_ref, map_ref, out_ref):
+def project_kernel(half_ref, rows_ref, map_ref, after_ref, out_ref):
     out_ref[0] = product(rows_ref[...], map_ref[0]).astype(jnp.bfloat16)
 
 
-def projected(rows, maps):
+def projected(rows, maps, half, after):
     count, voxels = rows.shape
-    blocks = H0 * W0
-    width = maps.shape[2] // blocks
+    blocks = H0 * W0 // 2
+    width = maps.shape[2] // (2 * blocks)
     return pl.pallas_call(
         project_kernel,
         name="project_rows",
-        grid=(blocks,),
-        in_specs=[
-            pl.BlockSpec((count, voxels), lambda step: (0, 0)),
-            pl.BlockSpec((1, voxels, width), lambda step: (0, 0, step)),
-        ],
-        out_specs=pl.BlockSpec((1, count, width), lambda step: (step, 0, 0)),
+        grid_spec=pltpu.PrefetchScalarGridSpec(
+            num_scalar_prefetch=1,
+            grid=(blocks,),
+            in_specs=[
+                pl.BlockSpec((count, voxels), lambda step, half: (0, 0)),
+                pl.BlockSpec((1, voxels, width), lambda step, half: (0, 0, half[0] * blocks + step)),
+                pl.BlockSpec(memory_space=pl.ANY),
+            ],
+            out_specs=pl.BlockSpec((1, count, width), lambda step, half: (step, 0, 0)),
+        ),
         out_shape=jax.ShapeDtypeStruct((blocks, count, width), jnp.bfloat16),
         compiler_params=params(1),
         cost_estimate=pl.CostEstimate(
-            flops=2 * count * voxels * maps.shape[2],
-            bytes_accessed=2 * voxels * maps.shape[2],
+            flops=count * voxels * maps.shape[2],
+            bytes_accessed=voxels * maps.shape[2],
             transcendentals=0,
         ),
-    )(rows, maps)
+    )(half, rows, maps, after)
 
 
 def collect_kernel(place_ref, first_ref, second_ref, out_ref):
@@ -439,6 +489,53 @@
         out_shape=jax.ShapeDtypeStruct((samples, first.shape[1] * first.shape[3]), jnp.bfloat16),
         compiler_params=params(),
     )(place, first, second)
+
+
+def finish_kernel(third_rows, side_ref, own_a, own_b, own_c, other_a, other_b, other_c, first_ref, second_ref, third_ref):
+    side = side_ref[0]
+    rows = own_a.shape[0]
+    for at, (source, half) in enumerate(((own_a, side), (own_b, side), (other_a, 1 - side), (other_b, 1 - side))):
+        start = pl.multiple_of((2 * half + at % 2) * rows, rows)
+        first_ref[pl.ds(start, rows), :] = source[...]
+    out_chan = second_ref.shape[1]
+    mid_chan = second_ref.shape[0] // 16
+    for parity in (0, 1):
+        mine = side == parity
+        for which in (0, 1):
+            for pair in (0, 1):
+                here = pl.ds((2 * which + pair) * mid_chan, mid_chan)
+                value = jnp.where(mine, own_c[here, :].astype(jnp.float32), other_c[here, :].astype(jnp.float32))
+                for inner in (0, 1):
+                    col_tap = COL_TAPS[2 * pair + inner]
+                    to = pl.ds((ROW_TAPS[parity][which] * 4 + col_tap) * mid_chan, mid_chan)
+                    second_ref[to, :] = value[:, inner * out_chan:(inner + 1) * out_chan].astype(jnp.bfloat16)
+        here = pl.ds(4 * mid_chan, third_rows)
+        value = jnp.where(mine, own_c[here, :].astype(jnp.float32), other_c[here, :].astype(jnp.float32)).T
+        chan = third_ref.shape[0]
+        inputs = third_rows // 2
+        for which in (0, 1):
+            for slot, col_tap in enumerate(COL_TAPS):
+                to = pl.ds((ROW_TAPS[parity][which] * 4 + col_tap) * inputs, inputs)
+                piece = value[slot * chan:(slot + 1) * chan, which * inputs:(which + 1) * inputs]
+                third_ref[:, to] = piece.astype(jnp.bfloat16)
+
+
+def finished(side, own, other, third_rows):
+    rows, lanes = own[0].shape
+    mid_chan = (own[2].shape[0] - third_rows) // 4
+    vmem = pl.BlockSpec(memory_space=pltpu.VMEM)
+    return pl.pallas_call(
+        functools.partial(finish_kernel, third_rows),
+        name="finish_gradients",
+        in_specs=[pl.BlockSpec(memory_space=pltpu.SMEM)] + [vmem] * 6,
+        out_specs=(vmem, vmem, vmem),
+        out_shape=(
+            jax.ShapeDtypeStruct((4 * rows, lanes), jnp.bfloat16),
+            jax.ShapeDtypeStruct((16 * mid_chan, lanes // 2), jnp.bfloat16),
+            jax.ShapeDtypeStruct((lanes // 4, 8 * third_rows), jnp.bfloat16),
+        ),
+        compiler_params=params(),
+    )(side, *own, *other)
 
 
 def rounded(values):
@@ -455,98 +552,144 @@
     return bits
 
 
-def exchanged(values, hop):
-    axis, bit = hop
-    return lax.ppermute(values, axis, [(at, at ^ bit) for at in range(lax.axis_size(axis))])
-
-
 def upper(hop):
     axis, bit = hop
     return (lax.axis_index(axis) // bit) % 2
 
 
-def summed_share(values, hops):
-    for hop in hops:
-        half = values.shape[0] // 2
-        side = upper(hop)
-        sent = lax.dynamic_slice_in_dim(values, (1 - side) * half, half, 0).astype(jnp.bfloat16)
-        kept = lax.dynamic_slice_in_dim(values, side * half, half, 0).astype(jnp.float32)
-        values = kept + exchanged(sent, hop).astype(jnp.float32)
-    return values
-
-
-def all_shares(values, hops):
-    for hop in reversed(hops):
-        other = exchanged(values, hop)
-        first = upper(hop) == 0
-        values = jnp.concatenate(
-            [jnp.where(first, values, other), jnp.where(first, other, values)], axis=0
-        )
-    return values
-
-
-def all_summed(values, hops):
-    return all_shares(summed_share(values, hops).astype(jnp.bfloat16), hops)
+def place_of(step):
+    return sum(upper(hop) * 2 ** at for at, hop in enumerate(step))
+
+
+def exchanged(values, step, change):
+    axis = step[0][0]
+    flip = sum(hop[1] for at, hop in enumerate(step) if change >> at & 1)
+    return lax.ppermute(values, axis, [(at, at ^ flip) for at in range(lax.axis_size(axis))])
+
+
+def summed(terms):
+    value = terms[0]
+    for term in terms[1:]:
+        value = value.astype(jnp.float32) + term.astype(jnp.float32)
+    return value
+
+
+def shared(chains, step):
+    ways = 2 ** len(step)
+    place = place_of(step)
+
+    def part(terms, which):
+        size = terms[0].shape[0] // ways
+        return summed([lax.dynamic_slice_in_dim(term, which * size, size, 0) for term in terms])
+
+    arrived = []
+    for change in range(1, ways):
+        sent = [part(terms, place ^ change).astype(jnp.bfloat16) for terms in chains]
+        joined = jnp.concatenate(sent, axis=0) if len(sent) > 1 else sent[0]
+        arrived.append(exchanged(joined, step, change))
+    result = []
+    start = 0
+    for terms in chains:
+        size = terms[0].shape[0] // ways
+        result.append([part(terms, place)] + [values[start:start + size] for values in arrived])
+        start += size
+    return result
+
+
+def gathered(chains, step):
+    ways = 2 ** len(step)
+    joined = jnp.concatenate(chains, axis=0) if len(chains) > 1 else chains[0]
+    pieces = [joined] + [exchanged(joined, step, change) for change in range(1, ways)]
+    place = place_of(step)
+    result = []
+    start = 0
+    for values in chains:
+        size = values.shape[0]
+        out = jnp.concatenate([values] * ways, axis=0)
+        for change in range(1, ways):
+            piece = pieces[change][start:start + size]
+            out = lax.dynamic_update_slice_in_dim(out, piece, (place ^ change) * size, 0)
+        result.append(out)
+        start += size
+    return result
+
+
+def over_chains(move, chains, steps):
+    result = [None] * len(chains)
+    for step in {tuple(step): step for step in steps}.values():
+        members = [at for at, own in enumerate(steps) if own == step]
+        for at, moved_chain in zip(members, move([chains[at] for at in members], step)):
+            result[at] = moved_chain
+    return result
 
 
 def shards(fmri, subject, ridge_maps, voxel_count, w_first, w_second, w_third, target):
     dp_count = lax.axis_size("dp")
+    holders = lax.axis_size("vox")
     samp_dev = fmri.shape[0]
     vox_local = fmri.shape[1]
     mid_chan = w_first.shape[1]
     last_chan = w_second.shape[1]
-    slots = samp_dev
-    room = slots // dp_count
+    room = samp_dev // dp_count
     vox_bits = bit_pairs("vox")
     dp_bits = bit_pairs("dp")
+    side = upper(vox_bits[0]).astype(jnp.int32).reshape(1)
     shift = (lax.axis_index("vox") * vox_local).astype(jnp.int32).reshape(1)
-    first, second, place = bucketed(subject, voxel_count, shift, fmri, slots)
-    first, second, target, w_second, w_third = lax.optimization_barrier(
-        (first, second, target, w_second, w_third)
-    )
+    first, second, place = bucketed(subject, voxel_count, shift, fmri, samp_dev)
 
     def routed(rows):
         sent = rows.reshape(dp_count, room, rows.shape[1])
         return lax.all_to_all(sent, "dp", split_axis=0, concat_axis=0, tiled=True).reshape(rows.shape)
 
-    def returned(rows):
-        partial_value = projected(rows, ridge_maps)
-        latent_part = rounded(summed_share(partial_value, vox_bits))
+    def vox_summed(rows, after):
+        sent = projected(rows, ridge_maps, 1 - side, after)
+        received = exchanged(sent, vox_bits[:1], 1)
+        terms = [projected(rows, ridge_maps, side, sent), received]
+        for hop in vox_bits[1:]:
+            terms, = shared([terms], [hop])
+        return terms, received
+
+    def returned(terms):
+        latent_part = rounded(summed(terms))
         blocks, _, width = latent_part.shape
         sent = latent_part.reshape(blocks, dp_count, room, width).swapaxes(0, 1)
         return lax.all_to_all(sent, "dp", split_axis=0, concat_axis=0, tiled=True)
 
     first = routed(first)
     second = routed(second)
+    terms_first, _ = vox_summed(first, voxel_count)
+    terms_second, core_second = vox_summed(second, terms_first[1])
     pair_two = paired_weight(w_second, mid_chan)
     pair_three = paired_weight(w_third, last_chan)
-    target_rows = spatial_first(target)
-    second, pair_two, pair_three, target_rows = lax.optimization_barrier(
-        (second, pair_two, pair_three, target_rows)
-    )
-    own_rows = collected(place, returned(first), returned(second))
-    holders = lax.axis_size("vox")
+    target_rows = spatial_first(target, core_second)
+    own_rows = collected(place, returned(terms_first), returned(terms_second))
     own_rows = own_rows.reshape(holders, samp_dev // holders, own_rows.shape[1])
     latent = lax.all_to_all(own_rows, "vox", split_axis=0, concat_axis=0, tiled=True)
     count = latent.shape[1]
     act_one, slope_one, act_two, slope_two = forward(latent, w_first, pair_two)
     decoded_rows, grad_two, paired_three = last_layer(act_two, slope_two, pair_three, target_rows)
-    grad_first, grad_second = backward(latent, act_one, slope_one, pair_two, grad_two, jnp.bfloat16)
-    core, across = vox_bits[:1], vox_bits[1:]
-    near, along = dp_bits[:1], dp_bits[:0:-1]
-    half = grad_first.shape[0] // 2
-    lanes = grad_second.shape[1]
-    flat_three = paired_three.astype(jnp.bfloat16)
-    pieces = [flat_three[:, :, at:at + lanes].reshape(-1, lanes) for at in range(0, flat_three.shape[2], lanes)]
-    small = jnp.concatenate([grad_second] + pieces, axis=0)
-    small = all_summed(small, core + along + across + near)
-    upper_half = all_summed(grad_first[:half], core + across + near + along)
-    lower_half = all_summed(grad_first[half:], core + near + across + along)
-    total_first = jnp.concatenate([upper_half, lower_half], axis=0)
-    total_second = small[: grad_second.shape[0]]
-    tail = small[grad_second.shape[0]:].reshape(len(pieces), 2, -1, lanes)
-    total_third = unpaired_third(jnp.concatenate([tail[at] for at in range(len(pieces))], axis=2), last_chan)
-    decoded = sample_first(decoded_rows, count, w_third.shape[1])
+    kept, sent = backward(side, latent, act_one, slope_one, pair_two, grad_two, paired_three)
+    third_rows = paired_three.shape[1]
+    quarter = w_first.shape[0] // 4
+    across = [[hop] for hop in vox_bits[1:]]
+    near = [dp_bits[:1]]
+    along = [dp_bits[at:at + 2] for at in range(1, len(dp_bits), 2)]
+    routes = (across + near + along, near + across + along, along + across + near)
+    received = exchanged(sent, vox_bits[:1], 1)
+    cuts = ((0, quarter), (quarter, 2 * quarter), (2 * quarter, kept.shape[0]))
+    parts = [[kept[low:high], received[low:high]] for low, high in cuts]
+    decoded = sample_first(decoded_rows, count, w_third.shape[1], received)
+    for stage in range(len(routes[0])):
+        parts = over_chains(shared, parts, [route[stage] for route in routes])
+        *tied, decoded = lax.optimization_barrier(tuple(terms[1] for terms in parts) + (decoded,))
+        parts = [terms[:1] + [arrived] + terms[2:] for terms, arrived in zip(parts, tied)]
+    shares = [summed(terms).astype(jnp.bfloat16) for terms in parts]
+    for stage in reversed(range(len(routes[0]))):
+        shares = over_chains(gathered, shares, [route[stage] for route in routes])
+        shares = lax.optimization_barrier(tuple(shares))
+    others = [exchanged(values, vox_bits[:1], 1) for values in shares]
+    total_first, total_second, third = finished(side, shares, others, third_rows)
+    total_third = third.T
     return (decoded, total_first, total_second, total_third)
 
 

time: 335 us -> 291 us (0.87)
  local copies, waits for them, and re-layouts: 53.2 us -> 12.1 us
  Pallas kernels: 66.9 us -> 92.8 us
  blocking collectives: 18.5 us -> 0 us
  waiting for transfers between devices: 124 us -> 115 us
  other arithmetic: 21.6 us -> 12.8 us
  starting transfers between devices: 48.1 us -> 55.9 us
    ppermute x34 -> x30, waiting for transfers between devices: 98.7 us -> 67.6 us  [exchanged(): lax.ppermute(values, axis, [(at, at ^ flip) for at in range(lax.axis_size...]
    reshape x4 -> x0, local copies, waits for them, and re-layouts: 29.3 us -> none  [the longest x2 18.2 us: spatial_first(): grid.reshape(count, height, breadth // 2, 2 * chan).transpose(1, 2, 0, 3)]
    pallas_call x2 -> x7, Pallas kernels: 23.4 us -> 46.8 us  [the longest x4 26.5 us: projected(): pl.pallas_call(project_kernel, name='project_rows', grid_spec=pltpu.Prefe...]
    all_to_all x1 -> x0, blocking collectives: 18.5 us -> none  [returned(): return lax.all_to_all(sent, 'dp', split_axis=0, concat_axis=0, tiled=True)]
    all_to_all x2, waiting for transfers between devices: 16.4 us -> 34.8 us  [routed(): lax.all_to_all(sent, 'dp', split_axis=0, concat_axis=0, tiled=True)]
    all_to_all x1 -> x2, waiting for transfers between devices: 0.01 us -> 13.1 us  [returned(): return lax.all_to_all(sent, 'dp', split_axis=0, concat_axis=0, tiled=True)]
    all_to_all x1, waiting for transfers between devices: 8.62 us -> 0.01 us  [shards(): lax.all_to_all(own_rows, 'vox', split_axis=0, concat_axis=0, tiled=True)]
    all_to_all x1 -> x2, starting transfers between devices: 3.64 us -> 11.8 us  [returned(): return lax.all_to_all(sent, 'dp', split_axis=0, concat_axis=0, tiled=True)]
  transfers between devices with their start and end apart: 38 -> 35, of which waited for: 29 -> 18; matrix products, arithmetic and copies ran while one was open for 19% -> 5% of each run, Pallas kernels for 7% -> 12%
where the time goes in v2:
time: 291 us; the launch traced here: 290 us
  waiting for transfers between devices  115 us (40%)
  Pallas kernels  92.8 us (32%)
  starting transfers between devices  55.9 us (19%)
  other arithmetic  12.8 us (4%)
  local copies, waits for them, and re-layouts  12.1 us (4%)
    ppermute x30, waiting for transfers between devices, exchanged(): lax.ppermute(values, axis, [(at, at ^ flip) for at in range(lax.axis_size...  67.6 us
    all_to_all x2, waiting for transfers between devices, routed(): lax.all_to_all(sent, 'dp', split_axis=0, concat_axis=0, tiled=True)  34.8 us
    ppermute x30, starting transfers between devices, exchanged(): lax.ppermute(values, axis, [(at, at ^ flip) for at in range(lax.axis_size...  29.5 us
    pallas_call x4, Pallas kernels, projected(): pl.pallas_call(project_kernel, name='project_rows', grid_spec=pltpu.Prefe...  26.5 us
    pallas_call x1, Pallas kernels, last_layer(): pl.pallas_call(functools.partial(last_kernel, count), name='decoder_last'...  15.5 us
    pallas_call x1, Pallas kernels, backward(): pl.pallas_call(functools.partial(backward_kernel, count), name='decoder_b...  13.2 us
    all_to_all x2, waiting for transfers between devices, returned(): return lax.all_to_all(sent, 'dp', split_axis=0, concat_axis=0, tiled=True)  13.1 us
    all_to_all x2, starting transfers between devices, returned(): return lax.all_to_all(sent, 'dp', split_axis=0, concat_axis=0, tiled=True)  11.8 us
  transfers between devices with their start and end apart: 35, of which 18 were waited for; matrix products, arithmetic and copies ran while one was open for 5% of the time, Pallas kernels for 12%

profile of v2, /device:TPU:0, one launch (start us, length us, event | category | flops | bytes accessed | tf_op | source)
XLA Modules:
  0.0 290.3 jit_solution(18101955938347788709)
XLA Ops:
  2.1 3.7 %bucket_rows.1 = (bf16[256,2048]{1,0:T(8,128)(2,1)}, bf16[256,2048]{1,0:T(8,128)(2,1)}, bf16[256,512]{1,0:T(8,128)(2,1)}) custom-call(s32[256,1]{1,0:T(8,128)} %copy.15.subject_ref, s32[8]{0:T(128)} %after_ref.1, s32[1]{0:T(128)} %bitcast.1.shift_ref, bf16[256,2048]{1,0:T(8,128)(2,1)} %fmri_ref.1), custom_call_target="tpu_custom_call" | custom-call | tf_op jit(solution)/shard_map/bucket_rows/pallas_call | solution.py:431
  5.8 7.3 %all-to-all-start = ((bf16[8,32,2048]{2,1,0:T(8,128)(2,1)}), bf16[8,32,2048]{2,1,0:T(8,128)(2,1)S(1)}, u32[]{:S(2)}, u32[]{:S(2)}) async-start(bf16[8,32,2048]{2,1,0:T(8,128)(2,1)} %bitcast.99), calls=%async_computation | async-start | bytes 2097152 | tf_op jit(solution)/shard_map/all_to_all | solution.py:642
  13.0 25.8 %all-to-all-done = bf16[8,32,2048]{2,1,0:T(8,128)(2,1)S(1)} async-done(((bf16[8,32,2048]{2,1,0:T(8,128)(2,1)}), bf16[8,32,2048]{2,1,0:T(8,128)(2,1)S(1)}, u32[]{:S(2)}, u32[]{:S(2)}) %all-to-all-start) | async-done | bytes 1048608 | tf_op jit(solution)/shard_map/all_to_all | solution.py:642
  38.8 3.6 %all-to-all-start.2 = ((bf16[8,32,2048]{2,1,0:T(8,128)(2,1)}), bf16[8,32,2048]{2,1,0:T(8,128)(2,1)S(1)}, u32[]{:S(2)}, u32[]{:S(2)}) async-start(bf16[8,32,2048]{2,1,0:T(8,128)(2,1)} %bitcast.6), calls=%async_computation.2 | async-start | bytes 2097152 | tf_op jit(solution)/shard_map/all_to_all | solution.py:642
  42.4 6.6 %project_rows.4.after_ref = bf16[4,256,512]{2,1,0:T(8,128)(2,1)} custom-call(s32[1]{0:T(128)S(6)} %sub.32.half_ref, bf16[256,2048]{1,0:T(8,128)(2,1)} %bitcast.92, bf16[1,2048,4096]{2,1,0:T(8,128)(2,1)} %map_ref.7, s32[8]{0:T(128)} %after_ref.1), custom_call_target="tpu_custom_call" | custom-call | flops 2147483648 | bytes 8388608 | tf_op jit(solution)/shard_map/project_rows/pallas_call | solution.py:453
  49.0 6.6 %project_rows.5 = bf16[4,256,512]{2,1,0:T(8,128)(2,1)} custom-call(s32[1]{0:T(128)} %bitcast.half_ref.side_ref, bf16[256,2048]{1,0:T(8,128)(2,1)} %bitcast.93, bf16[1,2048,4096]{2,1,0:T(8,128)(2,1)} %map_ref.7, bf16[4,256,512]{2,1,0:T(8,128)(2,1)} %project_rows.4.after_ref), custom_call_target="tpu_custom_call" | custom-call | flops 2147483648 | bytes 8388608 | tf_op jit(solution)/shard_map/project_rows/pallas_call | solution.py:453
  59.3 9.0 %all-to-all-done.2 = bf16[8,32,2048]{2,1,0:T(8,128)(2,1)S(1)} async-done(((bf16[8,32,2048]{2,1,0:T(8,128)(2,1)}), bf16[8,32,2048]{2,1,0:T(8,128)(2,1)S(1)}, u32[]{:S(2)}, u32[]{:S(2)}) %all-to-all-start.2) | async-done | bytes 1048608 | tf_op jit(solution)/shard_map/all_to_all | solution.py:642
  68.4 3.8 %collective-permute-done.1.after_ref = bf16[2,256,512]{2,1,0:T(8,128)(2,1)S(1)} collective-permute-done((bf16[2,256,512]{2,1,0:T(8,128)(2,1)S(1)}, bf16[2,256,512]{2,1,0:T(8,128)(2,1)S(1)}, u32[]{:S(2)}, u32[]{:S(2)}) %collective-permute-start.1) | collective-permute-done | bytes 524320 | tf_op jit(solution)/shard_map/ppermute | solution.py:567
  73.0 6.7 %project_rows.6.after_ref = bf16[4,256,512]{2,1,0:T(8,128)(2,1)} custom-call(s32[1]{0:T(128)S(6)} %sub.32.half_ref, bf16[256,2048]{1,0:T(8,128)(2,1)} %bitcast.90, bf16[1,2048,4096]{2,1,0:T(8,128)(2,1)} %map_ref.7, bf16[2,256,512]{2,1,0:T(8,128)(2,1)} %copy-done.11), custom_call_target="tpu_custom_call" | custom-call | flops 2147483648 | bytes 8388608 | tf_op jit(solution)/shard_map/project_rows/pallas_call | solution.py:453
  81.9 6.0 %all-to-all-start.1 = ((bf16[8,2,32,512]{3,2,1,0:T(8,128)(2,1)}), bf16[8,2,32,512]{3,2,1,0:T(8,128)(2,1)S(1)}, u32[]{:S(2)}, u32[]{:S(2)}) async-start(bf16[8,2,32,512]{3,2,1,0:T(8,128)(2,1)} %bitcast.89), calls=%async_computation.1 | async-start | bytes 1048576 | tf_op jit(solution)/shard_map/all_to_all | solution.py:656
  87.9 6.6 %project_rows.7 = bf16[4,256,512]{2,1,0:T(8,128)(2,1)} custom-call(s32[1]{0:T(128)} %bitcast.half_ref.side_ref, bf16[256,2048]{1,0:T(8,128)(2,1)} %bitcast.91, bf16[1,2048,4096]{2,1,0:T(8,128)(2,1)} %map_ref.7, bf16[4,256,512]{2,1,0:T(8,128)(2,1)} %project_rows.6.after_ref), custom_call_target="tpu_custom_call" | custom-call | flops 2147483648 | bytes 8388608 | tf_op jit(solution)/shard_map/project_rows/pallas_call | solution.py:453
  97.6 12.6 %collective-permute-done.3 = bf16[2,256,512]{2,1,0:T(8,128)(2,1)S(1)} collective-permute-done((bf16[2,256,512]{2,1,0:T(8,128)(2,1)S(1)}, bf16[2,256,512]{2,1,0:T(8,128)(2,1)S(1)}, u32[]{:S(2)}, u32[]{:S(2)}) %collective-permute-start.3) | collective-permute-done | bytes 524320 | tf_op jit(solution)/shard_map/ppermute | solution.py:567
  112.3 5.8 %all-to-all-start.3 = ((bf16[8,2,32,512]{3,2,1,0:T(8,128)(2,1)}), bf16[8,2,32,512]{3,2,1,0:T(8,128)(2,1)S(1)}, u32[]{:S(2)}, u32[]{:S(2)}) async-start(bf16[8,2,32,512]{3,2,1,0:T(8,128)(2,1)} %bitcast.88), calls=%async_computation.3 | async-start | bytes 1048576 | tf_op jit(solution)/shard_map/all_to_all | solution.py:656
  118.8 13.1 %all-to-all-done.3.second_ref = bf16[8,2,32,512]{3,2,1,0:T(8,128)(2,1)S(1)} async-done(((bf16[8,2,32,512]{3,2,1,0:T(8,128)(2,1)}), bf16[8,2,32,512]{3,2,1,0:T(8,128)(2,1)S(1)}, u32[]{:S(2)}, u32[]{:S(2)}) %all-to-all-start.3) | async-done | bytes 524320 | tf_op jit(solution)/shard_map/all_to_all | solution.py:656
  135.3 3.6 %all-to-all-start.4 = ((bf16[4,64,1024]{2,1,0:T(8,128)(2,1)}), bf16[4,64,1024]{2,1,0:T(8,128)(2,1)S(1)}, u32[]{:S(2)}, u32[]{:S(2)}) async-start(bf16[4,64,1024]{2,1,0:T(8,128)(2,1)} %bitcast.94), calls=%async_computation.4 | async-start | bytes 1048576 | tf_op jit(solution)/shard_map/all_to_all | solution.py:667
  140.8 7.1 %spatial_first.1.target_ref = bf16[16,1024,128]{2,1,0:T(8,128)(2,1)} custom-call(bf16[64,16,32,64]{3,2,1,0:T(8,128)(2,1)} %grid_ref.1, bf16[4,256,512]{2,1,0:T(8,128)(2,1)} %copy-done.9), custom_call_target="tpu_custom_call" | custom-call | bytes 28000000 | tf_op jit(solution)/shard_map/spatial_first/pallas_call | solution.py:351
  148.7 11.1 %decoder_forward.1 = (bf16[4,512,256]{2,1,0:T(8,128)(2,1)}, f32[4,512,256]{2,1,0:T(8,128)}, bf16[10,1024,128]{2,1,0:T(8,128)(2,1)}, f32[8,1024,128]{2,1,0:T(8,128)}) custom-call(bf16[4,64,1024]{2,1,0:T(8,128)(2,1)} %copy-done.3, bf16[8192,256]{1,0:T(8,128)(2,1)} %w_one_ref.1, bf16[2,512,512]{2,1,0:T(8,128)(2,1)} %pad_maximum_fusion.w_two_ref.w_ref), custom_call_target="tpu_custom_call" | custom-call | tf_op jit(solution)/shard_map/decoder_forward/pallas_call | solution.py:266
  159.8 15.5 %decoder_last.1 = (bf16[16,1024,128]{2,1,0:T(8,128)(2,1)}, bf16[8,1024,128]{2,1,0:T(8,128)(2,1)}, f32[2,256,256]{2,1,0:T(8,128)}) custom-call(bf16[10,1024,128]{2,1,0:T(8,128)(2,1)} %get-tuple-element.45.act_ref, f32[8,1024,128]{2,1,0:T(8,128)} %get-tuple-element.46.slope_ref, bf16[2,256,256]{2,1,0:T(8,128)(2,1)} %pad_maximum_fusion.8.w_ref, ...), custom_call_target="tpu_custom_call" | custom-call | tf_op jit(solution)/shard_map/decoder_last/pallas_call | solution.py:288
  175.4 13.2 %decoder_backward.1 = (bf16[5376,256]{1,0:T(8,128)(2,1)}, bf16[5376,256]{1,0:T(8,128)(2,1)}) custom-call(s32[1]{0:T(128)} %bitcast.half_ref.side_ref, bf16[4,64,1024]{2,1,0:T(8,128)(2,1)} %copy-done.3, bf16[4,512,256]{2,1,0:T(8,128)(2,1)} %get-tuple-element.43.act_ref, f32[4,512,256]{2,1,0:T(8,128)} %get-tuple-element.44.slope_ref, ...), custom_call_target="tpu_custom_call" | custom-call | tf_op jit(solution)/shard_map/decoder_backward/pallas_call | solution.py:321
  190.5 3.3 %collective-permute-done.4.after_ref = bf16[5376,256]{1,0:T(8,128)(2,1)S(1)} collective-permute-done((bf16[5376,256]{1,0:T(8,128)(2,1)}, bf16[5376,256]{1,0:T(8,128)(2,1)S(1)}, u32[]{:S(2)}, u32[]{:S(2)}) %collective-permute-start.4) | collective-permute-done | bytes 2752544 | tf_op jit(solution)/shard_map/ppermute | solution.py:567
  205.3 7.7 %sample_first.1 = bf16[64,16,32,64]{3,2,1,0:T(8,128)(2,1)} custom-call(bf16[16,1024,128]{2,1,0:T(8,128)(2,1)} %get-tuple-element.51.rows_ref, bf16[5376,256]{1,0:T(8,128)(2,1)} %copy-done), custom_call_target="tpu_custom_call" | custom-call | bytes 28000000 | tf_op jit(solution)/shard_map/sample_first/pallas_call | solution.py:382
  214.3 4.9 %collective-permute-done.9 = bf16[320,256]{1,0:T(8,128)(2,1)S(1)} collective-permute-done((bf16[320,256]{1,0:T(8,128)(2,1)S(1)}, bf16[320,256]{1,0:T(8,128)(2,1)S(1)}, u32[]{:S(2)}, u32[]{:S(2)}) %collective-permute-start.9) | collective-permute-done | bytes 163872 | tf_op jit(solution)/shard_map/ppermute | solution.py:567
  220.5 7.5 %collective-permute-done.11 = bf16[672,256]{1,0:T(8,128)(2,1)S(1)} collective-permute-done((bf16[672,256]{1,0:T(8,128)(2,1)S(1)}, bf16[672,256]{1,0:T(8,128)(2,1)S(1)}, u32[]{:S(2)}, u32[]{:S(2)}) %collective-permute-start.11) | collective-permute-done | bytes 344096 | tf_op jit(solution)/shard_map/ppermute | solution.py:567
  236.5 5.0 %collective-permute-done.14 = bf16[256,256]{1,0:T(8,128)(2,1)S(1)} collective-permute-done((bf16[256,256]{1,0:T(8,128)(2,1)S(1)}, bf16[256,256]{1,0:T(8,128)(2,1)S(1)}, u32[]{:S(2)}, u32[]{:S(2)}) %collective-permute-start.14) | collective-permute-done | bytes 131104 | tf_op jit(solution)/shard_map/ppermute | solution.py:567
  250.3 2.7 collective-permute-done.17
  255.6 4.1 %collective-permute-done.20 = bf16[512,256]{1,0:T(8,128)(2,1)S(1)} collective-permute-done((bf16[512,256]{1,0:T(8,128)(2,1)S(1)}, bf16[512,256]{1,0:T(8,128)(2,1)S(1)}, u32[]{:S(2)}, u32[]{:S(2)}) %collective-permute-start.20) | collective-permute-done | bytes 262176 | tf_op jit(solution)/shard_map/ppermute | solution.py:567
  259.7 4.9 %collective-permute-done.21 = bf16[672,256]{1,0:T(8,128)(2,1)S(1)} collective-permute-done((bf16[672,256]{1,0:T(8,128)(2,1)S(1)}, bf16[672,256]{1,0:T(8,128)(2,1)S(1)}, u32[]{:S(2)}, u32[]{:S(2)}) %collective-permute-start.21) | collective-permute-done | bytes 344096 | tf_op jit(solution)/shard_map/ppermute | solution.py:567
  265.9 2.8 collective-permute-start.25
  269.8 3.2 %collective-permute-done.24 = bf16[320,256]{1,0:T(8,128)(2,1)S(1)} collective-permute-done((bf16[320,256]{1,0:T(8,128)(2,1)S(1)}, bf16[320,256]{1,0:T(8,128)(2,1)S(1)}, u32[]{:S(2)}, u32[]{:S(2)}) %collective-permute-start.24) | collective-permute-done | bytes 163872 | tf_op jit(solution)/shard_map/ppermute | solution.py:567
  273.0 4.5 %collective-permute-done.25 = bf16[320,256]{1,0:T(8,128)(2,1)S(1)} collective-permute-done((bf16[320,256]{1,0:T(8,128)(2,1)S(1)}, bf16[320,256]{1,0:T(8,128)(2,1)S(1)}, u32[]{:S(2)}, u32[]{:S(2)}) %collective-permute-start.25) | collective-permute-done | bytes 163872 | tf_op jit(solution)/shard_map/ppermute | solution.py:567
  278.4 4.5 %collective-permute-done.29.other_c = bf16[1280,256]{1,0:T(8,128)(2,1)S(1)} collective-permute-done((bf16[1280,256]{1,0:T(8,128)(2,1)S(1)}, bf16[1280,256]{1,0:T(8,128)(2,1)S(1)}, u32[]{:S(2)}, u32[]{:S(2)}) %collective-permute-start.29) | collective-permute-done | bytes 655392 | tf_op jit(solution)/shard_map/ppermute | solution.py:567
  284.7 5.5 %finish_gradients.1 = (bf16[8192,256]{1,0:T(8,128)(2,1)}, bf16[4096,128]{1,0:T(8,128)(2,1)}, bf16[64,2048]{1,0:T(8,128)(2,1)}) custom-call(s32[1]{0:T(128)} %bitcast.half_ref.side_ref, bf16[2048,256]{1,0:T(8,128)(2,1)} %copy-done.8, bf16[2048,256]{1,0:T(8,128)(2,1)} %copy-done.7, bf16[1280,256]{1,0:T(8,128)(2,1)} %copy-done.10, ...), custom_call_target="tpu_custom_call" | custom-call | tf_op jit(solution)/shard_map/finish_gradients/pallas_call | solution.py:527
  (147 shorter events, 60.7 us)
Async XLA Ops:
  5.8 33.0 %all-to-all-start = ((bf16[8,32,2048]{2,1,0:T(8,128)(2,1)}), bf16[8,32,2048]{2,1,0:T(8,128)(2,1)S(1)}, u32[]{:S(2)}, u32[]{:S(2)}) async-start(bf16[8,32,2048]{2,1,0:T(8,128)(2,1)} %bitcast.99), calls=%async_computation | async-start | bytes 2097152 | tf_op jit(solution)/shard_map/all_to_all | solution.py:642
  38.8 29.5 %all-to-all-start.2 = ((bf16[8,32,2048]{2,1,0:T(8,128)(2,1)}), bf16[8,32,2048]{2,1,0:T(8,128)(2,1)S(1)}, u32[]{:S(2)}, u32[]{:S(2)}) async-start(bf16[8,32,2048]{2,1,0:T(8,128)(2,1)} %bitcast.6), calls=%async_computation.2 | async-start | bytes 2097152 | tf_op jit(solution)/shard_map/all_to_all | solution.py:642
  49.0 6.6 %collective-permute-start = (bf16[4,256,512]{2,1,0:T(8,128)(2,1)}, bf16[4,256,512]{2,1,0:T(8,128)(2,1)S(1)}, u32[]{:S(2)}, u32[]{:S(2)}) collective-permute-start(bf16[4,256,512]{2,1,0:T(8,128)(2,1)} %project_rows.4.after_ref), channel_id=1, source_target_pairs={{0,8},{8,0},{16,24},{24,16},{1,9},{9,1},{17,25},{25,17},{2,10},{10... | collective-permute-start | bytes 3145736 | tf_op jit(solution)/shard_map/ppermute | solution.py:567
  57.8 14.4 %collective-permute-start.1 = (bf16[2,256,512]{2,1,0:T(8,128)(2,1)S(1)}, bf16[2,256,512]{2,1,0:T(8,128)(2,1)S(1)}, u32[]{:S(2)}, u32[]{:S(2)}) collective-permute-start(bf16[2,256,512]{2,1,0:T(8,128)(2,1)S(1)} %add_convert_fusion.5), channel_id=1, source_target_pairs={{0,16},{8,24},{16,0},{24,8},{1,17},{9,25},{17,1},{25,9},{2,18},{10... | collective-permute-start | bytes 1572872 | tf_op jit(solution)/shard_map/ppermute | solution.py:567
  79.7 14.9 %collective-permute-start.2 = (bf16[4,256,512]{2,1,0:T(8,128)(2,1)}, bf16[4,256,512]{2,1,0:T(8,128)(2,1)S(1)}, u32[]{:S(2)}, u32[]{:S(2)}) collective-permute-start(bf16[4,256,512]{2,1,0:T(8,128)(2,1)} %project_rows.6.after_ref), channel_id=1, source_target_pairs={{0,8},{8,0},{16,24},{24,16},{1,9},{9,1},{17,25},{25,17},{2,10},{10... | collective-permute-start | bytes 3145736 | tf_op jit(solution)/shard_map/ppermute | solution.py:567
  81.9 30.3 %all-to-all-start.1 = ((bf16[8,2,32,512]{3,2,1,0:T(8,128)(2,1)}), bf16[8,2,32,512]{3,2,1,0:T(8,128)(2,1)S(1)}, u32[]{:S(2)}, u32[]{:S(2)}) async-start(bf16[8,2,32,512]{3,2,1,0:T(8,128)(2,1)} %bitcast.89), calls=%async_computation.1 | async-start | bytes 1048576 | tf_op jit(solution)/shard_map/all_to_all | solution.py:656
  96.1 14.1 %collective-permute-start.3 = (bf16[2,256,512]{2,1,0:T(8,128)(2,1)S(1)}, bf16[2,256,512]{2,1,0:T(8,128)(2,1)S(1)}, u32[]{:S(2)}, u32[]{:S(2)}) collective-permute-start(bf16[2,256,512]{2,1,0:T(8,128)(2,1)S(1)} %add_convert_fusion.3), channel_id=1, source_target_pairs={{0,16},{8,24},{16,0},{24,8},{1,17},{9,25},{17,1},{25,9},{2,18},{10... | collective-permute-start | bytes 1572872 | tf_op jit(solution)/shard_map/ppermute | solution.py:567
  112.3 19.6 %all-to-all-start.3 = ((bf16[8,2,32,512]{3,2,1,0:T(8,128)(2,1)}), bf16[8,2,32,512]{3,2,1,0:T(8,128)(2,1)S(1)}, u32[]{:S(2)}, u32[]{:S(2)}) async-start(bf16[8,2,32,512]{3,2,1,0:T(8,128)(2,1)} %bitcast.88), calls=%async_computation.3 | async-start | bytes 1048576 | tf_op jit(solution)/shard_map/all_to_all | solution.py:656
  135.3 12.7 %all-to-all-start.4 = ((bf16[4,64,1024]{2,1,0:T(8,128)(2,1)}), bf16[4,64,1024]{2,1,0:T(8,128)(2,1)S(1)}, u32[]{:S(2)}, u32[]{:S(2)}) async-start(bf16[4,64,1024]{2,1,0:T(8,128)(2,1)} %bitcast.94), calls=%async_computation.4 | async-start | bytes 1048576 | tf_op jit(solution)/shard_map/all_to_all | solution.py:667
  188.5 5.3 %collective-permute-start.4 = (bf16[5376,256]{1,0:T(8,128)(2,1)}, bf16[5376,256]{1,0:T(8,128)(2,1)S(1)}, u32[]{:S(2)}, u32[]{:S(2)}) collective-permute-start(bf16[5376,256]{1,0:T(8,128)(2,1)} %get-tuple-element.50), channel_id=1, source_target_pairs={{0,8},{8,0},{16,24},{24,16},{1,9},{9,1},{17,25},{25,17},{2,10},{10... | collective-permute-start | bytes 8257544 | tf_op jit(solution)/shard_map/ppermute | solution.py:567
  195.8 17.3 %collective-permute-start.5 = (bf16[1024,256]{1,0:T(8,128)(2,1)}, bf16[1024,256]{1,0:T(8,128)(2,1)S(1)}, u32[]{:S(2)}, u32[]{:S(2)}) collective-permute-start(bf16[1024,256]{1,0:T(8,128)(2,1)} %get-tuple-element.81), channel_id=1, source_target_pairs={{0,16},{8,24},{16,0},{24,8},{1,17},{9,25},{17,1},{25,9},{2,18},{10... | collective-permute-start | bytes 1572872 | tf_op jit(solution)/shard_map/ppermute | solution.py:567
  199.0 14.1 %collective-permute-start.6 = (bf16[1024,256]{1,0:T(8,128)(2,1)}, bf16[1024,256]{1,0:T(8,128)(2,1)}, u32[]{:S(2)}, u32[]{:S(2)}) collective-permute-start(bf16[1024,256]{1,0:T(8,128)(2,1)} %get-tuple-element.82), channel_id=1, source_target_pairs={{0,1},{1,0},{2,3},{3,2},{4,5},{5,4},{6,7},{7,6},{8,9},{9,8},{10,11... | collective-permute-start | bytes 1572872 | tf_op jit(solution)/shard_map/ppermute | solution.py:567
  201.7 11.3 %collective-permute-start.7 = (bf16[320,256]{1,0:T(8,128)(2,1)S(1)}, bf16[320,256]{1,0:T(8,128)(2,1)S(1)}, u32[]{:S(2)}, u32[]{:S(2)}) collective-permute-start(bf16[320,256]{1,0:T(8,128)(2,1)S(1)} %get-tuple-element.91), channel_id=1, source_target_pairs={{0,2},{1,3},{2,0},{3,1},{4,6},{5,7},{6,4},{7,5},{8,10},{9,11},{10,... | collective-permute-start | bytes 491528 | tf_op jit(solution)/shard_map/ppermute | solution.py:567
  201.8 12.5 %collective-permute-start.10 = (bf16[320,256]{1,0:T(8,128)(2,1)S(1)}, bf16[320,256]{1,0:T(8,128)(2,1)S(1)}, u32[]{:S(2)}, u32[]{:S(2)}) collective-permute-start(bf16[320,256]{1,0:T(8,128)(2,1)S(1)} %get-tuple-element.89), channel_id=1, source_target_pairs={{0,6},{1,7},{2,4},{3,5},{4,2},{5,3},{6,0},{7,1},{8,14},{9,15},{10,... | collective-permute-start | bytes 491528 | tf_op jit(solution)/shard_map/ppermute | solution.py:567
  203.4 15.8 %collective-permute-start.9 = (bf16[320,256]{1,0:T(8,128)(2,1)S(1)}, bf16[320,256]{1,0:T(8,128)(2,1)S(1)}, u32[]{:S(2)}, u32[]{:S(2)}) collective-permute-start(bf16[320,256]{1,0:T(8,128)(2,1)S(1)} %get-tuple-element.88), channel_id=1, source_target_pairs={{0,4},{1,5},{2,6},{3,7},{4,0},{5,1},{6,2},{7,3},{8,12},{9,13},{10,... | collective-permute-start | bytes 491528 | tf_op jit(solution)/shard_map/ppermute | solution.py:567
  219.3 8.7 %collective-permute-start.11 = (bf16[672,256]{1,0:T(8,128)(2,1)S(1)}, bf16[672,256]{1,0:T(8,128)(2,1)S(1)}, u32[]{:S(2)}, u32[]{:S(2)}) collective-permute-start(bf16[672,256]{1,0:T(8,128)(2,1)S(1)} %pad_maximum_fusion.6), channel_id=1, source_target_pairs={{0,16},{8,24},{16,0},{24,8},{1,17},{9,25},{17,1},{25,9},{2,18},{10... | collective-permute-start | bytes 1032200 | tf_op jit(solution)/shard_map/ppermute | solution.py:567
  219.9 8.2 %collective-permute-start.8 = (bf16[512,256]{1,0:T(8,128)(2,1)S(1)}, bf16[512,256]{1,0:T(8,128)(2,1)S(1)}, u32[]{:S(2)}, u32[]{:S(2)}) collective-permute-start(bf16[512,256]{1,0:T(8,128)(2,1)S(1)} %get-tuple-element.85), channel_id=1, source_target_pairs={{0,1},{1,0},{2,3},{3,2},{4,5},{5,4},{6,7},{7,6},{8,9},{9,8},{10,11... | collective-permute-start | bytes 786440 | tf_op jit(solution)/shard_map/ppermute | solution.py:567
  228.3 6.7 %collective-permute-start.12 = (bf16[256,256]{1,0:T(8,128)(2,1)S(1)}, bf16[256,256]{1,0:T(8,128)(2,1)S(1)}, u32[]{:S(2)}, u32[]{:S(2)}) collective-permute-start(bf16[256,256]{1,0:T(8,128)(2,1)S(1)} %pad_maximum_fusion.12), channel_id=1, source_target_pairs={{0,2},{1,3},{2,0},{3,1},{4,6},{5,7},{6,4},{7,5},{8,10},{9,11},{10,... | collective-permute-start | bytes 393224 | tf_op jit(solution)/shard_map/ppermute | solution.py:567
  228.4 6.6 %collective-permute-start.13 = (bf16[80,256]{1,0:T(8,128)(2,1)S(1)}, bf16[80,256]{1,0:T(8,128)(2,1)S(1)}, u32[]{:S(2)}, u32[]{:S(2)}) collective-permute-start(bf16[80,256]{1,0:T(8,128)(2,1)S(1)} %add_convert_fusion.21), channel_id=1, source_target_pairs={{0,1},{1,0},{2,3},{3,2},{4,5},{5,4},{6,7},{7,6},{8,9},{9,8},{10,11... | collective-permute-start | bytes 122888 | tf_op jit(solution)/shard_map/ppermute | solution.py:567
  229.0 7.5 %collective-permute-start.15 = (bf16[256,256]{1,0:T(8,128)(2,1)S(1)}, bf16[256,256]{1,0:T(8,128)(2,1)S(1)}, u32[]{:S(2)}, u32[]{:S(2)}) collective-permute-start(bf16[256,256]{1,0:T(8,128)(2,1)S(1)} %pad_maximum_fusion.14), channel_id=1, source_target_pairs={{0,6},{1,7},{2,4},{3,5},{4,2},{5,3},{6,0},{7,1},{8,14},{9,15},{10,... | collective-permute-start | bytes 393224 | tf_op jit(solution)/shard_map/ppermute | solution.py:567
  230.6 11.0 %collective-permute-start.14 = (bf16[256,256]{1,0:T(8,128)(2,1)S(1)}, bf16[256,256]{1,0:T(8,128)(2,1)S(1)}, u32[]{:S(2)}, u32[]{:S(2)}) collective-permute-start(bf16[256,256]{1,0:T(8,128)(2,1)S(1)} %pad_maximum_fusion.13), channel_id=1, source_target_pairs={{0,4},{1,5},{2,6},{3,7},{4,0},{5,1},{6,2},{7,3},{8,12},{9,13},{10,... | collective-permute-start | bytes 393224 | tf_op jit(solution)/shard_map/ppermute | solution.py:567
  241.7 8.5 %collective-permute-start.16 = (bf16[256,256]{1,0:T(8,128)(2,1)S(1)}, bf16[256,256]{1,0:T(8,128)(2,1)S(1)}, u32[]{:S(2)}, u32[]{:S(2)}) collective-permute-start(bf16[256,256]{1,0:T(8,128)(2,1)S(1)} %pad_maximum_fusion.15), channel_id=1, source_target_pairs={{0,2},{1,3},{2,0},{3,1},{4,6},{5,7},{6,4},{7,5},{8,10},{9,11},{10,... | collective-permute-start | bytes 393224 | tf_op jit(solution)/shard_map/ppermute | solution.py:567
  241.8 11.2 %collective-permute-start.17 = (bf16[256,256]{1,0:T(8,128)(2,1)S(1)}, bf16[256,256]{1,0:T(8,128)(2,1)S(1)}, u32[]{:S(2)}, u32[]{:S(2)}) collective-permute-start(bf16[256,256]{1,0:T(8,128)(2,1)S(1)} %pad_maximum_fusion.15), channel_id=1, source_target_pairs={{0,4},{1,5},{2,6},{3,7},{4,0},{5,1},{6,2},{7,3},{8,12},{9,13},{10,... | collective-permute-start | bytes 393224 | tf_op jit(solution)/shard_map/ppermute | solution.py:567
  244.1 8.9 %collective-permute-start.18 = (bf16[256,256]{1,0:T(8,128)(2,1)S(1)}, bf16[256,256]{1,0:T(8,128)(2,1)S(1)}, u32[]{:S(2)}, u32[]{:S(2)}) collective-permute-start(bf16[256,256]{1,0:T(8,128)(2,1)S(1)} %pad_maximum_fusion.15), channel_id=1, source_target_pairs={{0,6},{1,7},{2,4},{3,5},{4,2},{5,3},{6,0},{7,1},{8,14},{9,15},{10,... | collective-permute-start | bytes 393224 | tf_op jit(solution)/shard_map/ppermute | solution.py:567
  253.1 6.6 %collective-permute-start.20 = (bf16[512,256]{1,0:T(8,128)(2,1)S(1)}, bf16[512,256]{1,0:T(8,128)(2,1)S(1)}, u32[]{:S(2)}, u32[]{:S(2)}) collective-permute-start(bf16[512,256]{1,0:T(8,128)(2,1)S(1)} %get-tuple-element.64), channel_id=1, source_target_pairs={{0,1},{1,0},{2,3},{3,2},{4,5},{5,4},{6,7},{7,6},{8,9},{9,8},{10,11... | collective-permute-start | bytes 786440 | tf_op jit(solution)/shard_map/ppermute | solution.py:567
  255.1 9.5 %collective-permute-start.21 = (bf16[672,256]{1,0:T(8,128)(2,1)S(1)}, bf16[672,256]{1,0:T(8,128)(2,1)S(1)}, u32[]{:S(2)}, u32[]{:S(2)}) collective-permute-start(bf16[672,256]{1,0:T(8,128)(2,1)S(1)} %pad_maximum_fusion.7), channel_id=1, source_target_pairs={{0,16},{8,24},{16,0},{24,8},{1,17},{9,25},{17,1},{25,9},{2,18},{10... | collective-permute-start | bytes 1032200 | tf_op jit(solution)/shard_map/ppermute | solution.py:567
  264.8 12.8 %collective-permute-start.22 = (bf16[1024,256]{1,0:T(8,128)(2,1)S(1)}, bf16[1024,256]{1,0:T(8,128)(2,1)S(1)}, u32[]{:S(2)}, u32[]{:S(2)}) collective-permute-start(bf16[1024,256]{1,0:T(8,128)(2,1)S(1)} %constant_dynamic-update-slice_fusion.6), channel_id=1, source_target_pairs={{0,16},{8,24},{16,0},{24,8},{1,17},{9,25},{17,1},{25,9},{2,18},{10... | collective-permute-start | bytes 1572872 | tf_op jit(solution)/shard_map/ppermute | solution.py:567
  265.1 12.5 %collective-permute-start.23 = (bf16[1024,256]{1,0:T(8,128)(2,1)S(1)}, bf16[1024,256]{1,0:T(8,128)(2,1)S(1)}, u32[]{:S(2)}, u32[]{:S(2)}) collective-permute-start(bf16[1024,256]{1,0:T(8,128)(2,1)S(1)} %slice_dynamic-update-slice_fusion), channel_id=1, source_target_pairs={{0,1},{1,0},{2,3},{3,2},{4,5},{5,4},{6,7},{7,6},{8,9},{9,8},{10,11... | collective-permute-start | bytes 1572872 | tf_op jit(solution)/shard_map/ppermute | solution.py:567
  265.3 7.7 %collective-permute-start.24 = (bf16[320,256]{1,0:T(8,128)(2,1)S(1)}, bf16[320,256]{1,0:T(8,128)(2,1)S(1)}, u32[]{:S(2)}, u32[]{:S(2)}) collective-permute-start(bf16[320,256]{1,0:T(8,128)(2,1)S(1)} %slice_dynamic-update-slice_fusion.1), channel_id=1, source_target_pairs={{0,2},{1,3},{2,0},{3,1},{4,6},{5,7},{6,4},{7,5},{8,10},{9,11},{10,... | collective-permute-start | bytes 491528 | tf_op jit(solution)/shard_map/ppermute | solution.py:567
  265.9 11.6 %collective-permute-start.25 = (bf16[320,256]{1,0:T(8,128)(2,1)S(1)}, bf16[320,256]{1,0:T(8,128)(2,1)S(1)}, u32[]{:S(2)}, u32[]{:S(2)}) collective-permute-start(bf16[320,256]{1,0:T(8,128)(2,1)S(1)} %slice_dynamic-update-slice_fusion.1), channel_id=1, source_target_pairs={{0,4},{1,5},{2,6},{3,7},{4,0},{5,1},{6,2},{7,3},{8,12},{9,13},{10,... | collective-permute-start | bytes 491528 | tf_op jit(solution)/shard_map/ppermute | solution.py:567
  268.7 8.8 %collective-permute-start.26 = (bf16[320,256]{1,0:T(8,128)(2,1)S(1)}, bf16[320,256]{1,0:T(8,128)(2,1)S(1)}, u32[]{:S(2)}, u32[]{:S(2)}) collective-permute-start(bf16[320,256]{1,0:T(8,128)(2,1)S(1)} %slice_dynamic-update-slice_fusion.1), channel_id=1, source_target_pairs={{0,6},{1,7},{2,4},{3,5},{4,2},{5,3},{6,0},{7,1},{8,14},{9,15},{10,... | collective-permute-start | bytes 491528 | tf_op jit(solution)/shard_map/ppermute | solution.py:567
  277.8 5.9 %collective-permute-start.28 = (bf16[2048,256]{1,0:T(8,128)(2,1)S(1)}, bf16[2048,256]{1,0:T(8,128)(2,1)}, u32[]{:S(2)}, u32[]{:S(2)}) collective-permute-start(bf16[2048,256]{1,0:T(8,128)(2,1)S(1)} %constant_dynamic-update-slice_fusion.4.own_b), channel_id=1, source_target_pairs={{0,8},{8,0},{16,24},{24,16},{1,9},{9,1},{17,25},{25,17},{2,10},{10... | collective-permute-start | bytes 3145736 | tf_op jit(solution)/shard_map/ppermute | solution.py:567
  (22 other events, 126.3 us)

commit v3 on v2

--- a/solution.py
+++ b/solution.py
@@ -12,7 +12,6 @@
 ROW_TAPS = ((1, 3), (2, 0))
 ROW_SHIFT = (-1, 1)
 COL_TAPS = (1, 2, 3, 0)
-VMEM_BYTES = 60 * 1024 * 1024
 
 
 def paired_weight(weights, in_chan):
@@ -82,7 +81,7 @@
     return jnp.concatenate(pieces, axis=0)
 
 
-def forward_kernel(count, latent_ref, w_one_ref, w_two_ref, act_one_ref, slope_one_ref, act_two_ref, slope_two_ref, tmp_one, tmp_two):
+def forward_part(count, latent_ref, w_one_ref, w_two_ref, act_one_ref, slope_one_ref, act_two_ref, slope_two_ref, tmp_one, tmp_two):
     in_chan = w_one_ref.shape[0] // 16
     mid_chan = w_two_ref.shape[1] // 2
     out_chan = w_two_ref.shape[2] // 4
@@ -114,9 +113,7 @@
             up_rows(tmp_two, act_two_ref, slope_two_ref, at + 1, at, count, breadth, out_chan)
 
 
-def last_kernel(count, act_ref, slope_ref, w_ref, target_ref, decoded_ref, grad_ref, kgrad_ref, tmp, grads, adj):
-    step = pl.program_id(0)
-    steps = pl.num_programs(0)
+def last_part(count, step, steps, act_ref, slope_ref, w_ref, target_ref, decoded_ref, grad_ref, kgrad_ref, tmp, grads, adj):
     breadth = act_ref.shape[1] // count
     in_chan = act_ref.shape[2]
     lanes = 2 * (w_ref.shape[2] // 4)
@@ -176,7 +173,7 @@
     return jnp.concatenate(pieces, axis=0)
 
 
-def backward_kernel(count, side_ref, latent_ref, act_ref, slope_ref, w_ref, grad_two_ref, third_ref, kept_ref, sent_ref, grad_one, adj, total_one, total_two):
+def second_part(count, side_ref, act_ref, slope_ref, w_ref, grad_two_ref, third_ref, grad_one, kept_ref, sent_ref, adj, total_two):
     side = side_ref[0]
 
     def put(half, rows, values):
@@ -220,118 +217,149 @@
     for row in range(height):
         upstream = adj[row].astype(jnp.bfloat16).astype(jnp.float32)
         grad_one[row] = (upstream * slope_ref[row]).astype(jnp.bfloat16)
-    in_chan = latent_ref.shape[0] * latent_ref.shape[2] // (H0 * W0)
-    tail = 8 * in_chan
     lanes = 2 * out_chan
     for parity in (0, 1):
         for which in (0, 1):
             for pair in (0, 1):
-                rows = pl.ds(tail + (2 * which + pair) * mid_chan, mid_chan)
+                rows = pl.ds((2 * which + pair) * mid_chan, mid_chan)
                 above, left_edge = which * mid_chan, pair * lanes
                 put(
                     parity,
                     rows,
                     lambda: total_two[parity, above:above + mid_chan, left_edge:left_edge + lanes],
                 )
-        put(parity, pl.ds(tail + 4 * mid_chan, third_ref.shape[1]), lambda: third_ref[parity])
-    for parity in (0, 1):
-        for which in (0, 1):
-            lefts = []
-            rights = []
-            for row in range(H0):
-                source = row + (ROW_SHIFT[parity] if which else 0)
-                if 0 <= source < H0:
-                    lefts.append(latent_row(latent_ref, source))
-                    rights.append(side_taps(grad_one, 2 * row + parity, count, W0))
-            left = jnp.concatenate(lefts, axis=0) if len(lefts) > 1 else lefts[0]
-            right = jnp.concatenate(rights, axis=0) if len(rights) > 1 else rights[0]
-            total_one[...] = product_tn(left, right)
-            row_tap = ROW_TAPS[parity][which]
-            for slot, col_tap in enumerate(COL_TAPS):
-                rows = pl.ds(((row_tap % 2) * 4 + col_tap) * in_chan, in_chan)
-                put(row_tap // 2, rows, lambda: total_one[:, slot * mid_chan:(slot + 1) * mid_chan])
-
-
-def params(steps=0):
-    if steps:
-        return pltpu.CompilerParams(vmem_limit_bytes=VMEM_BYTES, dimension_semantics=("arbitrary",))
-    return pltpu.CompilerParams(vmem_limit_bytes=VMEM_BYTES)
-
-
-def forward(latent, w_one, w_two):
+        put(parity, pl.ds(4 * mid_chan, third_ref.shape[1]), lambda: third_ref[parity])
+
+
+def first_kernel(count, half_ref, latent_ref, grad_one, out_ref, total_one):
+    in_chan = latent_ref.shape[0] * latent_ref.shape[2] // (H0 * W0)
+    mid_chan = grad_one.shape[2]
+    for half in (0, 1):
+
+        @pl.when(half_ref[0] == half)
+        def _(half=half):
+            for row_tap in (2 * half, 2 * half + 1):
+                parity = 0 if row_tap in ROW_TAPS[0] else 1
+                shift = ROW_SHIFT[parity] if ROW_TAPS[parity][1] == row_tap else 0
+                rows = [row for row in range(H0) if 0 <= row + shift < H0]
+                lefts = [latent_row(latent_ref, row + shift) for row in rows]
+                rights = [side_taps(grad_one, 2 * row + parity, count, W0) for row in rows]
+                left = jnp.concatenate(lefts, axis=0) if len(lefts) > 1 else lefts[0]
+                right = jnp.concatenate(rights, axis=0) if len(rights) > 1 else rights[0]
+                total_one[...] = product_tn(left, right)
+                for slot, col_tap in enumerate(COL_TAPS):
+                    to = pl.ds(((row_tap % 2) * 4 + col_tap) * in_chan, in_chan)
+                    out_ref[to, :] = total_one[:, slot * mid_chan:(slot + 1) * mid_chan].astype(jnp.bfloat16)
+
+
+def decoder_kernel(
+    count, side_ref, latent_ref, w_one_ref, w_two_ref, w_three_ref, target_ref,
+    decoded_ref, grad_one_ref, kept_ref, sent_ref,
+    act_one, slope_one, act_two, slope_two, grad_two, kgrad_three, tmp_one, tmp_two, tmp_three, grads, adj_two, adj_one, total_two,
+):
+    step = pl.program_id(0)
+    steps = pl.num_programs(0)
+
+    @pl.when(step == 0)
+    def _():
+        forward_part(count, latent_ref, w_one_ref, w_two_ref, act_one, slope_one, act_two, slope_two, tmp_one, tmp_two)
+
+    last_part(
+        count, step, steps, act_two, slope_two, w_three_ref, target_ref, decoded_ref, grad_two, kgrad_three, tmp_three, grads, adj_two
+    )
+
+    @pl.when(step == steps - 1)
+    def _():
+        second_part(
+            count, side_ref, act_one, slope_one, w_two_ref, grad_two, kgrad_three, grad_one_ref, kept_ref, sent_ref, adj_one, total_two
+        )
+
+
+def params(mebibytes, gridded=False):
+    order = ("arbitrary",) if gridded else None
+    return pltpu.CompilerParams(vmem_limit_bytes=mebibytes * 1024 * 1024, dimension_semantics=order)
+
+
+def decoder(side, latent, w_one, w_two, w_three, target):
     count = latent.shape[1]
     mid_chan = w_two.shape[1] // 2
     out_chan = w_two.shape[2] // 4
     height, breadth = 2 * H0, 2 * W0
+    steps, flat, lanes = target.shape[0] // 2, target.shape[1], target.shape[2]
+    third_rows = w_three.shape[1]
+
+    def whole(shape):
+        return pl.BlockSpec(shape, lambda step: (0,) * len(shape))
+
+    act_one = (height, breadth * count, mid_chan)
+    act_two = (2 * height, flat, out_chan)
+    padded = (2 * height + 2, flat, out_chan)
+    tail = (4 * mid_chan + third_rows, mid_chan)
+    single = pl.Buffered(1)
     return pl.pallas_call(
-        functools.partial(forward_kernel, count),
-        name="decoder_forward",
-        out_shape=(
-            jax.ShapeDtypeStruct((height, breadth * count, mid_chan), jnp.bfloat16),
-            jax.ShapeDtypeStruct((height, breadth * count, mid_chan), jnp.float32),
-            jax.ShapeDtypeStruct((2 * height + 2, 2 * breadth * count, out_chan), jnp.bfloat16),
-            jax.ShapeDtypeStruct((2 * height, 2 * breadth * count, out_chan), jnp.float32),
-        ),
-        scratch_shapes=[
-            pltpu.VMEM((W0 * count, 4 * mid_chan), jnp.float32),
-            pltpu.VMEM((breadth * count, 4 * out_chan), jnp.float32),
-        ],
-        compiler_params=params(),
-    )(latent, w_one, w_two)
-
-
-def last_layer(act_two, slope_two, w_three, target):
-    steps, rows, in_chan = slope_two.shape
-    count = rows // (4 * W0)
-    lanes = target.shape[2]
-    whole = lambda shape: pl.BlockSpec(shape, lambda step: (0,) * len(shape))
-    return pl.pallas_call(
-        functools.partial(last_kernel, count),
-        name="decoder_last",
+        functools.partial(decoder_kernel, count),
+        name="decoder",
         grid=(steps,),
         in_specs=[
-            whole(act_two.shape),
-            whole(slope_two.shape),
-            whole(w_three.shape),
-            pl.BlockSpec((2, rows, lanes), lambda step: (step, 0, 0)),
+            pl.BlockSpec(memory_space=pltpu.SMEM),
+            pl.BlockSpec(latent.shape, lambda step: (0, 0, 0), pipeline_mode=single),
+            pl.BlockSpec(w_one.shape, lambda step: (0, 0), pipeline_mode=single),
+            pl.BlockSpec(w_two.shape, lambda step: (0, 0, 0), pipeline_mode=single),
+            pl.BlockSpec(w_three.shape, lambda step: (0, 0, 0), pipeline_mode=single),
+            pl.BlockSpec((2, flat, lanes), lambda step: (step, 0, 0)),
         ],
         out_specs=(
-            pl.BlockSpec((2, rows, lanes), lambda step: (step, 0, 0)),
-            whole(slope_two.shape),
-            whole(w_three.shape),
+            pl.BlockSpec((2, flat, lanes), lambda step: (step, 0, 0)),
+            whole(act_one),
+            whole(tail),
+            whole(tail),
         ),
         out_shape=(
             jax.ShapeDtypeStruct(target.shape, jnp.bfloat16),
-            jax.ShapeDtypeStruct(slope_two.shape, jnp.bfloat16),
-            jax.ShapeDtypeStruct(w_three.shape, jnp.float32),
+            jax.ShapeDtypeStruct(act_one, jnp.bfloat16),
+            jax.ShapeDtypeStruct(tail, jnp.bfloat16),
+            jax.ShapeDtypeStruct(tail, jnp.bfloat16),
         ),
         scratch_shapes=[
-            pltpu.VMEM((rows, 2 * lanes), jnp.float32),
-            pltpu.VMEM((rows + 2 * count, lanes), jnp.float32),
-            pltpu.VMEM((steps + 2, rows, in_chan), jnp.float32),
+            pltpu.VMEM(act_one, jnp.bfloat16),
+            pltpu.VMEM(act_one, jnp.float32),
+            pltpu.VMEM(padded, jnp.bfloat16),
+            pltpu.VMEM(act_two, jnp.float32),
+            pltpu.VMEM(act_two, jnp.bfloat16),
+            pltpu.VMEM(w_three.shape, jnp.float32),
+            pltpu.VMEM((W0 * count, 4 * mid_chan), jnp.float32),
+            pltpu.VMEM((breadth * count, 4 * out_chan), jnp.float32),
+            pltpu.VMEM((flat, 2 * lanes), jnp.float32),
+            pltpu.VMEM((flat + 2 * count, lanes), jnp.float32),
+            pltpu.VMEM(padded, jnp.float32),
+            pltpu.VMEM(act_one, jnp.float32),
+            pltpu.VMEM(w_two.shape, jnp.float32),
         ],
-        compiler_params=params(1),
-    )(act_two, slope_two, w_three, target)
-
-
-def backward(side, latent, act_one, slope_one, w_two, grad_two, third):
+        compiler_params=params(52, True),
+    )(side, latent, w_one, w_two, w_three, target)
+
+
+def first_grad(half, latent, grad_one, after):
     count = latent.shape[1]
     in_chan = latent.shape[0] * latent.shape[2] // (H0 * W0)
-    mid_chan = act_one.shape[2]
+    mid_chan = grad_one.shape[2]
+    vmem = pl.BlockSpec(memory_space=pltpu.VMEM)
+
+    def kernel(half_ref, latent_ref, grad_ref, after_ref, out_ref, total_one):
+        first_kernel(count, half_ref, latent_ref, grad_ref, out_ref, total_one)
+
     return pl.pallas_call(
-        functools.partial(backward_kernel, count),
-        name="decoder_backward",
-        in_specs=[pl.BlockSpec(memory_space=pltpu.SMEM)] + [pl.BlockSpec(memory_space=pltpu.VMEM)] * 6,
-        out_specs=(pl.BlockSpec(memory_space=pltpu.VMEM),) * 2,
-        out_shape=(jax.ShapeDtypeStruct((8 * in_chan + 4 * mid_chan + third.shape[1], mid_chan), jnp.bfloat16),) * 2,
-        scratch_shapes=[
-            pltpu.VMEM(act_one.shape, jnp.bfloat16),
-            pltpu.VMEM(act_one.shape, jnp.float32),
-            pltpu.VMEM((in_chan, 4 * mid_chan), jnp.float32),
-            pltpu.VMEM(w_two.shape, jnp.float32),
-        ],
-        compiler_params=params(),
-    )(side, latent, act_one, slope_one, w_two, grad_two, third)
+        kernel,
+        name="first_grad",
+        in_specs=[pl.BlockSpec(memory_space=pltpu.SMEM), vmem, vmem, pl.BlockSpec(memory_space=pl.ANY)],
+        out_specs=vmem,
+        out_shape=jax.ShapeDtypeStruct((8 * in_chan, mid_chan), jnp.bfloat16),
+        scratch_shapes=[pltpu.VMEM((in_chan, 4 * mid_chan), jnp.float32)],
+        compiler_params=params(24),
+        cost_estimate=pl.CostEstimate(
+            flops=64 * count * in_chan * mid_chan, bytes_accessed=16 * in_chan * mid_chan, transcendentals=0
+        ),
+    )(half, latent, grad_one, after)
 
 
 def spatial_first_kernel(grid_ref, after_ref, rows_ref, tmp):
@@ -359,7 +387,7 @@
         out_specs=pl.BlockSpec((per, flat, 2 * chan), lambda step: (step, 0, 0)),
         out_shape=jax.ShapeDtypeStruct((height, flat, 2 * chan), jnp.bfloat16),
         scratch_shapes=[pltpu.VMEM((count, breadth, chan), jnp.float32)],
-        compiler_params=params(1),
+        compiler_params=params(20, True),
         cost_estimate=pl.CostEstimate(flops=0, bytes_accessed=28000000, transcendentals=0),
     )(grid, after)
 
@@ -390,60 +418,58 @@
         out_specs=pl.BlockSpec((count, per, breadth, chan), lambda step: (0, step, 0, 0)),
         out_shape=jax.ShapeDtypeStruct((count, height, breadth, chan), jnp.bfloat16),
         scratch_shapes=[pltpu.VMEM((count, breadth, chan), jnp.float32)],
-        compiler_params=params(1),
+        compiler_params=params(20, True),
         cost_estimate=pl.CostEstimate(flops=0, bytes_accessed=28000000, transcendentals=0),
     )(rows, after)
 
 
-def bucket_kernel(subject_ref, count_ref, shift_ref, fmri_ref, first_ref, second_ref, place_ref):
+def bucket_kernel(half, subject_ref, count_ref, shift_ref, fmri_ref, after_ref, out_ref, place_ref):
     samples, voxels = fmri_ref.shape
-    slots = first_ref.shape[0]
+    slots = out_ref.shape[0]
     subjects = count_ref.shape[0]
     room = slots // subjects
     owner = subject_ref[...]
-    lane = lax.broadcasted_iota(jnp.int32, (samples, 128), 1)
-    onehot = jnp.where(owner == lane, 1.0, 0.0)
+    name = lax.broadcasted_iota(jnp.int32, (subjects, samples), 0)
+    onehot = jnp.where(owner == name, 1.0, 0.0)
     row = lax.broadcasted_iota(jnp.int32, (samples, samples), 0)
     col = lax.broadcasted_iota(jnp.int32, (samples, samples), 1)
-    before = jnp.where(col < row, 1.0, 0.0).astype(jnp.bfloat16)
-    earlier = product(before, onehot.astype(jnp.bfloat16))
-    rank = jnp.sum(earlier * onehot, axis=1, keepdims=True).astype(jnp.int32)
-    position = owner * room + rank + jnp.where(rank >= room, slots - room, 0)
-    slot = lax.broadcasted_iota(jnp.int32, (samples, 2 * slots), 1)
+    before = jnp.where(row < col, 1.0, 0.0).astype(jnp.bfloat16)
+    earlier = product(onehot.astype(jnp.bfloat16), before)
+    rank = jnp.sum(earlier * onehot, axis=0, keepdims=True).astype(jnp.int32) - half * room
+    position = jnp.where((rank >= 0) & (rank < room), owner * room + rank, -1)
+    slot = lax.broadcasted_iota(jnp.int32, (slots, samples), 0)
     place_ref[...] = jnp.where(slot == position, 1.0, 0.0).astype(jnp.bfloat16)
     voxel = lax.broadcasted_iota(jnp.int32, (room, voxels), 1) + shift_ref[0]
-    for half, out_ref in enumerate((first_ref, second_ref)):
-        for target in range(subjects):
-            here = pl.ds(half * slots + target * room, room)
-            if room * target % 128 == 0:
-                width = min(128, slots)
-                rows = product_tn(place_ref[:, pl.ds(half * slots + target * room, width)], fmri_ref[...])
-                for inner in range(width // room):
-                    keep = voxel < count_ref[target + inner]
-                    kept = jnp.where(keep, rows[inner * room:(inner + 1) * room], 0.0)
-                    out_ref[pl.ds((target + inner) * room, room), :] = kept.astype(jnp.bfloat16)
-
-
-def bucketed(subject, voxel_count, shift, fmri, slots):
+    together = max(1, 64 // room)
+    for start in range(0, subjects, together):
+        rows = product(place_ref[pl.ds(start * room, together * room), :], fmri_ref[...])
+        for inner in range(together):
+            kept = jnp.where(voxel < count_ref[start + inner], rows[inner * room:(inner + 1) * room], 0.0)
+            out_ref[pl.ds((start + inner) * room, room), :] = kept.astype(jnp.bfloat16)
+
+
+def bucketed(half, subject, voxel_count, shift, fmri, after):
     samples, voxels = fmri.shape
     vmem = pl.BlockSpec(memory_space=pltpu.VMEM)
     smem = pl.BlockSpec(memory_space=pltpu.SMEM)
     return pl.pallas_call(
-        bucket_kernel,
+        functools.partial(bucket_kernel, half),
         name="bucket_rows",
-        in_specs=[vmem, smem, smem, vmem],
-        out_specs=(vmem, vmem, vmem),
+        in_specs=[vmem, smem, smem, vmem, pl.BlockSpec(memory_space=pl.ANY)],
+        out_specs=(vmem, vmem),
         out_shape=(
-            jax.ShapeDtypeStruct((slots, voxels), jnp.bfloat16),
-            jax.ShapeDtypeStruct((slots, voxels), jnp.bfloat16),
-            jax.ShapeDtypeStruct((samples, 2 * slots), jnp.bfloat16),
+            jax.ShapeDtypeStruct((samples, voxels), jnp.bfloat16),
+            jax.ShapeDtypeStruct((samples, samples), jnp.bfloat16),
         ),
-        compiler_params=params(),
-    )(subject, voxel_count, shift, fmri)
+        compiler_params=params(60),
+    )(subject.reshape(1, samples), voxel_count, shift, fmri, after)
 
 
 def project_kernel(half_ref, rows_ref, map_ref, after_ref, out_ref):
-    out_ref[0] = product(rows_ref[...], map_ref[0]).astype(jnp.bfloat16)
+    width = out_ref.shape[2]
+    for block in range(out_ref.shape[0]):
+        value = product(rows_ref[...], map_ref[0, :, block * width:(block + 1) * width])
+        out_ref[block] = value.astype(jnp.bfloat16)
 
 
 def projected(rows, maps, half, after):
@@ -455,16 +481,16 @@
         name="project_rows",
         grid_spec=pltpu.PrefetchScalarGridSpec(
             num_scalar_prefetch=1,
-            grid=(blocks,),
+            grid=(blocks // 2,),
             in_specs=[
                 pl.BlockSpec((count, voxels), lambda step, half: (0, 0)),
-                pl.BlockSpec((1, voxels, width), lambda step, half: (0, 0, half[0] * blocks + step)),
+                pl.BlockSpec((1, voxels, 2 * width), lambda step, half: (0, 0, half[0] * (blocks // 2) + step)),
                 pl.BlockSpec(memory_space=pl.ANY),
             ],
-            out_specs=pl.BlockSpec((1, count, width), lambda step, half: (step, 0, 0)),
+            out_specs=pl.BlockSpec((2, count, width), lambda step, half: (step, 0, 0)),
         ),
         out_shape=jax.ShapeDtypeStruct((blocks, count, width), jnp.bfloat16),
-        compiler_params=params(1),
+        compiler_params=params(60, True),
         cost_estimate=pl.CostEstimate(
             flops=count * voxels * maps.shape[2],
             bytes_accessed=voxels * maps.shape[2],
@@ -473,22 +499,25 @@
     )(half, rows, maps, after)
 
 
-def collect_kernel(place_ref, first_ref, second_ref, out_ref):
+def collect_kernel(place_a_ref, place_b_ref, first_ref, second_ref, out_ref):
     subjects, blocks, room, width = first_ref.shape
     for block in range(blocks):
-        rows = [ref[subject, block] for ref in (first_ref, second_ref) for subject in range(subjects)]
-        value = product(place_ref[...], jnp.concatenate(rows, axis=0))
+        value = None
+        for place_ref, ref in ((place_a_ref, first_ref), (place_b_ref, second_ref)):
+            rows = jnp.concatenate([ref[subject, block] for subject in range(subjects)], axis=0)
+            term = product_tn(place_ref[...], rows)
+            value = term if value is None else value + term
         out_ref[:, pl.ds(block * width, width)] = value.astype(jnp.bfloat16)
 
 
-def collected(place, first, second):
-    samples = place.shape[0]
+def collected(places, first, second):
+    samples = places[0].shape[1]
     return pl.pallas_call(
         collect_kernel,
         name="collect_rows",
         out_shape=jax.ShapeDtypeStruct((samples, first.shape[1] * first.shape[3]), jnp.bfloat16),
-        compiler_params=params(),
-    )(place, first, second)
+        compiler_params=params(16),
+    )(*places, first, second)
 
 
 def finish_kernel(third_rows, side_ref, own_a, own_b, own_c, other_a, other_b, other_c, first_ref, second_ref, third_ref):
@@ -534,7 +563,7 @@
             jax.ShapeDtypeStruct((16 * mid_chan, lanes // 2), jnp.bfloat16),
             jax.ShapeDtypeStruct((lanes // 4, 8 * third_rows), jnp.bfloat16),
         ),
-        compiler_params=params(),
+        compiler_params=params(24),
     )(side, *own, *other)
 
 
@@ -635,19 +664,22 @@
     dp_bits = bit_pairs("dp")
     side = upper(vox_bits[0]).astype(jnp.int32).reshape(1)
     shift = (lax.axis_index("vox") * vox_local).astype(jnp.int32).reshape(1)
-    first, second, place = bucketed(subject, voxel_count, shift, fmri, samp_dev)
+    first, place_first = bucketed(0, subject, voxel_count, shift, fmri, voxel_count)
+    second, place_second = bucketed(1, subject, voxel_count, shift, fmri, place_first)
 
     def routed(rows):
         sent = rows.reshape(dp_count, room, rows.shape[1])
         return lax.all_to_all(sent, "dp", split_axis=0, concat_axis=0, tiled=True).reshape(rows.shape)
 
-    def vox_summed(rows, after):
+    def core_summed(rows, after):
         sent = projected(rows, ridge_maps, 1 - side, after)
         received = exchanged(sent, vox_bits[:1], 1)
-        terms = [projected(rows, ridge_maps, side, sent), received]
+        return [projected(rows, ridge_maps, side, sent), received]
+
+    def vox_summed(terms):
         for hop in vox_bits[1:]:
             terms, = shared([terms], [hop])
-        return terms, received
+        return terms
 
     def returned(terms):
         latent_part = rounded(summed(terms))
@@ -657,27 +689,31 @@
 
     first = routed(first)
     second = routed(second)
-    terms_first, _ = vox_summed(first, voxel_count)
-    terms_second, core_second = vox_summed(second, terms_first[1])
+    terms_first = vox_summed(core_summed(first, voxel_count))
+    terms_second = core_summed(second, terms_first[1])
+    core_second = terms_second[1]
     pair_two = paired_weight(w_second, mid_chan)
     pair_three = paired_weight(w_third, last_chan)
     target_rows = spatial_first(target, core_second)
-    own_rows = collected(place, returned(terms_first), returned(terms_second))
+    terms_first, terms_second = lax.optimization_barrier((terms_first, terms_second))
+    terms_second = vox_summed(terms_second)
+    places = (place_first, place_second)
+    own_rows = collected(places, returned(terms_first), returned(terms_second))
     own_rows = own_rows.reshape(holders, samp_dev // holders, own_rows.shape[1])
     latent = lax.all_to_all(own_rows, "vox", split_axis=0, concat_axis=0, tiled=True)
     count = latent.shape[1]
-    act_one, slope_one, act_two, slope_two = forward(latent, w_first, pair_two)
-    decoded_rows, grad_two, paired_three = last_layer(act_two, slope_two, pair_three, target_rows)
-    kept, sent = backward(side, latent, act_one, slope_one, pair_two, grad_two, paired_three)
-    third_rows = paired_three.shape[1]
+    decoded_rows, grad_one, kept_tail, sent_tail = decoder(side, latent, w_first, pair_two, pair_three, target_rows)
+    parts_tail = [kept_tail, exchanged(sent_tail, vox_bits[:1], 1)]
+    sent = first_grad(1 - side, latent, grad_one, grad_one)
+    received = exchanged(sent, vox_bits[:1], 1)
+    kept = first_grad(side, latent, grad_one, sent)
+    third_rows = pair_three.shape[1]
     quarter = w_first.shape[0] // 4
     across = [[hop] for hop in vox_bits[1:]]
     near = [dp_bits[:1]]
-    along = [dp_bits[at:at + 2] for at in range(1, len(dp_bits), 2)]
-    routes = (across + near + along, near + across + along, along + across + near)
-    received = exchanged(sent, vox_bits[:1], 1)
-    cuts = ((0, quarter), (quarter, 2 * quarter), (2 * quarter, kept.shape[0]))
-    parts = [[kept[low:high], received[low:high]] for low, high in cuts]
+    along = [[hop] for hop in dp_bits[1:]]
+    routes = (across + near + along, near + across + along, along[:1] + across + near + along[1:])
+    parts = [[kept[:quarter], received[:quarter]], [kept[quarter:], received[quarter:]], parts_tail]
     decoded = sample_first(decoded_rows, count, w_third.shape[1], received)
     for stage in range(len(routes[0])):
         parts = over_chains(shared, parts, [route[stage] for route in routes])
@@ -686,7 +722,7 @@
     shares = [summed(terms).astype(jnp.bfloat16) for terms in parts]
     for stage in reversed(range(len(routes[0]))):
         shares = over_chains(gathered, shares, [route[stage] for route in routes])
-        shares = lax.optimization_barrier(tuple(shares))
+        shares = list(lax.optimization_barrier(tuple(shares)))
     others = [exchanged(values, vox_bits[:1], 1) for values in shares]
     total_first, total_second, third = finished(side, shares, others, third_rows)
     total_third = third.T

time: 291 us -> 274 us (0.942)
  Pallas kernels: 92.8 us -> 70.1 us
  starting transfers between devices: 55.9 us -> 44.3 us
  waiting for transfers between devices: 115 us -> 123 us
  local copies, waits for them, and re-layouts: 12.1 us -> 19 us
    ppermute x30 -> x25, starting transfers between devices: 29.5 us -> 18.1 us  [exchanged(): lax.ppermute(values, axis, [(at, at ^ flip) for at in range(lax.axis_size...]
    ppermute x30 -> x25, waiting for transfers between devices: 67.6 us -> 79 us  [exchanged(): lax.ppermute(values, axis, [(at, at ^ flip) for at in range(lax.axis_size...]
    pallas_call x4 -> x5, Pallas kernels: 43.5 us -> 33.5 us  [the longest x1 24.6 us: decoder(): pl.pallas_call(functools.partial(decoder_kernel, count), name='decoder',...]
    unnamed x40 -> x43, local copies, waits for them, and re-layouts: 6.99 us -> 14.5 us
    pallas_call x1, Pallas kernels: 7.09 us -> 3.44 us  [spatial_first(): pl.pallas_call(spatial_first_kernel, name='spatial_first', grid=(height /...]
    add x3 -> x6, other arithmetic: 1.95 us -> 5.45 us  [summed(): value = value.astype(jnp.float32) + term.astype(jnp.float32)]
    pallas_call x4, Pallas kernels: 26.5 us -> 23.5 us  [projected(): pl.pallas_call(project_kernel, name='project_rows', grid_spec=pltpu.Prefe...]
  transfers between devices with their start and end apart: 35 -> 30, of which waited for: 18 -> 20; matrix products, arithmetic and copies ran while one was open for 5% -> 5% of each run, Pallas kernels for 12% -> 11%
where the time goes in v3:
time: 274 us; the launch traced here: 273 us
  waiting for transfers between devices  123 us (45%)
  Pallas kernels  70.1 us (26%)
  starting transfers between devices  44.3 us (16%)
  local copies, waits for them, and re-layouts  19 us (7%)
  other arithmetic  15.4 us (6%)
    ppermute x25, waiting for transfers between devices, exchanged(): lax.ppermute(values, axis, [(at, at ^ flip) for at in range(lax.axis_size...  79 us
    all_to_all x2, waiting for transfers between devices, routed(): lax.all_to_all(sent, 'dp', split_axis=0, concat_axis=0, tiled=True)  32.7 us
    pallas_call x1, Pallas kernels, decoder(): pl.pallas_call(functools.partial(decoder_kernel, count), name='decoder',...  24.6 us
    pallas_call x4, Pallas kernels, projected(): pl.pallas_call(project_kernel, name='project_rows', grid_spec=pltpu.Prefe...  23.5 us
    ppermute x25, starting transfers between devices, exchanged(): lax.ppermute(values, axis, [(at, at ^ flip) for at in range(lax.axis_size...  18.1 us
    unnamed x43, local copies, waits for them, and re-layouts  14.5 us
    all_to_all x2, starting transfers between devices, returned(): return lax.all_to_all(sent, 'dp', split_axis=0, concat_axis=0, tiled=True)  11.7 us
    all_to_all x2, waiting for transfers between devices, returned(): return lax.all_to_all(sent, 'dp', split_axis=0, concat_axis=0, tiled=True)  11.5 us
  transfers between devices with their start and end apart: 30, of which 20 were waited for; matrix products, arithmetic and copies ran while one was open for 5% of the time, Pallas kernels for 11%

profile of v3, /device:TPU:0, one launch (start us, length us, event | category | flops | bytes accessed | tf_op | source)
XLA Modules:
  0.0 273.2 jit_solution(11625693723802390674)
XLA Ops:
  0.6 3.3 %bucket_rows.2 = (bf16[256,2048]{1,0:T(8,128)(2,1)}, bf16[256,256]{1,0:T(8,128)(2,1)}) custom-call(s32[1,256]{1,0:T(1,128)} %bitcast.101, s32[8]{0:T(128)} %after_ref.3, s32[1]{0:T(128)} %bitcast.2.shift_ref, bf16[256,2048]{1,0:T(8,128)(2,1)} %fmri_ref.3, s32[8]{0:T(128)} %after_ref.3), custom_call_target="tpu_custom_call" | custom-call | tf_op jit(solution)/shard_map/bucket_rows/pallas_call | solution.py:455
  3.9 7.3 %all-to-all-start = ((bf16[8,32,2048]{2,1,0:T(8,128)(2,1)}), bf16[8,32,2048]{2,1,0:T(8,128)(2,1)S(1)}, u32[]{:S(2)}, u32[]{:S(2)}) async-start(bf16[8,32,2048]{2,1,0:T(8,128)(2,1)} %bitcast.100), calls=%async_computation | async-start | bytes 2097152 | tf_op jit(solution)/shard_map/all_to_all | solution.py:672
  11.2 3.3 %bucket_rows.3 = (bf16[256,2048]{1,0:T(8,128)(2,1)}, bf16[256,256]{1,0:T(8,128)(2,1)}) custom-call(s32[1,256]{1,0:T(1,128)} %bitcast.102, s32[8]{0:T(128)} %after_ref.3, s32[1]{0:T(128)} %bitcast.2.shift_ref, bf16[256,2048]{1,0:T(8,128)(2,1)} %fmri_ref.3, bf16[256,256]{1,0:T(8,128)(2,1)} %get-tuple-element.47.after_ref.place_a_ref), custom_call_target="tpu_custom_call" | custom-call | tf_op jit(solution)/shard_map/bucket_rows/pallas_call | solution.py:455
  14.5 22.5 %all-to-all-done = bf16[8,32,2048]{2,1,0:T(8,128)(2,1)S(1)} async-done(((bf16[8,32,2048]{2,1,0:T(8,128)(2,1)}), bf16[8,32,2048]{2,1,0:T(8,128)(2,1)S(1)}, u32[]{:S(2)}, u32[]{:S(2)}) %all-to-all-start) | async-done | bytes 1048608 | tf_op jit(solution)/shard_map/all_to_all | solution.py:672
  37.0 3.6 %all-to-all-start.1 = ((bf16[8,32,2048]{2,1,0:T(8,128)(2,1)}), bf16[8,32,2048]{2,1,0:T(8,128)(2,1)S(1)}, u32[]{:S(2)}, u32[]{:S(2)}) async-start(bf16[8,32,2048]{2,1,0:T(8,128)(2,1)} %bitcast.99), calls=%async_computation.1 | async-start | bytes 2097152 | tf_op jit(solution)/shard_map/all_to_all | solution.py:672
  40.6 5.9 %project_rows.4.after_ref = bf16[4,256,512]{2,1,0:T(8,128)(2,1)} custom-call(s32[1]{0:T(128)S(6)} %sub.31.half_ref, bf16[256,2048]{1,0:T(8,128)(2,1)} %bitcast.91, bf16[1,2048,4096]{2,1,0:T(8,128)(2,1)} %map_ref.7, s32[8]{0:T(128)} %after_ref.3), custom_call_target="tpu_custom_call" | custom-call | flops 2147483648 | bytes 8388608 | tf_op jit(solution)/shard_map/project_rows/pallas_call | solution.py:479
  46.4 5.9 %project_rows.5 = bf16[4,256,512]{2,1,0:T(8,128)(2,1)} custom-call(s32[1]{0:T(128)} %bitcast.half_ref.side_ref, bf16[256,2048]{1,0:T(8,128)(2,1)} %bitcast.92, bf16[1,2048,4096]{2,1,0:T(8,128)(2,1)} %map_ref.7, bf16[4,256,512]{2,1,0:T(8,128)(2,1)} %project_rows.4.after_ref), custom_call_target="tpu_custom_call" | custom-call | flops 2147483648 | bytes 8388608 | tf_op jit(solution)/shard_map/project_rows/pallas_call | solution.py:479
  52.3 2.4 add_convert_fusion.5
  56.3 10.2 %all-to-all-done.1 = bf16[8,32,2048]{2,1,0:T(8,128)(2,1)S(1)} async-done(((bf16[8,32,2048]{2,1,0:T(8,128)(2,1)}), bf16[8,32,2048]{2,1,0:T(8,128)(2,1)S(1)}, u32[]{:S(2)}, u32[]{:S(2)}) %all-to-all-start.1) | async-done | bytes 1048608 | tf_op jit(solution)/shard_map/all_to_all | solution.py:672
  66.5 2.6 collective-permute-done.1.after_ref
  69.9 5.8 %project_rows.6.after_ref = bf16[4,256,512]{2,1,0:T(8,128)(2,1)} custom-call(s32[1]{0:T(128)S(6)} %sub.31.half_ref, bf16[256,2048]{1,0:T(8,128)(2,1)} %bitcast.93, bf16[1,2048,4096]{2,1,0:T(8,128)(2,1)} %map_ref.7, bf16[2,256,512]{2,1,0:T(8,128)(2,1)} %copy-done.15), custom_call_target="tpu_custom_call" | custom-call | flops 2147483648 | bytes 8388608 | tf_op jit(solution)/shard_map/project_rows/pallas_call | solution.py:479
  75.8 5.9 %project_rows.7 = bf16[4,256,512]{2,1,0:T(8,128)(2,1)} custom-call(s32[1]{0:T(128)} %bitcast.half_ref.side_ref, bf16[256,2048]{1,0:T(8,128)(2,1)} %bitcast.94, bf16[1,2048,4096]{2,1,0:T(8,128)(2,1)} %map_ref.7, bf16[4,256,512]{2,1,0:T(8,128)(2,1)} %project_rows.6.after_ref), custom_call_target="tpu_custom_call" | custom-call | flops 2147483648 | bytes 8388608 | tf_op jit(solution)/shard_map/project_rows/pallas_call | solution.py:479
  84.0 6.0 %all-to-all-start.2 = ((bf16[8,2,32,512]{3,2,1,0:T(8,128)(2,1)}), bf16[8,2,32,512]{3,2,1,0:T(8,128)(2,1)S(1)}, u32[]{:S(2)}, u32[]{:S(2)}) async-start(bf16[8,2,32,512]{3,2,1,0:T(8,128)(2,1)} %bitcast.90), calls=%async_computation.2 | async-start | bytes 1048576 | tf_op jit(solution)/shard_map/all_to_all | solution.py:688
  91.7 12.5 %collective-permute-done.3 = bf16[2,256,512]{2,1,0:T(8,128)(2,1)S(1)} collective-permute-done((bf16[2,256,512]{2,1,0:T(8,128)(2,1)S(1)}, bf16[2,256,512]{2,1,0:T(8,128)(2,1)S(1)}, u32[]{:S(2)}, u32[]{:S(2)}) %collective-permute-start.3) | collective-permute-done | bytes 524320 | tf_op jit(solution)/shard_map/ppermute | solution.py:596
  105.3 5.7 %all-to-all-start.3 = ((bf16[8,2,32,512]{3,2,1,0:T(8,128)(2,1)}), bf16[8,2,32,512]{3,2,1,0:T(8,128)(2,1)S(1)}, u32[]{:S(2)}, u32[]{:S(2)}) async-start(bf16[8,2,32,512]{3,2,1,0:T(8,128)(2,1)} %bitcast.89), calls=%async_computation.3 | async-start | bytes 1048576 | tf_op jit(solution)/shard_map/all_to_all | solution.py:688
  113.2 11.5 %all-to-all-done.3.second_ref = bf16[8,2,32,512]{3,2,1,0:T(8,128)(2,1)S(1)} async-done(((bf16[8,2,32,512]{3,2,1,0:T(8,128)(2,1)}), bf16[8,2,32,512]{3,2,1,0:T(8,128)(2,1)S(1)}, u32[]{:S(2)}, u32[]{:S(2)}) %all-to-all-start.3) | async-done | bytes 524320 | tf_op jit(solution)/shard_map/all_to_all | solution.py:688
  126.0 3.7 %all-to-all-start.4 = ((bf16[4,64,1024]{2,1,0:T(8,128)(2,1)}), bf16[4,64,1024]{2,1,0:T(8,128)(2,1)S(1)}, u32[]{:S(2)}, u32[]{:S(2)}) async-start(bf16[4,64,1024]{2,1,0:T(8,128)(2,1)} %bitcast.11), calls=%async_computation.4 | async-start | bytes 1048576 | tf_op jit(solution)/shard_map/all_to_all | solution.py:703
  131.7 3.4 %copy-done.6 = bf16[64,16,32,64]{3,2,1,0:T(8,128)(2,1)S(1)} copy-done((bf16[64,16,32,64]{3,2,1,0:T(8,128)(2,1)S(1)}, bf16[64,16,32,64]{3,2,1,0:T(8,128)(2,1)}, u32[]{:S(2)}) %copy-start.6) | copy-done | bytes 4194328
  135.1 3.4 %spatial_first.1.target_ref = bf16[16,1024,128]{2,1,0:T(8,128)(2,1)S(1)} custom-call(bf16[64,16,32,64]{3,2,1,0:T(8,128)(2,1)S(1)} %copy-done.6, bf16[4,256,512]{2,1,0:T(8,128)(2,1)S(1)} %collective-permute-done.2.after_ref), custom_call_target="tpu_custom_call" | custom-call | bytes 28000000 | tf_op jit(solution)/shard_map/spatial_first/pallas_call | solution.py:379
  140.6 24.6 %decoder.1 = (bf16[16,1024,128]{2,1,0:T(8,128)(2,1)}, bf16[4,512,256]{2,1,0:T(8,128)(2,1)}, bf16[1280,256]{1,0:T(8,128)(2,1)S(1)}, bf16[1280,256]{1,0:T(8,128)(2,1)}) custom-call(s32[1]{0:T(128)} %bitcast.half_ref.side_ref, bf16[4,64,1024]{2,1,0:T(8,128)(2,1)S(1)} %all-to-all-done.4.latent_ref, bf16[8192,256]{1,0:T(8,128)(2,1)} %w_one_ref.1, ...), custom_call_target="tpu_custom_call" | custom-call | tf_op jit(solution)/shard_map/decoder/pallas_call | solution.py:299
  185.9 5.4 %sample_first.1 = bf16[64,16,32,64]{3,2,1,0:T(8,128)(2,1)} custom-call(bf16[16,1024,128]{2,1,0:T(8,128)(2,1)S(1)} %copy-done.7, bf16[4096,256]{1,0:T(8,128)(2,1)} %collective-permute-done.4.after_ref), custom_call_target="tpu_custom_call" | custom-call | bytes 28000000 | tf_op jit(solution)/shard_map/sample_first/pallas_call | solution.py:410
  199.4 7.7 %collective-permute-done.10 = bf16[832,256]{1,0:T(8,128)(2,1)S(1)} collective-permute-done((bf16[832,256]{1,0:T(8,128)(2,1)S(1)}, bf16[832,256]{1,0:T(8,128)(2,1)S(1)}, u32[]{:S(2)}, u32[]{:S(2)}) %collective-permute-start.10) | collective-permute-done | bytes 426016 | tf_op jit(solution)/shard_map/ppermute | solution.py:596
  210.6 4.8 %collective-permute-done.11 = bf16[512,256]{1,0:T(8,128)(2,1)S(1)} collective-permute-done((bf16[512,256]{1,0:T(8,128)(2,1)S(1)}, bf16[512,256]{1,0:T(8,128)(2,1)S(1)}, u32[]{:S(2)}, u32[]{:S(2)}) %collective-permute-start.11) | collective-permute-done | bytes 262176 | tf_op jit(solution)/shard_map/ppermute | solution.py:596
  216.3 10.6 %collective-permute-done.13 = bf16[336,256]{1,0:T(8,128)(2,1)S(1)} collective-permute-done((bf16[336,256]{1,0:T(8,128)(2,1)S(1)}, bf16[336,256]{1,0:T(8,128)(2,1)S(1)}, u32[]{:S(2)}, u32[]{:S(2)}) %collective-permute-start.13) | collective-permute-done | bytes 172064 | tf_op jit(solution)/shard_map/ppermute | solution.py:596
  227.2 6.7 %collective-permute-done.14 = bf16[336,256]{1,0:T(8,128)(2,1)S(1)} collective-permute-done((bf16[336,256]{1,0:T(8,128)(2,1)S(1)}, bf16[336,256]{1,0:T(8,128)(2,1)S(1)}, u32[]{:S(2)}, u32[]{:S(2)}) %collective-permute-start.14) | collective-permute-done | bytes 172064 | tf_op jit(solution)/shard_map/ppermute | solution.py:596
  235.1 4.3 %collective-permute-done.16 = bf16[160,256]{1,0:T(8,128)(2,1)S(1)} collective-permute-done((bf16[160,256]{1,0:T(8,128)(2,1)S(1)}, bf16[160,256]{1,0:T(8,128)(2,1)S(1)}, u32[]{:S(2)}, u32[]{:S(2)}) %collective-permute-start.16) | collective-permute-done | bytes 81952 | tf_op jit(solution)/shard_map/ppermute | solution.py:596
  242.8 4.1 %collective-permute-done.17 = bf16[512,256]{1,0:T(8,128)(2,1)S(1)} collective-permute-done((bf16[512,256]{1,0:T(8,128)(2,1)S(1)}, bf16[512,256]{1,0:T(8,128)(2,1)S(1)}, u32[]{:S(2)}, u32[]{:S(2)}) %collective-permute-start.17) | collective-permute-done | bytes 262176 | tf_op jit(solution)/shard_map/ppermute | solution.py:596
  246.9 4.3 %collective-permute-done.18 = bf16[832,256]{1,0:T(8,128)(2,1)S(1)} collective-permute-done((bf16[832,256]{1,0:T(8,128)(2,1)S(1)}, bf16[832,256]{1,0:T(8,128)(2,1)S(1)}, u32[]{:S(2)}, u32[]{:S(2)}) %collective-permute-start.18) | collective-permute-done | bytes 426016 | tf_op jit(solution)/shard_map/ppermute | solution.py:596
  254.2 4.2 %collective-permute-done.21 = bf16[640,256]{1,0:T(8,128)(2,1)S(1)} collective-permute-done((bf16[640,256]{1,0:T(8,128)(2,1)S(1)}, bf16[640,256]{1,0:T(8,128)(2,1)S(1)}, u32[]{:S(2)}, u32[]{:S(2)}) %collective-permute-start.21) | collective-permute-done | bytes 327712 | tf_op jit(solution)/shard_map/ppermute | solution.py:596
  258.4 5.1 %collective-permute-done.19 = bf16[1024,256]{1,0:T(8,128)(2,1)S(1)} collective-permute-done((bf16[1024,256]{1,0:T(8,128)(2,1)S(1)}, bf16[1024,256]{1,0:T(8,128)(2,1)S(1)}, u32[]{:S(2)}, u32[]{:S(2)}) %collective-permute-start.19) | collective-permute-done | bytes 524320 | tf_op jit(solution)/shard_map/ppermute | solution.py:596
  265.7 4.5 %collective-permute-done.24.other_c = bf16[1280,256]{1,0:T(8,128)(2,1)S(1)} collective-permute-done((bf16[1280,256]{1,0:T(8,128)(2,1)S(1)}, bf16[1280,256]{1,0:T(8,128)(2,1)S(1)}, u32[]{:S(2)}, u32[]{:S(2)}) %collective-permute-start.24) | collective-permute-done | bytes 655392 | tf_op jit(solution)/shard_map/ppermute | solution.py:596
  270.2 3.0 %finish_gradients.1 = (bf16[8192,256]{1,0:T(8,128)(2,1)}, bf16[4096,128]{1,0:T(8,128)(2,1)}, bf16[64,2048]{1,0:T(8,128)(2,1)}) custom-call(s32[1]{0:T(128)} %bitcast.half_ref.side_ref, bf16[2048,256]{1,0:T(8,128)(2,1)S(1)} %constant_dynamic-update-slice_fusion.2.own_a, bf16[2048,256]{1,0:T(8,128)(2,1)S(1)} %constant_dynamic-update-slice_fusion.1.own_b, ...), custom_call_target="tpu_custom_call" | custom-call | tf_op jit(solution)/shard_map/finish_gradients/pallas_call | solution.py:556
  (144 shorter events, 58.0 us)
Async XLA Ops:
  3.9 33.1 %all-to-all-start = ((bf16[8,32,2048]{2,1,0:T(8,128)(2,1)}), bf16[8,32,2048]{2,1,0:T(8,128)(2,1)S(1)}, u32[]{:S(2)}, u32[]{:S(2)}) async-start(bf16[8,32,2048]{2,1,0:T(8,128)(2,1)} %bitcast.100), calls=%async_computation | async-start | bytes 2097152 | tf_op jit(solution)/shard_map/all_to_all | solution.py:672
  37.0 29.5 %all-to-all-start.1 = ((bf16[8,32,2048]{2,1,0:T(8,128)(2,1)}), bf16[8,32,2048]{2,1,0:T(8,128)(2,1)S(1)}, u32[]{:S(2)}, u32[]{:S(2)}) async-start(bf16[8,32,2048]{2,1,0:T(8,128)(2,1)} %bitcast.99), calls=%async_computation.1 | async-start | bytes 2097152 | tf_op jit(solution)/shard_map/all_to_all | solution.py:672
  46.4 5.9 %collective-permute-start = (bf16[4,256,512]{2,1,0:T(8,128)(2,1)}, bf16[4,256,512]{2,1,0:T(8,128)(2,1)S(1)}, u32[]{:S(2)}, u32[]{:S(2)}) collective-permute-start(bf16[4,256,512]{2,1,0:T(8,128)(2,1)} %project_rows.4.after_ref), channel_id=1, source_target_pairs={{0,8},{8,0},{16,24},{24,16},{1,9},{9,1},{17,25},{25,17},{2,10},{10... | collective-permute-start | bytes 3145736 | tf_op jit(solution)/shard_map/ppermute | solution.py:596
  54.8 14.3 %collective-permute-start.1 = (bf16[2,256,512]{2,1,0:T(8,128)(2,1)S(1)}, bf16[2,256,512]{2,1,0:T(8,128)(2,1)S(1)}, u32[]{:S(2)}, u32[]{:S(2)}) collective-permute-start(bf16[2,256,512]{2,1,0:T(8,128)(2,1)S(1)} %get-tuple-element.98), channel_id=1, source_target_pairs={{0,16},{8,24},{16,0},{24,8},{1,17},{9,25},{17,1},{25,9},{2,18},{10... | collective-permute-start | bytes 1572872 | tf_op jit(solution)/shard_map/ppermute | solution.py:596
  75.8 5.9 %collective-permute-start.2 = (bf16[4,256,512]{2,1,0:T(8,128)(2,1)}, bf16[4,256,512]{2,1,0:T(8,128)(2,1)S(1)}, u32[]{:S(2)}, u32[]{:S(2)}) collective-permute-start(bf16[4,256,512]{2,1,0:T(8,128)(2,1)} %project_rows.6.after_ref), channel_id=1, source_target_pairs={{0,8},{8,0},{16,24},{24,16},{1,9},{9,1},{17,25},{25,17},{2,10},{10... | collective-permute-start | bytes 3145736 | tf_op jit(solution)/shard_map/ppermute | solution.py:596
  84.0 21.3 %all-to-all-start.2 = ((bf16[8,2,32,512]{3,2,1,0:T(8,128)(2,1)}), bf16[8,2,32,512]{3,2,1,0:T(8,128)(2,1)S(1)}, u32[]{:S(2)}, u32[]{:S(2)}) async-start(bf16[8,2,32,512]{3,2,1,0:T(8,128)(2,1)} %bitcast.90), calls=%async_computation.2 | async-start | bytes 1048576 | tf_op jit(solution)/shard_map/all_to_all | solution.py:688
  90.1 20.8 %copy-start.19 = (bf16[2048,64]{0,1:T(8,128)(2,1)S(1)}, bf16[2048,64]{0,1:T(8,128)(2,1)}, u32[]{:S(2)}) copy-start(bf16[2048,64]{0,1:T(8,128)(2,1)} %param.14) | copy-start | bytes 786436
  90.2 14.1 %collective-permute-start.3 = (bf16[2,256,512]{2,1,0:T(8,128)(2,1)S(1)}, bf16[2,256,512]{2,1,0:T(8,128)(2,1)S(1)}, u32[]{:S(2)}, u32[]{:S(2)}) collective-permute-start(bf16[2,256,512]{2,1,0:T(8,128)(2,1)S(1)} %add_convert_fusion.3), channel_id=1, source_target_pairs={{0,16},{8,24},{16,0},{24,8},{1,17},{9,25},{17,1},{25,9},{2,18},{10... | collective-permute-start | bytes 1572872 | tf_op jit(solution)/shard_map/ppermute | solution.py:596
  105.3 19.4 %all-to-all-start.3 = ((bf16[8,2,32,512]{3,2,1,0:T(8,128)(2,1)}), bf16[8,2,32,512]{3,2,1,0:T(8,128)(2,1)S(1)}, u32[]{:S(2)}, u32[]{:S(2)}) async-start(bf16[8,2,32,512]{3,2,1,0:T(8,128)(2,1)} %bitcast.89), calls=%async_computation.3 | async-start | bytes 1048576 | tf_op jit(solution)/shard_map/all_to_all | solution.py:688
  126.0 14.6 %all-to-all-start.4 = ((bf16[4,64,1024]{2,1,0:T(8,128)(2,1)}), bf16[4,64,1024]{2,1,0:T(8,128)(2,1)S(1)}, u32[]{:S(2)}, u32[]{:S(2)}) async-start(bf16[4,64,1024]{2,1,0:T(8,128)(2,1)} %bitcast.11), calls=%async_computation.4 | async-start | bytes 1048576 | tf_op jit(solution)/shard_map/all_to_all | solution.py:703
  140.6 24.6 %copy-start.3 = (bf16[4,64,1024]{2,1,0:T(8,128)(2,1)}, bf16[4,64,1024]{2,1,0:T(8,128)(2,1)S(1)}, u32[]{:S(2)}) copy-start(bf16[4,64,1024]{2,1,0:T(8,128)(2,1)S(1)} %all-to-all-done.4.latent_ref) | copy-start | bytes 1572868
  169.4 5.2 %collective-permute-start.4 = (bf16[4096,256]{1,0:T(8,128)(2,1)S(1)}, bf16[4096,256]{1,0:T(8,128)(2,1)}, u32[]{:S(2)}, u32[]{:S(2)}) collective-permute-start(bf16[4096,256]{1,0:T(8,128)(2,1)S(1)} %first_grad.2.after_ref), channel_id=1, source_target_pairs={{0,8},{8,0},{16,24},{24,16},{1,9},{9,1},{17,25},{25,17},{2,10},{10... | collective-permute-start | bytes 6291464 | tf_op jit(solution)/shard_map/ppermute | solution.py:596
  169.8 11.9 %collective-permute-start.7 = (bf16[1280,256]{1,0:T(8,128)(2,1)}, bf16[1280,256]{1,0:T(8,128)(2,1)}, u32[]{:S(2)}, u32[]{:S(2)}) collective-permute-start(bf16[1280,256]{1,0:T(8,128)(2,1)} %get-tuple-element.57), channel_id=1, source_target_pairs={{0,8},{8,0},{16,24},{24,16},{1,9},{9,1},{17,25},{25,17},{2,10},{10... | collective-permute-start | bytes 1966088 | tf_op jit(solution)/shard_map/ppermute | solution.py:596
  177.4 15.7 %collective-permute-start.5 = (bf16[1024,256]{1,0:T(8,128)(2,1)}, bf16[1024,256]{1,0:T(8,128)(2,1)}, u32[]{:S(2)}, u32[]{:S(2)}) collective-permute-start(bf16[1024,256]{1,0:T(8,128)(2,1)} %get-tuple-element.93), channel_id=1, source_target_pairs={{0,16},{8,24},{16,0},{24,8},{1,17},{9,25},{17,1},{25,9},{2,18},{10... | collective-permute-start | bytes 1572872 | tf_op jit(solution)/shard_map/ppermute | solution.py:596
  180.3 14.0 %collective-permute-start.6 = (bf16[1024,256]{1,0:T(8,128)(2,1)}, bf16[1024,256]{1,0:T(8,128)(2,1)}, u32[]{:S(2)}, u32[]{:S(2)}) collective-permute-start(bf16[1024,256]{1,0:T(8,128)(2,1)} %get-tuple-element.91), channel_id=1, source_target_pairs={{0,1},{1,0},{2,3},{3,2},{4,5},{5,4},{6,7},{7,6},{8,9},{9,8},{10,11... | collective-permute-start | bytes 1572872 | tf_op jit(solution)/shard_map/ppermute | solution.py:596
  183.7 9.4 %collective-permute-start.8 = (bf16[640,256]{1,0:T(8,128)(2,1)}, bf16[640,256]{1,0:T(8,128)(2,1)S(1)}, u32[]{:S(2)}, u32[]{:S(2)}) collective-permute-start(bf16[640,256]{1,0:T(8,128)(2,1)} %get-tuple-element.104), channel_id=1, source_target_pairs={{0,2},{1,3},{2,0},{3,1},{4,6},{5,7},{6,4},{7,5},{8,10},{9,11},{10,... | collective-permute-start | bytes 983048 | tf_op jit(solution)/shard_map/ppermute | solution.py:596
  196.3 10.8 %collective-permute-start.10 = (bf16[832,256]{1,0:T(8,128)(2,1)S(1)}, bf16[832,256]{1,0:T(8,128)(2,1)S(1)}, u32[]{:S(2)}, u32[]{:S(2)}) collective-permute-start(bf16[832,256]{1,0:T(8,128)(2,1)S(1)} %pad_maximum_fusion.6), channel_id=1, source_target_pairs={{0,16},{8,24},{16,0},{24,8},{1,17},{9,25},{17,1},{25,9},{2,18},{10... | collective-permute-start | bytes 1277960 | tf_op jit(solution)/shard_map/ppermute | solution.py:596
  197.9 9.2 %collective-permute-start.9 = (bf16[512,256]{1,0:T(8,128)(2,1)S(1)}, bf16[512,256]{1,0:T(8,128)(2,1)S(1)}, u32[]{:S(2)}, u32[]{:S(2)}) collective-permute-start(bf16[512,256]{1,0:T(8,128)(2,1)S(1)} %get-tuple-element.101), channel_id=1, source_target_pairs={{0,1},{1,0},{2,3},{3,2},{4,5},{5,4},{6,7},{7,6},{8,9},{9,8},{10,11... | collective-permute-start | bytes 786440 | tf_op jit(solution)/shard_map/ppermute | solution.py:596
  208.9 6.4 %collective-permute-start.11 = (bf16[512,256]{1,0:T(8,128)(2,1)S(1)}, bf16[512,256]{1,0:T(8,128)(2,1)S(1)}, u32[]{:S(2)}, u32[]{:S(2)}) collective-permute-start(bf16[512,256]{1,0:T(8,128)(2,1)S(1)} %pad_maximum_fusion.13), channel_id=1, source_target_pairs={{0,2},{1,3},{2,0},{3,1},{4,6},{5,7},{6,4},{7,5},{8,10},{9,11},{10,... | collective-permute-start | bytes 786440 | tf_op jit(solution)/shard_map/ppermute | solution.py:596
  209.8 5.6 %collective-permute-start.12 = (bf16[160,256]{1,0:T(8,128)(2,1)S(1)}, bf16[160,256]{1,0:T(8,128)(2,1)S(1)}, u32[]{:S(2)}, u32[]{:S(2)}) collective-permute-start(bf16[160,256]{1,0:T(8,128)(2,1)S(1)} %get-tuple-element.144), channel_id=1, source_target_pairs={{0,1},{1,0},{2,3},{3,2},{4,5},{5,4},{6,7},{7,6},{8,9},{9,8},{10,11... | collective-permute-start | bytes 245768 | tf_op jit(solution)/shard_map/ppermute | solution.py:596
  215.5 11.4 %collective-permute-start.13 = (bf16[336,256]{1,0:T(8,128)(2,1)S(1)}, bf16[336,256]{1,0:T(8,128)(2,1)S(1)}, u32[]{:S(2)}, u32[]{:S(2)}) collective-permute-start(bf16[336,256]{1,0:T(8,128)(2,1)S(1)} %pad_maximum_fusion.14), channel_id=1, source_target_pairs={{0,4},{1,5},{2,6},{3,7},{4,0},{5,1},{6,2},{7,3},{8,12},{9,13},{10,... | collective-permute-start | bytes 516104 | tf_op jit(solution)/shard_map/ppermute | solution.py:596
  227.1 6.8 %collective-permute-start.14 = (bf16[336,256]{1,0:T(8,128)(2,1)S(1)}, bf16[336,256]{1,0:T(8,128)(2,1)S(1)}, u32[]{:S(2)}, u32[]{:S(2)}) collective-permute-start(bf16[336,256]{1,0:T(8,128)(2,1)S(1)} %pad_maximum_fusion.15), channel_id=1, source_target_pairs={{0,4},{1,5},{2,6},{3,7},{4,0},{5,1},{6,2},{7,3},{8,12},{9,13},{10,... | collective-permute-start | bytes 516104 | tf_op jit(solution)/shard_map/ppermute | solution.py:596
  234.0 6.4 %collective-permute-start.15 = (bf16[512,256]{1,0:T(8,128)(2,1)S(1)}, bf16[512,256]{1,0:T(8,128)(2,1)S(1)}, u32[]{:S(2)}, u32[]{:S(2)}) collective-permute-start(bf16[512,256]{1,0:T(8,128)(2,1)S(1)} %get-tuple-element.155), channel_id=1, source_target_pairs={{0,2},{1,3},{2,0},{3,1},{4,6},{5,7},{6,4},{7,5},{8,10},{9,11},{10,... | collective-permute-start | bytes 786440 | tf_op jit(solution)/shard_map/ppermute | solution.py:596
  234.0 5.3 %collective-permute-start.16 = (bf16[160,256]{1,0:T(8,128)(2,1)S(1)}, bf16[160,256]{1,0:T(8,128)(2,1)S(1)}, u32[]{:S(2)}, u32[]{:S(2)}) collective-permute-start(bf16[160,256]{1,0:T(8,128)(2,1)S(1)} %slice_dynamic-update-slice_fusion.6), channel_id=1, source_target_pairs={{0,1},{1,0},{2,3},{3,2},{4,5},{5,4},{6,7},{7,6},{8,9},{9,8},{10,11... | collective-permute-start | bytes 245768 | tf_op jit(solution)/shard_map/ppermute | solution.py:596
  240.4 6.4 %collective-permute-start.17 = (bf16[512,256]{1,0:T(8,128)(2,1)S(1)}, bf16[512,256]{1,0:T(8,128)(2,1)S(1)}, u32[]{:S(2)}, u32[]{:S(2)}) collective-permute-start(bf16[512,256]{1,0:T(8,128)(2,1)S(1)} %get-tuple-element.78), channel_id=1, source_target_pairs={{0,1},{1,0},{2,3},{3,2},{4,5},{5,4},{6,7},{7,6},{8,9},{9,8},{10,11... | collective-permute-start | bytes 786440 | tf_op jit(solution)/shard_map/ppermute | solution.py:596
  241.5 9.7 %collective-permute-start.18 = (bf16[832,256]{1,0:T(8,128)(2,1)S(1)}, bf16[832,256]{1,0:T(8,128)(2,1)S(1)}, u32[]{:S(2)}, u32[]{:S(2)}) collective-permute-start(bf16[832,256]{1,0:T(8,128)(2,1)S(1)} %pad_maximum_fusion.7), channel_id=1, source_target_pairs={{0,16},{8,24},{16,0},{24,8},{1,17},{9,25},{17,1},{25,9},{2,18},{10... | collective-permute-start | bytes 1277960 | tf_op jit(solution)/shard_map/ppermute | solution.py:596
  251.3 7.1 %collective-permute-start.21 = (bf16[640,256]{1,0:T(8,128)(2,1)S(1)}, bf16[640,256]{1,0:T(8,128)(2,1)S(1)}, u32[]{:S(2)}, u32[]{:S(2)}) collective-permute-start(bf16[640,256]{1,0:T(8,128)(2,1)S(1)} %slice_dynamic-update-slice_fusion.1), channel_id=1, source_target_pairs={{0,2},{1,3},{2,0},{3,1},{4,6},{5,7},{6,4},{7,5},{8,10},{9,11},{10,... | collective-permute-start | bytes 983048 | tf_op jit(solution)/shard_map/ppermute | solution.py:596
  252.0 11.5 %collective-permute-start.19 = (bf16[1024,256]{1,0:T(8,128)(2,1)S(1)}, bf16[1024,256]{1,0:T(8,128)(2,1)S(1)}, u32[]{:S(2)}, u32[]{:S(2)}) collective-permute-start(bf16[1024,256]{1,0:T(8,128)(2,1)S(1)} %constant_dynamic-update-slice_fusion.3), channel_id=1, source_target_pairs={{0,16},{8,24},{16,0},{24,8},{1,17},{9,25},{17,1},{25,9},{2,18},{10... | collective-permute-start | bytes 1572872 | tf_op jit(solution)/shard_map/ppermute | solution.py:596
  253.8 11.2 %collective-permute-start.20 = (bf16[1024,256]{1,0:T(8,128)(2,1)S(1)}, bf16[1024,256]{1,0:T(8,128)(2,1)S(1)}, u32[]{:S(2)}, u32[]{:S(2)}) collective-permute-start(bf16[1024,256]{1,0:T(8,128)(2,1)S(1)} %slice_dynamic-update-slice_fusion), channel_id=1, source_target_pairs={{0,1},{1,0},{2,3},{3,2},{4,5},{5,4},{6,7},{7,6},{8,9},{9,8},{10,11... | collective-permute-start | bytes 1572872 | tf_op jit(solution)/shard_map/ppermute | solution.py:596
  265.0 5.2 %collective-permute-start.22 = (bf16[2048,256]{1,0:T(8,128)(2,1)S(1)}, bf16[2048,256]{1,0:T(8,128)(2,1)S(1)}, u32[]{:S(2)}, u32[]{:S(2)}) collective-permute-start(bf16[2048,256]{1,0:T(8,128)(2,1)S(1)} %constant_dynamic-update-slice_fusion.2.own_a), channel_id=1, source_target_pairs={{0,8},{8,0},{16,24},{24,16},{1,9},{9,1},{17,25},{25,17},{2,10},{10... | collective-permute-start | bytes 3145736 | tf_op jit(solution)/shard_map/ppermute | solution.py:596
  265.1 5.1 %collective-permute-start.23 = (bf16[2048,256]{1,0:T(8,128)(2,1)S(1)}, bf16[2048,256]{1,0:T(8,128)(2,1)S(1)}, u32[]{:S(2)}, u32[]{:S(2)}) collective-permute-start(bf16[2048,256]{1,0:T(8,128)(2,1)S(1)} %constant_dynamic-update-slice_fusion.1.own_b), channel_id=1, source_target_pairs={{0,8},{8,0},{16,24},{24,16},{1,9},{9,1},{17,25},{25,17},{2,10},{10... | collective-permute-start | bytes 3145736 | tf_op jit(solution)/shard_map/ppermute | solution.py:596
  265.6 4.6 %collective-permute-start.24 = (bf16[1280,256]{1,0:T(8,128)(2,1)S(1)}, bf16[1280,256]{1,0:T(8,128)(2,1)S(1)}, u32[]{:S(2)}, u32[]{:S(2)}) collective-permute-start(bf16[1280,256]{1,0:T(8,128)(2,1)S(1)} %constant_dynamic-update-slice_fusion.own_c), channel_id=1, source_target_pairs={{0,8},{8,0},{16,24},{24,16},{1,9},{9,1},{17,25},{25,17},{2,10},{10... | collective-permute-start | bytes 1966088 | tf_op jit(solution)/shard_map/ppermute | solution.py:596
  (19 other events, 79.6 us)

commit v4 on v3

--- a/solution.py
+++ b/solution.py
@@ -173,7 +173,7 @@
     return jnp.concatenate(pieces, axis=0)
 
 
-def second_part(count, side_ref, act_ref, slope_ref, w_ref, grad_two_ref, third_ref, grad_one, kept_ref, sent_ref, adj, total_two):
+def backward_part(count, side_ref, latent_ref, act_ref, slope_ref, w_ref, grad_two_ref, third_ref, grad_one, kept_ref, sent_ref, adj, total_one, total_two):
     side = side_ref[0]
 
     def put(half, rows, values):
@@ -217,45 +217,38 @@
     for row in range(height):
         upstream = adj[row].astype(jnp.bfloat16).astype(jnp.float32)
         grad_one[row] = (upstream * slope_ref[row]).astype(jnp.bfloat16)
+    in_chan = latent_ref.shape[0] * latent_ref.shape[2] // (H0 * W0)
+    tail = 8 * in_chan
     lanes = 2 * out_chan
     for parity in (0, 1):
         for which in (0, 1):
             for pair in (0, 1):
-                rows = pl.ds((2 * which + pair) * mid_chan, mid_chan)
+                rows = pl.ds(tail + (2 * which + pair) * mid_chan, mid_chan)
                 above, left_edge = which * mid_chan, pair * lanes
                 put(
                     parity,
                     rows,
                     lambda: total_two[parity, above:above + mid_chan, left_edge:left_edge + lanes],
                 )
-        put(parity, pl.ds(4 * mid_chan, third_ref.shape[1]), lambda: third_ref[parity])
-
-
-def first_kernel(count, half_ref, latent_ref, grad_one, out_ref, total_one):
-    in_chan = latent_ref.shape[0] * latent_ref.shape[2] // (H0 * W0)
-    mid_chan = grad_one.shape[2]
-    for half in (0, 1):
-
-        @pl.when(half_ref[0] == half)
-        def _(half=half):
-            for row_tap in (2 * half, 2 * half + 1):
-                parity = 0 if row_tap in ROW_TAPS[0] else 1
-                shift = ROW_SHIFT[parity] if ROW_TAPS[parity][1] == row_tap else 0
-                rows = [row for row in range(H0) if 0 <= row + shift < H0]
-                lefts = [latent_row(latent_ref, row + shift) for row in rows]
-                rights = [side_taps(grad_one, 2 * row + parity, count, W0) for row in rows]
-                left = jnp.concatenate(lefts, axis=0) if len(lefts) > 1 else lefts[0]
-                right = jnp.concatenate(rights, axis=0) if len(rights) > 1 else rights[0]
-                total_one[...] = product_tn(left, right)
-                for slot, col_tap in enumerate(COL_TAPS):
-                    to = pl.ds(((row_tap % 2) * 4 + col_tap) * in_chan, in_chan)
-                    out_ref[to, :] = total_one[:, slot * mid_chan:(slot + 1) * mid_chan].astype(jnp.bfloat16)
+        put(parity, pl.ds(tail + 4 * mid_chan, third_ref.shape[1]), lambda: third_ref[parity])
+    for row_tap in range(4):
+        parity = 0 if row_tap in ROW_TAPS[0] else 1
+        shift = ROW_SHIFT[parity] if ROW_TAPS[parity][1] == row_tap else 0
+        rows = [row for row in range(H0) if 0 <= row + shift < H0]
+        lefts = [latent_row(latent_ref, row + shift) for row in rows]
+        rights = [side_taps(grad_one, 2 * row + parity, count, W0) for row in rows]
+        left = jnp.concatenate(lefts, axis=0) if len(lefts) > 1 else lefts[0]
+        right = jnp.concatenate(rights, axis=0) if len(rights) > 1 else rights[0]
+        total_one[...] = product_tn(left, right)
+        for slot, col_tap in enumerate(COL_TAPS):
+            to = pl.ds(((row_tap % 2) * 4 + col_tap) * in_chan, in_chan)
+            put(row_tap // 2, to, lambda: total_one[:, slot * mid_chan:(slot + 1) * mid_chan])
 
 
 def decoder_kernel(
     count, side_ref, latent_ref, w_one_ref, w_two_ref, w_three_ref, target_ref,
-    decoded_ref, grad_one_ref, kept_ref, sent_ref,
-    act_one, slope_one, act_two, slope_two, grad_two, kgrad_three, tmp_one, tmp_two, tmp_three, grads, adj_two, adj_one, total_two,
+    decoded_ref, kept_ref, sent_ref,
+    grad_one, act_one, slope_one, act_two, slope_two, grad_two, kgrad_three, tmp_one, tmp_two, tmp_three, grads, adj_two, adj_one, total_one, total_two,
 ):
     step = pl.program_id(0)
     steps = pl.num_programs(0)
@@ -270,8 +263,9 @@
 
     @pl.when(step == steps - 1)
     def _():
-        second_part(
-            count, side_ref, act_one, slope_one, w_two_ref, grad_two, kgrad_three, grad_one_ref, kept_ref, sent_ref, adj_one, total_two
+        backward_part(
+            count, side_ref, latent_ref, act_one, slope_one, w_two_ref, grad_two, kgrad_three,
+            grad_one, kept_ref, sent_ref, adj_one, total_one, total_two,
         )
 
 
@@ -294,7 +288,8 @@
     act_one = (height, breadth * count, mid_chan)
     act_two = (2 * height, flat, out_chan)
     padded = (2 * height + 2, flat, out_chan)
-    tail = (4 * mid_chan + third_rows, mid_chan)
+    in_chan = w_one.shape[0] // 16
+    share = (8 * in_chan + 4 * mid_chan + third_rows, mid_chan)
     single = pl.Buffered(1)
     return pl.pallas_call(
         functools.partial(decoder_kernel, count),
@@ -310,17 +305,16 @@
         ],
         out_specs=(
             pl.BlockSpec((2, flat, lanes), lambda step: (step, 0, 0)),
-            whole(act_one),
-            whole(tail),
-            whole(tail),
+            whole(share),
+            whole(share),
         ),
         out_shape=(
             jax.ShapeDtypeStruct(target.shape, jnp.bfloat16),
-            jax.ShapeDtypeStruct(act_one, jnp.bfloat16),
-            jax.ShapeDtypeStruct(tail, jnp.bfloat16),
-            jax.ShapeDtypeStruct(tail, jnp.bfloat16),
+            jax.ShapeDtypeStruct(share, jnp.bfloat16),
+            jax.ShapeDtypeStruct(share, jnp.bfloat16),
         ),
         scratch_shapes=[
+            pltpu.VMEM(act_one, jnp.bfloat16),
             pltpu.VMEM(act_one, jnp.bfloat16),
             pltpu.VMEM(act_one, jnp.float32),
             pltpu.VMEM(padded, jnp.bfloat16),
@@ -333,33 +327,11 @@
             pltpu.VMEM((flat + 2 * count, lanes), jnp.float32),
             pltpu.VMEM(padded, jnp.float32),
             pltpu.VMEM(act_one, jnp.float32),
+            pltpu.VMEM((in_chan, 4 * mid_chan), jnp.float32),
             pltpu.VMEM(w_two.shape, jnp.float32),
         ],
-        compiler_params=params(52, True),
+        compiler_params=params(60, True),
     )(side, latent, w_one, w_two, w_three, target)
-
-
-def first_grad(half, latent, grad_one, after):
-    count = latent.shape[1]
-    in_chan = latent.shape[0] * latent.shape[2] // (H0 * W0)
-    mid_chan = grad_one.shape[2]
-    vmem = pl.BlockSpec(memory_space=pltpu.VMEM)
-
-    def kernel(half_ref, latent_ref, grad_ref, after_ref, out_ref, total_one):
-        first_kernel(count, half_ref, latent_ref, grad_ref, out_ref, total_one)
-
-    return pl.pallas_call(
-        kernel,
-        name="first_grad",
-        in_specs=[pl.BlockSpec(memory_space=pltpu.SMEM), vmem, vmem, pl.BlockSpec(memory_space=pl.ANY)],
-        out_specs=vmem,
-        out_shape=jax.ShapeDtypeStruct((8 * in_chan, mid_chan), jnp.bfloat16),
-        scratch_shapes=[pltpu.VMEM((in_chan, 4 * mid_chan), jnp.float32)],
-        compiler_params=params(24),
-        cost_estimate=pl.CostEstimate(
-            flops=64 * count * in_chan * mid_chan, bytes_accessed=16 * in_chan * mid_chan, transcendentals=0
-        ),
-    )(half, latent, grad_one, after)
 
 
 def spatial_first_kernel(grid_ref, after_ref, rows_ref, tmp):
@@ -465,41 +437,44 @@
     )(subject.reshape(1, samples), voxel_count, shift, fmri, after)
 
 
-def project_kernel(half_ref, rows_ref, map_ref, after_ref, out_ref):
+def project_kernel(quarter_ref, rows_ref, map_ref, *after_and_out):
+    out_ref = after_and_out[-1]
     width = out_ref.shape[2]
     for block in range(out_ref.shape[0]):
         value = product(rows_ref[...], map_ref[0, :, block * width:(block + 1) * width])
         out_ref[block] = value.astype(jnp.bfloat16)
 
 
-def projected(rows, maps, half, after):
+def projected(rows, maps, part, after, parts):
     count, voxels = rows.shape
-    blocks = H0 * W0 // 2
-    width = maps.shape[2] // (2 * blocks)
+    blocks = H0 * W0 // parts
+    width = maps.shape[2] // (H0 * W0)
+    step_blocks = max(1, blocks // 2)
+    steps = blocks // step_blocks
     return pl.pallas_call(
         project_kernel,
         name="project_rows",
         grid_spec=pltpu.PrefetchScalarGridSpec(
             num_scalar_prefetch=1,
-            grid=(blocks // 2,),
+            grid=(steps,),
             in_specs=[
-                pl.BlockSpec((count, voxels), lambda step, half: (0, 0)),
-                pl.BlockSpec((1, voxels, 2 * width), lambda step, half: (0, 0, half[0] * (blocks // 2) + step)),
-                pl.BlockSpec(memory_space=pl.ANY),
-            ],
-            out_specs=pl.BlockSpec((2, count, width), lambda step, half: (step, 0, 0)),
+                pl.BlockSpec((count, voxels), lambda step, part: (0, 0)),
+                pl.BlockSpec((1, voxels, step_blocks * width), lambda step, part: (0, 0, part[0] * steps + step)),
+            ] + [pl.BlockSpec(memory_space=pl.ANY)] * len(after),
+            out_specs=pl.BlockSpec((step_blocks, count, width), lambda step, part: (step, 0, 0)),
         ),
         out_shape=jax.ShapeDtypeStruct((blocks, count, width), jnp.bfloat16),
         compiler_params=params(60, True),
         cost_estimate=pl.CostEstimate(
-            flops=count * voxels * maps.shape[2],
-            bytes_accessed=voxels * maps.shape[2],
+            flops=2 * count * voxels * maps.shape[2] // parts,
+            bytes_accessed=2 * voxels * maps.shape[2] // parts,
             transcendentals=0,
         ),
-    )(half, rows, maps, after)
-
-
-def collect_kernel(place_a_ref, place_b_ref, first_ref, second_ref, out_ref):
+    )(part, rows, maps, *after)
+
+
+def collect_kernel(place_a_ref, place_b_ref, first_ref, second_ref, *after_and_out):
+    out_ref = after_and_out[-1]
     subjects, blocks, room, width = first_ref.shape
     for block in range(blocks):
         value = None
@@ -510,14 +485,17 @@
         out_ref[:, pl.ds(block * width, width)] = value.astype(jnp.bfloat16)
 
 
-def collected(places, first, second):
+def collected(places, first, second, after):
     samples = places[0].shape[1]
+    vmem = pl.BlockSpec(memory_space=pltpu.VMEM)
     return pl.pallas_call(
         collect_kernel,
         name="collect_rows",
+        in_specs=[vmem] * 4 + [pl.BlockSpec(memory_space=pl.ANY)] * len(after),
+        out_specs=vmem,
         out_shape=jax.ShapeDtypeStruct((samples, first.shape[1] * first.shape[3]), jnp.bfloat16),
         compiler_params=params(16),
-    )(*places, first, second)
+    )(*places, first, second, *after)
 
 
 def finish_kernel(third_rows, side_ref, own_a, own_b, own_c, other_a, other_b, other_c, first_ref, second_ref, third_ref):
@@ -608,8 +586,11 @@
     place = place_of(step)
 
     def part(terms, which):
-        size = terms[0].shape[0] // ways
-        return summed([lax.dynamic_slice_in_dim(term, which * size, size, 0) for term in terms])
+        cuts = []
+        for term in terms:
+            array, start, size = term if isinstance(term, tuple) else (term, 0, term.shape[0])
+            cuts.append(lax.dynamic_slice_in_dim(array, start + which * (size // ways), size // ways, 0))
+        return summed(cuts)
 
     arrived = []
     for change in range(1, ways):
@@ -619,7 +600,7 @@
     result = []
     start = 0
     for terms in chains:
-        size = terms[0].shape[0] // ways
+        size = (terms[0][2] if isinstance(terms[0], tuple) else terms[0].shape[0]) // ways
         result.append([part(terms, place)] + [values[start:start + size] for values in arrived])
         start += size
     return result
@@ -671,13 +652,25 @@
         sent = rows.reshape(dp_count, room, rows.shape[1])
         return lax.all_to_all(sent, "dp", split_axis=0, concat_axis=0, tiled=True).reshape(rows.shape)
 
-    def core_summed(rows, after):
-        sent = projected(rows, ridge_maps, 1 - side, after)
-        received = exchanged(sent, vox_bits[:1], 1)
-        return [projected(rows, ridge_maps, side, sent), received]
-
-    def vox_summed(terms):
-        for hop in vox_bits[1:]:
+    core_bit, cross_bit = upper(vox_bits[0]), upper(vox_bits[1])
+
+    def part_of(*bits):
+        return sum(bit * 2 ** at for at, bit in enumerate(bits[::-1])).astype(jnp.int32).reshape(1)
+
+    def to_cross(rows, *after):
+        for_core = projected(rows, ridge_maps, part_of(1 - core_bit), after, 2)
+        received = exchanged(for_core, vox_bits[:1], 1)
+        own = projected(rows, ridge_maps, part_of(core_bit, 1 - cross_bit), (for_core,), 4)
+        half = received.shape[0] // 2
+        added = lax.dynamic_slice_in_dim(received, (1 - cross_bit) * half, half, 0)
+        return summed([own, added]).astype(jnp.bfloat16), lax.dynamic_slice_in_dim(received, cross_bit * half, half, 0)
+
+    def own_part(rows, *after):
+        return projected(rows, ridge_maps, part_of(core_bit, cross_bit), after, 4)
+
+    def rest_summed(*terms):
+        terms = list(terms)
+        for hop in vox_bits[2:]:
             terms, = shared([terms], [hop])
         return terms
 
@@ -689,31 +682,34 @@
 
     first = routed(first)
     second = routed(second)
-    terms_first = vox_summed(core_summed(first, voxel_count))
-    terms_second = core_summed(second, terms_first[1])
-    core_second = terms_second[1]
+    across_first, added_first = to_cross(first, voxel_count)
+    arrived_first = exchanged(across_first, vox_bits[1:2], 1)
+    own_first = own_part(first, across_first)
+    across_second, added_second = to_cross(second, arrived_first, own_first)
+    arrived_second = exchanged(across_second, vox_bits[1:2], 1)
+    own_second = own_part(second, across_second)
+    terms_first = rest_summed(own_first, added_first, arrived_first)
     pair_two = paired_weight(w_second, mid_chan)
     pair_three = paired_weight(w_third, last_chan)
-    target_rows = spatial_first(target, core_second)
-    terms_first, terms_second = lax.optimization_barrier((terms_first, terms_second))
-    terms_second = vox_summed(terms_second)
+    target_rows = spatial_first(target, across_second)
     places = (place_first, place_second)
-    own_rows = collected(places, returned(terms_first), returned(terms_second))
+    back_first = returned(terms_first)
+    back_first, arrived_second = lax.optimization_barrier((back_first, arrived_second))
+    back_second = returned(rest_summed(own_second, added_second, arrived_second))
+    own_rows = collected(places, back_first, back_second, (target_rows, pair_two, pair_three))
     own_rows = own_rows.reshape(holders, samp_dev // holders, own_rows.shape[1])
     latent = lax.all_to_all(own_rows, "vox", split_axis=0, concat_axis=0, tiled=True)
     count = latent.shape[1]
-    decoded_rows, grad_one, kept_tail, sent_tail = decoder(side, latent, w_first, pair_two, pair_three, target_rows)
-    parts_tail = [kept_tail, exchanged(sent_tail, vox_bits[:1], 1)]
-    sent = first_grad(1 - side, latent, grad_one, grad_one)
-    received = exchanged(sent, vox_bits[:1], 1)
-    kept = first_grad(side, latent, grad_one, sent)
+    decoded_rows, kept, sent = decoder(side, latent, w_first, pair_two, pair_three, target_rows)
     third_rows = pair_three.shape[1]
     quarter = w_first.shape[0] // 4
+    received = exchanged(sent, vox_bits[:1], 1)
     across = [[hop] for hop in vox_bits[1:]]
     near = [dp_bits[:1]]
     along = [[hop] for hop in dp_bits[1:]]
     routes = (across + near + along, near + across + along, along[:1] + across + near + along[1:])
-    parts = [[kept[:quarter], received[:quarter]], [kept[quarter:], received[quarter:]], parts_tail]
+    cuts = ((0, quarter), (quarter, quarter), (2 * quarter, kept.shape[0] - 2 * quarter))
+    parts = [[(kept, *cut), (received, *cut)] for cut in cuts]
     decoded = sample_first(decoded_rows, count, w_third.shape[1], received)
     for stage in range(len(routes[0])):
         parts = over_chains(shared, parts, [route[stage] for route in routes])

time: 274 us -> 267 us (0.974)
  blocking collectives: 0 us -> 11.9 us
  waiting for transfers between devices: 123 us -> 112 us
  starting transfers between devices: 44.3 us -> 36.3 us
  Pallas kernels: 70.1 us -> 75.9 us
  local copies, waits for them, and re-layouts: 19 us -> 14.1 us
    all_to_all x0 -> x1, blocking collectives: none -> 11.9 us  [shards(): lax.all_to_all(own_rows, 'vox', split_axis=0, concat_axis=0, tiled=True)]
    ppermute x25 -> x24, waiting for transfers between devices: 79 us -> 72.4 us  [exchanged(): lax.ppermute(values, axis, [(at, at ^ flip) for at in range(lax.axis_size...]
    pallas_call x1, Pallas kernels: 24.6 us -> 29.1 us  [decoder(): pl.pallas_call(functools.partial(decoder_kernel, count), name='decoder',...]
    pallas_call x4 -> x6, Pallas kernels: 23.5 us -> 27.9 us  [projected(): pl.pallas_call(project_kernel, name='project_rows', grid_spec=pltpu.Prefe...]
    all_to_all x2, waiting for transfers between devices: 11.5 us -> 7.33 us  [returned(): return lax.all_to_all(sent, 'dp', split_axis=0, concat_axis=0, tiled=True)]
    all_to_all x1 -> x0, starting transfers between devices: 3.65 us -> none  [shards(): lax.all_to_all(own_rows, 'vox', split_axis=0, concat_axis=0, tiled=True)]
    ppermute x25 -> x24, starting transfers between devices: 18.1 us -> 14.5 us  [exchanged(): lax.ppermute(values, axis, [(at, at ^ flip) for at in range(lax.axis_size...]
    pallas_call x3 -> x1, Pallas kernels: 3.52 us -> 0.46 us  [collected(): pl.pallas_call(collect_kernel, name='collect_rows', in_specs=[vmem] * 4 +...]
  transfers between devices with their start and end apart: 30 -> 28, of which waited for: 20 -> 21; matrix products, arithmetic and copies ran while one was open for 5% -> 3% of each run, Pallas kernels for 11% -> 13%
where the time goes in v4:
time: 267 us; the launch traced here: 266 us
  waiting for transfers between devices  112 us (42%)
  Pallas kernels  75.9 us (28%)
  starting transfers between devices  36.3 us (14%)
  other arithmetic  15.1 us (6%)
  local copies, waits for them, and re-layouts  14.1 us (5%)
  blocking collectives  11.9 us (4%)
    ppermute x24, waiting for transfers between devices, exchanged(): lax.ppermute(values, axis, [(at, at ^ flip) for at in range(lax.axis_size...  72.4 us
    all_to_all x2, waiting for transfers between devices, routed(): lax.all_to_all(sent, 'dp', split_axis=0, concat_axis=0, tiled=True)  31.8 us
    pallas_call x1, Pallas kernels, decoder(): pl.pallas_call(functools.partial(decoder_kernel, count), name='decoder',...  29.1 us
    pallas_call x6, Pallas kernels, projected(): pl.pallas_call(project_kernel, name='project_rows', grid_spec=pltpu.Prefe...  27.9 us
    ppermute x24, starting transfers between devices, exchanged(): lax.ppermute(values, axis, [(at, at ^ flip) for at in range(lax.axis_size...  14.5 us
    unnamed x39, local copies, waits for them, and re-layouts  12 us
    all_to_all x1, blocking collectives, shards(): lax.all_to_all(own_rows, 'vox', split_axis=0, concat_axis=0, tiled=True)  11.9 us
    all_to_all x2, starting transfers between devices, routed(): lax.all_to_all(sent, 'dp', split_axis=0, concat_axis=0, tiled=True)  10.9 us
  transfers between devices with their start and end apart: 28, of which 21 were waited for; matrix products, arithmetic and copies ran while one was open for 3% of the time, Pallas kernels for 13%

profile of v4, /device:TPU:0, one launch (start us, length us, event | category | flops | bytes accessed | tf_op | source)
XLA Modules:
  0.0 266.1 jit_solution(2679089551842371723)
XLA Ops:
  0.6 3.3 %bucket_rows.2 = (bf16[256,2048]{1,0:T(8,128)(2,1)}, bf16[256,256]{1,0:T(8,128)(2,1)}) custom-call(s32[1,256]{1,0:T(1,128)} %bitcast.107, s32[8]{0:T(128)} %after_and_out_0_.1, s32[1]{0:T(128)} %bitcast.2.shift_ref, bf16[256,2048]{1,0:T(8,128)(2,1)} %fmri_ref.3, s32[8]{0:T(128)} %after_and_out_0_.1), custom_call_target="tpu_custom_call" | custom-call | tf_op jit(solution)/shard_map/bucket_rows/pallas_call | solution.py:427
  3.9 7.3 %all-to-all-start = ((bf16[8,32,2048]{2,1,0:T(8,128)(2,1)}), bf16[8,32,2048]{2,1,0:T(8,128)(2,1)S(1)}, u32[]{:S(2)}, u32[]{:S(2)}) async-start(bf16[8,32,2048]{2,1,0:T(8,128)(2,1)} %bitcast.106), calls=%async_computation | async-start | bytes 2097152 | tf_op jit(solution)/shard_map/all_to_all | solution.py:653
  14.5 22.5 %all-to-all-done = bf16[8,32,2048]{2,1,0:T(8,128)(2,1)S(1)} async-done(((bf16[8,32,2048]{2,1,0:T(8,128)(2,1)}), bf16[8,32,2048]{2,1,0:T(8,128)(2,1)S(1)}, u32[]{:S(2)}, u32[]{:S(2)}) %all-to-all-start) | async-done | bytes 1048608 | tf_op jit(solution)/shard_map/all_to_all | solution.py:653
  37.0 3.6 %all-to-all-start.2 = ((bf16[8,32,2048]{2,1,0:T(8,128)(2,1)}), bf16[8,32,2048]{2,1,0:T(8,128)(2,1)S(1)}, u32[]{:S(2)}, u32[]{:S(2)}) async-start(bf16[8,32,2048]{2,1,0:T(8,128)(2,1)} %bitcast.105), calls=%async_computation.2 | async-start | bytes 2097152 | tf_op jit(solution)/shard_map/all_to_all | solution.py:653
  40.6 5.9 %project_rows.6.after_and_out_0_ = bf16[4,256,512]{2,1,0:T(8,128)(2,1)} custom-call(s32[1]{0:T(128)} %bitcast.7.quarter_ref, bf16[256,2048]{1,0:T(8,128)(2,1)} %bitcast.98, bf16[1,2048,4096]{2,1,0:T(8,128)(2,1)} %map_ref.11, s32[8]{0:T(128)} %after_and_out_0_.1), custom_call_target="tpu_custom_call" | custom-call | flops 2147483648 | bytes 8388608 | tf_op jit(solution)/shard_map/project_rows/pallas_call | solution.py:454
  46.4 4.0 %project_rows.7 = bf16[2,256,512]{2,1,0:T(8,128)(2,1)} custom-call(s32[1]{0:T(128)} %bitcast.6.quarter_ref, bf16[256,2048]{1,0:T(8,128)(2,1)} %bitcast.99, bf16[1,2048,4096]{2,1,0:T(8,128)(2,1)} %map_ref.11, bf16[4,256,512]{2,1,0:T(8,128)(2,1)} %project_rows.6.after_and_out_0_), custom_call_target="tpu_custom_call" | custom-call | flops 1073741824 | bytes 4194304 | tf_op jit(solution)/shard_map/project_rows/pallas_call | solution.py:454
  53.2 4.0 %project_rows.8.after_and_out_1_ = bf16[2,256,512]{2,1,0:T(8,128)(2,1)} custom-call(s32[1]{0:T(128)} %bitcast.3.quarter_ref, bf16[256,2048]{1,0:T(8,128)(2,1)} %bitcast.100, bf16[1,2048,4096]{2,1,0:T(8,128)(2,1)} %map_ref.11, bf16[2,256,512]{2,1,0:T(8,128)(2,1)} %copy-done.16), custom_call_target="tpu_custom_call" | custom-call | flops 1073741824 | bytes 4194304 | tf_op jit(solution)/shard_map/project_rows/pallas_call | solution.py:454
  57.2 9.3 %all-to-all-done.2 = bf16[8,32,2048]{2,1,0:T(8,128)(2,1)S(1)} async-done(((bf16[8,32,2048]{2,1,0:T(8,128)(2,1)}), bf16[8,32,2048]{2,1,0:T(8,128)(2,1)S(1)}, u32[]{:S(2)}, u32[]{:S(2)}) %all-to-all-start.2) | async-done | bytes 1048608 | tf_op jit(solution)/shard_map/all_to_all | solution.py:653
  67.7 5.9 %project_rows.9.after_and_out_0_ = bf16[4,256,512]{2,1,0:T(8,128)(2,1)} custom-call(s32[1]{0:T(128)} %bitcast.7.quarter_ref, bf16[256,2048]{1,0:T(8,128)(2,1)} %bitcast.95, bf16[1,2048,4096]{2,1,0:T(8,128)(2,1)} %map_ref.11, bf16[2,256,512]{2,1,0:T(8,128)(2,1)} %copy-done.15, bf16[2,256,512]{2,1,0:T(8,128)(2,1)} %project_rows.8.after_and_out_1_), custom_call_target="tpu_custom_call" | custom-call | flops 2147483648 | bytes 8388608 | tf_op jit(solution)/shard_map/project_rows/pallas_call | solution.py:454
  75.6 5.2 %all-to-all-start.1 = ((bf16[8,2,32,512]{3,2,1,0:T(8,128)(2,1)}), bf16[8,2,32,512]{3,2,1,0:T(8,128)(2,1)S(1)}, u32[]{:S(2)}, u32[]{:S(2)}) async-start(bf16[8,2,32,512]{3,2,1,0:T(8,128)(2,1)} %bitcast.93), calls=%async_computation.1 | async-start | bytes 1048576 | tf_op jit(solution)/shard_map/all_to_all | solution.py:681
  80.8 4.1 %project_rows.10 = bf16[2,256,512]{2,1,0:T(8,128)(2,1)} custom-call(s32[1]{0:T(128)} %bitcast.6.quarter_ref, bf16[256,2048]{1,0:T(8,128)(2,1)} %bitcast.96, bf16[1,2048,4096]{2,1,0:T(8,128)(2,1)} %map_ref.11, bf16[4,256,512]{2,1,0:T(8,128)(2,1)} %project_rows.9.after_and_out_0_), custom_call_target="tpu_custom_call" | custom-call | flops 1073741824 | bytes 4194304 | tf_op jit(solution)/shard_map/project_rows/pallas_call | solution.py:454
  88.1 4.0 %project_rows.11 = bf16[2,256,512]{2,1,0:T(8,128)(2,1)} custom-call(s32[1]{0:T(128)} %bitcast.3.quarter_ref, bf16[256,2048]{1,0:T(8,128)(2,1)} %bitcast.97, bf16[1,2048,4096]{2,1,0:T(8,128)(2,1)} %map_ref.11, bf16[2,256,512]{2,1,0:T(8,128)(2,1)} %copy-done.4), custom_call_target="tpu_custom_call" | custom-call | flops 1073741824 | bytes 4194304 | tf_op jit(solution)/shard_map/project_rows/pallas_call | solution.py:454
  92.1 3.8 %all-to-all-done.1.first_ref = bf16[8,2,32,512]{3,2,1,0:T(8,128)(2,1)S(1)} async-done(((bf16[8,2,32,512]{3,2,1,0:T(8,128)(2,1)}), bf16[8,2,32,512]{3,2,1,0:T(8,128)(2,1)S(1)}, u32[]{:S(2)}, u32[]{:S(2)}) %all-to-all-start.1) | async-done | bytes 524320 | tf_op jit(solution)/shard_map/all_to_all | solution.py:681
  96.0 4.4 %collective-permute-done.3 = bf16[2,256,512]{2,1,0:T(8,128)(2,1)S(1)} collective-permute-done((bf16[2,256,512]{2,1,0:T(8,128)(2,1)S(1)}, bf16[2,256,512]{2,1,0:T(8,128)(2,1)S(1)}, u32[]{:S(2)}, u32[]{:S(2)}) %collective-permute-start.3) | collective-permute-done | bytes 524320 | tf_op jit(solution)/shard_map/ppermute | solution.py:574
  102.6 5.7 %all-to-all-start.3 = ((bf16[8,2,32,512]{3,2,1,0:T(8,128)(2,1)}), bf16[8,2,32,512]{3,2,1,0:T(8,128)(2,1)S(1)}, u32[]{:S(2)}, u32[]{:S(2)}) async-start(bf16[8,2,32,512]{3,2,1,0:T(8,128)(2,1)} %bitcast.92), calls=%async_computation.3 | async-start | bytes 1048576 | tf_op jit(solution)/shard_map/all_to_all | solution.py:681
  109.8 3.4 %copy-done.3 = bf16[64,16,32,64]{3,2,1,0:T(8,128)(2,1)S(1)} copy-done((bf16[64,16,32,64]{3,2,1,0:T(8,128)(2,1)S(1)}, bf16[64,16,32,64]{3,2,1,0:T(8,128)(2,1)}, u32[]{:S(2)}) %copy-start.3) | copy-done | bytes 4194328
  113.1 3.4 %spatial_first.1.after_and_out_0_.target_ref = bf16[16,1024,128]{2,1,0:T(8,128)(2,1)S(1)} custom-call(bf16[64,16,32,64]{3,2,1,0:T(8,128)(2,1)S(1)} %copy-done.3, bf16[2,256,512]{2,1,0:T(8,128)(2,1)S(1)} %copy-done.5), custom_call_target="tpu_custom_call" | custom-call | bytes 28000000 | tf_op jit(solution)/shard_map/spatial_first/pallas_call | solution.py:351
  118.6 3.5 %all-to-all-done.3.second_ref = bf16[8,2,32,512]{3,2,1,0:T(8,128)(2,1)S(1)} async-done(((bf16[8,2,32,512]{3,2,1,0:T(8,128)(2,1)}), bf16[8,2,32,512]{3,2,1,0:T(8,128)(2,1)S(1)}, u32[]{:S(2)}, u32[]{:S(2)}) %all-to-all-start.3) | async-done | bytes 524320 | tf_op jit(solution)/shard_map/all_to_all | solution.py:681
  124.8 11.9 %all_to_all.25.latent_ref = bf16[4,64,1024]{2,1,0:T(8,128)(2,1)} all-to-all(bf16[4,64,1024]{2,1,0:T(8,128)(2,1)S(1)} %bitcast.94), channel_id=1, replica_groups=mesh['vox'=4,'dp'=8] {'vox'}, dimensions={0} | all-to-all | bytes 1048576 | tf_op jit(solution)/shard_map/all_to_all | solution.py:701
  136.7 29.1 %decoder.1 = (bf16[16,1024,128]{2,1,0:T(8,128)(2,1)}, bf16[5376,256]{1,0:T(8,128)(2,1)}, bf16[5376,256]{1,0:T(8,128)(2,1)}) custom-call(s32[1]{0:T(128)} %bitcast.side_ref, bf16[4,64,1024]{2,1,0:T(8,128)(2,1)} %all_to_all.25.latent_ref, bf16[8192,256]{1,0:T(8,128)(2,1)} %w_one_ref.1, bf16[2,512,512]{2,1,0:T(8,128)(2,1)} %copy-done.2, ...), custom_call_target="tpu_custom_call" | custom-call | tf_op jit(solution)/shard_map/decoder/pallas_call | solution.py:294
  165.9 5.2 %collective-permute-done.4.after_ref = bf16[5376,256]{1,0:T(8,128)(2,1)S(1)} collective-permute-done((bf16[5376,256]{1,0:T(8,128)(2,1)}, bf16[5376,256]{1,0:T(8,128)(2,1)S(1)}, u32[]{:S(2)}, u32[]{:S(2)}) %collective-permute-start.4) | collective-permute-done | bytes 2752544 | tf_op jit(solution)/shard_map/ppermute | solution.py:574
  171.2 3.5 %convert_add_fusion = (f32[1024,256]{1,0:T(8,128)}, bf16[1024,256]{1,0:T(8,128)(2,1)}, bf16[1024,256]{1,0:T(8,128)(2,1)}, f32[1024,256]{1,0:T(8,128)}) fusion(bf16[5376,256]{1,0:T(8,128)(2,1)S(1)} %collective-permute-done.4.after_ref, s32[]{:T(128)S(6)} %select_n.206, bf16[5376,256]{1,0:T(8,128)(2,1)} %get-tuple-element.50, s32[]{:T(128)S(6)} %select_n.200, ...), kind=kLoop, calls=%fused_computation.3 | loop fusion | flops 3670016 | bytes 7340048 | tf_op jit(solution)/shard_map/add | solution.py:580
  180.5 5.4 %sample_first.1 = bf16[64,16,32,64]{3,2,1,0:T(8,128)(2,1)} custom-call(bf16[16,1024,128]{2,1,0:T(8,128)(2,1)S(1)} %copy-done.6, bf16[5376,256]{1,0:T(8,128)(2,1)S(1)} %collective-permute-done.4.after_ref), custom_call_target="tpu_custom_call" | custom-call | bytes 28000000 | tf_op jit(solution)/shard_map/sample_first/pallas_call | solution.py:382
  195.6 6.7 %collective-permute-done.9 = bf16[832,256]{1,0:T(8,128)(2,1)S(1)} collective-permute-done((bf16[832,256]{1,0:T(8,128)(2,1)S(1)}, bf16[832,256]{1,0:T(8,128)(2,1)S(1)}, u32[]{:S(2)}, u32[]{:S(2)}) %collective-permute-start.9) | collective-permute-done | bytes 426016 | tf_op jit(solution)/shard_map/ppermute | solution.py:574
  204.2 4.9 %collective-permute-done.10 = bf16[512,256]{1,0:T(8,128)(2,1)S(1)} collective-permute-done((bf16[512,256]{1,0:T(8,128)(2,1)S(1)}, bf16[512,256]{1,0:T(8,128)(2,1)S(1)}, u32[]{:S(2)}, u32[]{:S(2)}) %collective-permute-start.10) | collective-permute-done | bytes 262176 | tf_op jit(solution)/shard_map/ppermute | solution.py:574
  210.1 12.8 %collective-permute-done.12 = bf16[336,256]{1,0:T(8,128)(2,1)S(1)} collective-permute-done((bf16[336,256]{1,0:T(8,128)(2,1)S(1)}, bf16[336,256]{1,0:T(8,128)(2,1)S(1)}, u32[]{:S(2)}, u32[]{:S(2)}) %collective-permute-start.12) | collective-permute-done | bytes 172064 | tf_op jit(solution)/shard_map/ppermute | solution.py:574
  223.2 6.4 %collective-permute-done.13 = bf16[336,256]{1,0:T(8,128)(2,1)S(1)} collective-permute-done((bf16[336,256]{1,0:T(8,128)(2,1)S(1)}, bf16[336,256]{1,0:T(8,128)(2,1)S(1)}, u32[]{:S(2)}, u32[]{:S(2)}) %collective-permute-start.13) | collective-permute-done | bytes 172064 | tf_op jit(solution)/shard_map/ppermute | solution.py:574
  229.8 4.4 %collective-permute-done.15 = bf16[160,256]{1,0:T(8,128)(2,1)S(1)} collective-permute-done((bf16[160,256]{1,0:T(8,128)(2,1)S(1)}, bf16[160,256]{1,0:T(8,128)(2,1)S(1)}, u32[]{:S(2)}, u32[]{:S(2)}) %collective-permute-start.15) | collective-permute-done | bytes 81952 | tf_op jit(solution)/shard_map/ppermute | solution.py:574
  236.5 6.1 %collective-permute-done.16 = bf16[512,256]{1,0:T(8,128)(2,1)S(1)} collective-permute-done((bf16[512,256]{1,0:T(8,128)(2,1)S(1)}, bf16[512,256]{1,0:T(8,128)(2,1)S(1)}, u32[]{:S(2)}, u32[]{:S(2)}) %collective-permute-start.16) | collective-permute-done | bytes 262176 | tf_op jit(solution)/shard_map/ppermute | solution.py:574
  247.3 4.2 %collective-permute-done.20 = bf16[640,256]{1,0:T(8,128)(2,1)S(1)} collective-permute-done((bf16[640,256]{1,0:T(8,128)(2,1)S(1)}, bf16[640,256]{1,0:T(8,128)(2,1)S(1)}, u32[]{:S(2)}, u32[]{:S(2)}) %collective-permute-start.20) | collective-permute-done | bytes 327712 | tf_op jit(solution)/shard_map/ppermute | solution.py:574
  251.6 4.8 %collective-permute-done.19 = bf16[1024,256]{1,0:T(8,128)(2,1)S(1)} collective-permute-done((bf16[1024,256]{1,0:T(8,128)(2,1)S(1)}, bf16[1024,256]{1,0:T(8,128)(2,1)S(1)}, u32[]{:S(2)}, u32[]{:S(2)}) %collective-permute-start.19) | collective-permute-done | bytes 524320 | tf_op jit(solution)/shard_map/ppermute | solution.py:574
  258.6 4.5 %collective-permute-done.23.other_c = bf16[1280,256]{1,0:T(8,128)(2,1)S(1)} collective-permute-done((bf16[1280,256]{1,0:T(8,128)(2,1)S(1)}, bf16[1280,256]{1,0:T(8,128)(2,1)S(1)}, u32[]{:S(2)}, u32[]{:S(2)}) %collective-permute-start.23) | collective-permute-done | bytes 655392 | tf_op jit(solution)/shard_map/ppermute | solution.py:574
  (134 shorter events, 51.5 us)
Async XLA Ops:
  3.9 33.1 %all-to-all-start = ((bf16[8,32,2048]{2,1,0:T(8,128)(2,1)}), bf16[8,32,2048]{2,1,0:T(8,128)(2,1)S(1)}, u32[]{:S(2)}, u32[]{:S(2)}) async-start(bf16[8,32,2048]{2,1,0:T(8,128)(2,1)} %bitcast.106), calls=%async_computation | async-start | bytes 2097152 | tf_op jit(solution)/shard_map/all_to_all | solution.py:653
  37.0 29.5 %all-to-all-start.2 = ((bf16[8,32,2048]{2,1,0:T(8,128)(2,1)}), bf16[8,32,2048]{2,1,0:T(8,128)(2,1)S(1)}, u32[]{:S(2)}, u32[]{:S(2)}) async-start(bf16[8,32,2048]{2,1,0:T(8,128)(2,1)} %bitcast.105), calls=%async_computation.2 | async-start | bytes 2097152 | tf_op jit(solution)/shard_map/all_to_all | solution.py:653
  46.4 4.0 %collective-permute-start = (bf16[4,256,512]{2,1,0:T(8,128)(2,1)}, bf16[4,256,512]{2,1,0:T(8,128)(2,1)S(1)}, u32[]{:S(2)}, u32[]{:S(2)}) collective-permute-start(bf16[4,256,512]{2,1,0:T(8,128)(2,1)} %project_rows.6.after_and_out_0_), channel_id=1, source_target_pairs={{0,8},{8,0},{16,24},{24,16},{1,9},{9,1},{17,25},{25,17},{2,10},{10... | collective-permute-start | bytes 3145736 | tf_op jit(solution)/shard_map/ppermute | solution.py:574
  51.7 14.9 %collective-permute-start.1 = (bf16[2,256,512]{2,1,0:T(8,128)(2,1)S(1)}, bf16[2,256,512]{2,1,0:T(8,128)(2,1)S(1)}, u32[]{:S(2)}, u32[]{:S(2)}) collective-permute-start(bf16[2,256,512]{2,1,0:T(8,128)(2,1)S(1)} %add_convert_fusion.5.after_and_out_0_), channel_id=1, source_target_pairs={{0,16},{8,24},{16,0},{24,8},{1,17},{9,25},{17,1},{25,9},{2,18},{10... | collective-permute-start | bytes 1572872 | tf_op jit(solution)/shard_map/ppermute | solution.py:574
  73.5 11.3 %collective-permute-start.2 = (bf16[4,256,512]{2,1,0:T(8,128)(2,1)}, bf16[4,256,512]{2,1,0:T(8,128)(2,1)}, u32[]{:S(2)}, u32[]{:S(2)}) collective-permute-start(bf16[4,256,512]{2,1,0:T(8,128)(2,1)} %project_rows.9.after_and_out_0_), channel_id=1, source_target_pairs={{0,8},{8,0},{16,24},{24,16},{1,9},{9,1},{17,25},{25,17},{2,10},{10... | collective-permute-start | bytes 3145736 | tf_op jit(solution)/shard_map/ppermute | solution.py:574
  75.6 20.3 %all-to-all-start.1 = ((bf16[8,2,32,512]{3,2,1,0:T(8,128)(2,1)}), bf16[8,2,32,512]{3,2,1,0:T(8,128)(2,1)S(1)}, u32[]{:S(2)}, u32[]{:S(2)}) async-start(bf16[8,2,32,512]{3,2,1,0:T(8,128)(2,1)} %bitcast.93), calls=%async_computation.1 | async-start | bytes 1048576 | tf_op jit(solution)/shard_map/all_to_all | solution.py:681
  86.2 14.1 %collective-permute-start.3 = (bf16[2,256,512]{2,1,0:T(8,128)(2,1)S(1)}, bf16[2,256,512]{2,1,0:T(8,128)(2,1)S(1)}, u32[]{:S(2)}, u32[]{:S(2)}) collective-permute-start(bf16[2,256,512]{2,1,0:T(8,128)(2,1)S(1)} %add_convert_fusion.3.after_and_out_0_.after_ref), channel_id=1, source_target_pairs={{0,16},{8,24},{16,0},{24,8},{1,17},{9,25},{17,1},{25,9},{2,18},{10... | collective-permute-start | bytes 1572872 | tf_op jit(solution)/shard_map/ppermute | solution.py:574
  102.6 19.5 %all-to-all-start.3 = ((bf16[8,2,32,512]{3,2,1,0:T(8,128)(2,1)}), bf16[8,2,32,512]{3,2,1,0:T(8,128)(2,1)S(1)}, u32[]{:S(2)}, u32[]{:S(2)}) async-start(bf16[8,2,32,512]{3,2,1,0:T(8,128)(2,1)} %bitcast.92), calls=%async_computation.3 | async-start | bytes 1048576 | tf_op jit(solution)/shard_map/all_to_all | solution.py:681
  108.6 13.5 %copy-start.7 = (bf16[2,256,256]{2,1,0:T(8,128)(2,1)}, bf16[2,256,256]{2,1,0:T(8,128)(2,1)S(1)}, u32[]{:S(2)}) copy-start(bf16[2,256,256]{2,1,0:T(8,128)(2,1)S(1)} %pad_maximum_fusion.12.after_and_out_2_.w_three_ref) | copy-start | bytes 786436
  113.1 9.0 %copy-start.2 = (bf16[2,512,512]{2,1,0:T(8,128)(2,1)}, bf16[2,512,512]{2,1,0:T(8,128)(2,1)S(1)}, u32[]{:S(2)}) copy-start(bf16[2,512,512]{2,1,0:T(8,128)(2,1)S(1)} %pad_maximum_fusion.after_and_out_1_.w_two_ref) | copy-start | bytes 3145732
  113.1 9.0 %copy-start.8 = (bf16[256,256]{1,0:T(8,128)(2,1)S(1)}, bf16[256,256]{1,0:T(8,128)(2,1)}, u32[]{:S(2)}) copy-start(bf16[256,256]{1,0:T(8,128)(2,1)} %get-tuple-element.44.after_ref.place_a_ref) | copy-start | bytes 393220
  113.1 9.0 %copy-start.9 = (bf16[256,256]{1,0:T(8,128)(2,1)S(1)}, bf16[256,256]{1,0:T(8,128)(2,1)}, u32[]{:S(2)}) copy-start(bf16[256,256]{1,0:T(8,128)(2,1)} %get-tuple-element.45.place_b_ref) | copy-start | bytes 393220
  165.9 5.3 %collective-permute-start.4 = (bf16[5376,256]{1,0:T(8,128)(2,1)}, bf16[5376,256]{1,0:T(8,128)(2,1)S(1)}, u32[]{:S(2)}, u32[]{:S(2)}) collective-permute-start(bf16[5376,256]{1,0:T(8,128)(2,1)} %get-tuple-element.51), channel_id=1, source_target_pairs={{0,8},{8,0},{16,24},{24,16},{1,9},{9,1},{17,25},{25,17},{2,10},{10... | collective-permute-start | bytes 8257544 | tf_op jit(solution)/shard_map/ppermute | solution.py:574
  174.6 14.3 %collective-permute-start.5 = (bf16[1024,256]{1,0:T(8,128)(2,1)}, bf16[1024,256]{1,0:T(8,128)(2,1)}, u32[]{:S(2)}, u32[]{:S(2)}) collective-permute-start(bf16[1024,256]{1,0:T(8,128)(2,1)} %get-tuple-element.86), channel_id=1, source_target_pairs={{0,16},{8,24},{16,0},{24,8},{1,17},{9,25},{17,1},{25,9},{2,18},{10... | collective-permute-start | bytes 1572872 | tf_op jit(solution)/shard_map/ppermute | solution.py:574
  175.0 14.0 %collective-permute-start.6 = (bf16[1024,256]{1,0:T(8,128)(2,1)}, bf16[1024,256]{1,0:T(8,128)(2,1)}, u32[]{:S(2)}, u32[]{:S(2)}) collective-permute-start(bf16[1024,256]{1,0:T(8,128)(2,1)} %get-tuple-element.85), channel_id=1, source_target_pairs={{0,1},{1,0},{2,3},{3,2},{4,5},{5,4},{6,7},{7,6},{8,9},{9,8},{10,11... | collective-permute-start | bytes 1572872 | tf_op jit(solution)/shard_map/ppermute | solution.py:574
  178.3 9.5 %collective-permute-start.7 = (bf16[640,256]{1,0:T(8,128)(2,1)}, bf16[640,256]{1,0:T(8,128)(2,1)}, u32[]{:S(2)}, u32[]{:S(2)}) collective-permute-start(bf16[640,256]{1,0:T(8,128)(2,1)} %get-tuple-element.88), channel_id=1, source_target_pairs={{0,2},{1,3},{2,0},{3,1},{4,6},{5,7},{6,4},{7,5},{8,10},{9,11},{10,... | collective-permute-start | bytes 983048 | tf_op jit(solution)/shard_map/ppermute | solution.py:574
  191.2 11.0 %collective-permute-start.9 = (bf16[832,256]{1,0:T(8,128)(2,1)S(1)}, bf16[832,256]{1,0:T(8,128)(2,1)S(1)}, u32[]{:S(2)}, u32[]{:S(2)}) collective-permute-start(bf16[832,256]{1,0:T(8,128)(2,1)S(1)} %pad_maximum_fusion.6), channel_id=1, source_target_pairs={{0,16},{8,24},{16,0},{24,8},{1,17},{9,25},{17,1},{25,9},{2,18},{10... | collective-permute-start | bytes 1277960 | tf_op jit(solution)/shard_map/ppermute | solution.py:574
  194.1 8.2 %collective-permute-start.8 = (bf16[512,256]{1,0:T(8,128)(2,1)S(1)}, bf16[512,256]{1,0:T(8,128)(2,1)S(1)}, u32[]{:S(2)}, u32[]{:S(2)}) collective-permute-start(bf16[512,256]{1,0:T(8,128)(2,1)S(1)} %get-tuple-element.91), channel_id=1, source_target_pairs={{0,1},{1,0},{2,3},{3,2},{4,5},{5,4},{6,7},{7,6},{8,9},{9,8},{10,11... | collective-permute-start | bytes 786440 | tf_op jit(solution)/shard_map/ppermute | solution.py:574
  202.5 6.6 %collective-permute-start.10 = (bf16[512,256]{1,0:T(8,128)(2,1)S(1)}, bf16[512,256]{1,0:T(8,128)(2,1)S(1)}, u32[]{:S(2)}, u32[]{:S(2)}) collective-permute-start(bf16[512,256]{1,0:T(8,128)(2,1)S(1)} %pad_maximum_fusion.13), channel_id=1, source_target_pairs={{0,2},{1,3},{2,0},{3,1},{4,6},{5,7},{6,4},{7,5},{8,10},{9,11},{10,... | collective-permute-start | bytes 786440 | tf_op jit(solution)/shard_map/ppermute | solution.py:574
  203.3 5.8 %collective-permute-start.11 = (bf16[160,256]{1,0:T(8,128)(2,1)S(1)}, bf16[160,256]{1,0:T(8,128)(2,1)S(1)}, u32[]{:S(2)}, u32[]{:S(2)}) collective-permute-start(bf16[160,256]{1,0:T(8,128)(2,1)S(1)} %get-tuple-element.132), channel_id=1, source_target_pairs={{0,1},{1,0},{2,3},{3,2},{4,5},{5,4},{6,7},{7,6},{8,9},{9,8},{10,11... | collective-permute-start | bytes 245768 | tf_op jit(solution)/shard_map/ppermute | solution.py:574
  209.2 13.6 %collective-permute-start.12 = (bf16[336,256]{1,0:T(8,128)(2,1)S(1)}, bf16[336,256]{1,0:T(8,128)(2,1)S(1)}, u32[]{:S(2)}, u32[]{:S(2)}) collective-permute-start(bf16[336,256]{1,0:T(8,128)(2,1)S(1)} %pad_maximum_fusion.14), channel_id=1, source_target_pairs={{0,4},{1,5},{2,6},{3,7},{4,0},{5,1},{6,2},{7,3},{8,12},{9,13},{10,... | collective-permute-start | bytes 516104 | tf_op jit(solution)/shard_map/ppermute | solution.py:574
  223.0 6.5 %collective-permute-start.13 = (bf16[336,256]{1,0:T(8,128)(2,1)S(1)}, bf16[336,256]{1,0:T(8,128)(2,1)S(1)}, u32[]{:S(2)}, u32[]{:S(2)}) collective-permute-start(bf16[336,256]{1,0:T(8,128)(2,1)S(1)} %pad_maximum_fusion.15), channel_id=1, source_target_pairs={{0,4},{1,5},{2,6},{3,7},{4,0},{5,1},{6,2},{7,3},{8,12},{9,13},{10,... | collective-permute-start | bytes 516104 | tf_op jit(solution)/shard_map/ppermute | solution.py:574
  229.6 6.4 %collective-permute-start.14 = (bf16[512,256]{1,0:T(8,128)(2,1)S(1)}, bf16[512,256]{1,0:T(8,128)(2,1)S(1)}, u32[]{:S(2)}, u32[]{:S(2)}) collective-permute-start(bf16[512,256]{1,0:T(8,128)(2,1)S(1)} %get-tuple-element.143), channel_id=1, source_target_pairs={{0,2},{1,3},{2,0},{3,1},{4,6},{5,7},{6,4},{7,5},{8,10},{9,11},{10,... | collective-permute-start | bytes 786440 | tf_op jit(solution)/shard_map/ppermute | solution.py:574
  229.7 4.5 %collective-permute-start.15 = (bf16[160,256]{1,0:T(8,128)(2,1)S(1)}, bf16[160,256]{1,0:T(8,128)(2,1)S(1)}, u32[]{:S(2)}, u32[]{:S(2)}) collective-permute-start(bf16[160,256]{1,0:T(8,128)(2,1)S(1)} %slice_dynamic-update-slice_fusion.6), channel_id=1, source_target_pairs={{0,1},{1,0},{2,3},{3,2},{4,5},{5,4},{6,7},{7,6},{8,9},{9,8},{10,11... | collective-permute-start | bytes 245768 | tf_op jit(solution)/shard_map/ppermute | solution.py:574
  236.1 8.2 %collective-permute-start.17 = (bf16[832,256]{1,0:T(8,128)(2,1)S(1)}, bf16[832,256]{1,0:T(8,128)(2,1)S(1)}, u32[]{:S(2)}, u32[]{:S(2)}) collective-permute-start(bf16[832,256]{1,0:T(8,128)(2,1)S(1)} %pad_maximum_fusion.7), channel_id=1, source_target_pairs={{0,16},{8,24},{16,0},{24,8},{1,17},{9,25},{17,1},{25,9},{2,18},{10... | collective-permute-start | bytes 1277960 | tf_op jit(solution)/shard_map/ppermute | solution.py:574
  236.2 6.4 %collective-permute-start.16 = (bf16[512,256]{1,0:T(8,128)(2,1)S(1)}, bf16[512,256]{1,0:T(8,128)(2,1)S(1)}, u32[]{:S(2)}, u32[]{:S(2)}) collective-permute-start(bf16[512,256]{1,0:T(8,128)(2,1)S(1)} %get-tuple-element.72), channel_id=1, source_target_pairs={{0,1},{1,0},{2,3},{3,2},{4,5},{5,4},{6,7},{7,6},{8,9},{9,8},{10,11... | collective-permute-start | bytes 786440 | tf_op jit(solution)/shard_map/ppermute | solution.py:574
  244.4 7.1 %collective-permute-start.20 = (bf16[640,256]{1,0:T(8,128)(2,1)S(1)}, bf16[640,256]{1,0:T(8,128)(2,1)S(1)}, u32[]{:S(2)}, u32[]{:S(2)}) collective-permute-start(bf16[640,256]{1,0:T(8,128)(2,1)S(1)} %slice_dynamic-update-slice_fusion.1), channel_id=1, source_target_pairs={{0,2},{1,3},{2,0},{3,1},{4,6},{5,7},{6,4},{7,5},{8,10},{9,11},{10,... | collective-permute-start | bytes 983048 | tf_op jit(solution)/shard_map/ppermute | solution.py:574
  244.9 11.5 %collective-permute-start.19 = (bf16[1024,256]{1,0:T(8,128)(2,1)S(1)}, bf16[1024,256]{1,0:T(8,128)(2,1)S(1)}, u32[]{:S(2)}, u32[]{:S(2)}) collective-permute-start(bf16[1024,256]{1,0:T(8,128)(2,1)S(1)} %slice_dynamic-update-slice_fusion), channel_id=1, source_target_pairs={{0,1},{1,0},{2,3},{3,2},{4,5},{5,4},{6,7},{7,6},{8,9},{9,8},{10,11... | collective-permute-start | bytes 1572872 | tf_op jit(solution)/shard_map/ppermute | solution.py:574
  246.9 11.0 %collective-permute-start.18 = (bf16[1024,256]{1,0:T(8,128)(2,1)S(1)}, bf16[1024,256]{1,0:T(8,128)(2,1)S(1)}, u32[]{:S(2)}, u32[]{:S(2)}) collective-permute-start(bf16[1024,256]{1,0:T(8,128)(2,1)S(1)} %constant_dynamic-update-slice_fusion.1), channel_id=1, source_target_pairs={{0,16},{8,24},{16,0},{24,8},{1,17},{9,25},{17,1},{25,9},{2,18},{10... | collective-permute-start | bytes 1572872 | tf_op jit(solution)/shard_map/ppermute | solution.py:574
  257.9 5.2 %collective-permute-start.21 = (bf16[2048,256]{1,0:T(8,128)(2,1)S(1)}, bf16[2048,256]{1,0:T(8,128)(2,1)S(1)}, u32[]{:S(2)}, u32[]{:S(2)}) collective-permute-start(bf16[2048,256]{1,0:T(8,128)(2,1)S(1)} %constant_dynamic-update-slice_fusion.own_a), channel_id=1, source_target_pairs={{0,8},{8,0},{16,24},{24,16},{1,9},{9,1},{17,25},{25,17},{2,10},{10... | collective-permute-start | bytes 3145736 | tf_op jit(solution)/shard_map/ppermute | solution.py:574
  258.0 5.1 %collective-permute-start.22 = (bf16[2048,256]{1,0:T(8,128)(2,1)S(1)}, bf16[2048,256]{1,0:T(8,128)(2,1)S(1)}, u32[]{:S(2)}, u32[]{:S(2)}) collective-permute-start(bf16[2048,256]{1,0:T(8,128)(2,1)S(1)} %constant_dynamic-update-slice_fusion.4.own_b), channel_id=1, source_target_pairs={{0,8},{8,0},{16,24},{24,16},{1,9},{9,1},{17,25},{25,17},{2,10},{10... | collective-permute-start | bytes 3145736 | tf_op jit(solution)/shard_map/ppermute | solution.py:574
  258.5 4.6 %collective-permute-start.23 = (bf16[1280,256]{1,0:T(8,128)(2,1)S(1)}, bf16[1280,256]{1,0:T(8,128)(2,1)S(1)}, u32[]{:S(2)}, u32[]{:S(2)}) collective-permute-start(bf16[1280,256]{1,0:T(8,128)(2,1)S(1)} %constant_dynamic-update-slice_fusion.2.own_c), channel_id=1, source_target_pairs={{0,8},{8,0},{16,24},{24,16},{1,9},{9,1},{17,25},{25,17},{2,10},{10... | collective-permute-start | bytes 1966088 | tf_op jit(solution)/shard_map/ppermute | solution.py:574
  (15 other events, 55.2 us)

commit v5 on v4

--- a/solution.py
+++ b/solution.py
@@ -173,17 +173,20 @@
     return jnp.concatenate(pieces, axis=0)
 
 
-def backward_part(count, side_ref, latent_ref, act_ref, slope_ref, w_ref, grad_two_ref, third_ref, grad_one, kept_ref, sent_ref, adj, total_one, total_two):
+def backward_part(count, side_ref, latent_ref, act_ref, slope_ref, w_ref, grad_two_ref, third_ref, grad_one, kept_refs, sent_refs, adj, total_one, total_two):
     side = side_ref[0]
 
-    def put(half, rows, values):
+    def put(half, first, size, values):
+        at = min(first // sent_refs[0].shape[0], 2)
+        rows = pl.ds(first - at * sent_refs[0].shape[0], size)
+
         @pl.when(side == half)
         def _():
-            kept_ref[rows, :] = values().astype(jnp.bfloat16)
+            kept_refs[at][rows, :] = values().astype(jnp.bfloat16)
 
         @pl.when(side != half)
         def _():
-            sent_ref[rows, :] = values().astype(jnp.bfloat16)
+            sent_refs[at][rows, :] = values().astype(jnp.bfloat16)
 
     height = act_ref.shape[0]
     breadth = act_ref.shape[1] // count
@@ -223,14 +226,14 @@
     for parity in (0, 1):
         for which in (0, 1):
             for pair in (0, 1):
-                rows = pl.ds(tail + (2 * which + pair) * mid_chan, mid_chan)
                 above, left_edge = which * mid_chan, pair * lanes
                 put(
                     parity,
-                    rows,
+                    tail + (2 * which + pair) * mid_chan,
+                    mid_chan,
                     lambda: total_two[parity, above:above + mid_chan, left_edge:left_edge + lanes],
                 )
-        put(parity, pl.ds(tail + 4 * mid_chan, third_ref.shape[1]), lambda: third_ref[parity])
+        put(parity, tail + 4 * mid_chan, third_ref.shape[1], lambda: third_ref[parity])
     for row_tap in range(4):
         parity = 0 if row_tap in ROW_TAPS[0] else 1
         shift = ROW_SHIFT[parity] if ROW_TAPS[parity][1] == row_tap else 0
@@ -241,13 +244,13 @@
         right = jnp.concatenate(rights, axis=0) if len(rights) > 1 else rights[0]
         total_one[...] = product_tn(left, right)
         for slot, col_tap in enumerate(COL_TAPS):
-            to = pl.ds(((row_tap % 2) * 4 + col_tap) * in_chan, in_chan)
-            put(row_tap // 2, to, lambda: total_one[:, slot * mid_chan:(slot + 1) * mid_chan])
+            to = ((row_tap % 2) * 4 + col_tap) * in_chan
+            put(row_tap // 2, to, in_chan, lambda: total_one[:, slot * mid_chan:(slot + 1) * mid_chan])
 
 
 def decoder_kernel(
     count, side_ref, latent_ref, w_one_ref, w_two_ref, w_three_ref, target_ref,
-    decoded_ref, kept_ref, sent_ref,
+    decoded_ref, kept_a_ref, kept_b_ref, kept_c_ref, sent_a_ref, sent_b_ref, sent_c_ref,
     grad_one, act_one, slope_one, act_two, slope_two, grad_two, kgrad_three, tmp_one, tmp_two, tmp_three, grads, adj_two, adj_one, total_one, total_two,
 ):
     step = pl.program_id(0)
@@ -265,7 +268,7 @@
     def _():
         backward_part(
             count, side_ref, latent_ref, act_one, slope_one, w_two_ref, grad_two, kgrad_three,
-            grad_one, kept_ref, sent_ref, adj_one, total_one, total_two,
+            grad_one, (kept_a_ref, kept_b_ref, kept_c_ref), (sent_a_ref, sent_b_ref, sent_c_ref), adj_one, total_one, total_two,
         )
 
 
@@ -289,7 +292,7 @@
     act_two = (2 * height, flat, out_chan)
     padded = (2 * height + 2, flat, out_chan)
     in_chan = w_one.shape[0] // 16
-    share = (8 * in_chan + 4 * mid_chan + third_rows, mid_chan)
+    quarter, tail = (4 * in_chan, mid_chan), (4 * mid_chan + third_rows, mid_chan)
     single = pl.Buffered(1)
     return pl.pallas_call(
         functools.partial(decoder_kernel, count),
@@ -305,13 +308,11 @@
         ],
         out_specs=(
             pl.BlockSpec((2, flat, lanes), lambda step: (step, 0, 0)),
-            whole(share),
-            whole(share),
+            *map(whole, 2 * (quarter, quarter, tail)),
         ),
         out_shape=(
             jax.ShapeDtypeStruct(target.shape, jnp.bfloat16),
-            jax.ShapeDtypeStruct(share, jnp.bfloat16),
-            jax.ShapeDtypeStruct(share, jnp.bfloat16),
+            *(jax.ShapeDtypeStruct(shape, jnp.bfloat16) for shape in 2 * (quarter, quarter, tail)),
         ),
         scratch_shapes=[
             pltpu.VMEM(act_one, jnp.bfloat16),
@@ -586,11 +587,8 @@
     place = place_of(step)
 
     def part(terms, which):
-        cuts = []
-        for term in terms:
-            array, start, size = term if isinstance(term, tuple) else (term, 0, term.shape[0])
-            cuts.append(lax.dynamic_slice_in_dim(array, start + which * (size // ways), size // ways, 0))
-        return summed(cuts)
+        size = terms[0].shape[0] // ways
+        return summed([lax.dynamic_slice_in_dim(term, which * size, size, 0) for term in terms])
 
     arrived = []
     for change in range(1, ways):
@@ -600,7 +598,7 @@
     result = []
     start = 0
     for terms in chains:
-        size = (terms[0][2] if isinstance(terms[0], tuple) else terms[0].shape[0]) // ways
+        size = terms[0].shape[0] // ways
         result.append([part(terms, place)] + [values[start:start + size] for values in arrived])
         start += size
     return result
@@ -700,17 +698,15 @@
     own_rows = own_rows.reshape(holders, samp_dev // holders, own_rows.shape[1])
     latent = lax.all_to_all(own_rows, "vox", split_axis=0, concat_axis=0, tiled=True)
     count = latent.shape[1]
-    decoded_rows, kept, sent = decoder(side, latent, w_first, pair_two, pair_three, target_rows)
+    decoded_rows, *shares = decoder(side, latent, w_first, pair_two, pair_three, target_rows)
     third_rows = pair_three.shape[1]
-    quarter = w_first.shape[0] // 4
-    received = exchanged(sent, vox_bits[:1], 1)
+    received = [exchanged(values, vox_bits[:1], 1) for values in shares[3:]]
     across = [[hop] for hop in vox_bits[1:]]
     near = [dp_bits[:1]]
     along = [[hop] for hop in dp_bits[1:]]
     routes = (across + near + along, near + across + along, along[:1] + across + near + along[1:])
-    cuts = ((0, quarter), (quarter, quarter), (2 * quarter, kept.shape[0] - 2 * quarter))
-    parts = [[(kept, *cut), (received, *cut)] for cut in cuts]
-    decoded = sample_first(decoded_rows, count, w_third.shape[1], received)
+    parts = [list(pair) for pair in zip(shares[:3], received)]
+    decoded = sample_first(decoded_rows, count, w_third.shape[1], received[1])
     for stage in range(len(routes[0])):
         parts = over_chains(shared, parts, [route[stage] for route in routes])
         *tied, decoded = lax.optimization_barrier(tuple(terms[1] for terms in parts) + (decoded,))

time: 267 us -> 264 us (0.989)
  waiting for transfers between devices: 112 us -> 105 us
  starting transfers between devices: 36.3 us -> 39.6 us
    ppermute x24 -> x26, waiting for transfers between devices: 72.4 us -> 66.4 us  [exchanged(): lax.ppermute(values, axis, [(at, at ^ flip) for at in range(lax.axis_size...]
    ppermute x24 -> x26, starting transfers between devices: 14.5 us -> 17.8 us  [exchanged(): lax.ppermute(values, axis, [(at, at ^ flip) for at in range(lax.axis_size...]
    add x5 -> x6, other arithmetic: 5.85 us -> 6.4 us  [summed(): value = value.astype(jnp.float32) + term.astype(jnp.float32)]
  transfers between devices with their start and end apart: 28 -> 30, of which waited for: 21 -> 20; matrix products, arithmetic and copies ran while one was open for 3% -> 5% of each run, Pallas kernels for 13% -> 13%
where the time goes in v5:
time: 264 us; the launch traced here: 263 us
  waiting for transfers between devices  105 us (40%)
  Pallas kernels  76.1 us (29%)
  starting transfers between devices  39.6 us (15%)
  other arithmetic  15.1 us (6%)
  local copies, waits for them, and re-layouts  14.1 us (5%)
  blocking collectives  11.9 us (5%)
    ppermute x26, waiting for transfers between devices, exchanged(): lax.ppermute(values, axis, [(at, at ^ flip) for at in range(lax.axis_size...  66.4 us
    all_to_all x2, waiting for transfers between devices, routed(): lax.all_to_all(sent, 'dp', split_axis=0, concat_axis=0, tiled=True)  31.8 us
    pallas_call x1, Pallas kernels, decoder(): pl.pallas_call(functools.partial(decoder_kernel, count), name='decoder',...  29.3 us
    pallas_call x6, Pallas kernels, projected(): pl.pallas_call(project_kernel, name='project_rows', grid_spec=pltpu.Prefe...  27.9 us
    ppermute x26, starting transfers between devices, exchanged(): lax.ppermute(values, axis, [(at, at ^ flip) for at in range(lax.axis_size...  17.8 us
    unnamed x39, local copies, waits for them, and re-layouts  12 us
    all_to_all x1, blocking collectives, shards(): lax.all_to_all(own_rows, 'vox', split_axis=0, concat_axis=0, tiled=True)  11.9 us
    all_to_all x2, starting transfers between devices, returned(): return lax.all_to_all(sent, 'dp', split_axis=0, concat_axis=0, tiled=True)  10.9 us
  transfers between devices with their start and end apart: 30, of which 20 were waited for; matrix products, arithmetic and copies ran while one was open for 5% of the time, Pallas kernels for 13%

profile of v5, /device:TPU:0, one launch (start us, length us, event | category | flops | bytes accessed | tf_op | source)
XLA Modules:
  0.0 263.3 jit_solution(15248515453909185661)
XLA Ops:
  0.6 3.3 %bucket_rows.2 = (bf16[256,2048]{1,0:T(8,128)(2,1)}, bf16[256,256]{1,0:T(8,128)(2,1)}) custom-call(s32[1,256]{1,0:T(1,128)} %bitcast.107, s32[8]{0:T(128)} %after_and_out_0_.1, s32[1]{0:T(128)} %bitcast.2.shift_ref, bf16[256,2048]{1,0:T(8,128)(2,1)} %fmri_ref.3, s32[8]{0:T(128)} %after_and_out_0_.1), custom_call_target="tpu_custom_call" | custom-call | tf_op jit(solution)/shard_map/bucket_rows/pallas_call | solution.py:428
  3.9 7.3 %all-to-all-start = ((bf16[8,32,2048]{2,1,0:T(8,128)(2,1)}), bf16[8,32,2048]{2,1,0:T(8,128)(2,1)S(1)}, u32[]{:S(2)}, u32[]{:S(2)}) async-start(bf16[8,32,2048]{2,1,0:T(8,128)(2,1)} %bitcast.106), calls=%async_computation | async-start | bytes 2097152 | tf_op jit(solution)/shard_map/all_to_all | solution.py:651
  11.2 3.3 %bucket_rows.3 = (bf16[256,2048]{1,0:T(8,128)(2,1)}, bf16[256,256]{1,0:T(8,128)(2,1)}) custom-call(s32[1,256]{1,0:T(1,128)} %bitcast.108, s32[8]{0:T(128)} %after_and_out_0_.1, s32[1]{0:T(128)} %bitcast.2.shift_ref, bf16[256,2048]{1,0:T(8,128)(2,1)} %fmri_ref.3, bf16[256,256]{1,0:T(8,128)(2,1)} %get-tuple-element.48.after_ref.place_a_ref), custom_call_target="tpu_custom_call" | custom-call | tf_op jit(solution)/shard_map/bucket_rows/pallas_call | solution.py:428
  14.5 22.5 %all-to-all-done = bf16[8,32,2048]{2,1,0:T(8,128)(2,1)S(1)} async-done(((bf16[8,32,2048]{2,1,0:T(8,128)(2,1)}), bf16[8,32,2048]{2,1,0:T(8,128)(2,1)S(1)}, u32[]{:S(2)}, u32[]{:S(2)}) %all-to-all-start) | async-done | bytes 1048608 | tf_op jit(solution)/shard_map/all_to_all | solution.py:651
  37.0 3.6 %all-to-all-start.2 = ((bf16[8,32,2048]{2,1,0:T(8,128)(2,1)}), bf16[8,32,2048]{2,1,0:T(8,128)(2,1)S(1)}, u32[]{:S(2)}, u32[]{:S(2)}) async-start(bf16[8,32,2048]{2,1,0:T(8,128)(2,1)} %bitcast.105), calls=%async_computation.2 | async-start | bytes 2097152 | tf_op jit(solution)/shard_map/all_to_all | solution.py:651
  40.6 5.9 %project_rows.6.after_and_out_0_ = bf16[4,256,512]{2,1,0:T(8,128)(2,1)} custom-call(s32[1]{0:T(128)} %bitcast.7.quarter_ref, bf16[256,2048]{1,0:T(8,128)(2,1)} %bitcast.98, bf16[1,2048,4096]{2,1,0:T(8,128)(2,1)} %map_ref.11, s32[8]{0:T(128)} %after_and_out_0_.1), custom_call_target="tpu_custom_call" | custom-call | flops 2147483648 | bytes 8388608 | tf_op jit(solution)/shard_map/project_rows/pallas_call | solution.py:455
  46.4 4.0 %project_rows.7 = bf16[2,256,512]{2,1,0:T(8,128)(2,1)} custom-call(s32[1]{0:T(128)} %bitcast.6.quarter_ref, bf16[256,2048]{1,0:T(8,128)(2,1)} %bitcast.99, bf16[1,2048,4096]{2,1,0:T(8,128)(2,1)} %map_ref.11, bf16[4,256,512]{2,1,0:T(8,128)(2,1)} %project_rows.6.after_and_out_0_), custom_call_target="tpu_custom_call" | custom-call | flops 1073741824 | bytes 4194304 | tf_op jit(solution)/shard_map/project_rows/pallas_call | solution.py:455
  53.2 4.0 %project_rows.8.after_and_out_1_ = bf16[2,256,512]{2,1,0:T(8,128)(2,1)} custom-call(s32[1]{0:T(128)} %bitcast.3.quarter_ref, bf16[256,2048]{1,0:T(8,128)(2,1)} %bitcast.100, bf16[1,2048,4096]{2,1,0:T(8,128)(2,1)} %map_ref.11, bf16[2,256,512]{2,1,0:T(8,128)(2,1)} %copy-done.15), custom_call_target="tpu_custom_call" | custom-call | flops 1073741824 | bytes 4194304 | tf_op jit(solution)/shard_map/project_rows/pallas_call | solution.py:455
  57.2 9.3 %all-to-all-done.2 = bf16[8,32,2048]{2,1,0:T(8,128)(2,1)S(1)} async-done(((bf16[8,32,2048]{2,1,0:T(8,128)(2,1)}), bf16[8,32,2048]{2,1,0:T(8,128)(2,1)S(1)}, u32[]{:S(2)}, u32[]{:S(2)}) %all-to-all-start.2) | async-done | bytes 1048608 | tf_op jit(solution)/shard_map/all_to_all | solution.py:651
  67.7 5.9 %project_rows.9.after_and_out_0_ = bf16[4,256,512]{2,1,0:T(8,128)(2,1)} custom-call(s32[1]{0:T(128)} %bitcast.7.quarter_ref, bf16[256,2048]{1,0:T(8,128)(2,1)} %bitcast.95, bf16[1,2048,4096]{2,1,0:T(8,128)(2,1)} %map_ref.11, bf16[2,256,512]{2,1,0:T(8,128)(2,1)} %copy-done.14, bf16[2,256,512]{2,1,0:T(8,128)(2,1)} %project_rows.8.after_and_out_1_), custom_call_target="tpu_custom_call" | custom-call | flops 2147483648 | bytes 8388608 | tf_op jit(solution)/shard_map/project_rows/pallas_call | solution.py:455
  75.6 5.2 %all-to-all-start.1 = ((bf16[8,2,32,512]{3,2,1,0:T(8,128)(2,1)}), bf16[8,2,32,512]{3,2,1,0:T(8,128)(2,1)S(1)}, u32[]{:S(2)}, u32[]{:S(2)}) async-start(bf16[8,2,32,512]{3,2,1,0:T(8,128)(2,1)} %bitcast.93), calls=%async_computation.1 | async-start | bytes 1048576 | tf_op jit(solution)/shard_map/all_to_all | solution.py:679
  80.8 4.1 %project_rows.10 = bf16[2,256,512]{2,1,0:T(8,128)(2,1)} custom-call(s32[1]{0:T(128)} %bitcast.6.quarter_ref, bf16[256,2048]{1,0:T(8,128)(2,1)} %bitcast.96, bf16[1,2048,4096]{2,1,0:T(8,128)(2,1)} %map_ref.11, bf16[4,256,512]{2,1,0:T(8,128)(2,1)} %project_rows.9.after_and_out_0_), custom_call_target="tpu_custom_call" | custom-call | flops 1073741824 | bytes 4194304 | tf_op jit(solution)/shard_map/project_rows/pallas_call | solution.py:455
  88.1 4.0 %project_rows.11 = bf16[2,256,512]{2,1,0:T(8,128)(2,1)} custom-call(s32[1]{0:T(128)} %bitcast.3.quarter_ref, bf16[256,2048]{1,0:T(8,128)(2,1)} %bitcast.97, bf16[1,2048,4096]{2,1,0:T(8,128)(2,1)} %map_ref.11, bf16[2,256,512]{2,1,0:T(8,128)(2,1)} %copy-done.4), custom_call_target="tpu_custom_call" | custom-call | flops 1073741824 | bytes 4194304 | tf_op jit(solution)/shard_map/project_rows/pallas_call | solution.py:455
  92.1 3.8 %all-to-all-done.1.first_ref = bf16[8,2,32,512]{3,2,1,0:T(8,128)(2,1)S(1)} async-done(((bf16[8,2,32,512]{3,2,1,0:T(8,128)(2,1)}), bf16[8,2,32,512]{3,2,1,0:T(8,128)(2,1)S(1)}, u32[]{:S(2)}, u32[]{:S(2)}) %all-to-all-start.1) | async-done | bytes 524320 | tf_op jit(solution)/shard_map/all_to_all | solution.py:679
  96.0 4.4 %collective-permute-done.3 = bf16[2,256,512]{2,1,0:T(8,128)(2,1)S(1)} collective-permute-done((bf16[2,256,512]{2,1,0:T(8,128)(2,1)S(1)}, bf16[2,256,512]{2,1,0:T(8,128)(2,1)S(1)}, u32[]{:S(2)}, u32[]{:S(2)}) %collective-permute-start.3) | collective-permute-done | bytes 524320 | tf_op jit(solution)/shard_map/ppermute | solution.py:575
  102.6 5.7 %all-to-all-start.3 = ((bf16[8,2,32,512]{3,2,1,0:T(8,128)(2,1)}), bf16[8,2,32,512]{3,2,1,0:T(8,128)(2,1)S(1)}, u32[]{:S(2)}, u32[]{:S(2)}) async-start(bf16[8,2,32,512]{3,2,1,0:T(8,128)(2,1)} %bitcast.92), calls=%async_computation.3 | async-start | bytes 1048576 | tf_op jit(solution)/shard_map/all_to_all | solution.py:679
  109.8 3.4 %copy-done.3 = bf16[64,16,32,64]{3,2,1,0:T(8,128)(2,1)S(1)} copy-done((bf16[64,16,32,64]{3,2,1,0:T(8,128)(2,1)S(1)}, bf16[64,16,32,64]{3,2,1,0:T(8,128)(2,1)}, u32[]{:S(2)}) %copy-start.3) | copy-done | bytes 4194328
  113.2 3.4 %spatial_first.1.after_and_out_0_.target_ref = bf16[16,1024,128]{2,1,0:T(8,128)(2,1)S(1)} custom-call(bf16[64,16,32,64]{3,2,1,0:T(8,128)(2,1)S(1)} %copy-done.3, bf16[2,256,512]{2,1,0:T(8,128)(2,1)S(1)} %copy-done.5), custom_call_target="tpu_custom_call" | custom-call | bytes 28000000 | tf_op jit(solution)/shard_map/spatial_first/pallas_call | solution.py:352
  118.6 3.5 %all-to-all-done.3.second_ref = bf16[8,2,32,512]{3,2,1,0:T(8,128)(2,1)S(1)} async-done(((bf16[8,2,32,512]{3,2,1,0:T(8,128)(2,1)}), bf16[8,2,32,512]{3,2,1,0:T(8,128)(2,1)S(1)}, u32[]{:S(2)}, u32[]{:S(2)}) %all-to-all-start.3) | async-done | bytes 524320 | tf_op jit(solution)/shard_map/all_to_all | solution.py:679
  124.8 11.9 %all_to_all.25.latent_ref = bf16[4,64,1024]{2,1,0:T(8,128)(2,1)} all-to-all(bf16[4,64,1024]{2,1,0:T(8,128)(2,1)S(1)} %bitcast.94), channel_id=1, replica_groups=mesh['vox'=4,'dp'=8] {'vox'}, dimensions={0} | all-to-all | bytes 1048576 | tf_op jit(solution)/shard_map/all_to_all | solution.py:699
  136.7 29.3 %decoder.1 = (bf16[16,1024,128]{2,1,0:T(8,128)(2,1)}, bf16[2048,256]{1,0:T(8,128)(2,1)}, bf16[2048,256]{1,0:T(8,128)(2,1)}, bf16[1280,256]{1,0:T(8,128)(2,1)}, b...) custom-call(s32[1]{0:T(128)} %bitcast.side_ref, ...), custom_call_target="tpu_custom_call" | custom-call | tf_op jit(solution)/shard_map/decoder/pallas_call | solution.py:297
  178.6 5.4 %sample_first.1 = bf16[64,16,32,64]{3,2,1,0:T(8,128)(2,1)} custom-call(bf16[16,1024,128]{2,1,0:T(8,128)(2,1)S(1)} %copy-done.6, bf16[2048,256]{1,0:T(8,128)(2,1)S(1)} %collective-permute-done.6.after_ref), custom_call_target="tpu_custom_call" | custom-call | bytes 28000000 | tf_op jit(solution)/shard_map/sample_first/pallas_call | solution.py:383
  192.8 6.1 %collective-permute-done.11 = bf16[832,256]{1,0:T(8,128)(2,1)S(1)} collective-permute-done((bf16[832,256]{1,0:T(8,128)(2,1)S(1)}, bf16[832,256]{1,0:T(8,128)(2,1)S(1)}, u32[]{:S(2)}, u32[]{:S(2)}) %collective-permute-start.11) | collective-permute-done | bytes 426016 | tf_op jit(solution)/shard_map/ppermute | solution.py:575
  200.8 4.8 %collective-permute-done.12 = bf16[512,256]{1,0:T(8,128)(2,1)S(1)} collective-permute-done((bf16[512,256]{1,0:T(8,128)(2,1)S(1)}, bf16[512,256]{1,0:T(8,128)(2,1)S(1)}, u32[]{:S(2)}, u32[]{:S(2)}) %collective-permute-start.12) | collective-permute-done | bytes 262176 | tf_op jit(solution)/shard_map/ppermute | solution.py:575
  206.6 10.5 %collective-permute-done.14 = bf16[336,256]{1,0:T(8,128)(2,1)S(1)} collective-permute-done((bf16[336,256]{1,0:T(8,128)(2,1)S(1)}, bf16[336,256]{1,0:T(8,128)(2,1)S(1)}, u32[]{:S(2)}, u32[]{:S(2)}) %collective-permute-start.14) | collective-permute-done | bytes 172064 | tf_op jit(solution)/shard_map/ppermute | solution.py:575
  217.4 6.8 %collective-permute-done.15 = bf16[336,256]{1,0:T(8,128)(2,1)S(1)} collective-permute-done((bf16[336,256]{1,0:T(8,128)(2,1)S(1)}, bf16[336,256]{1,0:T(8,128)(2,1)S(1)}, u32[]{:S(2)}, u32[]{:S(2)}) %collective-permute-start.15) | collective-permute-done | bytes 172064 | tf_op jit(solution)/shard_map/ppermute | solution.py:575
  225.4 4.3 %collective-permute-done.17 = bf16[160,256]{1,0:T(8,128)(2,1)S(1)} collective-permute-done((bf16[160,256]{1,0:T(8,128)(2,1)S(1)}, bf16[160,256]{1,0:T(8,128)(2,1)S(1)}, u32[]{:S(2)}, u32[]{:S(2)}) %collective-permute-start.17) | collective-permute-done | bytes 81952 | tf_op jit(solution)/shard_map/ppermute | solution.py:575
  233.2 4.5 %collective-permute-done.18 = bf16[512,256]{1,0:T(8,128)(2,1)S(1)} collective-permute-done((bf16[512,256]{1,0:T(8,128)(2,1)S(1)}, bf16[512,256]{1,0:T(8,128)(2,1)S(1)}, u32[]{:S(2)}, u32[]{:S(2)}) %collective-permute-start.18) | collective-permute-done | bytes 262176 | tf_op jit(solution)/shard_map/ppermute | solution.py:575
  237.8 6.7 %collective-permute-done.19 = bf16[832,256]{1,0:T(8,128)(2,1)S(1)} collective-permute-done((bf16[832,256]{1,0:T(8,128)(2,1)S(1)}, bf16[832,256]{1,0:T(8,128)(2,1)S(1)}, u32[]{:S(2)}, u32[]{:S(2)}) %collective-permute-start.19) | collective-permute-done | bytes 426016 | tf_op jit(solution)/shard_map/ppermute | solution.py:575
  247.3 4.3 %collective-permute-done.22 = bf16[640,256]{1,0:T(8,128)(2,1)S(1)} collective-permute-done((bf16[640,256]{1,0:T(8,128)(2,1)S(1)}, bf16[640,256]{1,0:T(8,128)(2,1)S(1)}, u32[]{:S(2)}, u32[]{:S(2)}) %collective-permute-start.22) | collective-permute-done | bytes 327712 | tf_op jit(solution)/shard_map/ppermute | solution.py:575
  255.8 4.5 %collective-permute-done.25.other_c = bf16[1280,256]{1,0:T(8,128)(2,1)S(1)} collective-permute-done((bf16[1280,256]{1,0:T(8,128)(2,1)S(1)}, bf16[1280,256]{1,0:T(8,128)(2,1)S(1)}, u32[]{:S(2)}, u32[]{:S(2)}) %collective-permute-start.25) | collective-permute-done | bytes 655392 | tf_op jit(solution)/shard_map/ppermute | solution.py:575
  260.3 3.0 %finish_gradients.1 = (bf16[8192,256]{1,0:T(8,128)(2,1)}, bf16[4096,128]{1,0:T(8,128)(2,1)}, bf16[64,2048]{1,0:T(8,128)(2,1)}) custom-call(s32[1]{0:T(128)} %bitcast.side_ref, bf16[2048,256]{1,0:T(8,128)(2,1)S(1)} %constant_dynamic-update-slice_fusion.4.own_a, bf16[2048,256]{1,0:T(8,128)(2,1)S(1)} %constant_dynamic-update-slice_fusion.3.own_b, ...), custom_call_target="tpu_custom_call" | custom-call | tf_op jit(solution)/shard_map/finish_gradients/pallas_call | solution.py:535
  (139 shorter events, 53.5 us)
Async XLA Ops:
  3.9 33.1 %all-to-all-start = ((bf16[8,32,2048]{2,1,0:T(8,128)(2,1)}), bf16[8,32,2048]{2,1,0:T(8,128)(2,1)S(1)}, u32[]{:S(2)}, u32[]{:S(2)}) async-start(bf16[8,32,2048]{2,1,0:T(8,128)(2,1)} %bitcast.106), calls=%async_computation | async-start | bytes 2097152 | tf_op jit(solution)/shard_map/all_to_all | solution.py:651
  37.0 29.5 %all-to-all-start.2 = ((bf16[8,32,2048]{2,1,0:T(8,128)(2,1)}), bf16[8,32,2048]{2,1,0:T(8,128)(2,1)S(1)}, u32[]{:S(2)}, u32[]{:S(2)}) async-start(bf16[8,32,2048]{2,1,0:T(8,128)(2,1)} %bitcast.105), calls=%async_computation.2 | async-start | bytes 2097152 | tf_op jit(solution)/shard_map/all_to_all | solution.py:651
  46.4 4.0 %collective-permute-start = (bf16[4,256,512]{2,1,0:T(8,128)(2,1)}, bf16[4,256,512]{2,1,0:T(8,128)(2,1)S(1)}, u32[]{:S(2)}, u32[]{:S(2)}) collective-permute-start(bf16[4,256,512]{2,1,0:T(8,128)(2,1)} %project_rows.6.after_and_out_0_), channel_id=1, source_target_pairs={{0,8},{8,0},{16,24},{24,16},{1,9},{9,1},{17,25},{25,17},{2,10},{10... | collective-permute-start | bytes 3145736 | tf_op jit(solution)/shard_map/ppermute | solution.py:575
  51.7 14.9 %collective-permute-start.1 = (bf16[2,256,512]{2,1,0:T(8,128)(2,1)S(1)}, bf16[2,256,512]{2,1,0:T(8,128)(2,1)S(1)}, u32[]{:S(2)}, u32[]{:S(2)}) collective-permute-start(bf16[2,256,512]{2,1,0:T(8,128)(2,1)S(1)} %add_convert_fusion.5.after_and_out_0_), channel_id=1, source_target_pairs={{0,16},{8,24},{16,0},{24,8},{1,17},{9,25},{17,1},{25,9},{2,18},{10... | collective-permute-start | bytes 1572872 | tf_op jit(solution)/shard_map/ppermute | solution.py:575
  73.5 11.4 %collective-permute-start.2 = (bf16[4,256,512]{2,1,0:T(8,128)(2,1)}, bf16[4,256,512]{2,1,0:T(8,128)(2,1)}, u32[]{:S(2)}, u32[]{:S(2)}) collective-permute-start(bf16[4,256,512]{2,1,0:T(8,128)(2,1)} %project_rows.9.after_and_out_0_), channel_id=1, source_target_pairs={{0,8},{8,0},{16,24},{24,16},{1,9},{9,1},{17,25},{25,17},{2,10},{10... | collective-permute-start | bytes 3145736 | tf_op jit(solution)/shard_map/ppermute | solution.py:575
  75.6 20.3 %all-to-all-start.1 = ((bf16[8,2,32,512]{3,2,1,0:T(8,128)(2,1)}), bf16[8,2,32,512]{3,2,1,0:T(8,128)(2,1)S(1)}, u32[]{:S(2)}, u32[]{:S(2)}) async-start(bf16[8,2,32,512]{3,2,1,0:T(8,128)(2,1)} %bitcast.93), calls=%async_computation.1 | async-start | bytes 1048576 | tf_op jit(solution)/shard_map/all_to_all | solution.py:679
  86.2 14.1 %collective-permute-start.3 = (bf16[2,256,512]{2,1,0:T(8,128)(2,1)S(1)}, bf16[2,256,512]{2,1,0:T(8,128)(2,1)S(1)}, u32[]{:S(2)}, u32[]{:S(2)}) collective-permute-start(bf16[2,256,512]{2,1,0:T(8,128)(2,1)S(1)} %add_convert_fusion.3.after_and_out_0_.after_ref), channel_id=1, source_target_pairs={{0,16},{8,24},{16,0},{24,8},{1,17},{9,25},{17,1},{25,9},{2,18},{10... | collective-permute-start | bytes 1572872 | tf_op jit(solution)/shard_map/ppermute | solution.py:575
  102.6 19.5 %all-to-all-start.3 = ((bf16[8,2,32,512]{3,2,1,0:T(8,128)(2,1)}), bf16[8,2,32,512]{3,2,1,0:T(8,128)(2,1)S(1)}, u32[]{:S(2)}, u32[]{:S(2)}) async-start(bf16[8,2,32,512]{3,2,1,0:T(8,128)(2,1)} %bitcast.92), calls=%async_computation.3 | async-start | bytes 1048576 | tf_op jit(solution)/shard_map/all_to_all | solution.py:679
  108.6 13.5 %copy-start.7 = (bf16[2,256,256]{2,1,0:T(8,128)(2,1)}, bf16[2,256,256]{2,1,0:T(8,128)(2,1)S(1)}, u32[]{:S(2)}) copy-start(bf16[2,256,256]{2,1,0:T(8,128)(2,1)S(1)} %pad_maximum_fusion.12.after_and_out_2_.w_three_ref) | copy-start | bytes 786436
  113.2 9.0 %copy-start.9 = (bf16[256,256]{1,0:T(8,128)(2,1)S(1)}, bf16[256,256]{1,0:T(8,128)(2,1)}, u32[]{:S(2)}) copy-start(bf16[256,256]{1,0:T(8,128)(2,1)} %get-tuple-element.49.place_b_ref) | copy-start | bytes 393220
  166.0 2.9 %collective-permute-start.4 = (bf16[2048,256]{1,0:T(8,128)(2,1)}, bf16[2048,256]{1,0:T(8,128)(2,1)S(1)}, u32[]{:S(2)}, u32[]{:S(2)}) collective-permute-start(bf16[2048,256]{1,0:T(8,128)(2,1)} %get-tuple-element.55), channel_id=1, source_target_pairs={{0,8},{8,0},{16,24},{24,16},{1,9},{9,1},{17,25},{25,17},{2,10},{10... | collective-permute-start | bytes 3145736 | tf_op jit(solution)/shard_map/ppermute | solution.py:575
  166.1 5.4 %collective-permute-start.6 = (bf16[2048,256]{1,0:T(8,128)(2,1)}, bf16[2048,256]{1,0:T(8,128)(2,1)S(1)}, u32[]{:S(2)}, u32[]{:S(2)}) collective-permute-start(bf16[2048,256]{1,0:T(8,128)(2,1)} %get-tuple-element.57), channel_id=1, source_target_pairs={{0,8},{8,0},{16,24},{24,16},{1,9},{9,1},{17,25},{25,17},{2,10},{10... | collective-permute-start | bytes 3145736 | tf_op jit(solution)/shard_map/ppermute | solution.py:575
  166.6 7.4 %collective-permute-start.8 = (bf16[1280,256]{1,0:T(8,128)(2,1)}, bf16[1280,256]{1,0:T(8,128)(2,1)}, u32[]{:S(2)}, u32[]{:S(2)}) collective-permute-start(bf16[1280,256]{1,0:T(8,128)(2,1)} %get-tuple-element.59), channel_id=1, source_target_pairs={{0,8},{8,0},{16,24},{24,16},{1,9},{9,1},{17,25},{25,17},{2,10},{10... | collective-permute-start | bytes 1966088 | tf_op jit(solution)/shard_map/ppermute | solution.py:575
  171.2 14.7 %collective-permute-start.5 = (bf16[1024,256]{1,0:T(8,128)(2,1)}, bf16[1024,256]{1,0:T(8,128)(2,1)}, u32[]{:S(2)}, u32[]{:S(2)}) collective-permute-start(bf16[1024,256]{1,0:T(8,128)(2,1)} %get-tuple-element.95), channel_id=1, source_target_pairs={{0,16},{8,24},{16,0},{24,8},{1,17},{9,25},{17,1},{25,9},{2,18},{10... | collective-permute-start | bytes 1572872 | tf_op jit(solution)/shard_map/ppermute | solution.py:575
  172.6 14.1 %collective-permute-start.7 = (bf16[1024,256]{1,0:T(8,128)(2,1)}, bf16[1024,256]{1,0:T(8,128)(2,1)}, u32[]{:S(2)}, u32[]{:S(2)}) collective-permute-start(bf16[1024,256]{1,0:T(8,128)(2,1)} %get-tuple-element.93), channel_id=1, source_target_pairs={{0,1},{1,0},{2,3},{3,2},{4,5},{5,4},{6,7},{7,6},{8,9},{9,8},{10,11... | collective-permute-start | bytes 1572872 | tf_op jit(solution)/shard_map/ppermute | solution.py:575
  176.4 9.5 %collective-permute-start.9 = (bf16[640,256]{1,0:T(8,128)(2,1)}, bf16[640,256]{1,0:T(8,128)(2,1)S(1)}, u32[]{:S(2)}, u32[]{:S(2)}) collective-permute-start(bf16[640,256]{1,0:T(8,128)(2,1)} %get-tuple-element.100), channel_id=1, source_target_pairs={{0,2},{1,3},{2,0},{3,1},{4,6},{5,7},{6,4},{7,5},{8,10},{9,11},{10,... | collective-permute-start | bytes 983048 | tf_op jit(solution)/shard_map/ppermute | solution.py:575
  188.0 10.9 %collective-permute-start.11 = (bf16[832,256]{1,0:T(8,128)(2,1)S(1)}, bf16[832,256]{1,0:T(8,128)(2,1)S(1)}, u32[]{:S(2)}, u32[]{:S(2)}) collective-permute-start(bf16[832,256]{1,0:T(8,128)(2,1)S(1)} %pad_maximum_fusion.6), channel_id=1, source_target_pairs={{0,16},{8,24},{16,0},{24,8},{1,17},{9,25},{17,1},{25,9},{2,18},{10... | collective-permute-start | bytes 1277960 | tf_op jit(solution)/shard_map/ppermute | solution.py:575
  191.4 7.5 %collective-permute-start.10 = (bf16[512,256]{1,0:T(8,128)(2,1)}, bf16[512,256]{1,0:T(8,128)(2,1)S(1)}, u32[]{:S(2)}, u32[]{:S(2)}) collective-permute-start(bf16[512,256]{1,0:T(8,128)(2,1)} %get-tuple-element.97), channel_id=1, source_target_pairs={{0,1},{1,0},{2,3},{3,2},{4,5},{5,4},{6,7},{7,6},{8,9},{9,8},{10,11... | collective-permute-start | bytes 786440 | tf_op jit(solution)/shard_map/ppermute | solution.py:575
  199.1 6.5 %collective-permute-start.12 = (bf16[512,256]{1,0:T(8,128)(2,1)S(1)}, bf16[512,256]{1,0:T(8,128)(2,1)S(1)}, u32[]{:S(2)}, u32[]{:S(2)}) collective-permute-start(bf16[512,256]{1,0:T(8,128)(2,1)S(1)} %pad_maximum_fusion.13), channel_id=1, source_target_pairs={{0,2},{1,3},{2,0},{3,1},{4,6},{5,7},{6,4},{7,5},{8,10},{9,11},{10,... | collective-permute-start | bytes 786440 | tf_op jit(solution)/shard_map/ppermute | solution.py:575
  199.9 5.7 %collective-permute-start.13 = (bf16[160,256]{1,0:T(8,128)(2,1)S(1)}, bf16[160,256]{1,0:T(8,128)(2,1)S(1)}, u32[]{:S(2)}, u32[]{:S(2)}) collective-permute-start(bf16[160,256]{1,0:T(8,128)(2,1)S(1)} %get-tuple-element.140), channel_id=1, source_target_pairs={{0,1},{1,0},{2,3},{3,2},{4,5},{5,4},{6,7},{7,6},{8,9},{9,8},{10,11... | collective-permute-start | bytes 245768 | tf_op jit(solution)/shard_map/ppermute | solution.py:575
  205.7 11.4 %collective-permute-start.14 = (bf16[336,256]{1,0:T(8,128)(2,1)S(1)}, bf16[336,256]{1,0:T(8,128)(2,1)S(1)}, u32[]{:S(2)}, u32[]{:S(2)}) collective-permute-start(bf16[336,256]{1,0:T(8,128)(2,1)S(1)} %pad_maximum_fusion.14), channel_id=1, source_target_pairs={{0,4},{1,5},{2,6},{3,7},{4,0},{5,1},{6,2},{7,3},{8,12},{9,13},{10,... | collective-permute-start | bytes 516104 | tf_op jit(solution)/shard_map/ppermute | solution.py:575
  217.3 6.9 %collective-permute-start.15 = (bf16[336,256]{1,0:T(8,128)(2,1)S(1)}, bf16[336,256]{1,0:T(8,128)(2,1)S(1)}, u32[]{:S(2)}, u32[]{:S(2)}) collective-permute-start(bf16[336,256]{1,0:T(8,128)(2,1)S(1)} %pad_maximum_fusion.15), channel_id=1, source_target_pairs={{0,4},{1,5},{2,6},{3,7},{4,0},{5,1},{6,2},{7,3},{8,12},{9,13},{10,... | collective-permute-start | bytes 516104 | tf_op jit(solution)/shard_map/ppermute | solution.py:575
  224.3 6.4 %collective-permute-start.16 = (bf16[512,256]{1,0:T(8,128)(2,1)S(1)}, bf16[512,256]{1,0:T(8,128)(2,1)S(1)}, u32[]{:S(2)}, u32[]{:S(2)}) collective-permute-start(bf16[512,256]{1,0:T(8,128)(2,1)S(1)} %get-tuple-element.151), channel_id=1, source_target_pairs={{0,2},{1,3},{2,0},{3,1},{4,6},{5,7},{6,4},{7,5},{8,10},{9,11},{10,... | collective-permute-start | bytes 786440 | tf_op jit(solution)/shard_map/ppermute | solution.py:575
  224.4 5.3 %collective-permute-start.17 = (bf16[160,256]{1,0:T(8,128)(2,1)S(1)}, bf16[160,256]{1,0:T(8,128)(2,1)S(1)}, u32[]{:S(2)}, u32[]{:S(2)}) collective-permute-start(bf16[160,256]{1,0:T(8,128)(2,1)S(1)} %slice_dynamic-update-slice_fusion.6), channel_id=1, source_target_pairs={{0,1},{1,0},{2,3},{3,2},{4,5},{5,4},{6,7},{7,6},{8,9},{9,8},{10,11... | collective-permute-start | bytes 245768 | tf_op jit(solution)/shard_map/ppermute | solution.py:575
  230.7 7.0 %collective-permute-start.18 = (bf16[512,256]{1,0:T(8,128)(2,1)S(1)}, bf16[512,256]{1,0:T(8,128)(2,1)S(1)}, u32[]{:S(2)}, u32[]{:S(2)}) collective-permute-start(bf16[512,256]{1,0:T(8,128)(2,1)S(1)} %get-tuple-element.80), channel_id=1, source_target_pairs={{0,1},{1,0},{2,3},{3,2},{4,5},{5,4},{6,7},{7,6},{8,9},{9,8},{10,11... | collective-permute-start | bytes 786440 | tf_op jit(solution)/shard_map/ppermute | solution.py:575
  231.8 12.6 %collective-permute-start.19 = (bf16[832,256]{1,0:T(8,128)(2,1)S(1)}, bf16[832,256]{1,0:T(8,128)(2,1)S(1)}, u32[]{:S(2)}, u32[]{:S(2)}) collective-permute-start(bf16[832,256]{1,0:T(8,128)(2,1)S(1)} %pad_maximum_fusion.7), channel_id=1, source_target_pairs={{0,16},{8,24},{16,0},{24,8},{1,17},{9,25},{17,1},{25,9},{2,18},{10... | collective-permute-start | bytes 1277960 | tf_op jit(solution)/shard_map/ppermute | solution.py:575
  244.5 7.1 %collective-permute-start.22 = (bf16[640,256]{1,0:T(8,128)(2,1)S(1)}, bf16[640,256]{1,0:T(8,128)(2,1)S(1)}, u32[]{:S(2)}, u32[]{:S(2)}) collective-permute-start(bf16[640,256]{1,0:T(8,128)(2,1)S(1)} %slice_dynamic-update-slice_fusion.1), channel_id=1, source_target_pairs={{0,2},{1,3},{2,0},{3,1},{4,6},{5,7},{6,4},{7,5},{8,10},{9,11},{10,... | collective-permute-start | bytes 983048 | tf_op jit(solution)/shard_map/ppermute | solution.py:575
  244.6 9.2 %collective-permute-start.20 = (bf16[1024,256]{1,0:T(8,128)(2,1)S(1)}, bf16[1024,256]{1,0:T(8,128)(2,1)S(1)}, u32[]{:S(2)}, u32[]{:S(2)}) collective-permute-start(bf16[1024,256]{1,0:T(8,128)(2,1)S(1)} %constant_dynamic-update-slice_fusion.2), channel_id=1, source_target_pairs={{0,16},{8,24},{16,0},{24,8},{1,17},{9,25},{17,1},{25,9},{2,18},{10... | collective-permute-start | bytes 1572872 | tf_op jit(solution)/shard_map/ppermute | solution.py:575
  246.0 9.2 %collective-permute-start.21 = (bf16[1024,256]{1,0:T(8,128)(2,1)S(1)}, bf16[1024,256]{1,0:T(8,128)(2,1)S(1)}, u32[]{:S(2)}, u32[]{:S(2)}) collective-permute-start(bf16[1024,256]{1,0:T(8,128)(2,1)S(1)} %slice_dynamic-update-slice_fusion), channel_id=1, source_target_pairs={{0,1},{1,0},{2,3},{3,2},{4,5},{5,4},{6,7},{7,6},{8,9},{9,8},{10,11... | collective-permute-start | bytes 1572872 | tf_op jit(solution)/shard_map/ppermute | solution.py:575
  255.2 5.2 %collective-permute-start.23 = (bf16[2048,256]{1,0:T(8,128)(2,1)S(1)}, bf16[2048,256]{1,0:T(8,128)(2,1)S(1)}, u32[]{:S(2)}, u32[]{:S(2)}) collective-permute-start(bf16[2048,256]{1,0:T(8,128)(2,1)S(1)} %constant_dynamic-update-slice_fusion.4.own_a), channel_id=1, source_target_pairs={{0,8},{8,0},{16,24},{24,16},{1,9},{9,1},{17,25},{25,17},{2,10},{10... | collective-permute-start | bytes 3145736 | tf_op jit(solution)/shard_map/ppermute | solution.py:575
  255.3 5.1 %collective-permute-start.24 = (bf16[2048,256]{1,0:T(8,128)(2,1)S(1)}, bf16[2048,256]{1,0:T(8,128)(2,1)S(1)}, u32[]{:S(2)}, u32[]{:S(2)}) collective-permute-start(bf16[2048,256]{1,0:T(8,128)(2,1)S(1)} %constant_dynamic-update-slice_fusion.3.own_b), channel_id=1, source_target_pairs={{0,8},{8,0},{16,24},{24,16},{1,9},{9,1},{17,25},{25,17},{2,10},{10... | collective-permute-start | bytes 3145736 | tf_op jit(solution)/shard_map/ppermute | solution.py:575
  255.8 4.6 %collective-permute-start.25 = (bf16[1280,256]{1,0:T(8,128)(2,1)S(1)}, bf16[1280,256]{1,0:T(8,128)(2,1)S(1)}, u32[]{:S(2)}, u32[]{:S(2)}) collective-permute-start(bf16[1280,256]{1,0:T(8,128)(2,1)S(1)} %constant_dynamic-update-slice_fusion.1.own_c), channel_id=1, source_target_pairs={{0,8},{8,0},{16,24},{24,16},{1,9},{9,1},{17,25},{25,17},{2,10},{10... | collective-permute-start | bytes 1966088 | tf_op jit(solution)/shard_map/ppermute | solution.py:575
  (17 other events, 70.6 us)

commit v6 on v5

--- a/solution.py
+++ b/solution.py
@@ -714,7 +714,8 @@
     shares = [summed(terms).astype(jnp.bfloat16) for terms in parts]
     for stage in reversed(range(len(routes[0]))):
         shares = over_chains(gathered, shares, [route[stage] for route in routes])
-        shares = list(lax.optimization_barrier(tuple(shares)))
+        if stage > 1:
+            shares = list(lax.optimization_barrier(tuple(shares)))
     others = [exchanged(values, vox_bits[:1], 1) for values in shares]
     total_first, total_second, third = finished(side, shares, others, third_rows)
     total_third = third.T

time: 264 us -> 261 us (0.989)
  waiting for transfers between devices: 105 us -> 101 us
    ppermute x26, waiting for transfers between devices: 66.4 us -> 62.3 us  [exchanged(): lax.ppermute(values, axis, [(at, at ^ flip) for at in range(lax.axis_size...]
  transfers between devices with their start and end apart: 30 -> 30, of which waited for: 20 -> 19; matrix products, arithmetic and copies ran while one was open for 5% -> 5% of each run, Pallas kernels for 13% -> 13%
where the time goes in v6:
time: 261 us; the launch traced here: 260 us
  waiting for transfers between devices  101 us (39%)
  Pallas kernels  76.1 us (29%)
  starting transfers between devices  40.1 us (15%)
  other arithmetic  15.1 us (6%)
  local copies, waits for them, and re-layouts  14.1 us (5%)
  blocking collectives  11.9 us (5%)
    ppermute x26, waiting for transfers between devices, exchanged(): lax.ppermute(values, axis, [(at, at ^ flip) for at in range(lax.axis_size...  62.3 us
    all_to_all x2, waiting for transfers between devices, routed(): lax.all_to_all(sent, 'dp', split_axis=0, concat_axis=0, tiled=True)  31.8 us
    pallas_call x1, Pallas kernels, decoder(): pl.pallas_call(functools.partial(decoder_kernel, count), name='decoder',...  29.3 us
    pallas_call x6, Pallas kernels, projected(): pl.pallas_call(project_kernel, name='project_rows', grid_spec=pltpu.Prefe...  27.9 us
    ppermute x26, starting transfers between devices, exchanged(): lax.ppermute(values, axis, [(at, at ^ flip) for at in range(lax.axis_size...  18.3 us
    unnamed x39, local copies, waits for them, and re-layouts  12 us
    all_to_all x1, blocking collectives, shards(): lax.all_to_all(own_rows, 'vox', split_axis=0, concat_axis=0, tiled=True)  11.9 us
    all_to_all x2, starting transfers between devices, returned(): return lax.all_to_all(sent, 'dp', split_axis=0, concat_axis=0, tiled=True)  10.9 us
  transfers between devices with their start and end apart: 30, of which 19 were waited for; matrix products, arithmetic and copies ran while one was open for 5% of the time, Pallas kernels for 13%

profile of v6, /device:TPU:0, one launch (start us, length us, event | category | flops | bytes accessed | tf_op | source)
XLA Modules:
  0.0 259.7 jit_solution(9284947869513126086)
XLA Ops:
  0.6 3.3 %bucket_rows.2 = (bf16[256,2048]{1,0:T(8,128)(2,1)}, bf16[256,256]{1,0:T(8,128)(2,1)}) custom-call(s32[1,256]{1,0:T(1,128)} %bitcast.107, s32[8]{0:T(128)} %after_and_out_0_.1, s32[1]{0:T(128)} %bitcast.2.shift_ref, bf16[256,2048]{1,0:T(8,128)(2,1)} %fmri_ref.3, s32[8]{0:T(128)} %after_and_out_0_.1), custom_call_target="tpu_custom_call" | custom-call | tf_op jit(solution)/shard_map/bucket_rows/pallas_call | solution.py:428
  3.9 7.3 %all-to-all-start = ((bf16[8,32,2048]{2,1,0:T(8,128)(2,1)}), bf16[8,32,2048]{2,1,0:T(8,128)(2,1)S(1)}, u32[]{:S(2)}, u32[]{:S(2)}) async-start(bf16[8,32,2048]{2,1,0:T(8,128)(2,1)} %bitcast.106), calls=%async_computation | async-start | bytes 2097152 | tf_op jit(solution)/shard_map/all_to_all | solution.py:651
  11.2 3.3 %bucket_rows.3 = (bf16[256,2048]{1,0:T(8,128)(2,1)}, bf16[256,256]{1,0:T(8,128)(2,1)}) custom-call(s32[1,256]{1,0:T(1,128)} %bitcast.108, s32[8]{0:T(128)} %after_and_out_0_.1, s32[1]{0:T(128)} %bitcast.2.shift_ref, bf16[256,2048]{1,0:T(8,128)(2,1)} %fmri_ref.3, bf16[256,256]{1,0:T(8,128)(2,1)} %get-tuple-element.42.after_ref.place_a_ref), custom_call_target="tpu_custom_call" | custom-call | tf_op jit(solution)/shard_map/bucket_rows/pallas_call | solution.py:428
  14.5 22.5 %all-to-all-done = bf16[8,32,2048]{2,1,0:T(8,128)(2,1)S(1)} async-done(((bf16[8,32,2048]{2,1,0:T(8,128)(2,1)}), bf16[8,32,2048]{2,1,0:T(8,128)(2,1)S(1)}, u32[]{:S(2)}, u32[]{:S(2)}) %all-to-all-start) | async-done | bytes 1048608 | tf_op jit(solution)/shard_map/all_to_all | solution.py:651
  37.0 3.6 %all-to-all-start.2 = ((bf16[8,32,2048]{2,1,0:T(8,128)(2,1)}), bf16[8,32,2048]{2,1,0:T(8,128)(2,1)S(1)}, u32[]{:S(2)}, u32[]{:S(2)}) async-start(bf16[8,32,2048]{2,1,0:T(8,128)(2,1)} %bitcast.105), calls=%async_computation.2 | async-start | bytes 2097152 | tf_op jit(solution)/shard_map/all_to_all | solution.py:651
  40.6 5.9 %project_rows.6.after_and_out_0_ = bf16[4,256,512]{2,1,0:T(8,128)(2,1)} custom-call(s32[1]{0:T(128)} %bitcast.7.quarter_ref, bf16[256,2048]{1,0:T(8,128)(2,1)} %bitcast.98, bf16[1,2048,4096]{2,1,0:T(8,128)(2,1)} %map_ref.11, s32[8]{0:T(128)} %after_and_out_0_.1), custom_call_target="tpu_custom_call" | custom-call | flops 2147483648 | bytes 8388608 | tf_op jit(solution)/shard_map/project_rows/pallas_call | solution.py:455
  46.4 4.0 %project_rows.7 = bf16[2,256,512]{2,1,0:T(8,128)(2,1)} custom-call(s32[1]{0:T(128)} %bitcast.6.quarter_ref, bf16[256,2048]{1,0:T(8,128)(2,1)} %bitcast.99, bf16[1,2048,4096]{2,1,0:T(8,128)(2,1)} %map_ref.11, bf16[4,256,512]{2,1,0:T(8,128)(2,1)} %project_rows.6.after_and_out_0_), custom_call_target="tpu_custom_call" | custom-call | flops 1073741824 | bytes 4194304 | tf_op jit(solution)/shard_map/project_rows/pallas_call | solution.py:455
  53.2 4.0 %project_rows.8.after_and_out_1_ = bf16[2,256,512]{2,1,0:T(8,128)(2,1)} custom-call(s32[1]{0:T(128)} %bitcast.3.quarter_ref, bf16[256,2048]{1,0:T(8,128)(2,1)} %bitcast.100, bf16[1,2048,4096]{2,1,0:T(8,128)(2,1)} %map_ref.11, bf16[2,256,512]{2,1,0:T(8,128)(2,1)} %copy-done.15), custom_call_target="tpu_custom_call" | custom-call | flops 1073741824 | bytes 4194304 | tf_op jit(solution)/shard_map/project_rows/pallas_call | solution.py:455
  57.2 9.3 %all-to-all-done.2 = bf16[8,32,2048]{2,1,0:T(8,128)(2,1)S(1)} async-done(((bf16[8,32,2048]{2,1,0:T(8,128)(2,1)}), bf16[8,32,2048]{2,1,0:T(8,128)(2,1)S(1)}, u32[]{:S(2)}, u32[]{:S(2)}) %all-to-all-start.2) | async-done | bytes 1048608 | tf_op jit(solution)/shard_map/all_to_all | solution.py:651
  67.7 5.9 %project_rows.9.after_and_out_0_ = bf16[4,256,512]{2,1,0:T(8,128)(2,1)} custom-call(s32[1]{0:T(128)} %bitcast.7.quarter_ref, bf16[256,2048]{1,0:T(8,128)(2,1)} %bitcast.95, bf16[1,2048,4096]{2,1,0:T(8,128)(2,1)} %map_ref.11, bf16[2,256,512]{2,1,0:T(8,128)(2,1)} %copy-done.14, bf16[2,256,512]{2,1,0:T(8,128)(2,1)} %project_rows.8.after_and_out_1_), custom_call_target="tpu_custom_call" | custom-call | flops 2147483648 | bytes 8388608 | tf_op jit(solution)/shard_map/project_rows/pallas_call | solution.py:455
  75.6 5.2 %all-to-all-start.1 = ((bf16[8,2,32,512]{3,2,1,0:T(8,128)(2,1)}), bf16[8,2,32,512]{3,2,1,0:T(8,128)(2,1)S(1)}, u32[]{:S(2)}, u32[]{:S(2)}) async-start(bf16[8,2,32,512]{3,2,1,0:T(8,128)(2,1)} %bitcast.93), calls=%async_computation.1 | async-start | bytes 1048576 | tf_op jit(solution)/shard_map/all_to_all | solution.py:679
  80.8 4.1 %project_rows.10 = bf16[2,256,512]{2,1,0:T(8,128)(2,1)} custom-call(s32[1]{0:T(128)} %bitcast.6.quarter_ref, bf16[256,2048]{1,0:T(8,128)(2,1)} %bitcast.96, bf16[1,2048,4096]{2,1,0:T(8,128)(2,1)} %map_ref.11, bf16[4,256,512]{2,1,0:T(8,128)(2,1)} %project_rows.9.after_and_out_0_), custom_call_target="tpu_custom_call" | custom-call | flops 1073741824 | bytes 4194304 | tf_op jit(solution)/shard_map/project_rows/pallas_call | solution.py:455
  88.1 4.0 %project_rows.11 = bf16[2,256,512]{2,1,0:T(8,128)(2,1)} custom-call(s32[1]{0:T(128)} %bitcast.3.quarter_ref, bf16[256,2048]{1,0:T(8,128)(2,1)} %bitcast.97, bf16[1,2048,4096]{2,1,0:T(8,128)(2,1)} %map_ref.11, bf16[2,256,512]{2,1,0:T(8,128)(2,1)} %copy-done.4), custom_call_target="tpu_custom_call" | custom-call | flops 1073741824 | bytes 4194304 | tf_op jit(solution)/shard_map/project_rows/pallas_call | solution.py:455
  92.1 3.8 %all-to-all-done.1.first_ref = bf16[8,2,32,512]{3,2,1,0:T(8,128)(2,1)S(1)} async-done(((bf16[8,2,32,512]{3,2,1,0:T(8,128)(2,1)}), bf16[8,2,32,512]{3,2,1,0:T(8,128)(2,1)S(1)}, u32[]{:S(2)}, u32[]{:S(2)}) %all-to-all-start.1) | async-done | bytes 524320 | tf_op jit(solution)/shard_map/all_to_all | solution.py:679
  96.0 4.4 %collective-permute-done.3 = bf16[2,256,512]{2,1,0:T(8,128)(2,1)S(1)} collective-permute-done((bf16[2,256,512]{2,1,0:T(8,128)(2,1)S(1)}, bf16[2,256,512]{2,1,0:T(8,128)(2,1)S(1)}, u32[]{:S(2)}, u32[]{:S(2)}) %collective-permute-start.3) | collective-permute-done | bytes 524320 | tf_op jit(solution)/shard_map/ppermute | solution.py:575
  102.6 5.7 %all-to-all-start.3 = ((bf16[8,2,32,512]{3,2,1,0:T(8,128)(2,1)}), bf16[8,2,32,512]{3,2,1,0:T(8,128)(2,1)S(1)}, u32[]{:S(2)}, u32[]{:S(2)}) async-start(bf16[8,2,32,512]{3,2,1,0:T(8,128)(2,1)} %bitcast.92), calls=%async_computation.3 | async-start | bytes 1048576 | tf_op jit(solution)/shard_map/all_to_all | solution.py:679
  109.8 3.4 %copy-done.3 = bf16[64,16,32,64]{3,2,1,0:T(8,128)(2,1)S(1)} copy-done((bf16[64,16,32,64]{3,2,1,0:T(8,128)(2,1)S(1)}, bf16[64,16,32,64]{3,2,1,0:T(8,128)(2,1)}, u32[]{:S(2)}) %copy-start.3) | copy-done | bytes 4194328
  113.2 3.4 %spatial_first.1.after_and_out_0_.target_ref = bf16[16,1024,128]{2,1,0:T(8,128)(2,1)S(1)} custom-call(bf16[64,16,32,64]{3,2,1,0:T(8,128)(2,1)S(1)} %copy-done.3, bf16[2,256,512]{2,1,0:T(8,128)(2,1)S(1)} %copy-done.5), custom_call_target="tpu_custom_call" | custom-call | bytes 28000000 | tf_op jit(solution)/shard_map/spatial_first/pallas_call | solution.py:352
  118.6 3.5 %all-to-all-done.3.second_ref = bf16[8,2,32,512]{3,2,1,0:T(8,128)(2,1)S(1)} async-done(((bf16[8,2,32,512]{3,2,1,0:T(8,128)(2,1)}), bf16[8,2,32,512]{3,2,1,0:T(8,128)(2,1)S(1)}, u32[]{:S(2)}, u32[]{:S(2)}) %all-to-all-start.3) | async-done | bytes 524320 | tf_op jit(solution)/shard_map/all_to_all | solution.py:679
  124.8 11.9 %all_to_all.25.latent_ref = bf16[4,64,1024]{2,1,0:T(8,128)(2,1)} all-to-all(bf16[4,64,1024]{2,1,0:T(8,128)(2,1)S(1)} %bitcast.94), channel_id=1, replica_groups=mesh['vox'=4,'dp'=8] {'vox'}, dimensions={0} | all-to-all | bytes 1048576 | tf_op jit(solution)/shard_map/all_to_all | solution.py:699
  136.7 29.3 %decoder.1 = (bf16[16,1024,128]{2,1,0:T(8,128)(2,1)}, bf16[2048,256]{1,0:T(8,128)(2,1)}, bf16[2048,256]{1,0:T(8,128)(2,1)}, bf16[1280,256]{1,0:T(8,128)(2,1)}, b...) custom-call(s32[1]{0:T(128)} %bitcast.side_ref, ...), custom_call_target="tpu_custom_call" | custom-call | tf_op jit(solution)/shard_map/decoder/pallas_call | solution.py:297
  178.6 5.4 %sample_first.1 = bf16[64,16,32,64]{3,2,1,0:T(8,128)(2,1)} custom-call(bf16[16,1024,128]{2,1,0:T(8,128)(2,1)S(1)} %copy-done.6, bf16[2048,256]{1,0:T(8,128)(2,1)S(1)} %collective-permute-done.6.after_ref), custom_call_target="tpu_custom_call" | custom-call | bytes 28000000 | tf_op jit(solution)/shard_map/sample_first/pallas_call | solution.py:383
  192.8 6.1 %collective-permute-done.11 = bf16[832,256]{1,0:T(8,128)(2,1)S(1)} collective-permute-done((bf16[832,256]{1,0:T(8,128)(2,1)S(1)}, bf16[832,256]{1,0:T(8,128)(2,1)S(1)}, u32[]{:S(2)}, u32[]{:S(2)}) %collective-permute-start.11) | collective-permute-done | bytes 426016 | tf_op jit(solution)/shard_map/ppermute | solution.py:575
  200.8 4.8 %collective-permute-done.12 = bf16[512,256]{1,0:T(8,128)(2,1)S(1)} collective-permute-done((bf16[512,256]{1,0:T(8,128)(2,1)S(1)}, bf16[512,256]{1,0:T(8,128)(2,1)S(1)}, u32[]{:S(2)}, u32[]{:S(2)}) %collective-permute-start.12) | collective-permute-done | bytes 262176 | tf_op jit(solution)/shard_map/ppermute | solution.py:575
  206.6 10.5 %collective-permute-done.14 = bf16[336,256]{1,0:T(8,128)(2,1)S(1)} collective-permute-done((bf16[336,256]{1,0:T(8,128)(2,1)S(1)}, bf16[336,256]{1,0:T(8,128)(2,1)S(1)}, u32[]{:S(2)}, u32[]{:S(2)}) %collective-permute-start.14) | collective-permute-done | bytes 172064 | tf_op jit(solution)/shard_map/ppermute | solution.py:575
  217.4 6.8 %collective-permute-done.15 = bf16[336,256]{1,0:T(8,128)(2,1)S(1)} collective-permute-done((bf16[336,256]{1,0:T(8,128)(2,1)S(1)}, bf16[336,256]{1,0:T(8,128)(2,1)S(1)}, u32[]{:S(2)}, u32[]{:S(2)}) %collective-permute-start.15) | collective-permute-done | bytes 172064 | tf_op jit(solution)/shard_map/ppermute | solution.py:575
  225.4 4.3 %collective-permute-done.17 = bf16[160,256]{1,0:T(8,128)(2,1)S(1)} collective-permute-done((bf16[160,256]{1,0:T(8,128)(2,1)S(1)}, bf16[160,256]{1,0:T(8,128)(2,1)S(1)}, u32[]{:S(2)}, u32[]{:S(2)}) %collective-permute-start.17) | collective-permute-done | bytes 81952 | tf_op jit(solution)/shard_map/ppermute | solution.py:575
  233.2 5.7 %collective-permute-done.18 = bf16[512,256]{1,0:T(8,128)(2,1)S(1)} collective-permute-done((bf16[512,256]{1,0:T(8,128)(2,1)S(1)}, bf16[512,256]{1,0:T(8,128)(2,1)S(1)}, u32[]{:S(2)}, u32[]{:S(2)}) %collective-permute-start.18) | collective-permute-done | bytes 262176 | tf_op jit(solution)/shard_map/ppermute | solution.py:575
  240.4 3.3 %collective-permute-done.20 = bf16[832,256]{1,0:T(8,128)(2,1)S(1)} collective-permute-done((bf16[832,256]{1,0:T(8,128)(2,1)S(1)}, bf16[832,256]{1,0:T(8,128)(2,1)S(1)}, u32[]{:S(2)}, u32[]{:S(2)}) %collective-permute-start.20) | collective-permute-done | bytes 426016 | tf_op jit(solution)/shard_map/ppermute | solution.py:575
  245.4 3.9 %collective-permute-done.19 = bf16[1024,256]{1,0:T(8,128)(2,1)S(1)} collective-permute-done((bf16[1024,256]{1,0:T(8,128)(2,1)S(1)}, bf16[1024,256]{1,0:T(8,128)(2,1)S(1)}, u32[]{:S(2)}, u32[]{:S(2)}) %collective-permute-start.19) | collective-permute-done | bytes 524320 | tf_op jit(solution)/shard_map/ppermute | solution.py:575
  249.5 3.5 %collective-permute-done.21 = bf16[1024,256]{1,0:T(8,128)(2,1)S(1)} collective-permute-done((bf16[1024,256]{1,0:T(8,128)(2,1)S(1)}, bf16[1024,256]{1,0:T(8,128)(2,1)S(1)}, u32[]{:S(2)}, u32[]{:S(2)}) %collective-permute-start.21) | collective-permute-done | bytes 524320 | tf_op jit(solution)/shard_map/ppermute | solution.py:575
  256.7 3.0 %finish_gradients.1 = (bf16[8192,256]{1,0:T(8,128)(2,1)}, bf16[4096,128]{1,0:T(8,128)(2,1)}, bf16[64,2048]{1,0:T(8,128)(2,1)}) custom-call(s32[1]{0:T(128)} %bitcast.side_ref, bf16[2048,256]{1,0:T(8,128)(2,1)S(1)} %constant_dynamic-update-slice_fusion.1.own_a, bf16[2048,256]{1,0:T(8,128)(2,1)S(1)} %constant_dynamic-update-slice_fusion.4.own_b, ...), custom_call_target="tpu_custom_call" | custom-call | tf_op jit(solution)/shard_map/finish_gradients/pallas_call | solution.py:535
  (139 shorter events, 53.5 us)
Async XLA Ops:
  3.9 33.1 %all-to-all-start = ((bf16[8,32,2048]{2,1,0:T(8,128)(2,1)}), bf16[8,32,2048]{2,1,0:T(8,128)(2,1)S(1)}, u32[]{:S(2)}, u32[]{:S(2)}) async-start(bf16[8,32,2048]{2,1,0:T(8,128)(2,1)} %bitcast.106), calls=%async_computation | async-start | bytes 2097152 | tf_op jit(solution)/shard_map/all_to_all | solution.py:651
  37.0 29.5 %all-to-all-start.2 = ((bf16[8,32,2048]{2,1,0:T(8,128)(2,1)}), bf16[8,32,2048]{2,1,0:T(8,128)(2,1)S(1)}, u32[]{:S(2)}, u32[]{:S(2)}) async-start(bf16[8,32,2048]{2,1,0:T(8,128)(2,1)} %bitcast.105), calls=%async_computation.2 | async-start | bytes 2097152 | tf_op jit(solution)/shard_map/all_to_all | solution.py:651
  46.4 4.0 %collective-permute-start = (bf16[4,256,512]{2,1,0:T(8,128)(2,1)}, bf16[4,256,512]{2,1,0:T(8,128)(2,1)S(1)}, u32[]{:S(2)}, u32[]{:S(2)}) collective-permute-start(bf16[4,256,512]{2,1,0:T(8,128)(2,1)} %project_rows.6.after_and_out_0_), channel_id=1, source_target_pairs={{0,8},{8,0},{16,24},{24,16},{1,9},{9,1},{17,25},{25,17},{2,10},{10... | collective-permute-start | bytes 3145736 | tf_op jit(solution)/shard_map/ppermute | solution.py:575
  51.7 14.9 %collective-permute-start.1 = (bf16[2,256,512]{2,1,0:T(8,128)(2,1)S(1)}, bf16[2,256,512]{2,1,0:T(8,128)(2,1)S(1)}, u32[]{:S(2)}, u32[]{:S(2)}) collective-permute-start(bf16[2,256,512]{2,1,0:T(8,128)(2,1)S(1)} %add_convert_fusion.5.after_and_out_0_), channel_id=1, source_target_pairs={{0,16},{8,24},{16,0},{24,8},{1,17},{9,25},{17,1},{25,9},{2,18},{10... | collective-permute-start | bytes 1572872 | tf_op jit(solution)/shard_map/ppermute | solution.py:575
  73.5 11.4 %collective-permute-start.2 = (bf16[4,256,512]{2,1,0:T(8,128)(2,1)}, bf16[4,256,512]{2,1,0:T(8,128)(2,1)}, u32[]{:S(2)}, u32[]{:S(2)}) collective-permute-start(bf16[4,256,512]{2,1,0:T(8,128)(2,1)} %project_rows.9.after_and_out_0_), channel_id=1, source_target_pairs={{0,8},{8,0},{16,24},{24,16},{1,9},{9,1},{17,25},{25,17},{2,10},{10... | collective-permute-start | bytes 3145736 | tf_op jit(solution)/shard_map/ppermute | solution.py:575
  75.6 20.3 %all-to-all-start.1 = ((bf16[8,2,32,512]{3,2,1,0:T(8,128)(2,1)}), bf16[8,2,32,512]{3,2,1,0:T(8,128)(2,1)S(1)}, u32[]{:S(2)}, u32[]{:S(2)}) async-start(bf16[8,2,32,512]{3,2,1,0:T(8,128)(2,1)} %bitcast.93), calls=%async_computation.1 | async-start | bytes 1048576 | tf_op jit(solution)/shard_map/all_to_all | solution.py:679
  86.2 14.1 %collective-permute-start.3 = (bf16[2,256,512]{2,1,0:T(8,128)(2,1)S(1)}, bf16[2,256,512]{2,1,0:T(8,128)(2,1)S(1)}, u32[]{:S(2)}, u32[]{:S(2)}) collective-permute-start(bf16[2,256,512]{2,1,0:T(8,128)(2,1)S(1)} %add_convert_fusion.3.after_and_out_0_.after_ref), channel_id=1, source_target_pairs={{0,16},{8,24},{16,0},{24,8},{1,17},{9,25},{17,1},{25,9},{2,18},{10... | collective-permute-start | bytes 1572872 | tf_op jit(solution)/shard_map/ppermute | solution.py:575
  102.6 19.5 %all-to-all-start.3 = ((bf16[8,2,32,512]{3,2,1,0:T(8,128)(2,1)}), bf16[8,2,32,512]{3,2,1,0:T(8,128)(2,1)S(1)}, u32[]{:S(2)}, u32[]{:S(2)}) async-start(bf16[8,2,32,512]{3,2,1,0:T(8,128)(2,1)} %bitcast.92), calls=%async_computation.3 | async-start | bytes 1048576 | tf_op jit(solution)/shard_map/all_to_all | solution.py:679
  108.6 13.5 %copy-start.7 = (bf16[2,256,256]{2,1,0:T(8,128)(2,1)}, bf16[2,256,256]{2,1,0:T(8,128)(2,1)S(1)}, u32[]{:S(2)}) copy-start(bf16[2,256,256]{2,1,0:T(8,128)(2,1)S(1)} %pad_maximum_fusion.12.after_and_out_2_.w_three_ref) | copy-start | bytes 786436
  113.2 9.0 %copy-start.9 = (bf16[256,256]{1,0:T(8,128)(2,1)S(1)}, bf16[256,256]{1,0:T(8,128)(2,1)}, u32[]{:S(2)}) copy-start(bf16[256,256]{1,0:T(8,128)(2,1)} %get-tuple-element.43.place_b_ref) | copy-start | bytes 393220
  166.0 2.9 %collective-permute-start.4 = (bf16[2048,256]{1,0:T(8,128)(2,1)}, bf16[2048,256]{1,0:T(8,128)(2,1)S(1)}, u32[]{:S(2)}, u32[]{:S(2)}) collective-permute-start(bf16[2048,256]{1,0:T(8,128)(2,1)} %get-tuple-element.49), channel_id=1, source_target_pairs={{0,8},{8,0},{16,24},{24,16},{1,9},{9,1},{17,25},{25,17},{2,10},{10... | collective-permute-start | bytes 3145736 | tf_op jit(solution)/shard_map/ppermute | solution.py:575
  166.1 5.4 %collective-permute-start.6 = (bf16[2048,256]{1,0:T(8,128)(2,1)}, bf16[2048,256]{1,0:T(8,128)(2,1)S(1)}, u32[]{:S(2)}, u32[]{:S(2)}) collective-permute-start(bf16[2048,256]{1,0:T(8,128)(2,1)} %get-tuple-element.51), channel_id=1, source_target_pairs={{0,8},{8,0},{16,24},{24,16},{1,9},{9,1},{17,25},{25,17},{2,10},{10... | collective-permute-start | bytes 3145736 | tf_op jit(solution)/shard_map/ppermute | solution.py:575
  166.6 7.4 %collective-permute-start.8 = (bf16[1280,256]{1,0:T(8,128)(2,1)}, bf16[1280,256]{1,0:T(8,128)(2,1)}, u32[]{:S(2)}, u32[]{:S(2)}) collective-permute-start(bf16[1280,256]{1,0:T(8,128)(2,1)} %get-tuple-element.53), channel_id=1, source_target_pairs={{0,8},{8,0},{16,24},{24,16},{1,9},{9,1},{17,25},{25,17},{2,10},{10... | collective-permute-start | bytes 1966088 | tf_op jit(solution)/shard_map/ppermute | solution.py:575
  171.2 14.7 %collective-permute-start.5 = (bf16[1024,256]{1,0:T(8,128)(2,1)}, bf16[1024,256]{1,0:T(8,128)(2,1)}, u32[]{:S(2)}, u32[]{:S(2)}) collective-permute-start(bf16[1024,256]{1,0:T(8,128)(2,1)} %get-tuple-element.83), channel_id=1, source_target_pairs={{0,16},{8,24},{16,0},{24,8},{1,17},{9,25},{17,1},{25,9},{2,18},{10... | collective-permute-start | bytes 1572872 | tf_op jit(solution)/shard_map/ppermute | solution.py:575
  172.6 14.1 %collective-permute-start.7 = (bf16[1024,256]{1,0:T(8,128)(2,1)}, bf16[1024,256]{1,0:T(8,128)(2,1)}, u32[]{:S(2)}, u32[]{:S(2)}) collective-permute-start(bf16[1024,256]{1,0:T(8,128)(2,1)} %get-tuple-element.81), channel_id=1, source_target_pairs={{0,1},{1,0},{2,3},{3,2},{4,5},{5,4},{6,7},{7,6},{8,9},{9,8},{10,11... | collective-permute-start | bytes 1572872 | tf_op jit(solution)/shard_map/ppermute | solution.py:575
  176.4 9.5 %collective-permute-start.9 = (bf16[640,256]{1,0:T(8,128)(2,1)}, bf16[640,256]{1,0:T(8,128)(2,1)S(1)}, u32[]{:S(2)}, u32[]{:S(2)}) collective-permute-start(bf16[640,256]{1,0:T(8,128)(2,1)} %get-tuple-element.88), channel_id=1, source_target_pairs={{0,2},{1,3},{2,0},{3,1},{4,6},{5,7},{6,4},{7,5},{8,10},{9,11},{10,... | collective-permute-start | bytes 983048 | tf_op jit(solution)/shard_map/ppermute | solution.py:575
  188.0 10.9 %collective-permute-start.11 = (bf16[832,256]{1,0:T(8,128)(2,1)S(1)}, bf16[832,256]{1,0:T(8,128)(2,1)S(1)}, u32[]{:S(2)}, u32[]{:S(2)}) collective-permute-start(bf16[832,256]{1,0:T(8,128)(2,1)S(1)} %pad_maximum_fusion.6), channel_id=1, source_target_pairs={{0,16},{8,24},{16,0},{24,8},{1,17},{9,25},{17,1},{25,9},{2,18},{10... | collective-permute-start | bytes 1277960 | tf_op jit(solution)/shard_map/ppermute | solution.py:575
  191.4 7.5 %collective-permute-start.10 = (bf16[512,256]{1,0:T(8,128)(2,1)}, bf16[512,256]{1,0:T(8,128)(2,1)S(1)}, u32[]{:S(2)}, u32[]{:S(2)}) collective-permute-start(bf16[512,256]{1,0:T(8,128)(2,1)} %get-tuple-element.85), channel_id=1, source_target_pairs={{0,1},{1,0},{2,3},{3,2},{4,5},{5,4},{6,7},{7,6},{8,9},{9,8},{10,11... | collective-permute-start | bytes 786440 | tf_op jit(solution)/shard_map/ppermute | solution.py:575
  199.1 6.5 %collective-permute-start.12 = (bf16[512,256]{1,0:T(8,128)(2,1)S(1)}, bf16[512,256]{1,0:T(8,128)(2,1)S(1)}, u32[]{:S(2)}, u32[]{:S(2)}) collective-permute-start(bf16[512,256]{1,0:T(8,128)(2,1)S(1)} %pad_maximum_fusion.13), channel_id=1, source_target_pairs={{0,2},{1,3},{2,0},{3,1},{4,6},{5,7},{6,4},{7,5},{8,10},{9,11},{10,... | collective-permute-start | bytes 786440 | tf_op jit(solution)/shard_map/ppermute | solution.py:575
  199.9 5.7 %collective-permute-start.13 = (bf16[160,256]{1,0:T(8,128)(2,1)S(1)}, bf16[160,256]{1,0:T(8,128)(2,1)S(1)}, u32[]{:S(2)}, u32[]{:S(2)}) collective-permute-start(bf16[160,256]{1,0:T(8,128)(2,1)S(1)} %get-tuple-element.128), channel_id=1, source_target_pairs={{0,1},{1,0},{2,3},{3,2},{4,5},{5,4},{6,7},{7,6},{8,9},{9,8},{10,11... | collective-permute-start | bytes 245768 | tf_op jit(solution)/shard_map/ppermute | solution.py:575
  205.7 11.4 %collective-permute-start.14 = (bf16[336,256]{1,0:T(8,128)(2,1)S(1)}, bf16[336,256]{1,0:T(8,128)(2,1)S(1)}, u32[]{:S(2)}, u32[]{:S(2)}) collective-permute-start(bf16[336,256]{1,0:T(8,128)(2,1)S(1)} %pad_maximum_fusion.14), channel_id=1, source_target_pairs={{0,4},{1,5},{2,6},{3,7},{4,0},{5,1},{6,2},{7,3},{8,12},{9,13},{10,... | collective-permute-start | bytes 516104 | tf_op jit(solution)/shard_map/ppermute | solution.py:575
  217.3 6.9 %collective-permute-start.15 = (bf16[336,256]{1,0:T(8,128)(2,1)S(1)}, bf16[336,256]{1,0:T(8,128)(2,1)S(1)}, u32[]{:S(2)}, u32[]{:S(2)}) collective-permute-start(bf16[336,256]{1,0:T(8,128)(2,1)S(1)} %pad_maximum_fusion.15), channel_id=1, source_target_pairs={{0,4},{1,5},{2,6},{3,7},{4,0},{5,1},{6,2},{7,3},{8,12},{9,13},{10,... | collective-permute-start | bytes 516104 | tf_op jit(solution)/shard_map/ppermute | solution.py:575
  224.3 6.4 %collective-permute-start.16 = (bf16[512,256]{1,0:T(8,128)(2,1)S(1)}, bf16[512,256]{1,0:T(8,128)(2,1)S(1)}, u32[]{:S(2)}, u32[]{:S(2)}) collective-permute-start(bf16[512,256]{1,0:T(8,128)(2,1)S(1)} %get-tuple-element.139), channel_id=1, source_target_pairs={{0,2},{1,3},{2,0},{3,1},{4,6},{5,7},{6,4},{7,5},{8,10},{9,11},{10,... | collective-permute-start | bytes 786440 | tf_op jit(solution)/shard_map/ppermute | solution.py:575
  224.4 5.3 %collective-permute-start.17 = (bf16[160,256]{1,0:T(8,128)(2,1)S(1)}, bf16[160,256]{1,0:T(8,128)(2,1)S(1)}, u32[]{:S(2)}, u32[]{:S(2)}) collective-permute-start(bf16[160,256]{1,0:T(8,128)(2,1)S(1)} %slice_dynamic-update-slice_fusion.6), channel_id=1, source_target_pairs={{0,1},{1,0},{2,3},{3,2},{4,5},{5,4},{6,7},{7,6},{8,9},{9,8},{10,11... | collective-permute-start | bytes 245768 | tf_op jit(solution)/shard_map/ppermute | solution.py:575
  230.7 8.2 %collective-permute-start.18 = (bf16[512,256]{1,0:T(8,128)(2,1)S(1)}, bf16[512,256]{1,0:T(8,128)(2,1)S(1)}, u32[]{:S(2)}, u32[]{:S(2)}) collective-permute-start(bf16[512,256]{1,0:T(8,128)(2,1)S(1)} %get-tuple-element.74), channel_id=1, source_target_pairs={{0,1},{1,0},{2,3},{3,2},{4,5},{5,4},{6,7},{7,6},{8,9},{9,8},{10,11... | collective-permute-start | bytes 786440 | tf_op jit(solution)/shard_map/ppermute | solution.py:575
  231.8 11.9 %collective-permute-start.20 = (bf16[832,256]{1,0:T(8,128)(2,1)S(1)}, bf16[832,256]{1,0:T(8,128)(2,1)S(1)}, u32[]{:S(2)}, u32[]{:S(2)}) collective-permute-start(bf16[832,256]{1,0:T(8,128)(2,1)S(1)} %pad_maximum_fusion.7), channel_id=1, source_target_pairs={{0,16},{8,24},{16,0},{24,8},{1,17},{9,25},{17,1},{25,9},{2,18},{10... | collective-permute-start | bytes 1277960 | tf_op jit(solution)/shard_map/ppermute | solution.py:575
  238.9 10.4 %collective-permute-start.19 = (bf16[1024,256]{1,0:T(8,128)(2,1)S(1)}, bf16[1024,256]{1,0:T(8,128)(2,1)S(1)}, u32[]{:S(2)}, u32[]{:S(2)}) collective-permute-start(bf16[1024,256]{1,0:T(8,128)(2,1)S(1)} %constant_dynamic-update-slice_fusion.3), channel_id=1, source_target_pairs={{0,16},{8,24},{16,0},{24,8},{1,17},{9,25},{17,1},{25,9},{2,18},{10... | collective-permute-start | bytes 1572872 | tf_op jit(solution)/shard_map/ppermute | solution.py:575
  243.8 9.2 %collective-permute-start.21 = (bf16[1024,256]{1,0:T(8,128)(2,1)S(1)}, bf16[1024,256]{1,0:T(8,128)(2,1)S(1)}, u32[]{:S(2)}, u32[]{:S(2)}) collective-permute-start(bf16[1024,256]{1,0:T(8,128)(2,1)S(1)} %slice_dynamic-update-slice_fusion), channel_id=1, source_target_pairs={{0,1},{1,0},{2,3},{3,2},{4,5},{5,4},{6,7},{7,6},{8,9},{9,8},{10,11... | collective-permute-start | bytes 1572872 | tf_op jit(solution)/shard_map/ppermute | solution.py:575
  245.0 8.2 %collective-permute-start.22 = (bf16[640,256]{1,0:T(8,128)(2,1)S(1)}, bf16[640,256]{1,0:T(8,128)(2,1)S(1)}, u32[]{:S(2)}, u32[]{:S(2)}) collective-permute-start(bf16[640,256]{1,0:T(8,128)(2,1)S(1)} %slice_dynamic-update-slice_fusion.1), channel_id=1, source_target_pairs={{0,2},{1,3},{2,0},{3,1},{4,6},{5,7},{6,4},{7,5},{8,10},{9,11},{10,... | collective-permute-start | bytes 983048 | tf_op jit(solution)/shard_map/ppermute | solution.py:575
  249.4 7.3 %collective-permute-start.23 = (bf16[2048,256]{1,0:T(8,128)(2,1)S(1)}, bf16[2048,256]{1,0:T(8,128)(2,1)S(1)}, u32[]{:S(2)}, u32[]{:S(2)}) collective-permute-start(bf16[2048,256]{1,0:T(8,128)(2,1)S(1)} %constant_dynamic-update-slice_fusion.1.own_a), channel_id=1, source_target_pairs={{0,8},{8,0},{16,24},{24,16},{1,9},{9,1},{17,25},{25,17},{2,10},{10... | collective-permute-start | bytes 3145736 | tf_op jit(solution)/shard_map/ppermute | solution.py:575
  253.0 3.7 %collective-permute-start.24 = (bf16[2048,256]{1,0:T(8,128)(2,1)S(1)}, bf16[2048,256]{1,0:T(8,128)(2,1)S(1)}, u32[]{:S(2)}, u32[]{:S(2)}) collective-permute-start(bf16[2048,256]{1,0:T(8,128)(2,1)S(1)} %constant_dynamic-update-slice_fusion.4.own_b), channel_id=1, source_target_pairs={{0,8},{8,0},{16,24},{24,16},{1,9},{9,1},{17,25},{25,17},{2,10},{10... | collective-permute-start | bytes 3145736 | tf_op jit(solution)/shard_map/ppermute | solution.py:575
  253.2 3.5 %collective-permute-start.25 = (bf16[1280,256]{1,0:T(8,128)(2,1)S(1)}, bf16[1280,256]{1,0:T(8,128)(2,1)S(1)}, u32[]{:S(2)}, u32[]{:S(2)}) collective-permute-start(bf16[1280,256]{1,0:T(8,128)(2,1)S(1)} %constant_dynamic-update-slice_fusion.2.own_c), channel_id=1, source_target_pairs={{0,8},{8,0},{16,24},{24,16},{1,9},{9,1},{17,25},{25,17},{2,10},{10... | collective-permute-start | bytes 1966088 | tf_op jit(solution)/shard_map/ppermute | solution.py:575
  (17 other events, 70.6 us)

commit v7 on v6

--- a/solution.py
+++ b/solution.py
@@ -709,8 +709,9 @@
     decoded = sample_first(decoded_rows, count, w_third.shape[1], received[1])
     for stage in range(len(routes[0])):
         parts = over_chains(shared, parts, [route[stage] for route in routes])
-        *tied, decoded = lax.optimization_barrier(tuple(terms[1] for terms in parts) + (decoded,))
-        parts = [terms[:1] + [arrived] + terms[2:] for terms, arrived in zip(parts, tied)]
+        if stage < len(routes[0]) - 1:
+            *tied, decoded = lax.optimization_barrier(tuple(terms[1] for terms in parts) + (decoded,))
+            parts = [terms[:1] + [arrived] + terms[2:] for terms, arrived in zip(parts, tied)]
     shares = [summed(terms).astype(jnp.bfloat16) for terms in parts]
     for stage in reversed(range(len(routes[0]))):
         shares = over_chains(gathered, shares, [route[stage] for route in routes])

time: 261 us -> 261 us (level)
    add x6 -> x7, other arithmetic: 6.4 us -> 6.65 us  [summed(): value = value.astype(jnp.float32) + term.astype(jnp.float32)]
where the time goes in v7:
time: 261 us; the launch traced here: 260 us
  waiting for transfers between devices  101 us (39%)
  Pallas kernels  76.1 us (29%)
  starting transfers between devices  40 us (15%)
  other arithmetic  15.1 us (6%)
  local copies, waits for them, and re-layouts  14.1 us (5%)
  blocking collectives  11.9 us (5%)
    ppermute x26, waiting for transfers between devices, exchanged(): lax.ppermute(values, axis, [(at, at ^ flip) for at in range(lax.axis_size...  62.3 us
    all_to_all x2, waiting for transfers between devices, routed(): lax.all_to_all(sent, 'dp', split_axis=0, concat_axis=0, tiled=True)  31.8 us
    pallas_call x1, Pallas kernels, decoder(): pl.pallas_call(functools.partial(decoder_kernel, count), name='decoder',...  29.3 us
    pallas_call x6, Pallas kernels, projected(): pl.pallas_call(project_kernel, name='project_rows', grid_spec=pltpu.Prefe...  27.9 us
    ppermute x26, starting transfers between devices, exchanged(): lax.ppermute(values, axis, [(at, at ^ flip) for at in range(lax.axis_size...  18.3 us
    unnamed x39, local copies, waits for them, and re-layouts  12 us
    all_to_all x1, blocking collectives, shards(): lax.all_to_all(own_rows, 'vox', split_axis=0, concat_axis=0, tiled=True)  11.9 us
    all_to_all x2, starting transfers between devices, returned(): return lax.all_to_all(sent, 'dp', split_axis=0, concat_axis=0, tiled=True)  10.9 us
  transfers between devices with their start and end apart: 30, of which 19 were waited for; matrix products, arithmetic and copies ran while one was open for 5% of the time, Pallas kernels for 13%

profile of v7, /device:TPU:0, one launch (start us, length us, event | category | flops | bytes accessed | tf_op | source)
XLA Modules:
  0.0 259.7 jit_solution(4090380037752504645)
XLA Ops:
  0.6 3.3 %bucket_rows.2 = (bf16[256,2048]{1,0:T(8,128)(2,1)}, bf16[256,256]{1,0:T(8,128)(2,1)}) custom-call(s32[1,256]{1,0:T(1,128)} %bitcast.107, s32[8]{0:T(128)} %after_and_out_0_.1, s32[1]{0:T(128)} %bitcast.2.shift_ref, bf16[256,2048]{1,0:T(8,128)(2,1)} %fmri_ref.3, s32[8]{0:T(128)} %after_and_out_0_.1), custom_call_target="tpu_custom_call" | custom-call | tf_op jit(solution)/shard_map/bucket_rows/pallas_call | solution.py:428
  3.9 7.3 %all-to-all-start = ((bf16[8,32,2048]{2,1,0:T(8,128)(2,1)}), bf16[8,32,2048]{2,1,0:T(8,128)(2,1)S(1)}, u32[]{:S(2)}, u32[]{:S(2)}) async-start(bf16[8,32,2048]{2,1,0:T(8,128)(2,1)} %bitcast.106), calls=%async_computation | async-start | bytes 2097152 | tf_op jit(solution)/shard_map/all_to_all | solution.py:651
  11.2 3.3 %bucket_rows.3 = (bf16[256,2048]{1,0:T(8,128)(2,1)}, bf16[256,256]{1,0:T(8,128)(2,1)}) custom-call(s32[1,256]{1,0:T(1,128)} %bitcast.108, s32[8]{0:T(128)} %after_and_out_0_.1, s32[1]{0:T(128)} %bitcast.2.shift_ref, bf16[256,2048]{1,0:T(8,128)(2,1)} %fmri_ref.3, bf16[256,256]{1,0:T(8,128)(2,1)} %get-tuple-element.38.after_ref.place_a_ref), custom_call_target="tpu_custom_call" | custom-call | tf_op jit(solution)/shard_map/bucket_rows/pallas_call | solution.py:428
  14.5 22.5 %all-to-all-done = bf16[8,32,2048]{2,1,0:T(8,128)(2,1)S(1)} async-done(((bf16[8,32,2048]{2,1,0:T(8,128)(2,1)}), bf16[8,32,2048]{2,1,0:T(8,128)(2,1)S(1)}, u32[]{:S(2)}, u32[]{:S(2)}) %all-to-all-start) | async-done | bytes 1048608 | tf_op jit(solution)/shard_map/all_to_all | solution.py:651
  37.0 3.6 %all-to-all-start.2 = ((bf16[8,32,2048]{2,1,0:T(8,128)(2,1)}), bf16[8,32,2048]{2,1,0:T(8,128)(2,1)S(1)}, u32[]{:S(2)}, u32[]{:S(2)}) async-start(bf16[8,32,2048]{2,1,0:T(8,128)(2,1)} %bitcast.105), calls=%async_computation.2 | async-start | bytes 2097152 | tf_op jit(solution)/shard_map/all_to_all | solution.py:651
  40.6 5.9 %project_rows.6.after_and_out_0_ = bf16[4,256,512]{2,1,0:T(8,128)(2,1)} custom-call(s32[1]{0:T(128)} %bitcast.7.quarter_ref, bf16[256,2048]{1,0:T(8,128)(2,1)} %bitcast.98, bf16[1,2048,4096]{2,1,0:T(8,128)(2,1)} %map_ref.11, s32[8]{0:T(128)} %after_and_out_0_.1), custom_call_target="tpu_custom_call" | custom-call | flops 2147483648 | bytes 8388608 | tf_op jit(solution)/shard_map/project_rows/pallas_call | solution.py:455
  46.4 4.0 %project_rows.7 = bf16[2,256,512]{2,1,0:T(8,128)(2,1)} custom-call(s32[1]{0:T(128)} %bitcast.6.quarter_ref, bf16[256,2048]{1,0:T(8,128)(2,1)} %bitcast.99, bf16[1,2048,4096]{2,1,0:T(8,128)(2,1)} %map_ref.11, bf16[4,256,512]{2,1,0:T(8,128)(2,1)} %project_rows.6.after_and_out_0_), custom_call_target="tpu_custom_call" | custom-call | flops 1073741824 | bytes 4194304 | tf_op jit(solution)/shard_map/project_rows/pallas_call | solution.py:455
  53.2 4.0 %project_rows.8.after_and_out_1_ = bf16[2,256,512]{2,1,0:T(8,128)(2,1)} custom-call(s32[1]{0:T(128)} %bitcast.3.quarter_ref, bf16[256,2048]{1,0:T(8,128)(2,1)} %bitcast.100, bf16[1,2048,4096]{2,1,0:T(8,128)(2,1)} %map_ref.11, bf16[2,256,512]{2,1,0:T(8,128)(2,1)} %copy-done.15), custom_call_target="tpu_custom_call" | custom-call | flops 1073741824 | bytes 4194304 | tf_op jit(solution)/shard_map/project_rows/pallas_call | solution.py:455
  57.2 9.3 %all-to-all-done.2 = bf16[8,32,2048]{2,1,0:T(8,128)(2,1)S(1)} async-done(((bf16[8,32,2048]{2,1,0:T(8,128)(2,1)}), bf16[8,32,2048]{2,1,0:T(8,128)(2,1)S(1)}, u32[]{:S(2)}, u32[]{:S(2)}) %all-to-all-start.2) | async-done | bytes 1048608 | tf_op jit(solution)/shard_map/all_to_all | solution.py:651
  67.7 5.9 %project_rows.9.after_and_out_0_ = bf16[4,256,512]{2,1,0:T(8,128)(2,1)} custom-call(s32[1]{0:T(128)} %bitcast.7.quarter_ref, bf16[256,2048]{1,0:T(8,128)(2,1)} %bitcast.95, bf16[1,2048,4096]{2,1,0:T(8,128)(2,1)} %map_ref.11, bf16[2,256,512]{2,1,0:T(8,128)(2,1)} %copy-done.14, bf16[2,256,512]{2,1,0:T(8,128)(2,1)} %project_rows.8.after_and_out_1_), custom_call_target="tpu_custom_call" | custom-call | flops 2147483648 | bytes 8388608 | tf_op jit(solution)/shard_map/project_rows/pallas_call | solution.py:455
  75.6 5.2 %all-to-all-start.1 = ((bf16[8,2,32,512]{3,2,1,0:T(8,128)(2,1)}), bf16[8,2,32,512]{3,2,1,0:T(8,128)(2,1)S(1)}, u32[]{:S(2)}, u32[]{:S(2)}) async-start(bf16[8,2,32,512]{3,2,1,0:T(8,128)(2,1)} %bitcast.93), calls=%async_computation.1 | async-start | bytes 1048576 | tf_op jit(solution)/shard_map/all_to_all | solution.py:679
  80.8 4.1 %project_rows.10 = bf16[2,256,512]{2,1,0:T(8,128)(2,1)} custom-call(s32[1]{0:T(128)} %bitcast.6.quarter_ref, bf16[256,2048]{1,0:T(8,128)(2,1)} %bitcast.96, bf16[1,2048,4096]{2,1,0:T(8,128)(2,1)} %map_ref.11, bf16[4,256,512]{2,1,0:T(8,128)(2,1)} %project_rows.9.after_and_out_0_), custom_call_target="tpu_custom_call" | custom-call | flops 1073741824 | bytes 4194304 | tf_op jit(solution)/shard_map/project_rows/pallas_call | solution.py:455
  88.1 4.0 %project_rows.11 = bf16[2,256,512]{2,1,0:T(8,128)(2,1)} custom-call(s32[1]{0:T(128)} %bitcast.3.quarter_ref, bf16[256,2048]{1,0:T(8,128)(2,1)} %bitcast.97, bf16[1,2048,4096]{2,1,0:T(8,128)(2,1)} %map_ref.11, bf16[2,256,512]{2,1,0:T(8,128)(2,1)} %copy-done.4), custom_call_target="tpu_custom_call" | custom-call | flops 1073741824 | bytes 4194304 | tf_op jit(solution)/shard_map/project_rows/pallas_call | solution.py:455
  92.1 3.8 %all-to-all-done.1.first_ref = bf16[8,2,32,512]{3,2,1,0:T(8,128)(2,1)S(1)} async-done(((bf16[8,2,32,512]{3,2,1,0:T(8,128)(2,1)}), bf16[8,2,32,512]{3,2,1,0:T(8,128)(2,1)S(1)}, u32[]{:S(2)}, u32[]{:S(2)}) %all-to-all-start.1) | async-done | bytes 524320 | tf_op jit(solution)/shard_map/all_to_all | solution.py:679
  96.0 4.4 %collective-permute-done.3 = bf16[2,256,512]{2,1,0:T(8,128)(2,1)S(1)} collective-permute-done((bf16[2,256,512]{2,1,0:T(8,128)(2,1)S(1)}, bf16[2,256,512]{2,1,0:T(8,128)(2,1)S(1)}, u32[]{:S(2)}, u32[]{:S(2)}) %collective-permute-start.3) | collective-permute-done | bytes 524320 | tf_op jit(solution)/shard_map/ppermute | solution.py:575
  102.6 5.7 %all-to-all-start.3 = ((bf16[8,2,32,512]{3,2,1,0:T(8,128)(2,1)}), bf16[8,2,32,512]{3,2,1,0:T(8,128)(2,1)S(1)}, u32[]{:S(2)}, u32[]{:S(2)}) async-start(bf16[8,2,32,512]{3,2,1,0:T(8,128)(2,1)} %bitcast.92), calls=%async_computation.3 | async-start | bytes 1048576 | tf_op jit(solution)/shard_map/all_to_all | solution.py:679
  109.8 3.4 %copy-done.3 = bf16[64,16,32,64]{3,2,1,0:T(8,128)(2,1)S(1)} copy-done((bf16[64,16,32,64]{3,2,1,0:T(8,128)(2,1)S(1)}, bf16[64,16,32,64]{3,2,1,0:T(8,128)(2,1)}, u32[]{:S(2)}) %copy-start.3) | copy-done | bytes 4194328
  113.2 3.4 %spatial_first.1.after_and_out_0_.target_ref = bf16[16,1024,128]{2,1,0:T(8,128)(2,1)S(1)} custom-call(bf16[64,16,32,64]{3,2,1,0:T(8,128)(2,1)S(1)} %copy-done.3, bf16[2,256,512]{2,1,0:T(8,128)(2,1)S(1)} %copy-done.5), custom_call_target="tpu_custom_call" | custom-call | bytes 28000000 | tf_op jit(solution)/shard_map/spatial_first/pallas_call | solution.py:352
  118.6 3.5 %all-to-all-done.3.second_ref = bf16[8,2,32,512]{3,2,1,0:T(8,128)(2,1)S(1)} async-done(((bf16[8,2,32,512]{3,2,1,0:T(8,128)(2,1)}), bf16[8,2,32,512]{3,2,1,0:T(8,128)(2,1)S(1)}, u32[]{:S(2)}, u32[]{:S(2)}) %all-to-all-start.3) | async-done | bytes 524320 | tf_op jit(solution)/shard_map/all_to_all | solution.py:679
  124.8 11.9 %all_to_all.25.latent_ref = bf16[4,64,1024]{2,1,0:T(8,128)(2,1)} all-to-all(bf16[4,64,1024]{2,1,0:T(8,128)(2,1)S(1)} %bitcast.94), channel_id=1, replica_groups=mesh['vox'=4,'dp'=8] {'vox'}, dimensions={0} | all-to-all | bytes 1048576 | tf_op jit(solution)/shard_map/all_to_all | solution.py:699
  136.7 29.3 %decoder.1 = (bf16[16,1024,128]{2,1,0:T(8,128)(2,1)}, bf16[2048,256]{1,0:T(8,128)(2,1)}, bf16[2048,256]{1,0:T(8,128)(2,1)}, bf16[1280,256]{1,0:T(8,128)(2,1)}, b...) custom-call(s32[1]{0:T(128)} %bitcast.side_ref, ...), custom_call_target="tpu_custom_call" | custom-call | tf_op jit(solution)/shard_map/decoder/pallas_call | solution.py:297
  178.6 5.4 %sample_first.1 = bf16[64,16,32,64]{3,2,1,0:T(8,128)(2,1)} custom-call(bf16[16,1024,128]{2,1,0:T(8,128)(2,1)S(1)} %copy-done.6, bf16[2048,256]{1,0:T(8,128)(2,1)S(1)} %collective-permute-done.6.after_ref), custom_call_target="tpu_custom_call" | custom-call | bytes 28000000 | tf_op jit(solution)/shard_map/sample_first/pallas_call | solution.py:383
  192.8 6.1 %collective-permute-done.11 = bf16[832,256]{1,0:T(8,128)(2,1)S(1)} collective-permute-done((bf16[832,256]{1,0:T(8,128)(2,1)S(1)}, bf16[832,256]{1,0:T(8,128)(2,1)S(1)}, u32[]{:S(2)}, u32[]{:S(2)}) %collective-permute-start.11) | collective-permute-done | bytes 426016 | tf_op jit(solution)/shard_map/ppermute | solution.py:575
  200.8 4.8 %collective-permute-done.12 = bf16[512,256]{1,0:T(8,128)(2,1)S(1)} collective-permute-done((bf16[512,256]{1,0:T(8,128)(2,1)S(1)}, bf16[512,256]{1,0:T(8,128)(2,1)S(1)}, u32[]{:S(2)}, u32[]{:S(2)}) %collective-permute-start.12) | collective-permute-done | bytes 262176 | tf_op jit(solution)/shard_map/ppermute | solution.py:575
  206.6 10.6 %collective-permute-done.14 = bf16[336,256]{1,0:T(8,128)(2,1)S(1)} collective-permute-done((bf16[336,256]{1,0:T(8,128)(2,1)S(1)}, bf16[336,256]{1,0:T(8,128)(2,1)S(1)}, u32[]{:S(2)}, u32[]{:S(2)}) %collective-permute-start.14) | collective-permute-done | bytes 172064 | tf_op jit(solution)/shard_map/ppermute | solution.py:575
  217.4 6.8 %collective-permute-done.15 = bf16[336,256]{1,0:T(8,128)(2,1)S(1)} collective-permute-done((bf16[336,256]{1,0:T(8,128)(2,1)S(1)}, bf16[336,256]{1,0:T(8,128)(2,1)S(1)}, u32[]{:S(2)}, u32[]{:S(2)}) %collective-permute-start.15) | collective-permute-done | bytes 172064 | tf_op jit(solution)/shard_map/ppermute | solution.py:575
  225.4 4.3 %collective-permute-done.17 = bf16[160,256]{1,0:T(8,128)(2,1)S(1)} collective-permute-done((bf16[160,256]{1,0:T(8,128)(2,1)S(1)}, bf16[160,256]{1,0:T(8,128)(2,1)S(1)}, u32[]{:S(2)}, u32[]{:S(2)}) %collective-permute-start.17) | collective-permute-done | bytes 81952 | tf_op jit(solution)/shard_map/ppermute | solution.py:575
  233.2 5.7 %collective-permute-done.18 = bf16[512,256]{1,0:T(8,128)(2,1)S(1)} collective-permute-done((bf16[512,256]{1,0:T(8,128)(2,1)S(1)}, bf16[512,256]{1,0:T(8,128)(2,1)S(1)}, u32[]{:S(2)}, u32[]{:S(2)}) %collective-permute-start.18) | collective-permute-done | bytes 262176 | tf_op jit(solution)/shard_map/ppermute | solution.py:575
  240.4 3.3 %collective-permute-done.20 = bf16[832,256]{1,0:T(8,128)(2,1)S(1)} collective-permute-done((bf16[832,256]{1,0:T(8,128)(2,1)S(1)}, bf16[832,256]{1,0:T(8,128)(2,1)S(1)}, u32[]{:S(2)}, u32[]{:S(2)}) %collective-permute-start.20) | collective-permute-done | bytes 426016 | tf_op jit(solution)/shard_map/ppermute | solution.py:575
  245.4 3.9 %collective-permute-done.19 = bf16[1024,256]{1,0:T(8,128)(2,1)S(1)} collective-permute-done((bf16[1024,256]{1,0:T(8,128)(2,1)S(1)}, bf16[1024,256]{1,0:T(8,128)(2,1)S(1)}, u32[]{:S(2)}, u32[]{:S(2)}) %collective-permute-start.19) | collective-permute-done | bytes 524320 | tf_op jit(solution)/shard_map/ppermute | solution.py:575
  249.5 3.5 %collective-permute-done.21 = bf16[1024,256]{1,0:T(8,128)(2,1)S(1)} collective-permute-done((bf16[1024,256]{1,0:T(8,128)(2,1)S(1)}, bf16[1024,256]{1,0:T(8,128)(2,1)S(1)}, u32[]{:S(2)}, u32[]{:S(2)}) %collective-permute-start.21) | collective-permute-done | bytes 524320 | tf_op jit(solution)/shard_map/ppermute | solution.py:575
  256.7 3.0 %finish_gradients.1 = (bf16[8192,256]{1,0:T(8,128)(2,1)}, bf16[4096,128]{1,0:T(8,128)(2,1)}, bf16[64,2048]{1,0:T(8,128)(2,1)}) custom-call(s32[1]{0:T(128)} %bitcast.side_ref, bf16[2048,256]{1,0:T(8,128)(2,1)S(1)} %constant_dynamic-update-slice_fusion.1.own_a, bf16[2048,256]{1,0:T(8,128)(2,1)S(1)} %constant_dynamic-update-slice_fusion.4.own_b, ...), custom_call_target="tpu_custom_call" | custom-call | tf_op jit(solution)/shard_map/finish_gradients/pallas_call | solution.py:535
  (136 shorter events, 53.5 us)
Async XLA Ops:
  3.9 33.1 %all-to-all-start = ((bf16[8,32,2048]{2,1,0:T(8,128)(2,1)}), bf16[8,32,2048]{2,1,0:T(8,128)(2,1)S(1)}, u32[]{:S(2)}, u32[]{:S(2)}) async-start(bf16[8,32,2048]{2,1,0:T(8,128)(2,1)} %bitcast.106), calls=%async_computation | async-start | bytes 2097152 | tf_op jit(solution)/shard_map/all_to_all | solution.py:651
  37.0 29.5 %all-to-all-start.2 = ((bf16[8,32,2048]{2,1,0:T(8,128)(2,1)}), bf16[8,32,2048]{2,1,0:T(8,128)(2,1)S(1)}, u32[]{:S(2)}, u32[]{:S(2)}) async-start(bf16[8,32,2048]{2,1,0:T(8,128)(2,1)} %bitcast.105), calls=%async_computation.2 | async-start | bytes 2097152 | tf_op jit(solution)/shard_map/all_to_all | solution.py:651
  46.4 4.0 %collective-permute-start = (bf16[4,256,512]{2,1,0:T(8,128)(2,1)}, bf16[4,256,512]{2,1,0:T(8,128)(2,1)S(1)}, u32[]{:S(2)}, u32[]{:S(2)}) collective-permute-start(bf16[4,256,512]{2,1,0:T(8,128)(2,1)} %project_rows.6.after_and_out_0_), channel_id=1, source_target_pairs={{0,8},{8,0},{16,24},{24,16},{1,9},{9,1},{17,25},{25,17},{2,10},{10... | collective-permute-start | bytes 3145736 | tf_op jit(solution)/shard_map/ppermute | solution.py:575
  51.7 14.9 %collective-permute-start.1 = (bf16[2,256,512]{2,1,0:T(8,128)(2,1)S(1)}, bf16[2,256,512]{2,1,0:T(8,128)(2,1)S(1)}, u32[]{:S(2)}, u32[]{:S(2)}) collective-permute-start(bf16[2,256,512]{2,1,0:T(8,128)(2,1)S(1)} %add_convert_fusion.5.after_and_out_0_), channel_id=1, source_target_pairs={{0,16},{8,24},{16,0},{24,8},{1,17},{9,25},{17,1},{25,9},{2,18},{10... | collective-permute-start | bytes 1572872 | tf_op jit(solution)/shard_map/ppermute | solution.py:575
  73.5 11.4 %collective-permute-start.2 = (bf16[4,256,512]{2,1,0:T(8,128)(2,1)}, bf16[4,256,512]{2,1,0:T(8,128)(2,1)}, u32[]{:S(2)}, u32[]{:S(2)}) collective-permute-start(bf16[4,256,512]{2,1,0:T(8,128)(2,1)} %project_rows.9.after_and_out_0_), channel_id=1, source_target_pairs={{0,8},{8,0},{16,24},{24,16},{1,9},{9,1},{17,25},{25,17},{2,10},{10... | collective-permute-start | bytes 3145736 | tf_op jit(solution)/shard_map/ppermute | solution.py:575
  75.6 20.3 %all-to-all-start.1 = ((bf16[8,2,32,512]{3,2,1,0:T(8,128)(2,1)}), bf16[8,2,32,512]{3,2,1,0:T(8,128)(2,1)S(1)}, u32[]{:S(2)}, u32[]{:S(2)}) async-start(bf16[8,2,32,512]{3,2,1,0:T(8,128)(2,1)} %bitcast.93), calls=%async_computation.1 | async-start | bytes 1048576 | tf_op jit(solution)/shard_map/all_to_all | solution.py:679
  86.2 14.1 %collective-permute-start.3 = (bf16[2,256,512]{2,1,0:T(8,128)(2,1)S(1)}, bf16[2,256,512]{2,1,0:T(8,128)(2,1)S(1)}, u32[]{:S(2)}, u32[]{:S(2)}) collective-permute-start(bf16[2,256,512]{2,1,0:T(8,128)(2,1)S(1)} %add_convert_fusion.3.after_and_out_0_.after_ref), channel_id=1, source_target_pairs={{0,16},{8,24},{16,0},{24,8},{1,17},{9,25},{17,1},{25,9},{2,18},{10... | collective-permute-start | bytes 1572872 | tf_op jit(solution)/shard_map/ppermute | solution.py:575
  102.6 19.5 %all-to-all-start.3 = ((bf16[8,2,32,512]{3,2,1,0:T(8,128)(2,1)}), bf16[8,2,32,512]{3,2,1,0:T(8,128)(2,1)S(1)}, u32[]{:S(2)}, u32[]{:S(2)}) async-start(bf16[8,2,32,512]{3,2,1,0:T(8,128)(2,1)} %bitcast.92), calls=%async_computation.3 | async-start | bytes 1048576 | tf_op jit(solution)/shard_map/all_to_all | solution.py:679
  108.6 13.5 %copy-start.7 = (bf16[2,256,256]{2,1,0:T(8,128)(2,1)}, bf16[2,256,256]{2,1,0:T(8,128)(2,1)S(1)}, u32[]{:S(2)}) copy-start(bf16[2,256,256]{2,1,0:T(8,128)(2,1)S(1)} %pad_maximum_fusion.12.after_and_out_2_.w_three_ref) | copy-start | bytes 786436
  113.2 9.0 %copy-start.9 = (bf16[256,256]{1,0:T(8,128)(2,1)S(1)}, bf16[256,256]{1,0:T(8,128)(2,1)}, u32[]{:S(2)}) copy-start(bf16[256,256]{1,0:T(8,128)(2,1)} %get-tuple-element.39.place_b_ref) | copy-start | bytes 393220
  166.0 2.9 %collective-permute-start.4 = (bf16[2048,256]{1,0:T(8,128)(2,1)}, bf16[2048,256]{1,0:T(8,128)(2,1)S(1)}, u32[]{:S(2)}, u32[]{:S(2)}) collective-permute-start(bf16[2048,256]{1,0:T(8,128)(2,1)} %get-tuple-element.45), channel_id=1, source_target_pairs={{0,8},{8,0},{16,24},{24,16},{1,9},{9,1},{17,25},{25,17},{2,10},{10... | collective-permute-start | bytes 3145736 | tf_op jit(solution)/shard_map/ppermute | solution.py:575
  166.1 5.4 %collective-permute-start.6 = (bf16[2048,256]{1,0:T(8,128)(2,1)}, bf16[2048,256]{1,0:T(8,128)(2,1)S(1)}, u32[]{:S(2)}, u32[]{:S(2)}) collective-permute-start(bf16[2048,256]{1,0:T(8,128)(2,1)} %get-tuple-element.47), channel_id=1, source_target_pairs={{0,8},{8,0},{16,24},{24,16},{1,9},{9,1},{17,25},{25,17},{2,10},{10... | collective-permute-start | bytes 3145736 | tf_op jit(solution)/shard_map/ppermute | solution.py:575
  166.6 7.4 %collective-permute-start.8 = (bf16[1280,256]{1,0:T(8,128)(2,1)}, bf16[1280,256]{1,0:T(8,128)(2,1)}, u32[]{:S(2)}, u32[]{:S(2)}) collective-permute-start(bf16[1280,256]{1,0:T(8,128)(2,1)} %get-tuple-element.49), channel_id=1, source_target_pairs={{0,8},{8,0},{16,24},{24,16},{1,9},{9,1},{17,25},{25,17},{2,10},{10... | collective-permute-start | bytes 1966088 | tf_op jit(solution)/shard_map/ppermute | solution.py:575
  171.2 14.7 %collective-permute-start.5 = (bf16[1024,256]{1,0:T(8,128)(2,1)}, bf16[1024,256]{1,0:T(8,128)(2,1)}, u32[]{:S(2)}, u32[]{:S(2)}) collective-permute-start(bf16[1024,256]{1,0:T(8,128)(2,1)} %get-tuple-element.73), channel_id=1, source_target_pairs={{0,16},{8,24},{16,0},{24,8},{1,17},{9,25},{17,1},{25,9},{2,18},{10... | collective-permute-start | bytes 1572872 | tf_op jit(solution)/shard_map/ppermute | solution.py:575
  172.6 14.1 %collective-permute-start.7 = (bf16[1024,256]{1,0:T(8,128)(2,1)}, bf16[1024,256]{1,0:T(8,128)(2,1)}, u32[]{:S(2)}, u32[]{:S(2)}) collective-permute-start(bf16[1024,256]{1,0:T(8,128)(2,1)} %get-tuple-element.74), channel_id=1, source_target_pairs={{0,1},{1,0},{2,3},{3,2},{4,5},{5,4},{6,7},{7,6},{8,9},{9,8},{10,11... | collective-permute-start | bytes 1572872 | tf_op jit(solution)/shard_map/ppermute | solution.py:575
  176.4 9.5 %collective-permute-start.9 = (bf16[640,256]{1,0:T(8,128)(2,1)}, bf16[640,256]{1,0:T(8,128)(2,1)S(1)}, u32[]{:S(2)}, u32[]{:S(2)}) collective-permute-start(bf16[640,256]{1,0:T(8,128)(2,1)} %get-tuple-element.81), channel_id=1, source_target_pairs={{0,2},{1,3},{2,0},{3,1},{4,6},{5,7},{6,4},{7,5},{8,10},{9,11},{10,... | collective-permute-start | bytes 983048 | tf_op jit(solution)/shard_map/ppermute | solution.py:575
  188.0 10.9 %collective-permute-start.11 = (bf16[832,256]{1,0:T(8,128)(2,1)S(1)}, bf16[832,256]{1,0:T(8,128)(2,1)S(1)}, u32[]{:S(2)}, u32[]{:S(2)}) collective-permute-start(bf16[832,256]{1,0:T(8,128)(2,1)S(1)} %pad_maximum_fusion.6), channel_id=1, source_target_pairs={{0,16},{8,24},{16,0},{24,8},{1,17},{9,25},{17,1},{25,9},{2,18},{10... | collective-permute-start | bytes 1277960 | tf_op jit(solution)/shard_map/ppermute | solution.py:575
  191.4 7.5 %collective-permute-start.10 = (bf16[512,256]{1,0:T(8,128)(2,1)}, bf16[512,256]{1,0:T(8,128)(2,1)S(1)}, u32[]{:S(2)}, u32[]{:S(2)}) collective-permute-start(bf16[512,256]{1,0:T(8,128)(2,1)} %get-tuple-element.77), channel_id=1, source_target_pairs={{0,1},{1,0},{2,3},{3,2},{4,5},{5,4},{6,7},{7,6},{8,9},{9,8},{10,11... | collective-permute-start | bytes 786440 | tf_op jit(solution)/shard_map/ppermute | solution.py:575
  199.1 6.5 %collective-permute-start.12 = (bf16[512,256]{1,0:T(8,128)(2,1)S(1)}, bf16[512,256]{1,0:T(8,128)(2,1)S(1)}, u32[]{:S(2)}, u32[]{:S(2)}) collective-permute-start(bf16[512,256]{1,0:T(8,128)(2,1)S(1)} %pad_maximum_fusion.13), channel_id=1, source_target_pairs={{0,2},{1,3},{2,0},{3,1},{4,6},{5,7},{6,4},{7,5},{8,10},{9,11},{10,... | collective-permute-start | bytes 786440 | tf_op jit(solution)/shard_map/ppermute | solution.py:575
  199.9 5.7 %collective-permute-start.13 = (bf16[160,256]{1,0:T(8,128)(2,1)S(1)}, bf16[160,256]{1,0:T(8,128)(2,1)S(1)}, u32[]{:S(2)}, u32[]{:S(2)}) collective-permute-start(bf16[160,256]{1,0:T(8,128)(2,1)S(1)} %get-tuple-element.121), channel_id=1, source_target_pairs={{0,1},{1,0},{2,3},{3,2},{4,5},{5,4},{6,7},{7,6},{8,9},{9,8},{10,11... | collective-permute-start | bytes 245768 | tf_op jit(solution)/shard_map/ppermute | solution.py:575
  205.7 11.4 %collective-permute-start.14 = (bf16[336,256]{1,0:T(8,128)(2,1)S(1)}, bf16[336,256]{1,0:T(8,128)(2,1)S(1)}, u32[]{:S(2)}, u32[]{:S(2)}) collective-permute-start(bf16[336,256]{1,0:T(8,128)(2,1)S(1)} %pad_maximum_fusion.14), channel_id=1, source_target_pairs={{0,4},{1,5},{2,6},{3,7},{4,0},{5,1},{6,2},{7,3},{8,12},{9,13},{10,... | collective-permute-start | bytes 516104 | tf_op jit(solution)/shard_map/ppermute | solution.py:575
  217.3 6.9 %collective-permute-start.15 = (bf16[336,256]{1,0:T(8,128)(2,1)S(1)}, bf16[336,256]{1,0:T(8,128)(2,1)S(1)}, u32[]{:S(2)}, u32[]{:S(2)}) collective-permute-start(bf16[336,256]{1,0:T(8,128)(2,1)S(1)} %pad_maximum_fusion.15), channel_id=1, source_target_pairs={{0,4},{1,5},{2,6},{3,7},{4,0},{5,1},{6,2},{7,3},{8,12},{9,13},{10,... | collective-permute-start | bytes 516104 | tf_op jit(solution)/shard_map/ppermute | solution.py:575
  224.3 6.4 %collective-permute-start.16 = (bf16[512,256]{1,0:T(8,128)(2,1)S(1)}, bf16[512,256]{1,0:T(8,128)(2,1)S(1)}, u32[]{:S(2)}, u32[]{:S(2)}) collective-permute-start(bf16[512,256]{1,0:T(8,128)(2,1)S(1)} %get-tuple-element.131), channel_id=1, source_target_pairs={{0,2},{1,3},{2,0},{3,1},{4,6},{5,7},{6,4},{7,5},{8,10},{9,11},{10,... | collective-permute-start | bytes 786440 | tf_op jit(solution)/shard_map/ppermute | solution.py:575
  224.3 5.3 %collective-permute-start.17 = (bf16[160,256]{1,0:T(8,128)(2,1)S(1)}, bf16[160,256]{1,0:T(8,128)(2,1)S(1)}, u32[]{:S(2)}, u32[]{:S(2)}) collective-permute-start(bf16[160,256]{1,0:T(8,128)(2,1)S(1)} %slice_dynamic-update-slice_fusion.6), channel_id=1, source_target_pairs={{0,1},{1,0},{2,3},{3,2},{4,5},{5,4},{6,7},{7,6},{8,9},{9,8},{10,11... | collective-permute-start | bytes 245768 | tf_op jit(solution)/shard_map/ppermute | solution.py:575
  230.7 8.2 %collective-permute-start.18 = (bf16[512,256]{1,0:T(8,128)(2,1)S(1)}, bf16[512,256]{1,0:T(8,128)(2,1)S(1)}, u32[]{:S(2)}, u32[]{:S(2)}) collective-permute-start(bf16[512,256]{1,0:T(8,128)(2,1)S(1)} %get-tuple-element.66), channel_id=1, source_target_pairs={{0,1},{1,0},{2,3},{3,2},{4,5},{5,4},{6,7},{7,6},{8,9},{9,8},{10,11... | collective-permute-start | bytes 786440 | tf_op jit(solution)/shard_map/ppermute | solution.py:575
  231.8 11.9 %collective-permute-start.20 = (bf16[832,256]{1,0:T(8,128)(2,1)S(1)}, bf16[832,256]{1,0:T(8,128)(2,1)S(1)}, u32[]{:S(2)}, u32[]{:S(2)}) collective-permute-start(bf16[832,256]{1,0:T(8,128)(2,1)S(1)} %pad_maximum_fusion.7), channel_id=1, source_target_pairs={{0,16},{8,24},{16,0},{24,8},{1,17},{9,25},{17,1},{25,9},{2,18},{10... | collective-permute-start | bytes 1277960 | tf_op jit(solution)/shard_map/ppermute | solution.py:575
  238.9 10.4 %collective-permute-start.19 = (bf16[1024,256]{1,0:T(8,128)(2,1)S(1)}, bf16[1024,256]{1,0:T(8,128)(2,1)S(1)}, u32[]{:S(2)}, u32[]{:S(2)}) collective-permute-start(bf16[1024,256]{1,0:T(8,128)(2,1)S(1)} %constant_dynamic-update-slice_fusion.3), channel_id=1, source_target_pairs={{0,16},{8,24},{16,0},{24,8},{1,17},{9,25},{17,1},{25,9},{2,18},{10... | collective-permute-start | bytes 1572872 | tf_op jit(solution)/shard_map/ppermute | solution.py:575
  243.7 9.2 %collective-permute-start.21 = (bf16[1024,256]{1,0:T(8,128)(2,1)S(1)}, bf16[1024,256]{1,0:T(8,128)(2,1)S(1)}, u32[]{:S(2)}, u32[]{:S(2)}) collective-permute-start(bf16[1024,256]{1,0:T(8,128)(2,1)S(1)} %slice_dynamic-update-slice_fusion), channel_id=1, source_target_pairs={{0,1},{1,0},{2,3},{3,2},{4,5},{5,4},{6,7},{7,6},{8,9},{9,8},{10,11... | collective-permute-start | bytes 1572872 | tf_op jit(solution)/shard_map/ppermute | solution.py:575
  245.0 8.2 %collective-permute-start.22 = (bf16[640,256]{1,0:T(8,128)(2,1)S(1)}, bf16[640,256]{1,0:T(8,128)(2,1)S(1)}, u32[]{:S(2)}, u32[]{:S(2)}) collective-permute-start(bf16[640,256]{1,0:T(8,128)(2,1)S(1)} %slice_dynamic-update-slice_fusion.1), channel_id=1, source_target_pairs={{0,2},{1,3},{2,0},{3,1},{4,6},{5,7},{6,4},{7,5},{8,10},{9,11},{10,... | collective-permute-start | bytes 983048 | tf_op jit(solution)/shard_map/ppermute | solution.py:575
  249.4 7.3 %collective-permute-start.23 = (bf16[2048,256]{1,0:T(8,128)(2,1)S(1)}, bf16[2048,256]{1,0:T(8,128)(2,1)S(1)}, u32[]{:S(2)}, u32[]{:S(2)}) collective-permute-start(bf16[2048,256]{1,0:T(8,128)(2,1)S(1)} %constant_dynamic-update-slice_fusion.1.own_a), channel_id=1, source_target_pairs={{0,8},{8,0},{16,24},{24,16},{1,9},{9,1},{17,25},{25,17},{2,10},{10... | collective-permute-start | bytes 3145736 | tf_op jit(solution)/shard_map/ppermute | solution.py:575
  253.0 3.7 %collective-permute-start.24 = (bf16[2048,256]{1,0:T(8,128)(2,1)S(1)}, bf16[2048,256]{1,0:T(8,128)(2,1)S(1)}, u32[]{:S(2)}, u32[]{:S(2)}) collective-permute-start(bf16[2048,256]{1,0:T(8,128)(2,1)S(1)} %constant_dynamic-update-slice_fusion.4.own_b), channel_id=1, source_target_pairs={{0,8},{8,0},{16,24},{24,16},{1,9},{9,1},{17,25},{25,17},{2,10},{10... | collective-permute-start | bytes 3145736 | tf_op jit(solution)/shard_map/ppermute | solution.py:575
  253.2 3.5 %collective-permute-start.25 = (bf16[1280,256]{1,0:T(8,128)(2,1)S(1)}, bf16[1280,256]{1,0:T(8,128)(2,1)S(1)}, u32[]{:S(2)}, u32[]{:S(2)}) collective-permute-start(bf16[1280,256]{1,0:T(8,128)(2,1)S(1)} %constant_dynamic-update-slice_fusion.2.own_c), channel_id=1, source_target_pairs={{0,8},{8,0},{16,24},{24,16},{1,9},{9,1},{17,25},{25,17},{2,10},{10... | collective-permute-start | bytes 1966088 | tf_op jit(solution)/shard_map/ppermute | solution.py:575
  (17 other events, 70.6 us)
